TPU v7x, 32 devices: a whole 2x2x4 slice. The times are simulated.
32 devices in a mesh: ctx: 16 (over z, y, core), fsdp: 2 (over x).
Axes of the slice: x: 2, y: 2, z: 4, core: 2. Of those that a mesh axis runs over, the one named last changes fastest.
Arguments:
- stream_in: bfloat16 [1, 4096, 1280], P(None, ('ctx', 'fsdp')), may hold values from -24 to 24
- pairing: int32 [16], replicated, may hold values from 0 to 15, each once
- w_query: bfloat16 [1280, 1280], P('fsdp'), may hold values from -0.15625 to 0.15625
- w_key: bfloat16 [1280, 1280], P('fsdp'), may hold values from -0.15625 to 0.15625
- w_value: bfloat16 [1280, 1280], P('fsdp'), may hold values from -0.15625 to 0.15625
- w_output: bfloat16 [1280, 1280], P('fsdp'), may hold values from -4 to 4
- w_hidden: bfloat16 [1280, 1280], P('fsdp'), may hold values from -0.15625 to 0.15625
- w_return: bfloat16 [1280, 1280], P('fsdp'), may hold values from -0.15625 to 0.15625
- gain_attn: bfloat16 [1280], P('fsdp'), may hold values from 0.099609375 to 1.8984375
- gain_mlp: bfloat16 [1280], P('fsdp'), may hold values from 0.099609375 to 1.8984375
- query_scale: bfloat16 [80], P('fsdp'), may hold values from 0.69921875 to 2.1875
- cotangent: bfloat16 [1, 4096, 1280], P(None, ('ctx', 'fsdp')), may hold values from -6 to 6
Outputs:
- stream_out: bfloat16 [1, 4096, 1280], P(None, ('ctx', 'fsdp'))
- grad_in: bfloat16 [1, 4096, 1280], P(None, ('ctx', 'fsdp'))
- grad_query: float32 [1280, 1280], P('fsdp')
- grad_key: float32 [1280, 1280], P('fsdp')
- value_weight_gradient: float32 [1280, 1280], P('fsdp')
- grad_output: float32 [1280, 1280], P('fsdp')
- grad_hidden: float32 [1280, 1280], P('fsdp')
- return_weight_gradient: float32 [1280, 1280], P('fsdp')
- grad_gain_attn: float32 [1280], P('fsdp')
- grad_gain_mlp: float32 [1280], P('fsdp')
- grad_query_scale: float32 [80], P('fsdp')
- root_means: float32 [2], replicated
All inputs are finite; a program needn't handle non-finite values.
Results may differ from a plain program's by a relative error of at most 0.015.
Values may be sent and summed in bfloat16 or wider, within the bound.
No kernel may reach another device: no remote copies, remote signals or barrier semaphores. Data moves between devices by JAX's collectives and lax.ppermute only.
A program may use at most 576 MiB of HBM per device.

v0:
```python
import jax
import jax.numpy as jnp
from jax import lax
from jax.sharding import PartitionSpec as P

H = 16
HD = 80


EPSILON = 1e-06
LOWEST = -1e30


def split_tiles(shard_rows, half_rows):
    sequences, row_count, model_width = shard_rows.shape
    tiled = shard_rows.reshape(sequences, row_count // half_rows, half_rows, H, HD)
    return jnp.swapaxes(tiled, 0, 1)


def stats_tiles(table, row_count, half_rows):
    sequences = table.shape[0]
    return table.reshape(sequences, row_count // half_rows, half_rows, H).transpose(1, 0, 3, 2)


def tile_blocks(pairing, tile_count, block_count, per_pair):
    tiles = jnp.arange(tile_count, dtype=jnp.int32)
    chosen = jnp.take(pairing, tiles // 2 // per_pair)
    return jnp.where(tiles % 2 == 0, chosen, block_count - 1 - chosen)


def forward_tile(running, queries, key_tile, value_tile):
    maxima, totals, weighted = running
    scores = jnp.einsum("sqhd,skhd->shqk", queries, key_tile, preferred_element_type=jnp.float32)
    new_max = jnp.maximum(maxima, jnp.max(scores, axis=-1))
    rescale_factor = jnp.exp(maxima - new_max)
    weights = jnp.exp(scores - new_max[..., None]).astype(jnp.bfloat16)
    totals = totals * rescale_factor + jnp.sum(weights.astype(jnp.float32), axis=-1)
    weighted = weighted * rescale_factor[..., None] + jnp.einsum(
        "shqk,skhd->shqd", weights, value_tile, preferred_element_type=jnp.float32
    )
    return (new_max, totals, weighted)


def score_grads(queries, key_tile, value_tile, out_grad, log_totals, row_delta):
    scores = jnp.einsum("sqhd,skhd->shqk", queries, key_tile, preferred_element_type=jnp.float32)
    probability = jnp.exp(scores - log_totals[..., None])
    prob_grad = jnp.einsum(
        "sqhd,skhd->shqk", out_grad, value_tile, preferred_element_type=jnp.float32
    )
    score_grad = (probability * (prob_grad - row_delta[..., None])).astype(jnp.bfloat16)
    return (probability, score_grad)


def norm_back(grad_norm, unit, gain, inverse):
    scaled = grad_norm * gain
    return inverse * (scaled - unit * jnp.mean(scaled * unit, axis=-1, keepdims=True))


def per_device(
    stream_in,
    pairing,
    w_query,
    w_key,
    w_value,
    w_output,
    w_hidden,
    w_return,
    gain_attn,
    gain_mlp,
    query_scale,
    cotangent,
):
    sequences, dev_rows, model_width = stream_in.shape
    half_rows = dev_rows // 2
    tokens = sequences * dev_rows
    fsdp_count = lax.axis_size("fsdp")
    ctx_count = lax.axis_size("ctx")
    block_count = 2 * ctx_count
    devices = ctx_count * fsdp_count
    position = lax.axis_index("ctx") * fsdp_count + lax.axis_index("fsdp")
    my_pair = jnp.take(pairing, position // fsdp_count)
    own_blocks = (my_pair, block_count - 1 - my_pair)
    gathered = (
        lax.all_gather(w_query, "fsdp", axis=0, tiled=True),
        lax.all_gather(w_key, "fsdp", axis=0, tiled=True),
        lax.all_gather(w_value, "fsdp", axis=0, tiled=True),
        lax.all_gather(w_output, "fsdp", axis=0, tiled=True),
        lax.all_gather(w_hidden, "fsdp", axis=0, tiled=True),
        lax.all_gather(w_return, "fsdp", axis=0, tiled=True),
        lax.all_gather(gain_attn, "fsdp", axis=0, tiled=True),
        lax.all_gather(gain_mlp, "fsdp", axis=0, tiled=True),
        lax.all_gather(query_scale, "fsdp", axis=0, tiled=True),
    )
    (
        full_query,
        full_key,
        full_value,
        full_output,
        full_hidden,
        full_return,
        full_gain_one,
        full_gain_two,
        full_scale,
    ) = gathered
    inputs = stream_in.reshape(tokens, model_width).astype(jnp.float32)
    inv_one = lax.rsqrt(jnp.mean(inputs * inputs, axis=-1, keepdims=True) + EPSILON)
    unit_one = inputs * inv_one
    gain_one = full_gain_one.astype(jnp.float32)
    norm_one = (unit_one * gain_one).astype(jnp.bfloat16)
    w_qkv = jnp.concatenate([full_query, full_key, full_value], axis=1)
    projected = jnp.dot(norm_one, w_qkv, preferred_element_type=jnp.float32)
    q_pre = projected[:, :model_width]
    scale_vec = jnp.tile(full_scale.astype(jnp.float32), H) * HD ** (-0.5)
    q_rows = (q_pre * scale_vec).astype(jnp.bfloat16)
    k_rows = projected[:, model_width : 2 * model_width].astype(jnp.bfloat16)
    v_rows = projected[:, 2 * model_width :].astype(jnp.bfloat16)
    heads_shape = (sequences, 2, half_rows, H, HD)
    q_local = q_rows.reshape(heads_shape)
    k_local = k_rows.reshape(heads_shape)
    v_local = v_rows.reshape(heads_shape)

    def fresh_state():
        return (
            jnp.full((sequences, H, half_rows), LOWEST, jnp.float32),
            jnp.zeros((sequences, H, half_rows), jnp.float32),
            jnp.zeros((sequences, H, half_rows, HD), jnp.float32),
        )

    k_shard = k_rows.reshape(sequences, dev_rows, model_width)
    v_shard = v_rows.reshape(sequences, dev_rows, model_width)
    shard_rows = (
        lax.all_gather(k_shard, ("ctx", "fsdp"), axis=1, tiled=True),
        lax.all_gather(v_shard, ("ctx", "fsdp"), axis=1, tiled=True),
    )
    key_tiles = split_tiles(shard_rows[0], half_rows)
    value_tiles = split_tiles(shard_rows[1], half_rows)
    blocks_here = tile_blocks(pairing, key_tiles.shape[0], block_count, fsdp_count)

    def forward_advance(current, element):
        key_tile, value_tile, block_id = element
        updated = []
        for which_half in range(2):

            def forward_update(state, which_half=which_half):
                return forward_tile(state, q_local[:, which_half], key_tile, value_tile)

            updated.append(
                lax.cond(
                    block_id <= own_blocks[which_half],
                    forward_update,
                    lambda state: state,
                    current[which_half],
                )
            )
        return (tuple(updated), None)

    halves = lax.scan(
        forward_advance, (fresh_state(), fresh_state()), (key_tiles, value_tiles, blocks_here)
    )[0]

    def join_halves(pair_of):
        return jnp.stack([part.transpose(0, 2, 1, 3) for part in pair_of], axis=1).reshape(
            tokens, model_width
        )

    attended = join_halves(
        tuple((halves[which][2] / halves[which][1][..., None] for which in range(2)))
    )
    lse_half = tuple((halves[which][0] + jnp.log(halves[which][1]) for which in range(2)))
    attended_b = attended.astype(jnp.bfloat16)
    attn = jnp.dot(attended_b, full_output, preferred_element_type=jnp.float32)
    middle = inputs + attn
    inv_two = lax.rsqrt(jnp.mean(middle * middle, axis=-1, keepdims=True) + EPSILON)
    unit_two = middle * inv_two
    gain_two = full_gain_two.astype(jnp.float32)
    norm_two = (unit_two * gain_two).astype(jnp.bfloat16)
    hidden = jnp.dot(norm_two, full_hidden, preferred_element_type=jnp.float32)
    active = jax.nn.silu(hidden).astype(jnp.bfloat16)
    mlp = jnp.dot(active, full_return, preferred_element_type=jnp.float32)
    output = middle + mlp
    squares = lax.psum((jnp.sum(output * output), jnp.sum(attn * attn)), ("ctx", "fsdp"))
    root_means = jnp.sqrt(jnp.stack(squares) / (tokens * devices * model_width))
    again = (
        lax.all_gather(w_query, "fsdp", axis=0, tiled=True),
        lax.all_gather(w_key, "fsdp", axis=0, tiled=True),
        lax.all_gather(w_value, "fsdp", axis=0, tiled=True),
        lax.all_gather(w_output, "fsdp", axis=0, tiled=True),
        lax.all_gather(w_hidden, "fsdp", axis=0, tiled=True),
        lax.all_gather(w_return, "fsdp", axis=0, tiled=True),
        lax.all_gather(gain_attn, "fsdp", axis=0, tiled=True),
        lax.all_gather(gain_mlp, "fsdp", axis=0, tiled=True),
        lax.all_gather(query_scale, "fsdp", axis=0, tiled=True),
    )
    back_qkv = jnp.concatenate([again[0], again[1], again[2]], axis=1)
    back_output, backward_hidden_state, back_return = (again[3], again[4], again[5])
    out_grad = cotangent.reshape(tokens, model_width)
    return_weight_gradient = jnp.einsum(
        "tf,td->fd", active, out_grad, preferred_element_type=jnp.float32
    )
    d_active = jnp.einsum("td,fd->tf", out_grad, back_return, preferred_element_type=jnp.float32)
    sigmoid_h = jax.nn.sigmoid(hidden)
    d_hidden = (d_active * sigmoid_h * (1.0 + hidden * (1.0 - sigmoid_h))).astype(jnp.bfloat16)
    grad_hidden = jnp.einsum("td,tf->df", norm_two, d_hidden, preferred_element_type=jnp.float32)
    gradient_second_norm = jnp.einsum(
        "tf,df->td", d_hidden, backward_hidden_state, preferred_element_type=jnp.float32
    )
    grad_gain_two = jnp.sum(gradient_second_norm * unit_two, axis=0)
    d_middle = norm_back(gradient_second_norm, unit_two, gain_two, inv_two) + out_grad.astype(
        jnp.float32
    )
    d_middle_b = d_middle.astype(jnp.bfloat16)
    grad_output = jnp.einsum(
        "td,te->de", attended_b, d_middle_b, preferred_element_type=jnp.float32
    )
    d_att = jnp.einsum(
        "te,de->td", d_middle_b, back_output, preferred_element_type=jnp.float32
    ).astype(jnp.bfloat16)
    delta_rows = jnp.sum((d_att.astype(jnp.float32) * attended).reshape(heads_shape), axis=-1)
    delta_half = tuple((delta_rows[:, which].transpose(0, 2, 1) for which in range(2)))
    lse_rows = jnp.stack([lse_half[which].transpose(0, 2, 1) for which in range(2)], axis=1)
    d_att_local = d_att.reshape(heads_shape)
    lse_all, delta_all = (
        lax.all_gather(
            lse_rows.reshape(sequences, dev_rows, H), ("ctx", "fsdp"), axis=1, tiled=True
        ),
        lax.all_gather(
            delta_rows.reshape(sequences, dev_rows, H), ("ctx", "fsdp"), axis=1, tiled=True
        ),
    )

    def query_side(grads_q, key_tile, value_tile, block_id):
        updated = []
        for which_half in range(2):

            def query_update(summed, which_half=which_half):
                probability, score_grad = score_grads(
                    q_local[:, which_half],
                    key_tile,
                    value_tile,
                    d_att_local[:, which_half],
                    lse_half[which_half],
                    delta_half[which_half],
                )
                return summed + jnp.einsum(
                    "shqk,skhd->shqd", score_grad, key_tile, preferred_element_type=jnp.float32
                )

            updated.append(
                lax.cond(
                    block_id <= own_blocks[which_half],
                    query_update,
                    lambda summed: summed,
                    grads_q[which_half],
                )
            )
        return tuple(updated)

    def key_side(grads_kv, query_tile, grad_tile, lse_tile, delta_tile, block_id):
        updated = []
        for which_half in range(2):

            def key_update(summed, which_half=which_half):
                probability, score_grad = score_grads(
                    query_tile,
                    k_local[:, which_half],
                    v_local[:, which_half],
                    grad_tile,
                    lse_tile,
                    delta_tile,
                )
                key_grad = summed[0] + jnp.einsum(
                    "shqk,sqhd->shkd", score_grad, query_tile, preferred_element_type=jnp.float32
                )
                value_grad = summed[1] + jnp.einsum(
                    "shqk,sqhd->shkd",
                    probability.astype(jnp.bfloat16),
                    grad_tile,
                    preferred_element_type=jnp.float32,
                )
                return (key_grad, value_grad)

            updated.append(
                lax.cond(
                    block_id >= own_blocks[which_half],
                    key_update,
                    lambda summed: summed,
                    grads_kv[which_half],
                )
            )
        return tuple(updated)

    zeros_half = jnp.zeros((sequences, H, half_rows, HD), jnp.float32)
    start_q = (zeros_half, zeros_half)
    start_kv = ((zeros_half, zeros_half), (zeros_half, zeros_half))
    q_shard = q_rows.reshape(sequences, dev_rows, model_width)
    grad_shard = d_att.reshape(sequences, dev_rows, model_width)
    shard_rows = (
        lax.all_gather(k_shard, ("ctx", "fsdp"), axis=1, tiled=True),
        lax.all_gather(v_shard, ("ctx", "fsdp"), axis=1, tiled=True),
    )
    key_tiles = split_tiles(shard_rows[0], half_rows)
    value_tiles = split_tiles(shard_rows[1], half_rows)
    blocks_here = tile_blocks(pairing, key_tiles.shape[0], block_count, fsdp_count)

    def query_advance(current, element):
        return (query_side(current, element[0], element[1], element[2]), None)

    grads_q = lax.scan(query_advance, start_q, (key_tiles, value_tiles, blocks_here))[0]
    shard_rows = (
        lax.all_gather(q_shard, ("ctx", "fsdp"), axis=1, tiled=True),
        lax.all_gather(grad_shard, ("ctx", "fsdp"), axis=1, tiled=True),
    )
    query_tiles = split_tiles(shard_rows[0], half_rows)
    grad_tiles = split_tiles(shard_rows[1], half_rows)
    tile_count = query_tiles.shape[0]
    lse_tiles = stats_tiles(lse_all, tile_count * half_rows, half_rows)
    delta_tiles = stats_tiles(delta_all, tile_count * half_rows, half_rows)
    blocks_here = tile_blocks(pairing, tile_count, block_count, fsdp_count)

    def key_advance(current, element):
        return (key_side(current, element[0], element[1], element[2], element[3], element[4]), None)

    grads_kv = lax.scan(
        key_advance, start_kv, (query_tiles, grad_tiles, lse_tiles, delta_tiles, blocks_here)
    )[0]
    d_queries = join_halves(grads_q)
    d_keys = join_halves((grads_kv[0][0], grads_kv[1][0]))
    d_values = join_halves((grads_kv[0][1], grads_kv[1][1]))
    grad_scale = jnp.sum((d_queries * q_pre).reshape(tokens, H, HD), axis=(0, 1)) * HD ** (-0.5)
    d_qkv = jnp.concatenate(
        [
            (d_queries * scale_vec).astype(jnp.bfloat16),
            d_keys.astype(jnp.bfloat16),
            d_values.astype(jnp.bfloat16),
        ],
        axis=1,
    )
    grad_qkv = jnp.einsum("td,te->de", norm_one, d_qkv, preferred_element_type=jnp.float32)
    d_norm_one = jnp.einsum("te,de->td", d_qkv, back_qkv, preferred_element_type=jnp.float32)
    grad_gain_one = jnp.sum(d_norm_one * unit_one, axis=0)
    d_inputs = norm_back(d_norm_one, unit_one, gain_one, inv_one) + d_middle
    shares = (
        lax.psum_scatter(
            grad_qkv[:, :model_width].astype(jnp.bfloat16), "fsdp", scatter_dimension=0, tiled=True
        ).astype(jnp.float32),
        lax.psum_scatter(
            grad_qkv[:, model_width : 2 * model_width].astype(jnp.bfloat16),
            "fsdp",
            scatter_dimension=0,
            tiled=True,
        ).astype(jnp.float32),
        lax.psum_scatter(
            grad_qkv[:, 2 * model_width :].astype(jnp.bfloat16),
            "fsdp",
            scatter_dimension=0,
            tiled=True,
        ).astype(jnp.float32),
        lax.psum_scatter(
            grad_output.astype(jnp.bfloat16), "fsdp", scatter_dimension=0, tiled=True
        ).astype(jnp.float32),
        lax.psum_scatter(
            grad_hidden.astype(jnp.bfloat16), "fsdp", scatter_dimension=0, tiled=True
        ).astype(jnp.float32),
        lax.psum_scatter(
            return_weight_gradient.astype(jnp.bfloat16), "fsdp", scatter_dimension=0, tiled=True
        ).astype(jnp.float32),
        lax.psum_scatter(
            grad_gain_one.astype(jnp.bfloat16), "fsdp", scatter_dimension=0, tiled=True
        ).astype(jnp.float32),
        lax.psum_scatter(
            grad_gain_two.astype(jnp.bfloat16), "fsdp", scatter_dimension=0, tiled=True
        ).astype(jnp.float32),
        lax.psum_scatter(
            grad_scale.astype(jnp.bfloat16), "fsdp", scatter_dimension=0, tiled=True
        ).astype(jnp.float32),
    )
    totals = lax.psum(
        (
            shares[0],
            shares[1],
            shares[2],
            shares[3],
            shares[4],
            shares[5],
            shares[6],
            shares[7],
            shares[8],
        ),
        "ctx",
    )
    stream_out = output.astype(jnp.bfloat16).reshape(sequences, dev_rows, model_width)
    grad_in = d_inputs.astype(jnp.bfloat16).reshape(sequences, dev_rows, model_width)
    return (
        stream_out,
        grad_in,
        totals[0],
        totals[1],
        totals[2],
        totals[3],
        totals[4],
        totals[5],
        totals[6],
        totals[7],
        totals[8],
        root_means,
    )


def solution(mesh):
    return jax.shard_map(
        per_device,
        mesh=mesh,
        in_specs=(
            P(None, ("ctx", "fsdp"), None),
            P(),
            P("fsdp", None),
            P("fsdp", None),
            P("fsdp", None),
            P("fsdp", None),
            P("fsdp", None),
            P("fsdp", None),
            P("fsdp"),
            P("fsdp"),
            P("fsdp"),
            P(None, ("ctx", "fsdp"), None),
        ),
        out_specs=(
            P(None, ("ctx", "fsdp"), None),
            P(None, ("ctx", "fsdp"), None),
            P("fsdp", None),
            P("fsdp", None),
            P("fsdp", None),
            P("fsdp", None),
            P("fsdp", None),
            P("fsdp", None),
            P("fsdp"),
            P("fsdp"),
            P("fsdp"),
            P(),
        ),
        check_vma=False,
    )
```

profile of v0, /device:TPU:0, one launch (start us, length us, event | category | flops | bytes accessed | tf_op | source)
XLA Modules:
  0.0 2353.8 jit_solution(8535200155926572912)
XLA Ops:
  9.5 5.2 all-gather.4
  14.9 43.8 %all-gather.17.cloned.1.call-done = bf16[1280,1280]{1,0:T(8,128)(2,1)} async-done(((bf16[640,1280]{1,0:T(8,128)(2,1)}), bf16[1280,1280]{1,0:T(8,128)(2,1)}) %all-gather.17.cloned.1.call-update) | async-done | bytes 3276816 | tf_op jit(solution)/shard_map/all_gather | solution.py:84
  58.7 3.9 constant_dynamic-update-slice_fusion.2
  62.6 44.1 %all-gather.19.cloned.1.call-done = bf16[1280,1280]{1,0:T(8,128)(2,1)} async-done(((bf16[640,1280]{1,0:T(8,128)(2,1)}), bf16[1280,1280]{1,0:T(8,128)(2,1)}) %all-gather.19.cloned.1.call-update) | async-done | bytes 3276816 | tf_op jit(solution)/shard_map/all_gather | solution.py:85
  106.7 3.9 constant_dynamic-update-slice_fusion.1
  110.6 44.1 %all-gather.21.cloned.1.call-done = bf16[1280,1280]{1,0:T(8,128)(2,1)} async-done(((bf16[640,1280]{1,0:T(8,128)(2,1)}), bf16[1280,1280]{1,0:T(8,128)(2,1)}) %all-gather.21.cloned.1.call-update) | async-done | bytes 3276816 | tf_op jit(solution)/shard_map/all_gather | solution.py:86
  154.7 3.9 constant_dynamic-update-slice_fusion
  158.6 5.3 fusion.115
  169.1 4.9 all-reduce
  176.4 4.3 all-gather.5
  183.9 68.0 %all-gather.29.cloned.1.call-done = bf16[4096,1280]{1,0:T(8,128)(2,1)} async-done(((bf16[128,1280]{1,0:T(8,128)(2,1)}), bf16[4096,1280]{1,0:T(8,128)(2,1)}) %all-gather.29.cloned.1.call-update) | async-done | bytes 10485776 | tf_op jit(solution)/shard_map/all_gather | solution.py:132
  251.8 29.8 %transpose_reshape.14 = bf16[64,1,64,16,80]{4,3,2,0,1:T(8,128)(2,1)} reshape(bf16[4096,1280]{1,0:T(8,128)(2,1)} %all-gather.29.cloned.1.call-done) | data formatting | bytes 20971520 | tf_op jit(solution)/shard_map/transpose;reshape | solution.py:17
  281.7 16.6 copy.97
  298.3 42.2 %all-gather.31.cloned.1.call-done = bf16[4096,1280]{1,0:T(8,128)(2,1)} async-done(((bf16[128,1280]{1,0:T(8,128)(2,1)}), bf16[4096,1280]{1,0:T(8,128)(2,1)}) %all-gather.31.cloned.1.call-update) | async-done | bytes 10485776 | tf_op jit(solution)/shard_map/all_gather | solution.py:133
  340.5 29.7 %transpose_reshape.15 = bf16[64,1,64,16,80]{4,3,2,0,1:T(8,128)(2,1)} reshape(bf16[4096,1280]{1,0:T(8,128)(2,1)} %all-gather.31.cloned.1.call-done) | data formatting | bytes 20971520 | tf_op jit(solution)/shard_map/transpose;reshape | solution.py:17
  370.2 16.6 copy.98
  387.0 291.4 %while.55 = (s32[]{:T(128)}, f32[1,16,64]{2,1,0:T(8,128)S(1)}, f32[1,16,64]{2,1,0:T(8,128)S(1)}, f32[1,16,64,80]{3,2,1,0:T(8,128)S(1)}, f32[1,16,64]{2,1,0:T(8,1...) while((s32[]{:T(128)}, f32[1,16,64]{2,1,0:T(8,128)S(1)}, ...), condition=%wide.region_10.12_spmd, body=%wide.region_1.11_spmd.sunk | while | flops 43194372 | bytes 5046657 | solution.py:157
  682.2 3.2 multiply_reduce_fusion.5
  688.4 3.4 fusion.81
  696.4 3.8 convolution_convert_fusion.2
  717.9 345.4 %while.56 = (s32[]{:T(128)}, f32[1,16,64,80]{3,2,1,0:T(8,128)S(1)}, f32[1,16,64,80]{3,2,1,0:T(8,128)S(1)}, s32[64]{0:T(128)}, s32[]{:T(128)}, /*index=5*/bf16[64...) while((s32[]{:T(128)}, f32[1,16,64,80]{3,2,1,0:T(8,128)S(1)}, ...), condition=%wide.region_19.21_spmd, body=%wide.region_14.20_spmd.sunk | while | flops 63602692 | bytes 6578489 | solution.py:308
  1064.6 89.6 %all_gather.67 = f32[1,4096,16]{1,2,0:T(8,128)S(1)} all-gather(f32[1,128,16]{1,2,0:T(8,128)S(1)} %copy.124), channel_id=1, replica_groups=mesh['ctx'=16,'fsdp'=2] {'ctx','fsdp'}, dimensions={1}, use_global_device_ids=true | all-gather | bytes 270336 | tf_op jit(solution)/shard_map/all_gather | solution.py:226
  1156.0 64.7 %all_gather.65 = f32[1,4096,16]{1,2,0:T(8,128)S(1)} all-gather(f32[1,128,16]{1,2,0:T(8,128)S(1)} %reshape.331), channel_id=1, replica_groups=mesh['ctx'=16,'fsdp'=2] {'ctx','fsdp'}, dimensions={1}, use_global_device_ids=true | all-gather | bytes 270336 | tf_op jit(solution)/shard_map/all_gather | solution.py:223
  1226.9 29.7 %transpose_reshape.16 = bf16[64,1,64,16,80]{4,3,2,0,1:T(8,128)(2,1)} reshape(bf16[4096,1280]{1,0:T(8,128)(2,1)} %all-gather.33.cloned.1.call-done) | data formatting | bytes 20971520 | tf_op jit(solution)/shard_map/transpose;reshape | solution.py:17
  1256.6 29.7 %transpose_reshape.17 = bf16[64,1,64,16,80]{4,3,2,0,1:T(8,128)(2,1)} reshape(bf16[4096,1280]{1,0:T(8,128)(2,1)} %all-gather.35.cloned.1.call-done) | data formatting | bytes 20971520 | tf_op jit(solution)/shard_map/transpose;reshape | solution.py:17
  1286.5 500.7 %while.57 = (s32[]{:T(128)}, f32[1,16,64,80]{3,2,1,0:T(8,128)S(1)}, f32[1,16,64,80]{3,2,1,0:T(8,128)S(1)}, f32[1,16,64,80]{3,2,1,0:T(8,128)S(1)}, f32[1,16,64,80...) while((s32[]{:T(128)}, f32[1,16,64,80]{3,2,1,0:T(8,128)S(1)}, ...), condition=%wide.region_25.27_spmd, body=%wide.region_20.26_spmd.sunk | while | flops 84869120 | bytes 7897485 | solution.py:323
  1363.1 3.0 conditional.17
  1378.6 3.0 conditional.17
  1394.1 3.0 conditional.17
  1409.5 3.0 conditional.17
  1425.0 3.0 conditional.17
  1440.4 3.0 conditional.17
  1486.8 3.0 conditional.17
  1502.3 3.0 conditional.17
  1548.7 3.0 conditional.17
  1564.1 3.0 conditional.17
  1641.4 3.0 conditional.17
  1656.9 3.0 conditional.17
  1687.8 3.0 conditional.17
  1789.5 3.1 convolution_convert_fusion
  1792.7 3.9 fusion.112
  1798.9 4.1 multiply_reduce_fusion.1
  1803.0 38.3 %all-reduce.4 = (f32[1]{0:T(128)}, f32[1]{0:T(128)}) all-reduce(f32[1]{0:T(128)} %bitcast.96, f32[1]{0:T(128)} %bitcast.95), channel_id=1, replica_groups=mesh['ctx'=16,'fsdp'=2] {'ctx','fsdp'}, use_global_device_ids=true, to_apply=%region_52.54 | all-reduce | flops 2 | bytes 16 | tf_op jit(solution)/shard_map/psum | solution.py:181
  1843.4 8.2 fusion.92
  1851.6 5.5 all-reduce.6
  1859.4 29.1 %reduce-scatter.9.cloned.1.call-done = bf16[640,1280]{1,0:T(8,128)(2,1)} async-done(((bf16[1280,1280]{1,0:T(8,128)(2,1)}), bf16[640,1280]{1,0:T(8,128)(2,1)}) %reduce-scatter.9.cloned.1.call-update) | async-done | bytes 1638416 | tf_op jit(solution)/shard_map/reduce_scatter | solution.py:346
  1888.6 47.6 %reduce-scatter.11.cloned.1.call-done = bf16[640,1280]{1,0:T(8,128)(2,1)} async-done(((bf16[1280,1280]{1,0:T(8,128)(2,1)}), bf16[640,1280]{1,0:T(8,128)(2,1)}) %reduce-scatter.11.cloned.1.call-update) | async-done | bytes 1638416 | tf_op jit(solution)/shard_map/reduce_scatter | solution.py:352
  1936.1 410.9 %all-reduce.8 = (f32[640,1280]{1,0:T(8,128)}, f32[640,1280]{1,0:T(8,128)}, f32[640,1280]{1,0:T(8,128)}, f32[640,1280]{1,0:T(8,128)}, f32[640,1280]{1,0:T(8,128)}...) all-reduce(bf16[640,1280]{1,0:T(8,128)(2,1)} %reduce-scatter.7.clon, ...), channel_id=1, replica_groups=mesh['ctx'=16,'fsdp'=2] {'ctx'}, use_global_device_ids=true, to_apply=%region_28.30 | all-reduce | flops 4916520 | bytes 29501760 | tf_op jit(solution)/shard_map/psum | solution.py:377
  (1884 shorter events, 1256.2 us)
Async XLA Ops:
  7.2 2.3 copy-start.38
  7.2 7.6 copy-start.5
  7.2 51.5 %all-gather.17.cloned.1.call-start = ((), (), s32[]{:S(2)}) async-start(), calls=%async_computation.6 | async-start | bytes 4915200 | tf_op jit(solution)/shard_map/all_gather | solution.py:84
  7.9 98.8 %all-gather.19.cloned.1.call-start = ((), (), s32[]{:S(2)}) async-start(), calls=%async_computation.7 | async-start | bytes 4915200 | tf_op jit(solution)/shard_map/all_gather | solution.py:85
  8.7 146.0 %all-gather.21.cloned.1.call-start = ((), (), s32[]{:S(2)}) async-start(), calls=%async_computation.8 | async-start | bytes 4915200 | tf_op jit(solution)/shard_map/all_gather | solution.py:86
  9.4 242.4 %all-gather.29.cloned.1.call-start = ((), (), s32[]{:S(2)}) async-start(), calls=%async_computation.18 | async-start | bytes 10813440 | tf_op jit(solution)/shard_map/all_gather | solution.py:132
  14.8 143.8 %copy-start.30 = (f32[1280]{0:T(1024)}, f32[1280]{0:T(1024)S(1)}, u32[]{:S(2)}) copy-start(f32[1280]{0:T(1024)S(1)} %reshape.393) | copy-start | bytes 15364
  14.9 143.7 %copy-start.35 = (f32[128]{0:T(128)}, f32[128]{0:T(128)S(1)}, u32[]{:S(2)}) copy-start(f32[128]{0:T(128)S(1)} %add_rsqrt_fusion.1) | copy-start | bytes 1540
  163.9 10.2 copy-start.8
  163.9 3.7 copy-start.37
  163.9 4.9 copy-start.40
  164.9 175.6 %all-gather.31.cloned.1.call-start = ((), (), s32[]{:S(2)}) async-start(), calls=%async_computation.19 | async-start | bytes 10813440 | tf_op jit(solution)/shard_map/all_gather | solution.py:133
  164.9 10.1 copy-start
  165.4 10.9 copy-start.39
  165.5 516.7 %all-gather.23.cloned.1.call-start = ((), (), s32[]{:S(2)}) async-start(), calls=%async_computation.9 | async-start | bytes 4915200 | tf_op jit(solution)/shard_map/all_gather | solution.py:87
  166.0 519.4 %all-gather.25.cloned.1.call-start = ((), (), s32[]{:S(2)}) async-start(), calls=%async_computation.10 | async-start | bytes 4915200 | tf_op jit(solution)/shard_map/all_gather | solution.py:88
  166.8 521.6 %all-gather.27.cloned.1.call-start = ((), (), s32[]{:S(2)}) async-start(), calls=%async_computation.11 | async-start | bytes 4915200 | tf_op jit(solution)/shard_map/all_gather | solution.py:89
  167.5 1059.3 %all-gather.33.cloned.1.call-start = ((), (), s32[]{:S(2)}) async-start(), calls=%async_computation.20 | async-start | bytes 10813440 | tf_op jit(solution)/shard_map/all_gather | solution.py:310
  174.1 107.5 %copy-start.32 = (f32[1280]{0:T(1024)}, f32[1280]{0:T(1024)S(1)}, u32[]{:S(2)}) copy-start(f32[1280]{0:T(1024)S(1)} %mul.200) | copy-start | bytes 15364
  174.9 1081.7 %all-gather.35.cloned.1.call-start = ((), (), s32[]{:S(2)}) async-start(), calls=%async_computation.21 | async-start | bytes 10813440 | tf_op jit(solution)/shard_map/all_gather | solution.py:311
  678.4 3.7 copy-start.24
  678.4 3.7 copy-start.26
  685.4 11.0 copy-start.1
  685.5 2.9 copy-start.19
  688.3 3.4 copy-start.12
  688.4 3.4 copy-start.3
  693.9 20.5 copy-start.6
  696.1 4.2 copy-start.10
  696.1 5.8 copy-start.9
  696.2 1147.2 %reduce-scatter.15.cloned.1.call-start = ((), (), s32[]{:S(2)}) async-start(), calls=%async_computation.16 | async-start | bytes 4915200 | tf_op jit(solution)/shard_map/reduce_scatter | solution.py:361
  700.2 7.3 copy-start.11
  700.3 1143.1 %reduce-scatter.13.cloned.1.call-start = ((), (), s32[]{:S(2)}) async-start(), calls=%async_computation.15 | async-start | bytes 4915200 | tf_op jit(solution)/shard_map/reduce_scatter | solution.py:358
  703.5 5.6 copy-start.15
  703.5 10.3 copy-start.25
  703.5 10.3 copy-start.27
  709.1 4.5 copy-start.16
  717.2 1126.2 %reduce-scatter.17.cloned.1.call-start = ((), (), s32[]{:S(2)}) async-start(), calls=%async_computation.17 | async-start | bytes 4915200 | tf_op jit(solution)/shard_map/reduce_scatter | solution.py:364
  1063.4 158.3 %copy-start.33 = (f32[1280]{0:T(1024)S(1)}, f32[1280]{0:T(1024)}, u32[]{:S(2)}) copy-start(f32[1280]{0:T(1024)} %copy-done.32) | copy-start | bytes 15364
  1064.1 159.5 %copy-start.13 = (f32[128,1280]{1,0:T(8,128)S(1)}, f32[128,1280]{1,0:T(8,128)}, u32[]{:S(2)}) copy-start(f32[128,1280]{1,0:T(8,128)} %copy-done.12) | copy-start | bytes 1966084
  1064.1 159.5 %copy-start.21 = (bf16[1,128,1280]{2,1,0:T(8,128)(2,1)S(1)}, bf16[1,128,1280]{2,1,0:T(8,128)(2,1)}, u32[]{:S(2)}) copy-start(bf16[1,128,1280]{2,1,0:T(8,128)(2,1)} %param.43) | copy-start | bytes 983044
  1226.4 633.0 %reduce-scatter.7.cloned.1.call-start = ((), (), s32[]{:S(2)}) async-start(), calls=%async_computation.12 | async-start | bytes 4915200 | tf_op jit(solution)/shard_map/reduce_scatter | solution.py:343
  1789.5 3.2 copy-start.23
  1796.6 91.9 %reduce-scatter.9.cloned.1.call-start = ((), (), s32[]{:S(2)}) async-start(), calls=%async_computation.13 | async-start | bytes 4915200 | tf_op jit(solution)/shard_map/reduce_scatter | solution.py:346
  1796.7 2.2 copy-start.2
  1797.2 138.9 %reduce-scatter.11.cloned.1.call-start = ((), (), s32[]{:S(2)}) async-start(), calls=%async_computation.14 | async-start | bytes 4915200 | tf_op jit(solution)/shard_map/reduce_scatter | solution.py:352
  1843.3 8.3 copy-start.34
  1843.3 14.0 copy-start.7
  1843.4 92.8 %copy-start.17 = (bf16[640,1280]{1,0:T(8,128)(2,1)S(1)}, bf16[640,1280]{1,0:T(8,128)(2,1)}, u32[]{:S(2)}) copy-start(bf16[640,1280]{1,0:T(8,128)(2,1)} %reduce-scatter.15.cloned.1.call-done) | copy-start | bytes 4915204
  (9 other events, 15.9 us)
Sparse Core Ops, SparseCore 0:
  9.6 49.0 all-gather.16
  60.3 46.4 all-gather.18
  108.3 46.3 all-gather.20
  165.0 86.8 all-gather.28
  255.1 85.2 all-gather.30
  341.9 44.9 all-gather.22
  388.4 46.4 all-gather.24
  436.4 46.4 all-gather.26
  485.7 86.7 all-gather.32
  696.2 85.3 all-gather.34
  784.4 43.2 reduce-scatter.14
  830.5 44.7 reduce-scatter.12
  1226.5 42.8 reduce-scatter.16
  1796.7 43.6 reduce-scatter.6
  1843.1 45.3 reduce-scatter.8
  1891.3 44.7 reduce-scatter.10
where the time goes:
time: 2390 us; the launch traced here: 2350 us
  local copies, waits for them, and re-layouts  705 us (29%)
  blocking collectives  624 us (26%)
  matrix products  394 us (16%)
  waiting for transfers between devices  325 us (14%)
  loops' own time  268 us (11%)
    psum x1, blocking collectives, per_device(): lax.psum((shares[0], shares[1], shares[2], shares[3], shares[4], shares[5...  411 us
    dynamic_slice x384, local copies, waits for them, and re-layouts, per_device(): lax.scan(forward_advance, (fresh_state(), fresh_state()), (key_tiles, val...  316 us
    squeeze x128, local copies, waits for them, and re-layouts, per_device(): lax.scan(forward_advance, (fresh_state(), fresh_state()), (key_tiles, val...  137 us
    dot_general x132, matrix products, score_grads(): jnp.einsum('sqhd,skhd->shqk', queries, key_tile, preferred_element_type=j...  131 us
    another operation x4, local copies, waits for them, and re-layouts, split_tiles(): return jnp.swapaxes(tiled, 0, 1)  119 us
    dot_general x66, matrix products, key_update(): jnp.einsum('shqk,sqhd->shkd', score_grad, query_tile, preferred_element_t...  94.8 us
    all_gather x1, blocking collectives, per_device(): lax.all_gather(delta_rows.reshape(sequences, dev_rows, H), ('ctx', 'fsdp'...  89.6 us
    another operation x1, loops' own time, per_device(): lax.scan(key_advance, start_kv, (query_tiles, grad_tiles, lse_tiles, delt...  86.8 us
  transfers between devices with their start and end apart: 16, of which 7 were waited for; matrix products, arithmetic and copies ran while one was open for 47% of the time, Pallas kernels for 0%

commit v1 on v0

v1 whole, which is shorter than its diff:
```python
import functools

import jax
import jax.numpy as jnp
import numpy as np
from jax import lax
from jax.experimental import pallas as pl
from jax.experimental.pallas import tpu as pltpu
from jax.sharding import PartitionSpec as P

H = 16
HD = 80
EPSILON = 1e-06
LOWEST = -1e30
BF = jnp.bfloat16
F32 = jnp.float32
MIB = 1024 * 1024
FLOPS_A_US = 1.15e9

GROUP = 16
CHIPS = 8
RING = (0, 2, 4, 6, 7, 5, 3, 1)
ORDER = (
    ((0, 0), (0, 1))
    + tuple((off, core) for s in (1, 2, 3) for core in (0, 1) for off in (-s, s))
    + ((4, 0), (4, 1))
)
SOURCE = [
    [RING[(RING.index(h // 2) + off) % CHIPS] * 2 + ((h % 2) ^ core) for off, core in ORDER]
    for h in range(GROUP)
]
PLACE = [
    [((h % 2) ^ core) * CHIPS + (RING.index(h // 2) + off) % CHIPS for off, core in ORDER]
    for h in range(GROUP)
]

OWN_ENTRIES = (0, 2, 3, 6, 7, 10, 11, 14)
SIB_ENTRIES = (1, 4, 5, 8, 9, 12, 13, 15)

NN = (((1,), (0,)), ((), ()))
NT = (((1,), (1,)), ((), ()))
TN = (((0,), (0,)), ((), ()))


def dot(a, b, dims):
    return lax.dot_general(a, b, dims, preferred_element_type=F32)


def call(body, outs, ins, scratch=(), specs=None, out_specs=None, name=None, smem=0, after=(), grid=None, aliases=None, us=1.0, mib=24):
    given = len(ins)
    waits = len(after)

    def run(*refs):
        body(*refs[:given], *refs[given + waits :])

    if specs is None:
        specs = [pl.BlockSpec(memory_space=pltpu.VMEM)] * (given - smem)
    specs = list(specs) + [pl.BlockSpec(memory_space=pl.ANY)] * waits
    out_specs = out_specs or [pl.BlockSpec(memory_space=pltpu.VMEM)] * len(outs)
    if grid is None:
        how = dict(
            in_specs=[pl.BlockSpec(memory_space=pltpu.SMEM)] * smem + specs,
            out_specs=out_specs,
            scratch_shapes=list(scratch),
        )
    else:
        how = dict(
            grid_spec=pltpu.PrefetchScalarGridSpec(
                num_scalar_prefetch=smem,
                grid=grid,
                in_specs=specs,
                out_specs=out_specs,
                scratch_shapes=list(scratch),
            )
        )
    return pl.pallas_call(
        run,
        out_shape=[jax.ShapeDtypeStruct(shape, kind) for shape, kind in outs],
        compiler_params=pltpu.CompilerParams(vmem_limit_bytes=mib * MIB),
        cost_estimate=pl.CostEstimate(flops=int(us * FLOPS_A_US), bytes_accessed=1, transcendentals=0),
        input_output_aliases=aliases or {},
        name=name,
        **how,
    )(*ins, *after)


def start_copies(jobs, sems):
    copies = []
    for at, (source, target) in enumerate(jobs):
        copy = pltpu.make_async_copy(source, target, sems.at[at])
        copy.start()
        copies.append(copy)
    return copies


def slab_body(spot, q0, q1, k0, k1, v0, v1, gain_one, gain_two, scale, out, turned):
    start = spot[3] * HD
    off = pl.multiple_of(start - start // 128 * 128, 16)
    for w, (left, right) in enumerate(((q0, q1), (k0, k1), (v0, v1))):
        turned[:128] = left[...].astype(F32).T
        turned[128:] = right[...].astype(F32).T
        out[w * HD : w * HD + HD] = turned[pl.ds(off, HD)].astype(BF)
    width = out.shape[1]
    part = scale.shape[0]
    line = jnp.concatenate([line_of(scale), jnp.zeros((1, width - part), F32)], axis=1)
    tail = [line_of(gain_one), line_of(gain_two), line, jnp.zeros((13, width), F32)]
    out[3 * HD :] = jnp.concatenate(tail, axis=0).astype(BF)


def line_of(vector):
    return vector[...].astype(F32).reshape(1, vector.shape[0])


def setup_body(spot, slab, slab_x, weight, gains, scale_col, scale_row):
    width = slab.shape[1]
    f = spot[0]
    mine, theirs = slab[...], slab_x[...]
    left = jnp.where(f == 0, mine, theirs)
    right = jnp.where(f == 0, theirs, mine)
    weight[:, :width] = left[: 3 * HD]
    weight[:, width:] = right[: 3 * HD]
    left, right = left[3 * HD :].astype(F32), right[3 * HD :].astype(F32)
    gains[...] = jnp.concatenate([left[:8], right[:8]], axis=1)
    part = HD // 2
    row = jnp.concatenate([left[2:3, :part], right[2:3, :part], jnp.zeros((1, 128 - HD), F32)], axis=1)
    row = jnp.broadcast_to(row, (128, 128))
    scale_row[...] = row[:8]
    scale_col[...] = row.T[:HD, :1] * HD ** (-0.5)


def project_body(layout, spot, *refs):
    count, pieces, has_previous, jobs, slot = layout
    first = slot == 0
    xs, refs = refs[:count], refs[count:]
    (gains, weight, weight_sib, scale), refs = refs[:4], refs[4:]
    if has_previous:
        previous, refs = refs[0], refs[1:]
    moved, refs = refs[:jobs], refs[jobs:]
    refs = refs if first else refs[1:]
    (norm_out, q_out, kv_out, sib_out), refs = refs[:4], refs[4:]
    carried, (norm_vmem, sems, norm_sem) = refs[:-3], refs[-3:]
    copies = []
    for w, out in zip(moved, carried):
        quarter = out.shape[0]
        rows = pl.ds(pl.multiple_of(spot[1] * quarter, 16), quarter)
        copies.append((w.at[rows], out))
    copies = start_copies(copies, sems)
    x = jnp.concatenate([r[...] for r in xs], axis=0).astype(F32)
    inv = lax.rsqrt(jnp.mean(x * x, axis=-1, keepdims=True) + EPSILON)
    norm = (x * inv * gains[0:1]).astype(BF)
    norm_vmem[...] = norm.reshape(norm_vmem.shape)
    keep = pltpu.make_async_copy(norm_vmem, norm_out.at[pl.ds(slot, pieces)], norm_sem)
    keep.start()
    for which, table in enumerate((weight, weight_sib)):
        out = dot(table[...], norm, NT)
        q = (out[:HD] * scale[...]).astype(BF)
        kv = out[HD:].astype(BF)
        for j in range(pieces):
            lanes = slice(j * 128, (j + 1) * 128)
            if which == 0:
                q_out[j] = q[:, lanes]
                kv_out[j] = kv[:, lanes]
            else:
                sib_out[j, :HD] = q[:, lanes]
                sib_out[j, HD:] = kv[:, lanes]
    if has_previous:
        for j in range(previous.shape[0]):
            kv_out[pieces + j] = previous[j, HD:]
    for copy in copies:
        copy.wait()
    keep.wait()


def forward_body(layout, chunks, slots_q, slots_k, slots_out, full, total, qblock, *refs):
    count = layout["arrays"]
    arrays, refs = refs[:count], refs[count:]
    (pieces, q_t, k_t, k_rows, v_rows, att, lse), refs = refs[:7], refs[7:]
    block_q, block_kv, v_t, scores, block_out = refs
    for kind, which, index, row, entry, side in layout["blocks"]:
        for half in range(2):
            lanes = slice(half * 64, half * 64 + 64)
            if kind == "q":
                block_q[slots_q[entry, half]] = arrays[which][index, :HD, lanes]
            else:
                value = arrays[which][index, row : row + 2 * HD, lanes]
                block_kv[side, slots_k[entry, half]] = value
    rows = 2 * 256
    ones_row = jnp.where(lax.broadcasted_iota(jnp.int32, (16, rows), 0) == 0, 1.0, 0.0).astype(BF)

    @pl.loop(0, chunks)
    def _(c):
        tile = jnp.concatenate(
            [block_kv[side, 4 * c + m] for side in range(2) for m in range(4)], axis=1
        )
        k_t[c] = tile[:HD]
        k_rows[c] = tile[:HD].astype(F32).T.astype(BF)
        v_rows[c] = tile[HD:].astype(F32).T.astype(BF)
        v_t[c] = jnp.concatenate([tile[HD:], ones_row], axis=0)

    width = q_t.shape[2]
    per = width // 64

    @pl.loop(0, q_t.shape[0])
    def _(i):
        query = jnp.concatenate([block_q[per * i + m] for m in range(per)], axis=1)
        q_t[i] = query
        ids = qblock[i]

        def scan_max(masked, c, top):
            s = dot(k_rows[c], query, NN)
            if masked:
                s = jnp.where(block_of_row(width) + 4 * c <= ids, s, LOWEST)
            scores[c] = s
            return jnp.maximum(top, jnp.max(s.reshape(rows // 8, 8, width), axis=0))

        top = jnp.full((8, width), LOWEST, F32)
        top = lax.fori_loop(0, full[i], functools.partial(scan_max, False), top)
        top = lax.fori_loop(full[i], total[i], functools.partial(scan_max, True), top)
        top = jnp.max(top, axis=0, keepdims=True)

        def gather(c, acc):
            w = jnp.exp(scores[c] - top).astype(BF)
            return acc + dot(v_t[c], w, NN)

        acc = lax.fori_loop(0, total[i], gather, jnp.zeros((HD + 16, width), F32))
        sums = acc[HD : HD + 1]
        out = acc[:HD] / sums
        att[i] = out
        lse[i] = top + jnp.log(sums)
        low = out.astype(BF)
        for m in range(per):
            block_out[per * i + m] = low[:, m * 64 : m * 64 + 64]

    for c in range(GROUP):
        pieces[c] = jnp.concatenate(
            [block_out[slots_out[c, 0]], block_out[slots_out[c, 1]]], axis=1
        )


def block_of_row(width):
    return lax.broadcasted_iota(jnp.int32, (512, width), 0) % 256 // 64


def backward_body(first, last, low, slots_out, begin, clear, qblock, scale, *refs):
    (given, q_t, k_t, k_rows, v_rows, stat, lse), refs = refs[:7], refs[7:]
    if not first:
        dq_in, refs = refs[0], refs[1:]
    (dkv_own, dkv_other), refs = refs[:2], refs[2:]
    tiles, _, width = q_t.shape
    per = width // 64
    if first:
        (grad_t, delta_out, dq), refs = refs[:3], refs[3:]
        (blocks,) = refs
        for c in range(GROUP):
            for half in range(2):
                blocks[slots_out[c, half]] = given[c, :, half * 64 : half * 64 + 64]

        @pl.loop(0, tiles)
        def _(i):
            grad = jnp.concatenate([blocks[per * i + m] for m in range(per)], axis=1)
            grad_t[i] = grad
            delta_out[i] = jnp.sum(grad.astype(F32) * stat[i], axis=0, keepdims=True)
            dq[i] = jnp.zeros((HD, width), F32)

        delta = delta_out
    else:
        grad_t, delta = given, stat
        if last:
            (dq_pieces, scale_sum, dq, blocks) = refs
        else:
            (dq,) = refs
        dq[...] = dq_in[...]

    @pl.loop(0, dkv_own.shape[0])
    def _(at):
        c = low + at

        def step(masked, i, carry):
            d_k, d_v = carry
            query, grad = q_t[i], grad_t[i]
            prob = jnp.exp(dot(k_rows[c], query, NN) - lse[i])
            if masked:
                prob = jnp.where(block_of_row(width) + 4 * c <= qblock[i], prob, 0.0)
            d_score = (prob * (dot(v_rows[c], grad, NN) - delta[i])).astype(BF)
            dq[i] += dot(k_t[c], d_score, NN)
            return d_k + dot(query, d_score, NT), d_v + dot(grad, prob.astype(BF), NT)

        carry = (jnp.zeros((HD, 512), F32), jnp.zeros((HD, 512), F32))
        carry = lax.fori_loop(begin[c], clear[c], functools.partial(step, True), carry)
        d_k, d_v = lax.fori_loop(clear[c], tiles, functools.partial(step, False), carry)
        dkv_own[at, :HD] = d_k[:, :256]
        dkv_own[at, HD:] = d_v[:, :256]
        dkv_other[at, :HD] = d_k[:, 256:].astype(BF)
        dkv_other[at, HD:] = d_v[:, 256:].astype(BF)

    if last:
        total = jnp.zeros((HD, width), F32)
        for i in range(tiles):
            total = total + dq[i] * q_t[i].astype(F32)
            rounded = (dq[i] * scale[...]).astype(BF)
            for m in range(per):
                blocks[per * i + m] = rounded[:, m * 64 : m * 64 + 64]
        scale_sum[...] = total
        for c in range(GROUP):
            dq_pieces[c] = jnp.concatenate(
                [blocks[slots_out[c, 0]], blocks[slots_out[c, 1]]], axis=1
            )


def join_body(slots_kv, dq_pieces, *refs):
    parts, (pieces, blocks) = refs[:-2], refs[-2:]
    low = 0
    for own, received in zip(parts[: len(parts) // 2], parts[len(parts) // 2 :]):

        @pl.loop(0, own.shape[0])
        def _(at, low=low, own=own, received=received):
            tile = (own[at] + received[at].astype(F32)).astype(BF)
            for m in range(4):
                blocks[4 * (low + at) + m] = tile[:, m * 64 : m * 64 + 64]

        low += own.shape[0]

    for c in range(GROUP):
        pieces[c, :HD] = dq_pieces[c]
        pieces[c, HD:] = jnp.concatenate(
            [blocks[slots_kv[c, 0]], blocks[slots_kv[c, 1]]], axis=1
        )


def qkv_grad_body(source, spot, pieces, scale_sum, *refs):
    norms, (own, other, table) = refs[:-3], refs[-3:]
    total = jnp.zeros((3 * HD, table.shape[1]), F32)
    for norm, entries in zip(norms, (OWN_ENTRIES, SIB_ENTRIES)):
        for j, entry in enumerate(entries):
            total = total + dot(pieces[source[entry]], norm[j], NN)
    table[...] = total
    width = table.shape[1] // 2
    f = spot[0]
    own[: 3 * HD] = table[:, pl.ds(pl.multiple_of(f * width, 128), width)]
    other[: 3 * HD] = table[:, pl.ds(pl.multiple_of((1 - f) * width, 128), width)].astype(BF)
    column = jnp.broadcast_to(jnp.sum(scale_sum[...], axis=1, keepdims=True), (HD, 128))
    line = column.T[:1]
    high = line.astype(BF)
    low = (line - high.astype(F32)).astype(BF)
    own[3 * HD :] = jnp.zeros((16, width), F32)
    own[3 * HD : 3 * HD + 1, :HD] = line
    tail = jnp.concatenate([high.astype(F32), low.astype(F32), jnp.zeros((14, HD), F32)], axis=0)
    other[3 * HD :] = jnp.concatenate([tail, jnp.zeros((16, width - HD), F32)], axis=1).astype(BF)


def qkv_sum_body(own, received, slab, out):
    width = own.shape[1]
    total = own[: 3 * HD] + received[: 3 * HD].astype(F32)
    out[: 3 * HD] = total.astype(BF)
    gain = jnp.sum(total * slab[: 3 * HD].astype(F32), axis=0, keepdims=True)
    tail = received[3 * HD :].astype(F32)
    line = own[3 * HD : 3 * HD + 1] + tail[0:1] + tail[1:2]
    rows = []
    for value in (gain, line):
        high = value.astype(BF).astype(F32)
        rows += [high, value - high]
    out[3 * HD :] = jnp.concatenate(rows + [jnp.zeros((12, width), F32)], axis=0).astype(BF)


def pack_body(*refs):
    ins, out = refs[:-1], refs[-1]
    width = out.shape[1]
    row = 0
    for ref in ins:
        for at in range(0, ref.shape[1], width):
            out[row : row + ref.shape[0]] = ref[:, at : at + width]
            row += ref.shape[0]


def qkv_place_body(layout, source, spot, *refs):
    count, blocks = layout
    arrays, (gain, scale_row), refs = refs[:count], refs[count : count + 2], refs[count + 2 :]
    outs, (gain_out, scale_out, table) = refs[:3], refs[3:]
    width = gain.shape[0]
    tail = jnp.zeros((16, width), F32)
    for entry, parts in blocks:
        block = [arrays[which][row : row + size] for which, row, size in parts]
        block = jnp.concatenate(block, axis=0) if len(block) > 1 else block[0]
        head = pl.multiple_of(source[entry] * HD, 16)
        for w in range(3):
            table[w, pl.ds(head, HD)] = block[w * HD : w * HD + HD]
        tail = tail + block[3 * HD :].astype(F32)
    for w in range(3):
        for at in range(0, H * HD, 256):
            outs[w][:, at : at + 256] = table[w, at : at + 256].astype(F32).T
    gain_out[...] = ((tail[0:1] + tail[1:2]) / line_of(gain)).reshape(width)
    scale = (tail[2:3, :128] + tail[3:4, :128]) / scale_row[0:1]
    part = scale_out.shape[0]
    chosen = jnp.where(spot[0] == 0, scale[:, :part], scale[:, part : 2 * part])
    scale_out[...] = chosen.reshape(part)


def rows_body(
    spot,
    att_t,
    x_in,
    g_in,
    gain_in,
    *refs,
):
    weights = (refs[:5], refs[5:8], refs[8:11])
    refs = refs[11:]
    (stream_out, dy_out, datt_out), outs, sums_out = refs[:3], refs[3:7], refs[7]
    full = refs[8:11]
    turned, sems = refs[11:]
    f, k = spot[0], spot[1]
    half, quarter = weights[1][0].shape[0], weights[1][1].shape[0]
    copies = []
    for w in range(3):
        mine, *theirs = weights[w]
        jobs = [(mine, full[w].at[pl.ds(pl.multiple_of(f * half, 16), half)])]
        for at, piece in enumerate(theirs):
            core = k if at % 2 == 0 else 1 - k
            start = (1 - f) * half + core * quarter + (quarter - piece.shape[0]) * (at // 2)
            rows = pl.ds(pl.multiple_of(start, 16), piece.shape[0])
            jobs.append((piece, full[w].at[rows]))
        copies.append(start_copies(jobs, sems.at[w]))
    w_out, w_hid, w_ret = full
    x = x_in[...].astype(F32)
    gain = gain_in[1:2]
    for copy in copies[0]:
        copy.wait()
    attn = dot(att_t[...], w_out[...], TN)
    y1 = x + attn
    inv = lax.rsqrt(jnp.mean(y1 * y1, axis=-1, keepdims=True) + EPSILON)
    unit = y1 * inv
    norm = (unit * gain).astype(BF)
    for copy in copies[1]:
        copy.wait()
    h = dot(norm, w_hid[...], NN)
    sig = jax.nn.sigmoid(h)
    act = (h * sig).astype(BF)
    for copy in copies[2]:
        copy.wait()
    stream = y1 + dot(act, w_ret[...], NN)
    stream_out[...] = stream.astype(BF)
    squares = jnp.where(
        lax.broadcasted_iota(jnp.int32, (8, 128), 0) == 0,
        jnp.sum(stream * stream),
        jnp.sum(attn * attn),
    )
    sums_out[...] = squares
    g = g_in[...]
    d_act = dot(g, w_ret[...], NT)
    d_h = (d_act * sig * (1.0 + h * (1.0 - sig))).astype(BF)
    d_norm = dot(d_h, w_hid[...], NT)
    c2 = d_norm * gain
    dy = inv * (c2 - unit * jnp.mean(c2 * unit, axis=-1, keepdims=True)) + g.astype(F32)
    dy_out[...] = dy
    dy_b = dy.astype(BF)
    datt_out[...] = dot(w_out[...], dy_b, NT).astype(BF)
    turned[0] = att_t[...]
    turned[1] = norm.astype(F32).T.astype(BF)
    turned[2] = act.astype(F32).T.astype(BF)
    for ref, ff, kk in zip(outs, (f, f, 1 - f, 1 - f), (k, 1 - k, k, 1 - k)):
        at = pl.multiple_of(ff * half + kk * quarter, 16)
        for w in range(3):
            ref[w * quarter : (w + 1) * quarter] = turned[w, pl.ds(at, quarter)]
    rows = x.shape[0]
    for ref in outs[:3]:
        for w, right in enumerate((dy_b, d_h)):
            for c in range(right.shape[1] // 128):
                start = 3 * quarter + (w * (right.shape[1] // 128) + c) * rows
                ref[start : start + rows] = right[:, c * 128 : (c + 1) * 128]


def pooled_grad_body(own, sib, far, far_left, far_right, *refs):
    gs, out = refs[:4], refs[4]
    model = out.shape[2]
    columns = model // 128
    quarter = far_left.shape[0] // 3
    rows = 128
    totals = []
    for w in range(3):
        lefts, rights = [], []
        for at, (left, right) in enumerate(
            ((own, own), (sib, sib), (far, far), (far_left, far_right))
        ):
            lefts.append(left[w * quarter : (w + 1) * quarter])
            start = 3 * quarter + w * columns * rows
            if w == 2:
                rights.append(gs[at][...])
                continue
            rights.append(
                jnp.concatenate(
                    [right[start + c * rows : start + (c + 1) * rows] for c in range(columns)], axis=1
                )
            )
        left, right = jnp.concatenate(lefts, axis=1), jnp.concatenate(rights, axis=0)
        totals.append(dot(left, right, NN))
    for c in range(CHIPS):
        rows = [t[40 * c : 40 * c + 40] for t in totals] + [jnp.zeros((8, model), F32)]
        out[c] = jnp.concatenate(rows, axis=0).astype(BF)


def reduce_step_body(step, spot, up, down, *refs):
    received, (up_out, down_out) = refs[:-2], refs[-2:]
    model = up.shape[2]
    for side, (block, out) in enumerate(((up, up_out), (down, down_out))):
        near = slice(side * model // 2, (side + 1) * model // 2)
        if step == 0:
            out[...] = block[0, :, near]
            continue
        add = received[side][...].astype(F32)
        if step == 1:
            out[...] = block[0]
            out[:, near] = (block[0, :, near].astype(F32) + add).astype(BF)
        else:
            out[...] = (block[0].astype(F32) + add).astype(BF)


def reduce_end_body(spot, block, up, down, sums, sums_x, out):
    model = block.shape[2]
    total = block[0].astype(F32) + up[...].astype(F32) + down[...].astype(F32)
    pair = sums[...] + sums_x[...]
    high = pair.astype(BF).astype(F32)
    low = pair - high
    lane = lax.broadcasted_iota(jnp.int32, (8, 128), 1)
    row = lax.broadcasted_iota(jnp.int32, (8, 128), 0)
    first = jnp.where(row == 0, high[0:1], low[0:1])
    second = jnp.where(row == 0, high[1:2], low[1:2])
    tail = jnp.where(row < 2, jnp.where(lane == 0, first, jnp.where(lane == 1, second, 0.0)), 0.0)
    tail = jnp.concatenate([tail, jnp.zeros((8, model - 128), F32)], axis=1)
    out[...] = jnp.concatenate([total[:120], tail], axis=0).astype(BF)


def rows_place_body(layout, elements, place, *refs):
    count, blocks = layout
    arrays, (w_hidden, gain), refs = refs[:count], refs[count : count + 2], refs[count + 2 :]
    outs, (gain_out, means_out) = refs[:3], refs[3:]
    tail = jnp.zeros((8, 128), F32)
    for entry, parts in blocks:
        block = [arrays[which][row : row + 128] for which, row in parts]
        block = jnp.concatenate(block, axis=1) if len(block) > 1 else block[0]
        block = block.astype(F32)
        at = pl.multiple_of(place[entry] * 40, 8)
        for w in range(3):
            outs[w][pl.ds(at, 40)] = block[w * 40 : w * 40 + 40]
        tail = tail + block[120:, :128]
    means = jnp.sqrt((tail[0:1, :2] + tail[1:2, :2]) / elements)
    means_out[...] = means.reshape(2)
    half, model = w_hidden.shape
    total = jnp.zeros((half, 128), F32)
    for at in range(0, model, 128):
        total = total + outs[1][:, at : at + 128] * w_hidden[:, at : at + 128].astype(F32)
    line = jnp.sum(total.T, axis=0, keepdims=True) / line_of(gain)
    gain_out[...] = line.reshape(half)


def inputs_product_body(back, back_x, w_q, w_k, w_v, own, other, turned):
    for side, pieces in enumerate((back, back_x)):
        for h in range(H):
            for w in range(3):
                turned[w, h * HD : h * HD + HD, side * 128 : side * 128 + 128] = pieces[
                    h, w * HD : w * HD + HD
                ]
    total = dot(w_q[...], turned[0], NN) + dot(w_k[...], turned[1], NN)
    total = total + dot(w_v[...], turned[2], NN)
    own[...] = total[:, :128]
    other[...] = total[:, 128:].astype(BF)


def inputs_grad_body(spot, x_in, dy_in, gains, own, received, out):
    mine, theirs = own[...].T, received[...].astype(F32).T
    f = spot[0]
    left = jnp.where(f == 0, mine, theirs)
    right = jnp.where(f == 0, theirs, mine)
    x = x_in[...].astype(F32)
    inv = lax.rsqrt(jnp.mean(x * x, axis=-1, keepdims=True) + EPSILON)
    unit = x * inv
    c1 = jnp.concatenate([left, right], axis=1) * gains[0:1]
    dx = inv * (c1 - unit * jnp.mean(c1 * unit, axis=-1, keepdims=True)) + dy_in[...]
    out[...] = dx.astype(BF)


def per_device(
    ctx_count,
    stream_in,
    pairing,
    w_query,
    w_key,
    w_value,
    w_output,
    w_hidden,
    w_return,
    gain_attn,
    gain_mlp,
    query_scale,
    cotangent,
):
    sequences, dev_rows, model = stream_in.shape
    half = w_query.shape[0]
    quarter = half // 2
    groups = ctx_count // GROUP
    blocks = 2 * ctx_count
    chunks = blocks // 4
    ctx = lax.axis_index("ctx")
    f = lax.axis_index("fsdp")
    head = ctx % GROUP
    k = head % 2

    def ring(a, shift):
        pairs = [
            (
                g * GROUP + RING[i] * 2 + core,
                g * GROUP + RING[(i + shift) % CHIPS] * 2 + core,
            )
            for g in range(groups)
            for i in range(CHIPS)
            for core in range(2)
        ]
        return lax.ppermute(a, "ctx", pairs)

    def swap_core(a):
        return lax.ppermute(a, "ctx", [(c, c ^ 1) for c in range(ctx_count)])

    def swap_x(a):
        return lax.ppermute(a, "fsdp", [(0, 1), (1, 0)])

    def turn_groups(a, by):
        return lax.ppermute(
            a, "ctx", [(c, (c + by * GROUP) % ctx_count) for c in range(ctx_count)]
        )

    def sum_groups(a, kind):
        total = a
        for by in range(1, groups):
            total = total + turn_groups(a.astype(kind), by).astype(a.dtype)
        return total

    def exchange(a):
        which = (
            None
            if groups == 1
            else [[g * GROUP + h for h in range(GROUP)] for g in range(groups)]
        )
        return lax.all_to_all(a, "ctx", 0, 0, axis_index_groups=which, tiled=True)

    def swap_cores(arrays):
        swapped = []
        for a in arrays:
            swapped.append(swap_core(a))
        return swapped

    def ring_step(up, down):
        return ring(up, 1), ring(down, -1)

    def ring_gather(a, axis, cut, hold=lambda v: v):
        up = down = a
        found = [(a, swap_core(a))]
        for _ in range(3):
            up, down = ring(up, 1), ring(down, -1)
            found.append((up, down, swap_core(up), swap_core(down)))
        size = a.shape[axis]
        up = ring(hold(lax.slice_in_dim(up, 0, cut, axis=axis)), 1)
        down = ring(hold(lax.slice_in_dim(down, cut, size, axis=axis)), -1)
        found.append((up, down, swap_core(up), swap_core(down)))
        return found

    source = jnp.asarray(SOURCE, jnp.int32)[head]
    place = jnp.asarray(PLACE, jnp.int32)[head]
    chip = head // 2
    ring_at = jnp.where(chip % 2 == 0, chip // 2, CHIPS - 1 - chip // 2)
    spot = jnp.stack([f, k, ring_at, head]).astype(jnp.int32)
    group = ctx // GROUP

    def pairs_of(which):
        return lax.dynamic_slice_in_dim(pairing, which * GROUP, GROUP, 0)

    def slots_of(pairs):
        return jnp.stack([pairs, blocks - 1 - pairs], axis=1).astype(jnp.int32)

    my_pairs = pairs_of(group)
    slots_ctx = slots_of(my_pairs)
    slots_ring = slots_ctx[source]
    if groups == 1:
        ids = np.arange(2 * GROUP, dtype=np.int32)
        slots_q, slots_out = slots_ring, slots_ctx
        slots_k = slots_ring
    else:
        flat = slots_ctx.reshape(-1)
        rank = jnp.sum((flat[None, :] < flat[:, None]).astype(jnp.int32), axis=1)
        ids = jnp.sum(
            jnp.where(rank[None, :] == jnp.arange(2 * GROUP)[:, None], flat[None, :], 0), axis=1
        ).astype(jnp.int32)
        slots_out = rank.reshape(GROUP, 2).astype(jnp.int32)
        slots_q = slots_out[source]
        slots_k = jnp.concatenate(
            [slots_of(pairs_of((group - by) % groups))[source] for by in range(groups)], axis=0
        )
    tiles, width = (4, 512) if groups == 1 else (8, 256)
    by_tile = ids.reshape(tiles, width // 64)
    full = jnp.asarray((by_tile[:, 0] + 1) // 4, jnp.int32)
    total = jnp.asarray(by_tile[:, -1] // 4 + 1, jnp.int32)
    every = np.arange(chunks)[:, None]
    begin = (total[None, :] <= every).sum(axis=1).astype(jnp.int32)
    clear = (full[None, :] <= every).sum(axis=1).astype(jnp.int32)
    qblock = jnp.asarray(ids.repeat(64).reshape(tiles, 1, width), jnp.int32)
    if groups == 1:
        full, total, begin, clear = [
            jnp.asarray(a, jnp.int32)
            for a in (
                (by_tile[:, 0] + 1) // 4,
                by_tile[:, -1] // 4 + 1,
                (by_tile[None, :, -1] // 4 + 1 <= every).sum(axis=1),
                ((by_tile[None, :, 0] + 1) // 4 <= every).sum(axis=1),
            )
        ]

    any_spec = pl.BlockSpec(memory_space=pl.ANY)
    vmem_spec = pl.BlockSpec(memory_space=pltpu.VMEM)
    x = stream_in.reshape(dev_rows, model)
    g_rows = cotangent.reshape(dev_rows, model)
    last = model // 128 - 1

    def columns(more):
        def at(i, spot):
            return (0, jnp.minimum(spot[3] * HD // 128 + more, last))

        return pl.BlockSpec((half, 128), at)

    def whole(shape):
        return pl.BlockSpec(shape, lambda i, spot: (0,) * len(shape))

    part = query_scale.shape[0]
    def gates(arrays, after):
        return call(
            lambda *refs: None,
            [(a.shape, a.dtype) for a in arrays],
            arrays,
            specs=[any_spec] * len(arrays),
            out_specs=[any_spec] * len(arrays),
            after=after,
            aliases={at: at for at in range(len(arrays))},
            name="gate",
        mib=1,
        us=0.1,
        )

    def gate(a, after):
        return gates([a], after)[0]

    steps = [(x,), ring_step(x, x)]
    for step in range(2, 5):
        up, down = steps[-1]
        if step == 4:
            up, down = up[: dev_rows // 2], down[dev_rows // 2 :]
        steps.append(ring_step(up, down))
    early = quarter // 5 * 2
    out_xs = [swap_x(lax.dynamic_slice_in_dim(w_output, k * quarter, early, 0))]
    (slab,) = call(
        slab_body,
        [((3 * HD + 16, half), BF)],
        [
            spot,
            *[w for w in (w_query, w_key, w_value) for _ in range(2)],
            gain_attn,
            gain_mlp,
            query_scale,
        ],
        specs=[columns(0), columns(1)] * 3
        + [pl.BlockSpec((n,), lambda i, spot: (0,)) for n in (half, half, part)],
        out_specs=[whole((3 * HD + 16, half))],
        scratch=[pltpu.VMEM((256, half), F32)],
        smem=1,
        grid=(1,),
        name="slab",
        us=3,
        mib=60,
    )
    slab_x = swap_x(slab)
    late = lax.dynamic_slice_in_dim(w_output, k * quarter + early, quarter - early, 0)
    out_xs.append(swap_x(gate(late, [slab_x])))
    weight_t, gains, scale_col, scale_row = call(
        setup_body,
        [((3 * HD, model), BF), ((8, model), F32), ((HD, 1), F32), ((8, 128), F32)],
        [spot, slab, slab_x],
        smem=1,
        after=[*steps[2], *out_xs[:1]],
        name="setup",
        mib=6,
        us=2,
    )
    weight_sib = swap_core(weight_t)

    norms = None
    sibs, queries, keys, others = [], [], [], []
    norms = None
    slot = 0
    for step, arrays in enumerate(([x, *steps[1], *steps[2]], steps[3], steps[4])):
        count = sum(a.shape[0] for a in arrays) // dev_rows
        moved = (w_hidden, w_return) if step == 2 else ()
        previous = sibs[-1:]
        outs = [
            ((CHIPS, dev_rows, model), BF),
            ((count, HD, 128), BF),
            ((count + sum(p.shape[0] for p in previous), 2 * HD, 128), BF),
            ((count, 3 * HD, 128), BF),
        ]
        outs += [((quarter, model), BF)] * len(moved)
        ins = [spot, *arrays, gains, weight_t, weight_sib, scale_col, *previous, *moved]
        ins += [norms] if step else []
        norms, q_part, kv_part, sib_part, *moved_parts = call(
            functools.partial(
                project_body, (len(arrays), count, bool(previous), len(moved), slot)
            ),
            outs,
            ins,
            specs=[vmem_spec] * (len(arrays) + 4 + len(previous))
            + [any_spec] * (len(moved) + bool(step)),
            out_specs=[any_spec] + [vmem_spec] * (len(outs) - 1),
            scratch=[
                pltpu.VMEM((count, dev_rows, model), BF),
                pltpu.SemaphoreType.DMA((max(1, len(moved)),)),
                pltpu.SemaphoreType.DMA,
            ],
            smem=1,
            after=[(), out_xs[1:], others[:1]][step],
            aliases={len(ins) - 1: 0} if step else None,
            name="project",
            us=[3, 2, 2, 2][step],
            mib=16,
        )
        slot += count
        queries.append(q_part)
        keys.append(kv_part)
        sibs.append(swap_core(sib_part))
        others.append(swap_x(kv_part))
    hid_part, ret_part = moved_parts
    others.append(swap_x(sibs[-1]))
    norms_sib = swap_core(norms)
    parts = [w_output]
    for out_x in out_xs:
        out_x = gate(out_x, [norms])
        parts += [out_x, swap_core(out_x)]
    hid_x = swap_x(gate(hid_part, others))
    ret_x = swap_x(gate(ret_part, others))

    arrays = queries + sibs + keys + others
    n_steps = len(queries)
    places = []
    own_entries, sib_entries = list(OWN_ENTRIES), list(SIB_ENTRIES)
    at = 0
    for step in range(n_steps):
        count = queries[step].shape[0]
        for j in range(count):
            own, sib = own_entries[at + j], sib_entries[at + j]
            places.append(("q", step, j, 0, own, 0))
            places.append(("q", n_steps + step, j, 0, sib, 0))
            places.append(("kv", 2 * n_steps + step, j, 0, own, 0))
            places.append(("kv", 3 * n_steps + step, j, 0, own, 1))
            if step + 1 < n_steps:
                index = queries[step + 1].shape[0] + j
                places.append(("kv", 2 * n_steps + step + 1, index, 0, sib, 0))
                places.append(("kv", 3 * n_steps + step + 1, index, 0, sib, 1))
            else:
                places.append(("kv", n_steps + step, j, HD, sib, 0))
                places.append(("kv", 4 * n_steps, j, HD, sib, 1))
        at += count
    if groups > 1:
        mine = [*keys, sibs[-1][:, HD:]]
        theirs = [*others[:-1], others[-1][:, HD:]]
        order = []
        at = 0
        for step in range(n_steps + 1):
            count = queries[step].shape[0] if step < n_steps else 0
            order += own_entries[at : at + count]
            if step:
                before = queries[step - 1].shape[0]
                order += sib_entries[at - before : at]
            at += count
        for by in range(1, groups):
            for side, parts_of in enumerate((mine, theirs)):
                which = len(arrays)
                arrays.append(turn_groups(jnp.concatenate(parts_of, axis=0), by))
                for j in range(GROUP):
                    places.append(("kv", which, j, 0, by * GROUP + order[j], side))
    pieces, q_t, k_t, k_rows, v_rows, att, lse = call(
        functools.partial(forward_body, {"arrays": len(arrays), "blocks": places}, chunks),
        [
            ((GROUP, HD, 128), BF),
            ((tiles, HD, width), BF),
            ((chunks, HD, 512), BF),
            ((chunks, 512, HD), BF),
            ((chunks, 512, HD), BF),
            ((tiles, HD, width), F32),
            ((tiles, 1, width), F32),
        ],
        [slots_q, slots_k, slots_out, full, total, qblock, *arrays],
        scratch=[
            pltpu.VMEM((2 * GROUP, HD, 64), BF),
            pltpu.VMEM((2, blocks, 2 * HD, 64), BF),
            pltpu.VMEM((chunks, HD + 16, 512), BF),
            pltpu.VMEM((chunks, 512, width), F32),
            pltpu.VMEM((2 * GROUP, HD, 64), BF),
        ],
        smem=5,
        name="attention_forward",
        us=20,
        mib=36 if groups == 1 else 60,
    )
    att_t = exchange(pieces).reshape(model, dev_rows)
    for first, w, when in ((hid_x, w_hidden, pieces), (ret_x, w_return, att_t)):
        first = gate(first, [when])
        parts += [w, first, swap_core(first)]

    g_sib = swap_core(g_rows)
    g_x = swap_x(gate(g_rows, [pieces]))

    share_rows = 3 * quarter + 2 * (model // 128) * dev_rows
    stream, dy, datt_t, f_own, f_sib, f_x, f_xs, sums = call(
        rows_body,
        [
            ((dev_rows, model), BF),
            ((dev_rows, model), F32),
            ((model, dev_rows), BF),
            ((share_rows, 128), BF),
            ((share_rows, 128), BF),
            ((share_rows, 128), BF),
            ((3 * quarter, 128), BF),
            ((8, 128), F32),
        ],
        [spot, att_t, x, g_rows, gains, *parts],
        specs=[vmem_spec] * 4 + [any_spec] * 11,
        scratch=[pltpu.VMEM((model, model), BF)] * 3
        + [pltpu.VMEM((3, model, dev_rows), BF), pltpu.SemaphoreType.DMA((3, 5))],
        smem=1,
        name="row_part",
        mib=60,
        us=10,
    )
    datt_t, g_sib, g_x = gates([datt_t, g_sib, g_x], ())
    grads = exchange(datt_t.reshape(GROUP, HD, dev_rows))
    g_xs, sums_x = swap_core(g_x), swap_x(sums)

    from_x = swap_x(f_x)
    from_sib = swap_core(f_sib)
    forward = swap_core(f_xs)
    from_xs = swap_x(forward)

    def chunk_call(body, shifts, ins, outs, name, after):
        def at(shift):
            return pl.BlockSpec((1, 128, model), lambda i, spot: ((spot[2] + shift) % CHIPS, 0, 0))

        return call(
            body,
            outs,
            [spot, *([partial] * len(shifts)), *ins],
            specs=[at(s) for s in shifts] + [whole(a.shape) for a in ins],
            out_specs=[whole(shape) for shape, _ in outs],
            smem=1,
            grid=(1,),
            after=after,
            name=name,
            us=2.8,
            mib=8,
        )

    def reduce_step(step, received, after):
        shift = 4 - step
        up, down = chunk_call(
            functools.partial(reduce_step_body, step),
            (shift, CHIPS - shift),
            received,
            [((128, model if step else model // 2), BF)] * 2,
            "reduce_step",
            after,
        )
        return (ring(up, 1), ring(down, -1)), [up]

    low = chunks // 4

    def backward(first, size, outs, ins, scratch, after, us):
        return call(
            functools.partial(backward_body, first, not first, low if first else 0),
            [((size, 2 * HD, 256), F32), ((size, 2 * HD, 256), BF), *outs],
            [slots_out, begin, clear, qblock, scale_col, *ins],
            scratch=[*scratch, pltpu.VMEM((2 * GROUP, HD, 64), BF)],
            smem=3,
            after=after,
            name="attention_backward",
            us=us,
            mib=60,
        )

    state = [((tiles, HD, width), BF), ((tiles, 1, width), F32), ((tiles, HD, width), F32)]
    ins = [q_t, k_t, k_rows, v_rows]
    own_high, other_high, grad_t, delta, dq = backward(
        True, chunks - low, state, [grads, *ins, att, lse], [], [forward], 16
    )
    high_x = swap_x(other_high)
    from_x, from_sib, from_xs, g_xs, sums_x = gates(
        [from_x, from_sib, from_xs, g_xs, sums_x], [own_high]
    )
    back_xs = swap_core(from_x)
    (partial,) = call(
        pooled_grad_body,
        [((CHIPS, 128, model), BF)],
        [f_own, from_sib, from_x, from_xs, back_xs, g_rows, g_sib, g_x, g_xs],
        name="pooled_grads",
        us=2,
        mib=24,
    )
    received, done = reduce_step(0, (), ())
    own_low, other_low, dq_pieces, scale_sum = backward(
        False,
        low,
        [((GROUP, HD, 128), BF), ((HD, width), F32)],
        [grad_t, *ins, delta, lse, dq],
        [pltpu.VMEM((tiles, HD, width), F32)],
        done,
        10,
    )
    low_x = swap_x(other_low)
    owns, receiveds = [own_low, own_high], [low_x, high_x]

    received, done = reduce_step(1, received, [dq_pieces, high_x])
    if groups > 1:
        for at in range(2):
            owns[at] = sum_groups(owns[at] + receiveds[at].astype(F32), BF)
            receiveds[at] = jnp.zeros_like(receiveds[at])
    (d_pieces,) = call(
        join_body,
        [((GROUP, 3 * HD, 128), BF)],
        [slots_ctx, dq_pieces, *owns, *receiveds],
        scratch=[pltpu.VMEM((blocks, 2 * HD, 64), BF)],
        smem=1,
        after=received,
        name="join",
        us=2,
        mib=24 if groups == 1 else 60,
    )
    back = exchange(d_pieces)
    received, done = reduce_step(2, received, [d_pieces])
    own_share, other_share = call(
        qkv_grad_body,
        [((3 * HD + 16, half), F32), ((3 * HD + 16, half), BF)],
        [source, spot, d_pieces, scale_sum, norms, norms_sib],
        scratch=[pltpu.VMEM((3 * HD, model), F32)],
        smem=2,
        after=done,
        name="qkv_grads",
        us=4.7,
        mib=24,
    )
    share_x = swap_x(other_share)
    (share,) = call(
        qkv_sum_body,
        [((3 * HD + 16, half), BF)],
        [own_share, share_x, slab],
        name="qkv_sum",
        us=1,
        mib=8,
    )
    share = sum_groups(share.astype(F32), BF).astype(BF) if groups > 1 else share

    def handed(arrays, after=()):
        rows = sum(a.shape[0] * (a.shape[1] // half) for a in arrays)
        (packed,) = call(
            pack_body, [((rows, half), BF)], arrays, after=after, name="pack", us=1, mib=8
        )
        return swap_core(packed)

    q_now, q_sib = ring_step(share, share), swap_core(share)
    received, done = reduce_step(3, received, [share])
    back = gate(back, received)
    back_x = swap_x(back)
    (mine,) = chunk_call(
        reduce_end_body, (0,), (*received, sums, sums_x), [((128, model), BF)], "reduce_end", q_now
    )
    mine = sum_groups(mine.astype(F32), BF).astype(BF) if groups > 1 else mine
    sibs = [handed([*q_now, mine])]
    q_own, m_own = [share, *q_now], [mine]
    q_now, m_now = ring_step(*q_now), ring_step(mine, mine)
    product, product_other = call(
        inputs_product_body,
        [((half, dev_rows), F32), ((half, dev_rows), BF)],
        [back, back_x, w_query, w_key, w_value],
        scratch=[pltpu.VMEM((3, model, 2 * dev_rows), BF)],
        after=[mine],
        name="inputs_product",
        us=3,
        mib=24,
    )
    product_x = swap_x(product_other)
    for step in (2, 3, 4):
        waits = {2: [product], 3: [product_x], 4: ()}[step]
        sibs.append(handed([*q_now, *m_now], waits))
        q_own += q_now
        m_own += m_now
        if step == 2:
            q_now, m_now = ring_step(*q_now), ring_step(*m_now)
        elif step == 3:
            q_now, m_now = ring_step(q_now[0][:128], q_now[1][128:]), ring_step(*m_now)
            (d_in,) = call(
                inputs_grad_body,
                [((dev_rows, model), BF)],
                [spot, x, dy, gains, product, product_x],
                smem=1,
                after=sibs[-1:],
                name="inputs_grad",
                us=2,
                mib=16,
            )
        else:
            m_now = ring_step(m_now[0][:, : model // 2], m_now[1][:, model // 2 :])

    q_arrays = [*q_own, q_sib, *sibs]
    q_blocks = [(entry, [(at, 0, 256)]) for at, entry in enumerate(OWN_ENTRIES[:7])]
    q_blocks.append((OWN_ENTRIES[7], [(7, 0, 128), (8, 0, 128)]))
    q_blocks.append((SIB_ENTRIES[0], [(9, 0, 256)]))
    q_blocks += [
        (entry, [(10 + at // 2, at % 2 * 256, 256)]) for at, entry in enumerate(SIB_ENTRIES[1:])
    ]
    grad_query, grad_key, grad_value, gain_one_grad, scale_grad = call(
        functools.partial(qkv_place_body, (len(q_arrays), q_blocks)),
        [((half, model), F32)] * 3 + [((half,), F32), ((part,), F32)],
        [source, spot, *q_arrays, gain_attn, scale_row],
        scratch=[pltpu.VMEM((3, model, half), BF)],
        smem=2,
        after=[d_in],
        name="qkv_place",
        us=6,
        mib=40,
    )
    m_now = gates(m_now, [grad_query])
    m_own += m_now
    m_arrays = [*m_own, *sibs, *swap_cores(m_now)]
    m_blocks = [(entry, [(at, 0)]) for at, entry in enumerate(OWN_ENTRIES[:7])]
    m_blocks.append((OWN_ENTRIES[7], [(7, 0), (8, 0)]))
    first = len(m_own)
    starts = [(0, 512), (1, 512), (1, 768), (2, 512), (2, 768), (3, 256), (3, 512)]
    m_blocks += [
        (entry, [(first + at, row), (first + at, row + 128)])
        for entry, (at, row) in zip(SIB_ENTRIES, starts)
    ]
    m_blocks.append((SIB_ENTRIES[7], [(first + 4, 0), (first + 5, 0)]))
    elements = float(ctx_count * 2 * dev_rows * model)
    grad_output, grad_hidden, grad_return, gain_two_grad, root_means = call(
        functools.partial(rows_place_body, (len(m_arrays), m_blocks), elements),
        [((half, model), F32)] * 3 + [((half,), F32), ((2,), F32)],
        [place, *m_arrays, w_hidden, gain_mlp],
        smem=1,
        name="rows_place",
        us=5,
        mib=40,
    )
    return (
        stream.reshape(stream_in.shape),
        d_in.reshape(stream_in.shape),
        grad_query,
        grad_key,
        grad_value,
        grad_output,
        grad_hidden,
        grad_return,
        gain_one_grad,
        gain_two_grad,
        scale_grad,
        root_means,
    )


def solution(mesh):
    rows = P(None, ("ctx", "fsdp"), None)
    weight, vector = P("fsdp", None), P("fsdp")
    return jax.shard_map(
        functools.partial(per_device, mesh.shape["ctx"]),
        mesh=mesh,
        in_specs=(rows, P(), *([weight] * 6), *([vector] * 3), rows),
        out_specs=(rows, rows, *([weight] * 6), *([vector] * 3), P()),
        check_vma=False,
    )
```

time: 2390 us -> 323 us (0.14); the launches traced: 2350 us -> 322 us
  local copies, waits for them, and re-layouts: 705 us -> 38.6 us
  blocking collectives: 624 us -> 16.9 us
  matrix products: 394 us -> 0 us
  loops' own time: 268 us -> 0 us
  waiting for transfers between devices: 325 us -> 94.2 us
  Pallas kernels: 0 us -> 96.1 us
  starting transfers between devices: 1.25 us -> 73.1 us
    psum x2 -> x0, blocking collectives: 449 us -> none  [the longest x1 411 us: per_device(): lax.psum((shares[0], shares[1], shares[2], shares[3], shares[4], shares[5...]
    dot_general x474 -> x0, matrix products: 394 us -> none  [the longest x132 131 us: score_grads(): jnp.einsum('sqhd,skhd->shqk', queries, key_tile, preferred_element_type=j...]
    dynamic_slice x448 -> x2, local copies, waits for them, and re-layouts: 373 us -> 2.2 us  [the longest x1 1.21 us: per_device(): lax.dynamic_slice_in_dim(w_output, k * quarter + early, quarter - early, 0)]
    another operation x387 -> x0, loops' own time: 268 us -> none  [the longest x1 86.8 us: per_device(): lax.scan(key_advance, start_kv, (query_tiles, grad_tiles, lse_tiles, delt...]
    all_gather x10 -> x0, waiting for transfers between devices: 242 us -> none  [the longest x1 68 us: per_device(): lax.all_gather(k_shard, ('ctx', 'fsdp'), axis=1, tiled=True)]
    all_gather x4 -> x0, blocking collectives: 164 us -> none  [the longest x1 89.6 us: per_device(): lax.all_gather(delta_rows.reshape(sequences, dev_rows, H), ('ctx', 'fsdp'...]
    squeeze x128 -> x2, local copies, waits for them, and re-layouts: 137 us -> 1.38 us  [the longest x1 0.69 us: per_device(): source = jnp.asarray(SOURCE, jnp.int32)[head]]
    another operation x23 -> x1, local copies, waits for them, and re-layouts: 123 us -> 0.09 us  [slots_of(): return jnp.stack([pairs, blocks - 1 - pairs], axis=1).astype(jnp.int32)]
  transfers between devices with their start and end apart: 16 -> 73, of which waited for: 7 -> 29; matrix products, arithmetic and copies ran while one was open for 47% -> 2% of each run, Pallas kernels for 0% -> 28%
where the time goes in v1:
time: 323 us; the launch traced here: 322 us
  Pallas kernels  96.1 us (30%)
  waiting for transfers between devices  94.2 us (29%)
  starting transfers between devices  73.1 us (23%)
  local copies, waits for them, and re-layouts  38.6 us (12%)
  blocking collectives  16.9 us (5%)
    pallas_call x38, Pallas kernels, call(): pl.pallas_call(run, out_shape=[jax.ShapeDtypeStruct(shape, kind) for shap...  96.1 us
    ppermute x32, waiting for transfers between devices, ring(): return lax.ppermute(a, 'ctx', pairs)  55.6 us
    ppermute x32, starting transfers between devices, ring(): return lax.ppermute(a, 'ctx', pairs)  37.9 us
    unnamed x173, local copies, waits for them, and re-layouts  32.4 us
    ppermute x18, waiting for transfers between devices, swap_x(): return lax.ppermute(a, 'fsdp', [(0, 1), (1, 0)])  25.7 us
    ppermute x18, starting transfers between devices, swap_x(): return lax.ppermute(a, 'fsdp', [(0, 1), (1, 0)])  20.5 us
    all_to_all x1, blocking collectives, exchange(): return lax.all_to_all(a, 'ctx', 0, 0, axis_index_groups=which, tiled=True)  16.9 us
    all_to_all x2, starting transfers between devices, exchange(): return lax.all_to_all(a, 'ctx', 0, 0, axis_index_groups=which, tiled=True)  10.7 us
  transfers between devices with their start and end apart: 73, of which 29 were waited for; matrix products, arithmetic and copies ran while one was open for 2% of the time, Pallas kernels for 28%

profile of v1, /device:TPU:0, one launch (start us, length us, event | category | flops | bytes accessed | tf_op | source)
XLA Modules:
  0.0 321.7 jit_solution(15800587242429506430)
XLA Ops:
  0.6 3.0 collective-permute-start.1
  4.3 3.2 %slab.1.refs_1_.refs_2_ = bf16[256,640]{1,0:T(8,128)(2,1)} custom-call(s32[4]{0:T(128)} %pad_add_fusion.1.refs_0_.refs_1_, bf16[640,1280]{1,0:T(8,128)(2,1)} %refs_2_.5, bf16[640,1280]{1,0:T(8,128)(2,1)} %refs_2_.5, bf16[640,1280]{1,0:T(8,128)(2,1)} %refs_3_.6, bf16[640,1280]{1,0:T(8,128)(2,1)} %refs_3_.6, bf16[640,1280]{1,0:T(8,128)(2,1)} %refs_4_.4, ...), custom_call_target="tpu_custom_call" | custom-call | flops 3449999872 | bytes 1 | tf_op jit(solution)/shard_map/slab/pallas_call | solution.py:76
  7.6 1.9 collective-permute-start.4
  11.6 1.7 collective-permute-start.3
  15.1 3.3 %collective-permute-done.4.refs_2_.refs_1_ = bf16[256,640]{1,0:T(8,128)(2,1)S(1)} collective-permute-done((bf16[256,640]{1,0:T(8,128)(2,1)}, bf16[256,640]{1,0:T(8,128)(2,1)S(1)}, u32[]{:S(2)}, u32[]{:S(2)}) %collective-permute-start.4) | collective-permute-done | bytes 327712 | tf_op jit(solution)/shard_map/ppermute | solution.py:623
  18.4 5.6 %collective-permute-done.5.refs_5_.refs_0_ = bf16[128,1280]{1,0:T(8,128)(2,1)S(1)} collective-permute-done((bf16[128,1280]{1,0:T(8,128)(2,1)S(1)}, bf16[128,1280]{1,0:T(8,128)(2,1)S(1)}, u32[]{:S(2)}, u32[]{:S(2)}) %collective-permute-start.5) | collective-permute-done | bytes 327712 | tf_op jit(solution)/shard_map/ppermute | solution.py:623
  36.8 3.9 %project.3 = (bf16[8,128,1280]{2,1,0:T(8,128)(2,1)S(1)}, bf16[5,80,128]{2,1,0:T(8,128)(2,1)S(1)}, bf16[5,160,128]{2,1,0:T(8,128)(2,1)}, bf16[5,240,128]{2,1,0:T(8,128)(2,1)}) custom-call(s32[4]{0:T(128)S(1)} %copy-done.20, bf16[128,1280]{1,0:T(8,128)(2,1)S(1)} %bitcast.31, bf16[128,1280]{1,0:T(8,128)(2,1)S(1)} %copy-done.41, ...), custom_call_target="tpu_custom_call" | custom-call | flops 3449999872 | bytes 1 | tf_op jit(solution)/shard_map/project/pallas_call | solution.py:76
  49.5 2.4 project.4
  54.9 2.5 project.5
  62.0 3.6 %collective-permute-done.17.refs_17_.refs_3_ = bf16[3,160,128]{2,1,0:T(8,128)(2,1)S(1)} collective-permute-done((bf16[3,160,128]{2,1,0:T(8,128)(2,1)}, bf16[3,160,128]{2,1,0:T(8,128)(2,1)S(1)}, u32[]{:S(2)}, u32[]{:S(2)}) %collective-permute-start.17) | collective-permute-done | bytes 122912 | tf_op jit(solution)/shard_map/ppermute | solution.py:623
  68.7 16.8 %attention_forward.1 = (bf16[16,80,128]{2,1,0:T(8,128)(2,1)S(1)}, bf16[4,80,512]{2,1,0:T(8,128)(2,1)S(1)}, bf16[8,80,512]{2,1,0:T(8,128)(2,1)S(1)}, bf16[8,512,8...) custom-call(s32[16,2]{1,0:T(8,128)S(1)} %gather_fusion, ...), custom_call_target="tpu_custom_call" | custom-call | flops 23000000512 | bytes 1 | tf_op jit(solution)/shard_map/attention_forward/pallas_call | solution.py:76
  86.5 16.9 %all_to_all.15 = bf16[16,80,128]{2,1,0:T(8,128)(2,1)S(1)} all-to-all(bf16[16,80,128]{2,1,0:T(8,128)(2,1)S(1)} %get-tuple-element.100.refs_1_), channel_id=1, replica_groups=mesh['ctx'=16,'fsdp'=2] {'ctx'}, dimensions={0} | all-to-all | bytes 655360 | tf_op jit(solution)/shard_map/all_to_all | solution.py:642
  106.7 2.2 collective-permute-done.19.refs_7_
  112.2 10.5 %row_part.1 = (bf16[128,1280]{1,0:T(8,128)(2,1)}, f32[128,1280]{1,0:T(8,128)}, bf16[1280,128]{1,0:T(8,128)(2,1)}, bf16[3520,128]{1,0:T(8,128)(2,1)}, bf16[3520,1...) custom-call(s32[4]{0:T(128)} %pad_add_fusion.1.refs_0_.refs_1_, ...), custom_call_target="tpu_custom_call" | custom-call | flops 11500000256 | bytes 1 | tf_op jit(solution)/shard_map/row_part/pallas_call | solution.py:76
  124.4 6.0 %all-to-all-start.1 = ((bf16[16,80,128]{2,1,0:T(8,128)(2,1)}), bf16[16,80,128]{2,1,0:T(8,128)(2,1)}, u32[]{:S(2)}, u32[]{:S(2)}) async-start(bf16[16,80,128]{2,1,0:T(8,128)(2,1)} %bitcast.21), calls=%async_computation.1 | async-start | bytes 655360 | tf_op jit(solution)/shard_map/all_to_all | solution.py:642
  133.6 7.9 %all-to-all-done.1.refs_5_ = bf16[16,80,128]{2,1,0:T(8,128)(2,1)} async-done(((bf16[16,80,128]{2,1,0:T(8,128)(2,1)}), bf16[16,80,128]{2,1,0:T(8,128)(2,1)}, u32[]{:S(2)}, u32[]{:S(2)}) %all-to-all-start.1) | async-done | bytes 327712 | tf_op jit(solution)/shard_map/all_to_all | solution.py:642
  141.6 16.0 %attention_backward.2 = (f32[6,160,256]{2,1,0:T(8,128)}, bf16[6,160,256]{2,1,0:T(8,128)(2,1)}, bf16[4,80,512]{2,1,0:T(8,128)(2,1)}, f32[4,1,512]{2,1,0:T(1,128)}, f32[4,80,512]{2,1,0:T(8,128)}) custom-call(s32[16,2]{1,0:T(8,128)} %copy-done.13, s32[8]{0:T(128)} %constant.96.clone.refs_1_, s32[8]{0:T(128)} %constant.97.clone.refs_2_, ...), custom_call_target="tpu_custom_call" | custom-call | flops 18400000000 | bytes 1 | tf_op jit(solution)/shard_map/attention_backward/pallas_call | solution.py:76
  157.5 1.8 collective-permute-done.30.refs_2_
  163.6 3.1 pooled_grads.1.refs_1_.refs_2_
  168.2 1.7 collective-permute-start.37
  170.2 11.2 %attention_backward.3 = (f32[2,160,256]{2,1,0:T(8,128)}, bf16[2,160,256]{2,1,0:T(8,128)(2,1)}, bf16[16,80,128]{2,1,0:T(8,128)(2,1)}, f32[80,512]{1,0:T(8,128)}) custom-call(s32[16,2]{1,0:T(8,128)} %copy-done.13, s32[8]{0:T(128)} %constant.96.clone.refs_1_, s32[8]{0:T(128)} %constant.97.clone.refs_2_, s32[4,1,512]{2,1,0:T(1,128)} %constant.93.clone.refs_5_.refs_3_, ...), custom_call_target="tpu_custom_call" | custom-call | flops 11500000256 | bytes 1 | tf_op jit(solution)/shard_map/attention_backward/pallas_call | solution.py:76
  181.5 1.7 copy-done.52
  184.8 1.7 collective-permute-start.38
  189.1 3.2 collective-permute-done.34.refs_4_
  192.2 1.8 collective-permute-done.38.refs_6_.refs_3_
  195.5 1.8 join.1.refs_5_.refs_2_
  198.3 4.7 %all-to-all-start.2 = ((bf16[16,240,128]{2,1,0:T(8,128)(2,1)}), bf16[16,240,128]{2,1,0:T(8,128)(2,1)}, u32[]{:S(2)}, u32[]{:S(2)}) async-start(bf16[16,240,128]{2,1,0:T(8,128)(2,1)} %copy-done.6), calls=%async_computation.2 | async-start | bytes 1966080 | tf_op jit(solution)/shard_map/all_to_all | solution.py:642
  204.2 1.7 copy-done.53
  207.2 4.6 %qkv_grads.1 = (f32[256,640]{1,0:T(8,128)S(1)}, bf16[256,640]{1,0:T(8,128)(2,1)S(1)}) custom-call(s32[16]{0:T(128)S(1)} %fusion.2.refs_0_, s32[4]{0:T(128)S(1)} %copy-done.21, bf16[16,240,128]{2,1,0:T(8,128)(2,1)S(1)} %copy-done.8, f32[80,512]{1,0:T(8,128)S(1)} %copy-done.73, bf16[8,128,1280]{2,1,0:T(8,128)(2,1)S(1)} %get-tuple-element.101.refs_1_.refs_4_, ...), custom_call_target="tpu_custom_call" | custom-call | flops 5405000192 | bytes 1 | tf_op jit(solution)/shard_map/qkv_grads/pallas_call | solution.py:76
  213.3 1.9 collective-permute-start.41
  215.3 6.5 %collective-permute-done.43.refs_1_ = bf16[256,640]{1,0:T(8,128)(2,1)S(1)} collective-permute-done((bf16[256,640]{1,0:T(8,128)(2,1)S(1)}, bf16[256,640]{1,0:T(8,128)(2,1)S(1)}, u32[]{:S(2)}, u32[]{:S(2)}) %collective-permute-start.43) | collective-permute-done | bytes 327712 | tf_op jit(solution)/shard_map/ppermute | solution.py:623
  221.9 6.9 %collective-permute-done.41.refs_4_ = bf16[128,1280]{1,0:T(8,128)(2,1)S(1)} collective-permute-done((bf16[128,1280]{1,0:T(8,128)(2,1)S(1)}, bf16[128,1280]{1,0:T(8,128)(2,1)S(1)}, u32[]{:S(2)}, u32[]{:S(2)}) %collective-permute-start.41) | collective-permute-done | bytes 327712 | tf_op jit(solution)/shard_map/ppermute | solution.py:617
  229.6 6.9 %collective-permute-start.44 = (bf16[128,1280]{1,0:T(8,128)(2,1)S(1)}, bf16[128,1280]{1,0:T(8,128)(2,1)S(1)}, u32[]{:S(2)}, u32[]{:S(2)}) collective-permute-start(bf16[128,1280]{1,0:T(8,128)(2,1)S(1)} %get-tuple-element.142), channel_id=1, source_target_pairs={{0,8},{2,10},{8,16},{10,18},{16,24},{18,26},{24,28},{26,30},{28,20... | collective-permute-start | bytes 983048 | tf_op jit(solution)/shard_map/ppermute | solution.py:617
  236.5 6.8 %collective-permute-done.44.refs_1_.refs_2_ = bf16[128,1280]{1,0:T(8,128)(2,1)S(1)} collective-permute-done((bf16[128,1280]{1,0:T(8,128)(2,1)S(1)}, bf16[128,1280]{1,0:T(8,128)(2,1)S(1)}, u32[]{:S(2)}, u32[]{:S(2)}) %collective-permute-start.44) | collective-permute-done | bytes 327712 | tf_op jit(solution)/shard_map/ppermute | solution.py:617
  243.3 2.2 collective-permute-done.45.refs_2_.refs_3_
  247.2 1.7 collective-permute-start.47
  248.9 5.8 %collective-permute-done.48.refs_7_.refs_1_.refs_4_ = bf16[256,640]{1,0:T(8,128)(2,1)S(1)} collective-permute-done((bf16[256,640]{1,0:T(8,128)(2,1)S(1)}, bf16[256,640]{1,0:T(8,128)(2,1)S(1)}, u32[]{:S(2)}, u32[]{:S(2)}) %collective-permute-start.48) | collective-permute-done | bytes 327712 | tf_op jit(solution)/shard_map/ppermute | solution.py:617
  259.6 5.8 %collective-permute-done.52.refs_1_.refs_6_ = bf16[256,640]{1,0:T(8,128)(2,1)S(1)} collective-permute-done((bf16[256,640]{1,0:T(8,128)(2,1)S(1)}, bf16[256,640]{1,0:T(8,128)(2,1)S(1)}, u32[]{:S(2)}, u32[]{:S(2)}) %collective-permute-start.52) | collective-permute-done | bytes 327712 | tf_op jit(solution)/shard_map/ppermute | solution.py:617
  266.0 6.4 %collective-permute-done.56.refs_3_ = bf16[128,1280]{1,0:T(8,128)(2,1)S(1)} collective-permute-done((bf16[128,1280]{1,0:T(8,128)(2,1)S(1)}, bf16[128,1280]{1,0:T(8,128)(2,1)S(1)}, u32[]{:S(2)}, u32[]{:S(2)}) %collective-permute-start.56) | collective-permute-done | bytes 327712 | tf_op jit(solution)/shard_map/ppermute | solution.py:617
  275.1 2.8 inputs_product.1
  279.3 3.5 %collective-permute-done.57.refs_3_.refs_5_ = bf16[128,1280]{1,0:T(8,128)(2,1)S(1)} collective-permute-done((bf16[128,1280]{1,0:T(8,128)(2,1)S(1)}, bf16[128,1280]{1,0:T(8,128)(2,1)S(1)}, u32[]{:S(2)}, u32[]{:S(2)}) %collective-permute-start.57) | collective-permute-done | bytes 327712 | tf_op jit(solution)/shard_map/ppermute | solution.py:617
  282.8 2.5 collective-permute-done.51.refs_0_.refs_7_
  288.8 3.7 %collective-permute-done.60.refs_1_.refs_10_ = bf16[128,640]{1,0:T(8,128)(2,1)S(1)} collective-permute-done((bf16[128,640]{1,0:T(8,128)(2,1)S(1)}, bf16[128,640]{1,0:T(8,128)(2,1)S(1)}, u32[]{:S(2)}, u32[]{:S(2)}) %collective-permute-start.60) | collective-permute-done | bytes 163872 | tf_op jit(solution)/shard_map/ppermute | solution.py:617
  293.3 6.9 %collective-permute-done.59.refs_0_.refs_9_ = bf16[128,640]{1,0:T(8,128)(2,1)S(1)} collective-permute-done((bf16[128,640]{1,0:T(8,128)(2,1)S(1)}, bf16[128,640]{1,0:T(8,128)(2,1)S(1)}, u32[]{:S(2)}, u32[]{:S(2)}) %collective-permute-start.59) | collective-permute-done | bytes 163872 | tf_op jit(solution)/shard_map/ppermute | solution.py:617
  302.0 1.8 inputs_grad.1.refs_18_
  307.1 6.1 %qkv_place.1 = (f32[640,1280]{1,0:T(8,128)}, f32[640,1280]{1,0:T(8,128)}, f32[640,1280]{1,0:T(8,128)}, f32[640]{0:T(1024)}, f32[40]{0:T(128)}) custom-call(s32[16]{0:T(128)S(1)} %fusion.2.refs_0_, s32[4]{0:T(128)S(1)} %copy-done.21, bf16[256,640]{1,0:T(8,128)(2,1)S(1)} %qkv_sum.1.refs_5_.refs_2_, ...), custom_call_target="tpu_custom_call" | custom-call | flops 6899999744 | bytes 1 | tf_op jit(solution)/shard_map/qkv_place/pallas_call | solution.py:76
  313.2 1.9 copy-done
  316.7 4.9 %rows_place.1 = (f32[640,1280]{1,0:T(8,128)}, f32[640,1280]{1,0:T(8,128)}, f32[640,1280]{1,0:T(8,128)}, f32[640]{0:T(1024)}, f32[2]{0:T(128)}) custom-call(s32[16]{0:T(128)S(1)} %fusion.refs_0_, bf16[128,1280]{1,0:T(8,128)(2,1)S(1)} %reduce_end.1.refs_5_.refs_2_.refs_1_, bf16[128,1280]{1,0:T(8,128)(2,1)S(1)} %collective-permute-done.54.refs_2_, ...), custom_call_target="tpu_custom_call" | custom-call | flops 5750000128 | bytes 1 | tf_op jit(solution)/shard_map/rows_place/pallas_call | solution.py:76
  (328 shorter events, 88.6 us)
Async XLA Ops:
  0.6 11.0 %collective-permute-start.1 = (bf16[128,1280]{1,0:T(8,128)(2,1)}, bf16[128,1280]{1,0:T(8,128)(2,1)S(1)}, u32[]{:S(2)}, u32[]{:S(2)}) collective-permute-start(bf16[128,1280]{1,0:T(8,128)(2,1)} %bitcast.28), channel_id=1, source_target_pairs={{0,4},{2,6},{8,0},{10,2},{16,8},{18,10},{24,16},{26,18},{28,24},{3... | collective-permute-start | bytes 983048 | tf_op jit(solution)/shard_map/ppermute | solution.py:617
  3.7 10.4 %collective-permute-start = (bf16[128,1280]{1,0:T(8,128)(2,1)}, bf16[128,1280]{1,0:T(8,128)(2,1)S(1)}, u32[]{:S(2)}, u32[]{:S(2)}) collective-permute-start(bf16[128,1280]{1,0:T(8,128)(2,1)} %bitcast.29), channel_id=1, source_target_pairs={{0,8},{2,10},{8,16},{10,18},{16,24},{18,26},{24,28},{26,30},{28,20... | collective-permute-start | bytes 983048 | tf_op jit(solution)/shard_map/ppermute | solution.py:617
  7.6 10.8 %collective-permute-start.4 = (bf16[256,640]{1,0:T(8,128)(2,1)}, bf16[256,640]{1,0:T(8,128)(2,1)S(1)}, u32[]{:S(2)}, u32[]{:S(2)}) collective-permute-start(bf16[256,640]{1,0:T(8,128)(2,1)} %slab.1.refs_1_.refs_2_), channel_id=1, source_target_pairs={{0,1},{1,0},{2,3},{3,2},{4,5},{5,4},{6,7},{7,6},{8,9},{9,8},{10,11... | collective-permute-start | bytes 983048 | tf_op jit(solution)/shard_map/ppermute | solution.py:623
  10.4 13.5 %collective-permute-start.5 = (bf16[128,1280]{1,0:T(8,128)(2,1)S(1)}, bf16[128,1280]{1,0:T(8,128)(2,1)S(1)}, u32[]{:S(2)}, u32[]{:S(2)}) collective-permute-start(bf16[128,1280]{1,0:T(8,128)(2,1)S(1)} %constant_dynamic-slice_fusion.2), channel_id=1, source_target_pairs={{0,1},{1,0},{2,3},{3,2},{4,5},{5,4},{6,7},{7,6},{8,9},{9,8},{10,11... | collective-permute-start | bytes 983048 | tf_op jit(solution)/shard_map/ppermute | solution.py:623
  11.6 12.3 %collective-permute-start.3 = (bf16[128,1280]{1,0:T(8,128)(2,1)S(1)}, bf16[128,1280]{1,0:T(8,128)(2,1)}, u32[]{:S(2)}, u32[]{:S(2)}) collective-permute-start(bf16[128,1280]{1,0:T(8,128)(2,1)S(1)} %collective-permute-done.1.refs_3_), channel_id=1, source_target_pairs={{0,4},{2,6},{8,0},{10,2},{16,8},{18,10},{24,16},{26,18},{28,24},{3... | collective-permute-start | bytes 983048 | tf_op jit(solution)/shard_map/ppermute | solution.py:617
  14.1 9.9 %collective-permute-start.2 = (bf16[128,1280]{1,0:T(8,128)(2,1)S(1)}, bf16[128,1280]{1,0:T(8,128)(2,1)}, u32[]{:S(2)}, u32[]{:S(2)}) collective-permute-start(bf16[128,1280]{1,0:T(8,128)(2,1)S(1)} %collective-permute-done.refs_2_), channel_id=1, source_target_pairs={{0,8},{2,10},{8,16},{10,18},{16,24},{18,26},{24,28},{26,30},{28,20... | collective-permute-start | bytes 983048 | tf_op jit(solution)/shard_map/ppermute | solution.py:617
  27.2 18.6 %collective-permute-start.10 = (bf16[192,1280]{1,0:T(8,128)(2,1)S(1)}, bf16[192,1280]{1,0:T(8,128)(2,1)}, u32[]{:S(2)}, u32[]{:S(2)}) collective-permute-start(bf16[192,1280]{1,0:T(8,128)(2,1)S(1)} %gate.12), channel_id=1, source_target_pairs={{0,1},{1,0},{2,3},{3,2},{4,5},{5,4},{6,7},{7,6},{8,9},{9,8},{10,11... | collective-permute-start | bytes 1474568 | tf_op jit(solution)/shard_map/ppermute | solution.py:623
  28.9 12.5 %collective-permute-start.8 = (bf16[128,1280]{1,0:T(8,128)(2,1)}, bf16[128,1280]{1,0:T(8,128)(2,1)}, u32[]{:S(2)}, u32[]{:S(2)}) collective-permute-start(bf16[128,1280]{1,0:T(8,128)(2,1)} %collective-permute-done.3.refs_4_.refs_5_), channel_id=1, source_target_pairs={{0,4},{2,6},{8,0},{10,2},{16,8},{18,10},{24,16},{26,18},{28,24},{3... | collective-permute-start | bytes 983048 | tf_op jit(solution)/shard_map/ppermute | solution.py:617
  30.4 13.5 %collective-permute-start.7 = (bf16[128,1280]{1,0:T(8,128)(2,1)}, bf16[128,1280]{1,0:T(8,128)(2,1)}, u32[]{:S(2)}, u32[]{:S(2)}) collective-permute-start(bf16[128,1280]{1,0:T(8,128)(2,1)} %collective-permute-done.2.refs_3_.refs_4_), channel_id=1, source_target_pairs={{0,8},{2,10},{8,16},{10,18},{16,24},{18,26},{24,28},{26,30},{28,20... | collective-permute-start | bytes 983048 | tf_op jit(solution)/shard_map/ppermute | solution.py:617
  42.3 12.6 %collective-permute-start.12 = (bf16[64,1280]{1,0:T(8,128)(2,1)S(1)}, bf16[64,1280]{1,0:T(8,128)(2,1)S(1)}, u32[]{:S(2)}, u32[]{:S(2)}) collective-permute-start(bf16[64,1280]{1,0:T(8,128)(2,1)S(1)} %slice.27), channel_id=1, source_target_pairs={{0,4},{2,6},{8,0},{10,2},{16,8},{18,10},{24,16},{26,18},{28,24},{3... | collective-permute-start | bytes 491528 | tf_op jit(solution)/shard_map/ppermute | solution.py:617
  44.8 10.1 %collective-permute-start.11 = (bf16[64,1280]{1,0:T(8,128)(2,1)S(1)}, bf16[64,1280]{1,0:T(8,128)(2,1)S(1)}, u32[]{:S(2)}, u32[]{:S(2)}) collective-permute-start(bf16[64,1280]{1,0:T(8,128)(2,1)S(1)} %slice.26), channel_id=1, source_target_pairs={{0,8},{2,10},{8,16},{10,18},{16,24},{18,26},{24,28},{26,30},{28,20... | collective-permute-start | bytes 491528 | tf_op jit(solution)/shard_map/ppermute | solution.py:617
  45.4 9.5 %collective-permute-start.14 = (bf16[5,160,128]{2,1,0:T(8,128)(2,1)}, bf16[5,160,128]{2,1,0:T(8,128)(2,1)S(1)}, u32[]{:S(2)}, u32[]{:S(2)}) collective-permute-start(bf16[5,160,128]{2,1,0:T(8,128)(2,1)} %get-tuple-element.95.refs_12_), channel_id=1, source_target_pairs={{0,1},{1,0},{2,3},{3,2},{4,5},{5,4},{6,7},{7,6},{8,9},{9,8},{10,11... | collective-permute-start | bytes 614408 | tf_op jit(solution)/shard_map/ppermute | solution.py:623
  53.2 13.3 %collective-permute-start.16 = (bf16[7,160,128]{2,1,0:T(8,128)(2,1)S(1)}, bf16[7,160,128]{2,1,0:T(8,128)(2,1)S(1)}, u32[]{:S(2)}, u32[]{:S(2)}) collective-permute-start(bf16[7,160,128]{2,1,0:T(8,128)(2,1)S(1)} %get-tuple-element.98.refs_13_), channel_id=1, source_target_pairs={{0,1},{1,0},{2,3},{3,2},{4,5},{5,4},{6,7},{7,6},{8,9},{9,8},{10,11... | collective-permute-start | bytes 860168 | tf_op jit(solution)/shard_map/ppermute | solution.py:623
  66.5 37.7 %collective-permute-start.21 = (bf16[320,1280]{1,0:T(8,128)(2,1)}, bf16[320,1280]{1,0:T(8,128)(2,1)S(1)}, u32[]{:S(2)}, u32[]{:S(2)}) collective-permute-start(bf16[320,1280]{1,0:T(8,128)(2,1)} %gate.15), channel_id=1, source_target_pairs={{0,1},{1,0},{2,3},{3,2},{4,5},{5,4},{6,7},{7,6},{8,9},{9,8},{10,11... | collective-permute-start | bytes 2457608 | tf_op jit(solution)/shard_map/ppermute | solution.py:623
  68.2 36.1 %collective-permute-start.23 = (bf16[320,1280]{1,0:T(8,128)(2,1)S(1)}, bf16[320,1280]{1,0:T(8,128)(2,1)S(1)}, u32[]{:S(2)}, u32[]{:S(2)}) collective-permute-start(bf16[320,1280]{1,0:T(8,128)(2,1)S(1)} %gate.17), channel_id=1, source_target_pairs={{0,1},{1,0},{2,3},{3,2},{4,5},{5,4},{6,7},{7,6},{8,9},{9,8},{10,11... | collective-permute-start | bytes 2457608 | tf_op jit(solution)/shard_map/ppermute | solution.py:623
  106.4 16.3 %collective-permute-start.25 = (bf16[128,1280]{1,0:T(8,128)(2,1)S(1)}, bf16[128,1280]{1,0:T(8,128)(2,1)}, u32[]{:S(2)}, u32[]{:S(2)}) collective-permute-start(bf16[128,1280]{1,0:T(8,128)(2,1)S(1)} %bitcast.25), channel_id=1, source_target_pairs={{0,2},{2,0},{4,6},{6,4},{8,10},{10,8},{12,14},{14,12},{16,18},{18,... | collective-permute-start | bytes 983048 | tf_op jit(solution)/shard_map/ppermute | solution.py:620
  108.9 13.8 %collective-permute-start.26 = (bf16[128,1280]{1,0:T(8,128)(2,1)S(1)}, bf16[128,1280]{1,0:T(8,128)(2,1)}, u32[]{:S(2)}, u32[]{:S(2)}) collective-permute-start(bf16[128,1280]{1,0:T(8,128)(2,1)S(1)} %gate.19), channel_id=1, source_target_pairs={{0,1},{1,0},{2,3},{3,2},{4,5},{5,4},{6,7},{7,6},{8,9},{9,8},{10,11... | collective-permute-start | bytes 983048 | tf_op jit(solution)/shard_map/ppermute | solution.py:623
  124.4 17.2 %all-to-all-start.1 = ((bf16[16,80,128]{2,1,0:T(8,128)(2,1)}), bf16[16,80,128]{2,1,0:T(8,128)(2,1)}, u32[]{:S(2)}, u32[]{:S(2)}) async-start(bf16[16,80,128]{2,1,0:T(8,128)(2,1)} %bitcast.21), calls=%async_computation.1 | async-start | bytes 655360 | tf_op jit(solution)/shard_map/all_to_all | solution.py:642
  130.8 26.8 %collective-permute-start.32 = (f32[8,128]{1,0:T(8,128)S(1)}, f32[8,128]{1,0:T(8,128)S(1)}, u32[]{:S(2)}, u32[]{:S(2)}) collective-permute-start(f32[8,128]{1,0:T(8,128)S(1)} %copy-done.45), channel_id=1, source_target_pairs={{0,1},{1,0},{2,3},{3,2},{4,5},{5,4},{6,7},{7,6},{8,9},{9,8},{10,11... | collective-permute-start | bytes 12296 | tf_op jit(solution)/shard_map/ppermute | solution.py:623
  131.4 26.2 %collective-permute-start.31 = (bf16[128,1280]{1,0:T(8,128)(2,1)}, bf16[128,1280]{1,0:T(8,128)(2,1)}, u32[]{:S(2)}, u32[]{:S(2)}) collective-permute-start(bf16[128,1280]{1,0:T(8,128)(2,1)} %get-tuple-element.121.refs_7_), channel_id=1, source_target_pairs={{0,2},{2,0},{4,6},{6,4},{8,10},{10,8},{12,14},{14,12},{16,18},{18,... | collective-permute-start | bytes 983048 | tf_op jit(solution)/shard_map/ppermute | solution.py:620
  131.4 28.0 %collective-permute-start.28 = (bf16[3520,128]{1,0:T(8,128)(2,1)}, bf16[3520,128]{1,0:T(8,128)(2,1)S(1)}, u32[]{:S(2)}, u32[]{:S(2)}) collective-permute-start(bf16[3520,128]{1,0:T(8,128)(2,1)} %get-tuple-element.119), channel_id=1, source_target_pairs={{0,1},{1,0},{2,3},{3,2},{4,5},{5,4},{6,7},{7,6},{8,9},{9,8},{10,11... | collective-permute-start | bytes 2703368 | tf_op jit(solution)/shard_map/ppermute | solution.py:623
  132.8 26.6 %collective-permute-start.29 = (bf16[3520,128]{1,0:T(8,128)(2,1)}, bf16[3520,128]{1,0:T(8,128)(2,1)}, u32[]{:S(2)}, u32[]{:S(2)}) collective-permute-start(bf16[3520,128]{1,0:T(8,128)(2,1)} %get-tuple-element.120), channel_id=1, source_target_pairs={{0,2},{2,0},{4,6},{6,4},{8,10},{10,8},{12,14},{14,12},{16,18},{18,... | collective-permute-start | bytes 2703368 | tf_op jit(solution)/shard_map/ppermute | solution.py:620
  133.0 26.3 %collective-permute-start.30 = (bf16[960,128]{1,0:T(8,128)(2,1)}, bf16[960,128]{1,0:T(8,128)(2,1)}, u32[]{:S(2)}, u32[]{:S(2)}) collective-permute-start(bf16[960,128]{1,0:T(8,128)(2,1)} %collective-permute-done.27.refs_12_), channel_id=1, source_target_pairs={{0,1},{1,0},{2,3},{3,2},{4,5},{5,4},{6,7},{7,6},{8,9},{9,8},{10,11... | collective-permute-start | bytes 737288 | tf_op jit(solution)/shard_map/ppermute | solution.py:623
  160.6 46.1 %collective-permute-start.42 = (bf16[8,128,1280]{2,1,0:T(8,128)(2,1)S(1)}, bf16[8,128,1280]{2,1,0:T(8,128)(2,1)}, u32[]{:S(2)}, u32[]{:S(2)}) collective-permute-start(bf16[8,128,1280]{2,1,0:T(8,128)(2,1)S(1)} %get-tuple-element.101.refs_1_.refs_4_), channel_id=1, source_target_pairs={{0,2},{2,0},{4,6},{6,4},{8,10},{10,8},{12,14},{14,12},{16,18},{18,... | collective-permute-start | bytes 7864328 | tf_op jit(solution)/shard_map/ppermute | solution.py:620
  161.1 20.3 %collective-permute-start.35 = (bf16[6,160,256]{2,1,0:T(8,128)(2,1)}, bf16[6,160,256]{2,1,0:T(8,128)(2,1)S(1)}, u32[]{:S(2)}, u32[]{:S(2)}) collective-permute-start(bf16[6,160,256]{2,1,0:T(8,128)(2,1)} %get-tuple-element.133), channel_id=1, source_target_pairs={{0,1},{1,0},{2,3},{3,2},{4,5},{5,4},{6,7},{7,6},{8,9},{9,8},{10,11... | collective-permute-start | bytes 1474568 | tf_op jit(solution)/shard_map/ppermute | solution.py:623
  168.2 13.2 %collective-permute-start.37 = (bf16[128,640]{1,0:T(8,128)(2,1)S(1)}, bf16[128,640]{1,0:T(8,128)(2,1)S(1)}, u32[]{:S(2)}, u32[]{:S(2)}) collective-permute-start(bf16[128,640]{1,0:T(8,128)(2,1)S(1)} %get-tuple-element.134), channel_id=1, source_target_pairs={{0,4},{2,6},{8,0},{10,2},{16,8},{18,10},{24,16},{26,18},{28,24},{3... | collective-permute-start | bytes 491528 | tf_op jit(solution)/shard_map/ppermute | solution.py:617
  169.9 11.6 %collective-permute-start.36 = (bf16[128,640]{1,0:T(8,128)(2,1)S(1)}, bf16[128,640]{1,0:T(8,128)(2,1)S(1)}, u32[]{:S(2)}, u32[]{:S(2)}) collective-permute-start(bf16[128,640]{1,0:T(8,128)(2,1)S(1)} %get-tuple-element.129.refs_13_), channel_id=1, source_target_pairs={{0,8},{2,10},{8,16},{10,18},{16,24},{18,26},{24,28},{26,30},{28,20... | collective-permute-start | bytes 491528 | tf_op jit(solution)/shard_map/ppermute | solution.py:617
  184.8 9.2 %collective-permute-start.38 = (bf16[128,1280]{1,0:T(8,128)(2,1)S(1)}, bf16[128,1280]{1,0:T(8,128)(2,1)S(1)}, u32[]{:S(2)}, u32[]{:S(2)}) collective-permute-start(bf16[128,1280]{1,0:T(8,128)(2,1)S(1)} %get-tuple-element.135), channel_id=1, source_target_pairs={{0,8},{2,10},{8,16},{10,18},{16,24},{18,26},{24,28},{26,30},{28,20... | collective-permute-start | bytes 983048 | tf_op jit(solution)/shard_map/ppermute | solution.py:617
  198.3 47.2 %all-to-all-start.2 = ((bf16[16,240,128]{2,1,0:T(8,128)(2,1)}), bf16[16,240,128]{2,1,0:T(8,128)(2,1)}, u32[]{:S(2)}, u32[]{:S(2)}) async-start(bf16[16,240,128]{2,1,0:T(8,128)(2,1)} %copy-done.6), calls=%async_computation.2 | async-start | bytes 1966080 | tf_op jit(solution)/shard_map/all_to_all | solution.py:642
  211.8 10.0 %collective-permute-start.43 = (bf16[256,640]{1,0:T(8,128)(2,1)S(1)}, bf16[256,640]{1,0:T(8,128)(2,1)S(1)}, u32[]{:S(2)}, u32[]{:S(2)}) collective-permute-start(bf16[256,640]{1,0:T(8,128)(2,1)S(1)} %get-tuple-element.141), channel_id=1, source_target_pairs={{0,1},{1,0},{2,3},{3,2},{4,5},{5,4},{6,7},{7,6},{8,9},{9,8},{10,11... | collective-permute-start | bytes 983048 | tf_op jit(solution)/shard_map/ppermute | solution.py:623
  213.3 15.6 %collective-permute-start.41 = (bf16[128,1280]{1,0:T(8,128)(2,1)S(1)}, bf16[128,1280]{1,0:T(8,128)(2,1)S(1)}, u32[]{:S(2)}, u32[]{:S(2)}) collective-permute-start(bf16[128,1280]{1,0:T(8,128)(2,1)S(1)} %get-tuple-element.138), channel_id=1, source_target_pairs={{0,4},{2,6},{8,0},{10,2},{16,8},{18,10},{24,16},{26,18},{28,24},{3... | collective-permute-start | bytes 983048 | tf_op jit(solution)/shard_map/ppermute | solution.py:617
  215.1 13.8 %collective-permute-start.40 = (bf16[128,1280]{1,0:T(8,128)(2,1)S(1)}, bf16[128,1280]{1,0:T(8,128)(2,1)S(1)}, u32[]{:S(2)}, u32[]{:S(2)}) collective-permute-start(bf16[128,1280]{1,0:T(8,128)(2,1)S(1)} %get-tuple-element.137.refs_6_), channel_id=1, source_target_pairs={{0,8},{2,10},{8,16},{10,18},{16,24},{18,26},{24,28},{26,30},{28,20... | collective-permute-start | bytes 983048 | tf_op jit(solution)/shard_map/ppermute | solution.py:617
  229.6 13.6 %collective-permute-start.44 = (bf16[128,1280]{1,0:T(8,128)(2,1)S(1)}, bf16[128,1280]{1,0:T(8,128)(2,1)S(1)}, u32[]{:S(2)}, u32[]{:S(2)}) collective-permute-start(bf16[128,1280]{1,0:T(8,128)(2,1)S(1)} %get-tuple-element.142), channel_id=1, source_target_pairs={{0,8},{2,10},{8,16},{10,18},{16,24},{18,26},{24,28},{26,30},{28,20... | collective-permute-start | bytes 983048 | tf_op jit(solution)/shard_map/ppermute | solution.py:617
  236.5 9.0 %collective-permute-start.45 = (bf16[128,1280]{1,0:T(8,128)(2,1)S(1)}, bf16[128,1280]{1,0:T(8,128)(2,1)S(1)}, u32[]{:S(2)}, u32[]{:S(2)}) collective-permute-start(bf16[128,1280]{1,0:T(8,128)(2,1)S(1)} %get-tuple-element.143), channel_id=1, source_target_pairs={{0,4},{2,6},{8,0},{10,2},{16,8},{18,10},{24,16},{26,18},{28,24},{3... | collective-permute-start | bytes 983048 | tf_op jit(solution)/shard_map/ppermute | solution.py:617
  245.5 29.6 %collective-permute-start.46 = (bf16[16,240,128]{2,1,0:T(8,128)(2,1)}, bf16[16,240,128]{2,1,0:T(8,128)(2,1)S(1)}, u32[]{:S(2)}, u32[]{:S(2)}) collective-permute-start(bf16[16,240,128]{2,1,0:T(8,128)(2,1)} %gate.22.refs_0_), channel_id=1, source_target_pairs={{0,1},{1,0},{2,3},{3,2},{4,5},{5,4},{6,7},{7,6},{8,9},{9,8},{10,11... | collective-permute-start | bytes 2949128 | tf_op jit(solution)/shard_map/ppermute | solution.py:623
  254.8 10.6 %collective-permute-start.52 = (bf16[256,640]{1,0:T(8,128)(2,1)S(1)}, bf16[256,640]{1,0:T(8,128)(2,1)S(1)}, u32[]{:S(2)}, u32[]{:S(2)}) collective-permute-start(bf16[256,640]{1,0:T(8,128)(2,1)S(1)} %collective-permute-done.48.refs_7_.refs_1_.refs_4_), channel_id=1, source_target_pairs={{0,4},{2,6},{8,0},{10,2},{16,8},{18,10},{24,16},{26,18},{28,24},{3... | collective-permute-start | bytes 983048 | tf_op jit(solution)/shard_map/ppermute | solution.py:617
  256.1 16.4 %collective-permute-start.56 = (bf16[128,1280]{1,0:T(8,128)(2,1)S(1)}, bf16[128,1280]{1,0:T(8,128)(2,1)S(1)}, u32[]{:S(2)}, u32[]{:S(2)}) collective-permute-start(bf16[128,1280]{1,0:T(8,128)(2,1)S(1)} %reduce_end.1.refs_5_.refs_2_.refs_1_), channel_id=1, source_target_pairs={{0,4},{2,6},{8,0},{10,2},{16,8},{18,10},{24,16},{26,18},{28,24},{3... | collective-permute-start | bytes 983048 | tf_op jit(solution)/shard_map/ppermute | solution.py:617
  257.6 15.5 %collective-permute-start.54 = (bf16[128,1280]{1,0:T(8,128)(2,1)S(1)}, bf16[128,1280]{1,0:T(8,128)(2,1)S(1)}, u32[]{:S(2)}, u32[]{:S(2)}) collective-permute-start(bf16[128,1280]{1,0:T(8,128)(2,1)S(1)} %reduce_end.1.refs_5_.refs_2_.refs_1_), channel_id=1, source_target_pairs={{0,8},{2,10},{8,16},{10,18},{16,24},{18,26},{24,28},{26,30},{28,20... | collective-permute-start | bytes 983048 | tf_op jit(solution)/shard_map/ppermute | solution.py:617
  258.2 16.3 %collective-permute-start.50 = (bf16[256,640]{1,0:T(8,128)(2,1)S(1)}, bf16[256,640]{1,0:T(8,128)(2,1)S(1)}, u32[]{:S(2)}, u32[]{:S(2)}) collective-permute-start(bf16[256,640]{1,0:T(8,128)(2,1)S(1)} %collective-permute-done.47.refs_6_.refs_0_.refs_3_), channel_id=1, source_target_pairs={{0,8},{2,10},{8,16},{10,18},{16,24},{18,26},{24,28},{26,30},{28,20... | collective-permute-start | bytes 983048 | tf_op jit(solution)/shard_map/ppermute | solution.py:617
  265.4 13.8 %collective-permute-start.53 = (bf16[256,640]{1,0:T(8,128)(2,1)S(1)}, bf16[256,640]{1,0:T(8,128)(2,1)S(1)}, u32[]{:S(2)}, u32[]{:S(2)}) collective-permute-start(bf16[256,640]{1,0:T(8,128)(2,1)S(1)} %collective-permute-done.52.refs_1_.refs_6_), channel_id=1, source_target_pairs={{0,4},{2,6},{8,0},{10,2},{16,8},{18,10},{24,16},{26,18},{28,24},{3... | collective-permute-start | bytes 983048 | tf_op jit(solution)/shard_map/ppermute | solution.py:617
  272.5 10.3 %collective-permute-start.57 = (bf16[128,1280]{1,0:T(8,128)(2,1)S(1)}, bf16[128,1280]{1,0:T(8,128)(2,1)S(1)}, u32[]{:S(2)}, u32[]{:S(2)}) collective-permute-start(bf16[128,1280]{1,0:T(8,128)(2,1)S(1)} %collective-permute-done.56.refs_3_), channel_id=1, source_target_pairs={{0,4},{2,6},{8,0},{10,2},{16,8},{18,10},{24,16},{26,18},{28,24},{3... | collective-permute-start | bytes 983048 | tf_op jit(solution)/shard_map/ppermute | solution.py:617
  273.1 9.7 %collective-permute-start.55 = (bf16[128,1280]{1,0:T(8,128)(2,1)S(1)}, bf16[128,1280]{1,0:T(8,128)(2,1)S(1)}, u32[]{:S(2)}, u32[]{:S(2)}) collective-permute-start(bf16[128,1280]{1,0:T(8,128)(2,1)S(1)} %collective-permute-done.54.refs_2_), channel_id=1, source_target_pairs={{0,8},{2,10},{8,16},{10,18},{16,24},{18,26},{24,28},{26,30},{28,20... | collective-permute-start | bytes 983048 | tf_op jit(solution)/shard_map/ppermute | solution.py:617
  274.5 10.7 %collective-permute-start.51 = (bf16[256,640]{1,0:T(8,128)(2,1)S(1)}, bf16[256,640]{1,0:T(8,128)(2,1)S(1)}, u32[]{:S(2)}, u32[]{:S(2)}) collective-permute-start(bf16[256,640]{1,0:T(8,128)(2,1)S(1)} %collective-permute-done.50.refs_0_.refs_5_), channel_id=1, source_target_pairs={{0,8},{2,10},{8,16},{10,18},{16,24},{18,26},{24,28},{26,30},{28,20... | collective-permute-start | bytes 983048 | tf_op jit(solution)/shard_map/ppermute | solution.py:617
  285.3 15.6 %collective-permute-start.58 = (bf16[1024,640]{1,0:T(8,128)(2,1)S(1)}, bf16[1024,640]{1,0:T(8,128)(2,1)S(1)}, u32[]{:S(2)}, u32[]{:S(2)}) collective-permute-start(bf16[1024,640]{1,0:T(8,128)(2,1)S(1)} %pack.4), channel_id=1, source_target_pairs={{0,2},{2,0},{4,6},{6,4},{8,10},{10,8},{12,14},{14,12},{16,18},{18,... | collective-permute-start | bytes 3932168 | tf_op jit(solution)/shard_map/ppermute | solution.py:620
  286.5 13.7 %collective-permute-start.65 = (bf16[128,1280]{1,0:T(8,128)(2,1)S(1)}, bf16[128,1280]{1,0:T(8,128)(2,1)S(1)}, u32[]{:S(2)}, u32[]{:S(2)}) collective-permute-start(bf16[128,1280]{1,0:T(8,128)(2,1)S(1)} %collective-permute-done.57.refs_3_.refs_5_), channel_id=1, source_target_pairs={{0,4},{2,6},{8,0},{10,2},{16,8},{18,10},{24,16},{26,18},{28,24},{3... | collective-permute-start | bytes 983048 | tf_op jit(solution)/shard_map/ppermute | solution.py:617
  287.1 13.1 %collective-permute-start.64 = (bf16[128,1280]{1,0:T(8,128)(2,1)S(1)}, bf16[128,1280]{1,0:T(8,128)(2,1)S(1)}, u32[]{:S(2)}, u32[]{:S(2)}) collective-permute-start(bf16[128,1280]{1,0:T(8,128)(2,1)S(1)} %collective-permute-done.55.refs_2_.refs_4_), channel_id=1, source_target_pairs={{0,8},{2,10},{8,16},{10,18},{16,24},{18,26},{24,28},{26,30},{28,20... | collective-permute-start | bytes 983048 | tf_op jit(solution)/shard_map/ppermute | solution.py:617
  288.7 17.4 %collective-permute-start.63 = (bf16[1024,640]{1,0:T(8,128)(2,1)S(1)}, bf16[1024,640]{1,0:T(8,128)(2,1)S(1)}, u32[]{:S(2)}, u32[]{:S(2)}) collective-permute-start(bf16[1024,640]{1,0:T(8,128)(2,1)S(1)} %pack.6), channel_id=1, source_target_pairs={{0,2},{2,0},{4,6},{6,4},{8,10},{10,8},{12,14},{14,12},{16,18},{18,... | collective-permute-start | bytes 3932168 | tf_op jit(solution)/shard_map/ppermute | solution.py:620
  301.0 12.2 %collective-permute-start.68 = (bf16[128,640]{1,0:T(8,128)(2,1)S(1)}, bf16[128,640]{1,0:T(8,128)(2,1)S(1)}, u32[]{:S(2)}, u32[]{:S(2)}) collective-permute-start(bf16[128,640]{1,0:T(8,128)(2,1)S(1)} %slice.31), channel_id=1, source_target_pairs={{0,4},{2,6},{8,0},{10,2},{16,8},{18,10},{24,16},{26,18},{28,24},{3... | collective-permute-start | bytes 491528 | tf_op jit(solution)/shard_map/ppermute | solution.py:617
  (111 other events, 574.0 us)

commit v2 on v1

--- a/solution.py
+++ b/solution.py
@@ -129,20 +129,17 @@
 
 
 def project_body(layout, spot, *refs):
-    count, pieces, has_previous, jobs, slot = layout
-    first = slot == 0
+    count, pieces, carried, slot = layout
     xs, refs = refs[:count], refs[count:]
     (gains, weight, weight_sib, scale), refs = refs[:4], refs[4:]
-    if has_previous:
-        previous, refs = refs[0], refs[1:]
-    moved, refs = refs[:jobs], refs[jobs:]
-    refs = refs if first else refs[1:]
-    (norm_out, q_out, kv_out, sib_out), refs = refs[:4], refs[4:]
-    carried, (norm_vmem, sems, norm_sem) = refs[:-3], refs[-3:]
+    moved, refs = refs[:carried], refs[carried:]
+    refs = refs if slot == 0 else refs[1:]
+    (norm_out, q_out, kv_out, near_out, far_out), refs = refs[:5], refs[5:]
+    outs, (norm_vmem, sems, norm_sem) = refs[:-3], refs[-3:]
     copies = []
-    for w, out in zip(moved, carried):
-        quarter = out.shape[0]
-        rows = pl.ds(pl.multiple_of(spot[1] * quarter, 16), quarter)
+    for w, out in zip(moved, outs):
+        size = out.shape[0]
+        rows = pl.ds(pl.multiple_of(spot[1] * size, 16), size)
         copies.append((w.at[rows], out))
     copies = start_copies(copies, sems)
     x = jnp.concatenate([r[...] for r in xs], axis=0).astype(F32)
@@ -151,21 +148,19 @@
     norm_vmem[...] = norm.reshape(norm_vmem.shape)
     keep = pltpu.make_async_copy(norm_vmem, norm_out.at[pl.ds(slot, pieces)], norm_sem)
     keep.start()
-    for which, table in enumerate((weight, weight_sib)):
+    for table, other in ((weight, False), (weight_sib, True)):
         out = dot(table[...], norm, NT)
         q = (out[:HD] * scale[...]).astype(BF)
         kv = out[HD:].astype(BF)
         for j in range(pieces):
             lanes = slice(j * 128, (j + 1) * 128)
-            if which == 0:
+            if other:
+                near_out[j, :HD] = q[:, lanes]
+                near_out[j, HD:] = kv[:, lanes]
+                far_out[j] = kv[:, lanes]
+            else:
                 q_out[j] = q[:, lanes]
                 kv_out[j] = kv[:, lanes]
-            else:
-                sib_out[j, :HD] = q[:, lanes]
-                sib_out[j, HD:] = kv[:, lanes]
-    if has_previous:
-        for j in range(previous.shape[0]):
-            kv_out[pieces + j] = previous[j, HD:]
     for copy in copies:
         copy.wait()
     keep.wait()
@@ -176,14 +171,14 @@
     arrays, refs = refs[:count], refs[count:]
     (pieces, q_t, k_t, k_rows, v_rows, att, lse), refs = refs[:7], refs[7:]
     block_q, block_kv, v_t, scores, block_out = refs
-    for kind, which, index, row, entry, side in layout["blocks"]:
+    for kind, which, index, entry, side in layout["blocks"]:
         for half in range(2):
             lanes = slice(half * 64, half * 64 + 64)
             if kind == "q":
                 block_q[slots_q[entry, half]] = arrays[which][index, :HD, lanes]
             else:
-                value = arrays[which][index, row : row + 2 * HD, lanes]
-                block_kv[side, slots_k[entry, half]] = value
+                value = arrays[which][index, :, lanes]
+                block_kv[side, slots_k[entry, half]] = value[value.shape[0] - 2 * HD :]
     rows = 2 * 256
     ones_row = jnp.where(lax.broadcasted_iota(jnp.int32, (16, rows), 0) == 0, 1.0, 0.0).astype(BF)
 
@@ -242,10 +237,15 @@
 
 
 def backward_body(first, last, low, slots_out, begin, clear, qblock, scale, *refs):
-    (given, q_t, k_t, k_rows, v_rows, stat, lse), refs = refs[:7], refs[7:]
+    (given, q_t, stat, lse), refs = refs[:4], refs[4:]
     if not first:
         dq_in, refs = refs[0], refs[1:]
-    (dkv_own, dkv_other), refs = refs[:2], refs[2:]
+    sources, (dkv_own, dkv_other), refs = refs[:3], refs[3:5], refs[5:]
+    (k_t, k_rows, v_rows, sems), refs = refs[-4:], refs[:-4]
+    size = dkv_own.shape[0]
+    copies = start_copies(
+        [(a.at[pl.ds(low, size)], o) for a, o in zip(sources, (k_t, k_rows, v_rows))], sems
+    )
     tiles, _, width = q_t.shape
     per = width // 64
     if first:
@@ -271,18 +271,21 @@
             (dq,) = refs
         dq[...] = dq_in[...]
 
-    @pl.loop(0, dkv_own.shape[0])
+    for copy in copies:
+        copy.wait()
+
+    @pl.loop(0, size)
     def _(at):
         c = low + at
 
         def step(masked, i, carry):
             d_k, d_v = carry
             query, grad = q_t[i], grad_t[i]
-            prob = jnp.exp(dot(k_rows[c], query, NN) - lse[i])
+            prob = jnp.exp(dot(k_rows[at], query, NN) - lse[i])
             if masked:
                 prob = jnp.where(block_of_row(width) + 4 * c <= qblock[i], prob, 0.0)
-            d_score = (prob * (dot(v_rows[c], grad, NN) - delta[i])).astype(BF)
-            dq[i] += dot(k_t[c], d_score, NN)
+            d_score = (prob * (dot(v_rows[at], grad, NN) - delta[i])).astype(BF)
+            dq[i] += dot(k_t[at], d_score, NN)
             return d_k + dot(query, d_score, NT), d_v + dot(grad, prob.astype(BF), NT)
 
         carry = (jnp.zeros((HD, 512), F32), jnp.zeros((HD, 512), F32))
@@ -307,8 +310,8 @@
             )
 
 
-def join_body(slots_kv, dq_pieces, *refs):
-    parts, (pieces, blocks) = refs[:-2], refs[-2:]
+def join_body(slots_kv, spot, dq_pieces, *refs):
+    parts, (pieces, other, blocks) = refs[:-3], refs[-3:]
     low = 0
     for own, received in zip(parts[: len(parts) // 2], parts[len(parts) // 2 :]):
 
@@ -320,19 +323,37 @@
 
         low += own.shape[0]
 
-    for c in range(GROUP):
-        pieces[c, :HD] = dq_pieces[c]
-        pieces[c, HD:] = jnp.concatenate(
-            [blocks[slots_kv[c, 0]], blocks[slots_kv[c, 1]]], axis=1
-        )
-
-
-def qkv_grad_body(source, spot, pieces, scale_sum, *refs):
+    for p in range(CHIPS):
+        for core in range(2):
+            c = RING[p] * 2 + core
+            pieces[2 * p + core, :HD] = dq_pieces[c]
+            pieces[2 * p + core, HD:] = jnp.concatenate(
+                [blocks[slots_kv[c, 0]], blocks[slots_kv[c, 1]]], axis=1
+            )
+    sign = 1 - 2 * spot[1]
+    for j in range(5):
+        pos = lax.rem(spot[2] + CHIPS - sign * j, CHIPS)
+        for core in range(2):
+            other[2 * j + core] = pieces[2 * pos + core]
+
+
+def products_body(spot, pieces, near, weight, weight_sib, out):
+    sign = 1 - 2 * spot[1]
+    for j in range(5):
+        pos = lax.rem(spot[2] + CHIPS + sign * j, CHIPS)
+        for core in range(2):
+            total = dot(pieces[2 * pos + core], weight[...], TN)
+            total = total + dot(near[2 * j + core], weight_sib[...], TN)
+            out[j, core * 128 : core * 128 + 128] = total.astype(BF)
+
+
+def qkv_grad_body(place, spot, pieces, scale_sum, *refs):
     norms, (own, other, table) = refs[:-3], refs[-3:]
     total = jnp.zeros((3 * HD, table.shape[1]), F32)
     for norm, entries in zip(norms, (OWN_ENTRIES, SIB_ENTRIES)):
         for j, entry in enumerate(entries):
-            total = total + dot(pieces[source[entry]], norm[j], NN)
+            at = 2 * lax.rem(place[entry], CHIPS) + place[entry] // CHIPS
+            total = total + dot(pieces[at], norm[j], NN)
     table[...] = total
     width = table.shape[1] // 2
     f = spot[0]
@@ -362,29 +383,33 @@
     out[3 * HD :] = jnp.concatenate(rows + [jnp.zeros((12, width), F32)], axis=0).astype(BF)
 
 
-def pack_body(*refs):
-    ins, out = refs[:-1], refs[-1]
-    width = out.shape[1]
-    row = 0
-    for ref in ins:
-        for at in range(0, ref.shape[1], width):
-            out[row : row + ref.shape[0]] = ref[:, at : at + width]
-            row += ref.shape[0]
-
-
-def qkv_place_body(layout, source, spot, *refs):
-    count, blocks = layout
-    arrays, (gain, scale_row), refs = refs[:count], refs[count : count + 2], refs[count + 2 :]
+def chip_pack_body(spot, own, near, out):
+    rows = own.shape[0]
+    out[pl.ds(pl.multiple_of(spot[1] * rows, 16), rows)] = own[...]
+    out[pl.ds(pl.multiple_of((1 - spot[1]) * rows, 16), rows)] = near[...]
+
+
+def ring_positions(spot):
+    sign = 1 - 2 * spot[1]
+    offsets = [0] + [-sign * s for s in (1, 2, 3)] + [sign * s for s in (1, 2, 3)] + [4]
+    return [lax.rem(spot[2] + CHIPS + off, CHIPS) for off in offsets]
+
+
+def qkv_place_body(spot, *refs):
+    arrays, (gain, scale_row), refs = refs[:9], refs[9:11], refs[11:]
     outs, (gain_out, scale_out, table) = refs[:3], refs[3:]
     width = gain.shape[0]
+    size = 3 * HD + 16
     tail = jnp.zeros((16, width), F32)
-    for entry, parts in blocks:
-        block = [arrays[which][row : row + size] for which, row, size in parts]
-        block = jnp.concatenate(block, axis=0) if len(block) > 1 else block[0]
-        head = pl.multiple_of(source[entry] * HD, 16)
+    positions = ring_positions(spot)
+    blocks = [(arrays[at], c * size, positions[at], c) for at in range(7) for c in range(2)]
+    blocks += [(arrays[7], 0, positions[7], spot[1]), (arrays[8], 0, positions[7], 1 - spot[1])]
+    for ref, row, pos, core in blocks:
+        chip = jnp.where(pos < 4, 2 * pos, 15 - 2 * pos)
+        head = pl.multiple_of((2 * chip + core) * HD, 16)
         for w in range(3):
-            table[w, pl.ds(head, HD)] = block[w * HD : w * HD + HD]
-        tail = tail + block[3 * HD :].astype(F32)
+            table[w, pl.ds(head, HD)] = ref[row + w * HD : row + w * HD + HD]
+        tail = tail + ref[row + 3 * HD : row + size].astype(F32)
     for w in range(3):
         for at in range(0, H * HD, 256):
             outs[w][:, at : at + 256] = table[w, at : at + 256].astype(F32).T
@@ -405,19 +430,23 @@
 ):
     weights = (refs[:5], refs[5:8], refs[8:11])
     refs = refs[11:]
-    (stream_out, dy_out, datt_out), outs, sums_out = refs[:3], refs[3:7], refs[7]
-    full = refs[8:11]
-    turned, sems = refs[11:]
+    (stream_out, dy_out, datt_out), outs = refs[:3], refs[3:7]
+    full = refs[7:10]
+    turned, sems = refs[10:]
     f, k = spot[0], spot[1]
-    half, quarter = weights[1][0].shape[0], weights[1][1].shape[0]
+    half = weights[0][0].shape[0]
+    quarter = half // 2
+    early = weights[0][1].shape[0]
+    places = [
+        [k * quarter, (1 - k) * quarter, k * quarter + early, (1 - k) * quarter + early],
+        *[[k * quarter, (1 - k) * quarter]] * 2,
+    ]
     copies = []
     for w in range(3):
         mine, *theirs = weights[w]
         jobs = [(mine, full[w].at[pl.ds(pl.multiple_of(f * half, 16), half)])]
-        for at, piece in enumerate(theirs):
-            core = k if at % 2 == 0 else 1 - k
-            start = (1 - f) * half + core * quarter + (quarter - piece.shape[0]) * (at // 2)
-            rows = pl.ds(pl.multiple_of(start, 16), piece.shape[0])
+        for piece, start in zip(theirs, places[w]):
+            rows = pl.ds(pl.multiple_of((1 - f) * half + start, 16), piece.shape[0])
             jobs.append((piece, full[w].at[rows]))
         copies.append(start_copies(jobs, sems.at[w]))
     w_out, w_hid, w_ret = full
@@ -444,7 +473,6 @@
         jnp.sum(stream * stream),
         jnp.sum(attn * attn),
     )
-    sums_out[...] = squares
     g = g_in[...]
     d_act = dot(g, w_ret[...], NT)
     d_h = (d_act * sig * (1.0 + h * (1.0 - sig))).astype(BF)
@@ -457,23 +485,46 @@
     turned[0] = att_t[...]
     turned[1] = norm.astype(F32).T.astype(BF)
     turned[2] = act.astype(F32).T.astype(BF)
-    for ref, ff, kk in zip(outs, (f, f, 1 - f, 1 - f), (k, 1 - k, k, 1 - k)):
-        at = pl.multiple_of(ff * half + kk * quarter, 16)
-        for w in range(3):
-            ref[w * quarter : (w + 1) * quarter] = turned[w, pl.ds(at, quarter)]
     rows = x.shape[0]
+    columns = x.shape[1] // 128
+    chunk = half // CHIPS
+    sign = 1 - 2 * k
+    for ref, part, way in zip(outs, (f, f, 1 - f, 1 - f), (sign, -sign, sign, -sign)):
+        for j in range(5):
+            pos = lax.rem(spot[2] + CHIPS + way * j, CHIPS)
+            at = pl.multiple_of(part * half + pos * chunk, 16)
+            for w in range(3):
+                start = (w * 5 + j) * chunk
+                ref[start : start + chunk] = turned[w, pl.ds(at, chunk)]
+    line = sums_line(squares)
+    tail = jnp.concatenate([sums_tail(line, 128), jnp.zeros((8, 128), F32)], axis=0).astype(BF)
     for ref in outs[:3]:
-        for w, right in enumerate((dy_b, d_h)):
-            for c in range(right.shape[1] // 128):
-                start = 3 * quarter + (w * (right.shape[1] // 128) + c) * rows
+        start = 15 * chunk
+        for right in (dy_b, d_h):
+            for c in range(columns):
                 ref[start : start + rows] = right[:, c * 128 : (c + 1) * 128]
+                start += rows
+        ref[start : start + 16] = tail
+
+
+def sums_tail(line, width):
+    high = line.astype(BF).astype(F32)
+    row = lax.broadcasted_iota(jnp.int32, (8, 128), 0)
+    tail = jnp.where(row == 0, high, jnp.where(row == 1, line - high, 0.0))
+    return tail if width == 128 else jnp.concatenate([tail, jnp.zeros((8, width - 128), F32)], axis=1)
+
+
+def sums_line(sums):
+    lane = lax.broadcasted_iota(jnp.int32, (1, 128), 1)
+    return jnp.where(lane == 0, sums[0:1], jnp.where(lane == 1, sums[1:2], 0.0))
 
 
 def pooled_grad_body(own, sib, far, far_left, far_right, *refs):
     gs, out = refs[:4], refs[4]
     model = out.shape[2]
     columns = model // 128
-    quarter = far_left.shape[0] // 3
+    group = far_left.shape[0] // 3
+    chunk = group // 5
     rows = 128
     totals = []
     for w in range(3):
@@ -481,8 +532,8 @@
         for at, (left, right) in enumerate(
             ((own, own), (sib, sib), (far, far), (far_left, far_right))
         ):
-            lefts.append(left[w * quarter : (w + 1) * quarter])
-            start = 3 * quarter + w * columns * rows
+            lefts.append(left[w * group : (w + 1) * group])
+            start = 3 * group + w * columns * rows
             if w == 2:
                 rights.append(gs[at][...])
                 continue
@@ -493,55 +544,56 @@
             )
         left, right = jnp.concatenate(lefts, axis=1), jnp.concatenate(rights, axis=0)
         totals.append(dot(left, right, NN))
-    for c in range(CHIPS):
-        rows = [t[40 * c : 40 * c + 40] for t in totals] + [jnp.zeros((8, model), F32)]
-        out[c] = jnp.concatenate(rows, axis=0).astype(BF)
-
-
-def reduce_step_body(step, spot, up, down, *refs):
-    received, (up_out, down_out) = refs[:-2], refs[-2:]
-    model = up.shape[2]
-    for side, (block, out) in enumerate(((up, up_out), (down, down_out))):
-        near = slice(side * model // 2, (side + 1) * model // 2)
-        if step == 0:
-            out[...] = block[0, :, near]
-            continue
-        add = received[side][...].astype(F32)
-        if step == 1:
-            out[...] = block[0]
-            out[:, near] = (block[0, :, near].astype(F32) + add).astype(BF)
+    line = jnp.zeros((1, 128), F32)
+    for ref in (own, sib, far, far_right):
+        tail = ref[ref.shape[0] - 16 :].astype(F32)
+        line = line + tail[0:1] + tail[1:2]
+    for j in range(5):
+        parts = [t[chunk * j : chunk * (j + 1)] for t in totals]
+        tail = jnp.zeros((16, model), F32)
+        if j == 0:
+            tail = jnp.concatenate([sums_tail(line, model), tail[:8]], axis=0)
+        out[j] = jnp.concatenate([*parts, tail], axis=0).astype(BF)
+
+
+def reduce_step_body(step, spot, block, *refs):
+    received, out = refs[:-1], refs[-1]
+    half = block.shape[2] // 2
+    near = pl.ds(pl.multiple_of(spot[1] * half, 128), half)
+    if step == 0:
+        out[...] = block[0, :, near]
+    elif step == 1:
+        out[...] = block[0]
+        out[:, near] = (block[0, :, near].astype(F32) + received[0][...].astype(F32)).astype(BF)
+    else:
+        out[...] = (block[0].astype(F32) + received[0][...].astype(F32)).astype(BF)
+
+
+def reduce_end_body(spot, block, mine, near, out):
+    out[...] = (block[0].astype(F32) + mine[...].astype(F32) + near[...].astype(F32)).astype(BF)
+
+
+def rows_place_body(elements, spot, *refs):
+    arrays, (w_hidden, gain), refs = refs[:9], refs[9:11], refs[11:]
+    outs, (gain_out, means_out) = refs[:3], refs[3:]
+    chunk = outs[0].shape[0] // CHIPS
+    tail = jnp.zeros((8, 128), F32)
+    positions = ring_positions(spot)
+    for at in range(9):
+        block = arrays[at][...].astype(F32)
+        rows = pl.ds(pl.multiple_of(positions[min(at, 7)] * chunk, 16), chunk)
+        core = spot[1] if at == 7 else 1 - spot[1]
+        width = block.shape[1]
+        for w in range(3):
+            part = block[w * chunk : (w + 1) * chunk]
+            if at < 7:
+                outs[w][rows] = part
+            else:
+                outs[w][rows, pl.ds(pl.multiple_of(core * width, 128), width)] = part
+        if at < 7:
+            tail = tail + block[3 * chunk : 3 * chunk + 8, :128]
         else:
-            out[...] = (block[0].astype(F32) + add).astype(BF)
-
-
-def reduce_end_body(spot, block, up, down, sums, sums_x, out):
-    model = block.shape[2]
-    total = block[0].astype(F32) + up[...].astype(F32) + down[...].astype(F32)
-    pair = sums[...] + sums_x[...]
-    high = pair.astype(BF).astype(F32)
-    low = pair - high
-    lane = lax.broadcasted_iota(jnp.int32, (8, 128), 1)
-    row = lax.broadcasted_iota(jnp.int32, (8, 128), 0)
-    first = jnp.where(row == 0, high[0:1], low[0:1])
-    second = jnp.where(row == 0, high[1:2], low[1:2])
-    tail = jnp.where(row < 2, jnp.where(lane == 0, first, jnp.where(lane == 1, second, 0.0)), 0.0)
-    tail = jnp.concatenate([tail, jnp.zeros((8, model - 128), F32)], axis=1)
-    out[...] = jnp.concatenate([total[:120], tail], axis=0).astype(BF)
-
-
-def rows_place_body(layout, elements, place, *refs):
-    count, blocks = layout
-    arrays, (w_hidden, gain), refs = refs[:count], refs[count : count + 2], refs[count + 2 :]
-    outs, (gain_out, means_out) = refs[:3], refs[3:]
-    tail = jnp.zeros((8, 128), F32)
-    for entry, parts in blocks:
-        block = [arrays[which][row : row + 128] for which, row in parts]
-        block = jnp.concatenate(block, axis=1) if len(block) > 1 else block[0]
-        block = block.astype(F32)
-        at = pl.multiple_of(place[entry] * 40, 8)
-        for w in range(3):
-            outs[w][pl.ds(at, 40)] = block[w * 40 : w * 40 + 40]
-        tail = tail + block[120:, :128]
+            tail = tail + jnp.where(core == 0, block[3 * chunk : 3 * chunk + 8, :128], 0.0)
     means = jnp.sqrt((tail[0:1, :2] + tail[1:2, :2]) / elements)
     means_out[...] = means.reshape(2)
     half, model = w_hidden.shape
@@ -552,28 +604,14 @@
     gain_out[...] = line.reshape(half)
 
 
-def inputs_product_body(back, back_x, w_q, w_k, w_v, own, other, turned):
-    for side, pieces in enumerate((back, back_x)):
-        for h in range(H):
-            for w in range(3):
-                turned[w, h * HD : h * HD + HD, side * 128 : side * 128 + 128] = pieces[
-                    h, w * HD : w * HD + HD
-                ]
-    total = dot(w_q[...], turned[0], NN) + dot(w_k[...], turned[1], NN)
-    total = total + dot(w_v[...], turned[2], NN)
-    own[...] = total[:, :128]
-    other[...] = total[:, 128:].astype(BF)
-
-
-def inputs_grad_body(spot, x_in, dy_in, gains, own, received, out):
-    mine, theirs = own[...].T, received[...].astype(F32).T
-    f = spot[0]
-    left = jnp.where(f == 0, mine, theirs)
-    right = jnp.where(f == 0, theirs, mine)
+def inputs_grad_body(spot, block, mine, near, x_in, dy_in, gains, out):
+    size = out.shape[0]
+    rows = pl.ds(pl.multiple_of(spot[1] * size, 16), size)
+    d_norm = block[0, rows].astype(F32) + mine[rows].astype(F32) + near[rows].astype(F32)
     x = x_in[...].astype(F32)
     inv = lax.rsqrt(jnp.mean(x * x, axis=-1, keepdims=True) + EPSILON)
     unit = x * inv
-    c1 = jnp.concatenate([left, right], axis=1) * gains[0:1]
+    c1 = d_norm * gains[0:1]
     dx = inv * (c1 - unit * jnp.mean(c1 * unit, axis=-1, keepdims=True)) + dy_in[...]
     out[...] = dx.astype(BF)
 
@@ -616,8 +654,26 @@
         ]
         return lax.ppermute(a, "ctx", pairs)
 
+    def ring_by_core(a):
+        pairs = [
+            (
+                g * GROUP + RING[i] * 2 + core,
+                g * GROUP + RING[(i + 1 - 2 * core) % CHIPS] * 2 + core,
+            )
+            for g in range(groups)
+            for i in range(CHIPS)
+            for core in range(2)
+        ]
+        return lax.ppermute(a, "ctx", pairs)
+
     def swap_core(a):
         return lax.ppermute(a, "ctx", [(c, c ^ 1) for c in range(ctx_count)])
+
+    def swap_far(a):
+        pairs = [
+            (2 * c + side, 2 * (c ^ 1) + 1 - side) for c in range(ctx_count) for side in range(2)
+        ]
+        return lax.ppermute(a, ("ctx", "fsdp"), pairs)
 
     def swap_x(a):
         return lax.ppermute(a, "fsdp", [(0, 1), (1, 0)])
@@ -649,18 +705,6 @@
 
     def ring_step(up, down):
         return ring(up, 1), ring(down, -1)
-
-    def ring_gather(a, axis, cut, hold=lambda v: v):
-        up = down = a
-        found = [(a, swap_core(a))]
-        for _ in range(3):
-            up, down = ring(up, 1), ring(down, -1)
-            found.append((up, down, swap_core(up), swap_core(down)))
-        size = a.shape[axis]
-        up = ring(hold(lax.slice_in_dim(up, 0, cut, axis=axis)), 1)
-        down = ring(hold(lax.slice_in_dim(down, cut, size, axis=axis)), -1)
-        found.append((up, down, swap_core(up), swap_core(down)))
-        return found
 
     source = jnp.asarray(SOURCE, jnp.int32)[head]
     place = jnp.asarray(PLACE, jnp.int32)[head]
@@ -746,11 +790,8 @@
         return gates([a], after)[0]
 
     steps = [(x,), ring_step(x, x)]
-    for step in range(2, 5):
-        up, down = steps[-1]
-        if step == 4:
-            up, down = up[: dev_rows // 2], down[dev_rows // 2 :]
-        steps.append(ring_step(up, down))
+    for _ in range(2):
+        steps.append(ring_step(*steps[-1]))
     early = quarter // 5 * 2
     out_xs = [swap_x(lax.dynamic_slice_in_dim(w_output, k * quarter, early, 0))]
     (slab,) = call(
@@ -789,30 +830,28 @@
     weight_sib = swap_core(weight_t)
 
     norms = None
-    sibs, queries, keys, others = [], [], [], []
+    queries, keys, far_keys, near = [], [], [], []
     norms = None
     slot = 0
-    for step, arrays in enumerate(([x, *steps[1], *steps[2]], steps[3], steps[4])):
+    for step in range(2):
+        if step:
+            up, down = gates(steps[3], queries)
+            arrays = [up, down, *ring_step(up[: dev_rows // 2], down[dev_rows // 2 :])]
+        else:
+            arrays = [x, *steps[1], *steps[2]]
         count = sum(a.shape[0] for a in arrays) // dev_rows
-        moved = (w_hidden, w_return) if step == 2 else ()
-        previous = sibs[-1:]
-        outs = [
-            ((CHIPS, dev_rows, model), BF),
-            ((count, HD, 128), BF),
-            ((count + sum(p.shape[0] for p in previous), 2 * HD, 128), BF),
-            ((count, 3 * HD, 128), BF),
-        ]
+        moved = (w_hidden, w_return) if step else ()
+        outs = [((CHIPS, dev_rows, model), BF)]
+        outs += [((count, HD, 128), BF), ((count, 2 * HD, 128), BF)]
+        outs += [((count, 3 * HD, 128), BF), ((count, 2 * HD, 128), BF)]
         outs += [((quarter, model), BF)] * len(moved)
-        ins = [spot, *arrays, gains, weight_t, weight_sib, scale_col, *previous, *moved]
+        ins = [spot, *arrays, gains, weight_t, weight_sib, scale_col, *moved]
         ins += [norms] if step else []
-        norms, q_part, kv_part, sib_part, *moved_parts = call(
-            functools.partial(
-                project_body, (len(arrays), count, bool(previous), len(moved), slot)
-            ),
+        norms, q_part, kv_part, near_part, far_part, *moved_parts = call(
+            functools.partial(project_body, (len(arrays), count, len(moved), slot)),
             outs,
             ins,
-            specs=[vmem_spec] * (len(arrays) + 4 + len(previous))
-            + [any_spec] * (len(moved) + bool(step)),
+            specs=[vmem_spec] * (len(arrays) + 4) + [any_spec] * (len(moved) + bool(step)),
             out_specs=[any_spec] + [vmem_spec] * (len(outs) - 1),
             scratch=[
                 pltpu.VMEM((count, dev_rows, model), BF),
@@ -820,66 +859,50 @@
                 pltpu.SemaphoreType.DMA,
             ],
             smem=1,
-            after=[(), out_xs[1:], others[:1]][step],
+            after=[(), out_xs[1:]][step],
             aliases={len(ins) - 1: 0} if step else None,
             name="project",
-            us=[3, 2, 2, 2][step],
-            mib=16,
+            us=[3, 3][step],
+            mib=60,
         )
         slot += count
         queries.append(q_part)
         keys.append(kv_part)
-        sibs.append(swap_core(sib_part))
-        others.append(swap_x(kv_part))
+        far_keys += [swap_x(kv_part), swap_far(far_part)]
+        near.append(swap_core(near_part))
     hid_part, ret_part = moved_parts
-    others.append(swap_x(sibs[-1]))
     norms_sib = swap_core(norms)
     parts = [w_output]
     for out_x in out_xs:
         out_x = gate(out_x, [norms])
         parts += [out_x, swap_core(out_x)]
-    hid_x = swap_x(gate(hid_part, others))
-    ret_x = swap_x(gate(ret_part, others))
-
-    arrays = queries + sibs + keys + others
-    n_steps = len(queries)
-    places = []
-    own_entries, sib_entries = list(OWN_ENTRIES), list(SIB_ENTRIES)
+    hid_x = swap_x(gate(hid_part, far_keys))
+    ret_x = swap_x(gate(ret_part, far_keys))
+
+    arrays, places = [], []
     at = 0
-    for step in range(n_steps):
-        count = queries[step].shape[0]
-        for j in range(count):
-            own, sib = own_entries[at + j], sib_entries[at + j]
-            places.append(("q", step, j, 0, own, 0))
-            places.append(("q", n_steps + step, j, 0, sib, 0))
-            places.append(("kv", 2 * n_steps + step, j, 0, own, 0))
-            places.append(("kv", 3 * n_steps + step, j, 0, own, 1))
-            if step + 1 < n_steps:
-                index = queries[step + 1].shape[0] + j
-                places.append(("kv", 2 * n_steps + step + 1, index, 0, sib, 0))
-                places.append(("kv", 3 * n_steps + step + 1, index, 0, sib, 1))
-            else:
-                places.append(("kv", n_steps + step, j, HD, sib, 0))
-                places.append(("kv", 4 * n_steps, j, HD, sib, 1))
+    for step, q_part in enumerate(queries):
+        mine, theirs = (q_part, keys[step], far_keys[2 * step]), (near[step], far_keys[2 * step + 1])
+        count = q_part.shape[0]
+        for entries, blocks_of in ((OWN_ENTRIES, mine), (SIB_ENTRIES, theirs)):
+            for j in range(count):
+                entry = entries[at + j]
+                last = len(arrays) + len(blocks_of) - 1
+                places.append(("q", len(arrays), j, entry, 0))
+                places.append(("kv", last - 1, j, entry, 0))
+                places.append(("kv", last, j, entry, 1))
+            arrays += blocks_of
         at += count
     if groups > 1:
-        mine = [*keys, sibs[-1][:, HD:]]
-        theirs = [*others[:-1], others[-1][:, HD:]]
-        order = []
-        at = 0
-        for step in range(n_steps + 1):
-            count = queries[step].shape[0] if step < n_steps else 0
-            order += own_entries[at : at + count]
-            if step:
-                before = queries[step - 1].shape[0]
-                order += sib_entries[at - before : at]
-            at += count
+        order = OWN_ENTRIES + SIB_ENTRIES
+        mine = jnp.concatenate([*keys, *[a[:, HD:] for a in near]], axis=0)
+        theirs = jnp.concatenate([*far_keys[::2], *far_keys[1::2]], axis=0)
         for by in range(1, groups):
-            for side, parts_of in enumerate((mine, theirs)):
-                which = len(arrays)
-                arrays.append(turn_groups(jnp.concatenate(parts_of, axis=0), by))
-                for j in range(GROUP):
-                    places.append(("kv", which, j, 0, by * GROUP + order[j], side))
+            for side, a in enumerate((mine, theirs)):
+                places += [
+                    ("kv", len(arrays), j, by * GROUP + order[j], side) for j in range(GROUP)
+                ]
+                arrays.append(turn_groups(a, by))
     pieces, q_t, k_t, k_rows, v_rows, att, lse = call(
         functools.partial(forward_body, {"arrays": len(arrays), "blocks": places}, chunks),
         [
@@ -905,15 +928,15 @@
         mib=36 if groups == 1 else 60,
     )
     att_t = exchange(pieces).reshape(model, dev_rows)
-    for first, w, when in ((hid_x, w_hidden, pieces), (ret_x, w_return, att_t)):
-        first = gate(first, [when])
+    hid_x, ret_x = gates([hid_x, ret_x], [att_t])
+    for w, first in ((w_hidden, hid_x), (w_return, ret_x)):
         parts += [w, first, swap_core(first)]
 
-    g_sib = swap_core(g_rows)
-    g_x = swap_x(gate(g_rows, [pieces]))
-
-    share_rows = 3 * quarter + 2 * (model // 128) * dev_rows
-    stream, dy, datt_t, f_own, f_sib, f_x, f_xs, sums = call(
+    g_sib, g_x = swap_core(g_rows), swap_x(gate(g_rows, [pieces]))
+
+    left_rows = 15 * (half // CHIPS)
+    share_rows = left_rows + 2 * (model // 128) * dev_rows + 16
+    stream, dy, datt_t, f_own, f_sib, f_x, f_xs = call(
         rows_body,
         [
             ((dev_rows, model), BF),
@@ -922,8 +945,7 @@
             ((share_rows, 128), BF),
             ((share_rows, 128), BF),
             ((share_rows, 128), BF),
-            ((3 * quarter, 128), BF),
-            ((8, 128), F32),
+            ((left_rows, 128), BF),
         ],
         [spot, att_t, x, g_rows, gains, *parts],
         specs=[vmem_spec] * 4 + [any_spec] * 11,
@@ -934,217 +956,210 @@
         mib=60,
         us=10,
     )
-    datt_t, g_sib, g_x = gates([datt_t, g_sib, g_x], ())
+    datt_t, g_x = gates([datt_t, g_x], ())
     grads = exchange(datt_t.reshape(GROUP, HD, dev_rows))
-    g_xs, sums_x = swap_core(g_x), swap_x(sums)
+    g_xs = swap_core(g_x)
 
     from_x = swap_x(f_x)
-    from_sib = swap_core(f_sib)
     forward = swap_core(f_xs)
-    from_xs = swap_x(forward)
-
-    def chunk_call(body, shifts, ins, outs, name, after):
-        def at(shift):
-            return pl.BlockSpec((1, 128, model), lambda i, spot: ((spot[2] + shift) % CHIPS, 0, 0))
-
+    from_sib, from_xs = swap_core(f_sib), swap_x(forward)
+
+    def chunk_call(table, body, chunk, ins, outs, name, after):
         return call(
             body,
             outs,
-            [spot, *([partial] * len(shifts)), *ins],
-            specs=[at(s) for s in shifts] + [whole(a.shape) for a in ins],
+            [spot, table, *ins],
+            specs=[pl.BlockSpec((1, 256, model), lambda i, spot: (chunk, 0, 0))]
+            + [whole(a.shape) for a in ins],
             out_specs=[whole(shape) for shape, _ in outs],
             smem=1,
             grid=(1,),
             after=after,
             name=name,
-            us=2.8,
-            mib=8,
+            us=2,
+            mib=16,
         )
 
-    def reduce_step(step, received, after):
-        shift = 4 - step
-        up, down = chunk_call(
+    def reduce_step(table, step, received, after):
+        outs = chunk_call(
+            table,
             functools.partial(reduce_step_body, step),
-            (shift, CHIPS - shift),
+            4 - step,
             received,
-            [((128, model if step else model // 2), BF)] * 2,
+            [((256, model if step else model // 2), BF)],
             "reduce_step",
             after,
         )
-        return (ring(up, 1), ring(down, -1)), [up]
-
-    low = chunks // 4
-
-    def backward(first, size, outs, ins, scratch, after, us):
-        return call(
-            functools.partial(backward_body, first, not first, low if first else 0),
-            [((size, 2 * HD, 256), F32), ((size, 2 * HD, 256), BF), *outs],
-            [slots_out, begin, clear, qblock, scale_col, *ins],
-            scratch=[*scratch, pltpu.VMEM((2 * GROUP, HD, 64), BF)],
+        return [ring_by_core(outs[0])], outs
+
+    cuts = (chunks, chunks // 8, 0)
+    state = [((tiles, HD, width), BF), ((tiles, 1, width), F32), ((tiles, HD, width), F32)]
+    owns, receiveds = [], []
+    handed = [grads, att]
+    dq, done = [], [forward]
+    for at in range(2):
+        low, size = cuts[at + 1], cuts[at] - cuts[at + 1]
+        given, stat = handed
+        outs = [((size, 2 * HD, 256), F32), ((size, 2 * HD, 256), BF)]
+        outs += [((GROUP, HD, 128), BF), ((HD, width), F32)] if at else state
+        own, other, *more = call(
+            functools.partial(backward_body, at == 0, at == 1, low),
+            outs,
+            [slots_out, begin, clear, qblock, scale_col]
+            + [given, q_t, stat, lse, *dq, k_t, k_rows, v_rows],
+            specs=[vmem_spec] * (6 + len(dq)) + [any_spec] * 3,
+            scratch=[pltpu.VMEM((tiles, HD, width), F32)] * at
+            + [
+                pltpu.VMEM((2 * GROUP, HD, 64), BF),
+                pltpu.VMEM((size, HD, 512), BF),
+                pltpu.VMEM((size, 512, HD), BF),
+                pltpu.VMEM((size, 512, HD), BF),
+                pltpu.SemaphoreType.DMA((3,)),
+            ],
             smem=3,
-            after=after,
+            after=done,
             name="attention_backward",
-            us=us,
+            us=[20, 7][at],
             mib=60,
         )
-
-    state = [((tiles, HD, width), BF), ((tiles, 1, width), F32), ((tiles, HD, width), F32)]
-    ins = [q_t, k_t, k_rows, v_rows]
-    own_high, other_high, grad_t, delta, dq = backward(
-        True, chunks - low, state, [grads, *ins, att, lse], [], [forward], 16
-    )
-    high_x = swap_x(other_high)
-    from_x, from_sib, from_xs, g_xs, sums_x = gates(
-        [from_x, from_sib, from_xs, g_xs, sums_x], [own_high]
-    )
-    back_xs = swap_core(from_x)
+        owns.insert(0, own)
+        receiveds.insert(0, swap_x(other))
+        if not at:
+            *handed, dq_now = more
+            dq, done = [dq_now], []
+            from_x, from_sib, from_xs, g_xs, norms_sib = gates(
+                [from_x, from_sib, from_xs, g_xs, norms_sib], [own]
+            )
+            back_xs = swap_core(from_x)
+    dq_pieces, scale_sum = more
     (partial,) = call(
         pooled_grad_body,
-        [((CHIPS, 128, model), BF)],
+        [((5, 256, model), BF)],
         [f_own, from_sib, from_x, from_xs, back_xs, g_rows, g_sib, g_x, g_xs],
+        after=[dq_pieces],
         name="pooled_grads",
-        us=2,
+        us=3,
         mib=24,
     )
-    received, done = reduce_step(0, (), ())
-    own_low, other_low, dq_pieces, scale_sum = backward(
-        False,
-        low,
-        [((GROUP, HD, 128), BF), ((HD, width), F32)],
-        [grad_t, *ins, delta, lse, dq],
-        [pltpu.VMEM((tiles, HD, width), F32)],
-        done,
-        10,
-    )
-    low_x = swap_x(other_low)
-    owns, receiveds = [own_low, own_high], [low_x, high_x]
-
-    received, done = reduce_step(1, received, [dq_pieces, high_x])
+    received, done = reduce_step(partial, 0, (), ())
     if groups > 1:
         for at in range(2):
             owns[at] = sum_groups(owns[at] + receiveds[at].astype(F32), BF)
             receiveds[at] = jnp.zeros_like(receiveds[at])
-    (d_pieces,) = call(
+    d_pieces, d_other = call(
         join_body,
-        [((GROUP, 3 * HD, 128), BF)],
-        [slots_ctx, dq_pieces, *owns, *receiveds],
+        [((GROUP, 3 * HD, 128), BF), ((10, 3 * HD, 128), BF)],
+        [slots_ctx, spot, dq_pieces, *owns, *receiveds],
         scratch=[pltpu.VMEM((blocks, 2 * HD, 64), BF)],
-        smem=1,
-        after=received,
+        smem=2,
+        after=done,
         name="join",
         us=2,
         mib=24 if groups == 1 else 60,
     )
-    back = exchange(d_pieces)
-    received, done = reduce_step(2, received, [d_pieces])
+    d_near = swap_core(d_other)
     own_share, other_share = call(
         qkv_grad_body,
         [((3 * HD + 16, half), F32), ((3 * HD + 16, half), BF)],
-        [source, spot, d_pieces, scale_sum, norms, norms_sib],
+        [place, spot, d_pieces, scale_sum, norms, norms_sib],
         scratch=[pltpu.VMEM((3 * HD, model), F32)],
         smem=2,
-        after=done,
         name="qkv_grads",
         us=4.7,
         mib=24,
     )
     share_x = swap_x(other_share)
+    received, done = reduce_step(partial, 1, received, [own_share])
+
+    (table,) = call(
+        products_body,
+        [((5, 256, model), BF)],
+        [spot, d_pieces, d_near, weight_t, weight_sib],
+        smem=1,
+        after=done,
+        name="products",
+        us=4,
+        mib=24,
+    )
+    first, done = reduce_step(table, 0, (), ())
     (share,) = call(
         qkv_sum_body,
         [((3 * HD + 16, half), BF)],
         [own_share, share_x, slab],
+        after=done,
         name="qkv_sum",
         us=1,
         mib=8,
     )
     share = sum_groups(share.astype(F32), BF).astype(BF) if groups > 1 else share
-
-    def handed(arrays, after=()):
-        rows = sum(a.shape[0] * (a.shape[1] // half) for a in arrays)
-        (packed,) = call(
-            pack_body, [((rows, half), BF)], arrays, after=after, name="pack", us=1, mib=8
-        )
-        return swap_core(packed)
-
-    q_now, q_sib = ring_step(share, share), swap_core(share)
-    received, done = reduce_step(3, received, [share])
-    back = gate(back, received)
-    back_x = swap_x(back)
+    share_near = swap_core(share)
+    received, done = reduce_step(partial, 2, received, [share, *first])
+    first, done = reduce_step(table, 1, first, done)
+    (chip_share,) = call(
+        chip_pack_body,
+        [((2 * (3 * HD + 16), half), BF)],
+        [spot, share, share_near],
+        smem=1,
+        after=done,
+        name="chip_pack",
+        us=1,
+        mib=8,
+    )
+    q_steps = [chip_share, ring_by_core(chip_share)]
+    received, done = reduce_step(partial, 3, received, [chip_share])
+    received_near = swap_core(received[0])
+    first, done = reduce_step(table, 2, first, [*done, q_steps[1]])
     (mine,) = chunk_call(
-        reduce_end_body, (0,), (*received, sums, sums_x), [((128, model), BF)], "reduce_end", q_now
+        partial,
+        reduce_end_body,
+        0,
+        (*received, received_near),
+        [((256, model), BF)],
+        "reduce_end",
+        done,
     )
     mine = sum_groups(mine.astype(F32), BF).astype(BF) if groups > 1 else mine
-    sibs = [handed([*q_now, mine])]
-    q_own, m_own = [share, *q_now], [mine]
-    q_now, m_now = ring_step(*q_now), ring_step(mine, mine)
-    product, product_other = call(
-        inputs_product_body,
-        [((half, dev_rows), F32), ((half, dev_rows), BF)],
-        [back, back_x, w_query, w_key, w_value],
-        scratch=[pltpu.VMEM((3, model, 2 * dev_rows), BF)],
-        after=[mine],
-        name="inputs_product",
-        us=3,
-        mib=24,
-    )
-    product_x = swap_x(product_other)
-    for step in (2, 3, 4):
-        waits = {2: [product], 3: [product_x], 4: ()}[step]
-        sibs.append(handed([*q_now, *m_now], waits))
-        q_own += q_now
-        m_own += m_now
-        if step == 2:
-            q_now, m_now = ring_step(*q_now), ring_step(*m_now)
-        elif step == 3:
-            q_now, m_now = ring_step(q_now[0][:128], q_now[1][128:]), ring_step(*m_now)
-            (d_in,) = call(
-                inputs_grad_body,
-                [((dev_rows, model), BF)],
-                [spot, x, dy, gains, product, product_x],
-                smem=1,
-                after=sibs[-1:],
-                name="inputs_grad",
-                us=2,
-                mib=16,
-            )
-        else:
-            m_now = ring_step(m_now[0][:, : model // 2], m_now[1][:, model // 2 :])
-
-    q_arrays = [*q_own, q_sib, *sibs]
-    q_blocks = [(entry, [(at, 0, 256)]) for at, entry in enumerate(OWN_ENTRIES[:7])]
-    q_blocks.append((OWN_ENTRIES[7], [(7, 0, 128), (8, 0, 128)]))
-    q_blocks.append((SIB_ENTRIES[0], [(9, 0, 256)]))
-    q_blocks += [
-        (entry, [(10 + at // 2, at % 2 * 256, 256)]) for at, entry in enumerate(SIB_ENTRIES[1:])
-    ]
+    m_steps = [mine, ring_by_core(mine)]
+    q_steps.append(ring_by_core(q_steps[-1]))
+    first, done = reduce_step(table, 3, first, [mine, q_steps[2]])
+    m_steps.append(ring_by_core(m_steps[-1]))
+    q_steps.append(ring_by_core(q_steps[-1]))
+    m_steps.append(ring_by_core(m_steps[-1]))
+    first_near = swap_core(first[0])
+    (d_in,) = chunk_call(
+        table,
+        inputs_grad_body,
+        0,
+        (*first, first_near, x, dy, gains),
+        [((dev_rows, model), BF)],
+        "inputs_grad",
+        [m_steps[2], q_steps[3]],
+    )
+
+    def last_step(a, axis):
+        size = a.shape[axis] // 2
+        return ring_by_core(lax.dynamic_slice_in_dim(a, k * size, size, axis))
+
+    q_last, m_last = last_step(q_steps[-1], 0), last_step(m_steps[-1], 1)
+    q_near = [swap_core(a) for a in q_steps[1:]]
+    m_near = [swap_core(a) for a in m_steps[1:]]
     grad_query, grad_key, grad_value, gain_one_grad, scale_grad = call(
-        functools.partial(qkv_place_body, (len(q_arrays), q_blocks)),
+        qkv_place_body,
         [((half, model), F32)] * 3 + [((half,), F32), ((part,), F32)],
-        [source, spot, *q_arrays, gain_attn, scale_row],
+        [spot, *q_steps, *q_near, q_last, swap_core(q_last), gain_attn, scale_row],
         scratch=[pltpu.VMEM((3, model, half), BF)],
-        smem=2,
+        smem=1,
         after=[d_in],
         name="qkv_place",
         us=6,
         mib=40,
     )
-    m_now = gates(m_now, [grad_query])
-    m_own += m_now
-    m_arrays = [*m_own, *sibs, *swap_cores(m_now)]
-    m_blocks = [(entry, [(at, 0)]) for at, entry in enumerate(OWN_ENTRIES[:7])]
-    m_blocks.append((OWN_ENTRIES[7], [(7, 0), (8, 0)]))
-    first = len(m_own)
-    starts = [(0, 512), (1, 512), (1, 768), (2, 512), (2, 768), (3, 256), (3, 512)]
-    m_blocks += [
-        (entry, [(first + at, row), (first + at, row + 128)])
-        for entry, (at, row) in zip(SIB_ENTRIES, starts)
-    ]
-    m_blocks.append((SIB_ENTRIES[7], [(first + 4, 0), (first + 5, 0)]))
+    (m_last,) = gates([m_last], [grad_query])
     elements = float(ctx_count * 2 * dev_rows * model)
     grad_output, grad_hidden, grad_return, gain_two_grad, root_means = call(
-        functools.partial(rows_place_body, (len(m_arrays), m_blocks), elements),
+        functools.partial(rows_place_body, elements),
         [((half, model), F32)] * 3 + [((half,), F32), ((2,), F32)],
-        [place, *m_arrays, w_hidden, gain_mlp],
+        [spot, *m_steps, *m_near, m_last, swap_core(m_last), w_hidden, gain_mlp],
         smem=1,
         name="rows_place",
         us=5,

time: 323 us -> 310 us (0.960)
  starting transfers between devices: 73.1 us -> 54.8 us
  local copies, waits for them, and re-layouts: 38.6 us -> 28.4 us
  Pallas kernels: 96.1 us -> 105 us
  waiting for transfers between devices: 94.2 us -> 103 us
    ppermute x0 -> x18, waiting for transfers between devices: none -> 66.4 us  [the longest x16 63.2 us: ring_by_core(): return lax.ppermute(a, 'ctx', pairs)]
    ppermute x32 -> x8, waiting for transfers between devices: 55.6 us -> 5.41 us  [ring(): return lax.ppermute(a, 'ctx', pairs)]
    ppermute x32 -> x8, starting transfers between devices: 37.9 us -> 9.33 us  [ring(): return lax.ppermute(a, 'ctx', pairs)]
    ppermute x0 -> x18, starting transfers between devices: none -> 24.2 us  [the longest x16 24.1 us: ring_by_core(): return lax.ppermute(a, 'ctx', pairs)]
    ppermute x18 -> x13, waiting for transfers between devices: 25.7 us -> 16.7 us  [swap_x(): return lax.ppermute(a, 'fsdp', [(0, 1), (1, 0)])]
    pallas_call x38 -> x37, Pallas kernels: 96.1 us -> 105 us  [call(): pl.pallas_call(run, out_shape=[jax.ShapeDtypeStruct(shape, kind) for shap...]
    ppermute x18 -> x13, starting transfers between devices: 20.5 us -> 12.4 us  [swap_x(): return lax.ppermute(a, 'fsdp', [(0, 1), (1, 0)])]
    unnamed x173 -> x155, local copies, waits for them, and re-layouts: 32.4 us -> 24.7 us
  transfers between devices with their start and end apart: 73 -> 65, of which waited for: 29 -> 29; matrix products, arithmetic and copies ran while one was open for 2% -> 2% of each run, Pallas kernels for 28% -> 31%
where the time goes in v2:
time: 310 us; the launch traced here: 309 us
  Pallas kernels  105 us (34%)
  waiting for transfers between devices  103 us (33%)
  starting transfers between devices  54.8 us (18%)
  local copies, waits for them, and re-layouts  28.4 us (9%)
  blocking collectives  15.3 us (5%)
    pallas_call x37, Pallas kernels, call(): pl.pallas_call(run, out_shape=[jax.ShapeDtypeStruct(shape, kind) for shap...  105 us
    ppermute x16, waiting for transfers between devices, ring_by_core(): return lax.ppermute(a, 'ctx', pairs)  63.2 us
    unnamed x155, local copies, waits for them, and re-layouts  24.7 us
    ppermute x16, starting transfers between devices, ring_by_core(): return lax.ppermute(a, 'ctx', pairs)  24.1 us
    ppermute x13, waiting for transfers between devices, swap_x(): return lax.ppermute(a, 'fsdp', [(0, 1), (1, 0)])  16.7 us
    all_to_all x1, blocking collectives, exchange(): return lax.all_to_all(a, 'ctx', 0, 0, axis_index_groups=which, tiled=True)  15.3 us
    ppermute x13, starting transfers between devices, swap_x(): return lax.ppermute(a, 'fsdp', [(0, 1), (1, 0)])  12.4 us
    ppermute x8, starting transfers between devices, ring(): return lax.ppermute(a, 'ctx', pairs)  9.33 us
  transfers between devices with their start and end apart: 65, of which 29 were waited for; matrix products, arithmetic and copies ran while one was open for 2% of the time, Pallas kernels for 31%

profile of v2, /device:TPU:0, one launch (start us, length us, event | category | flops | bytes accessed | tf_op | source)
XLA Modules:
  0.0 309.1 jit_solution(14513906149119044825)
XLA Ops:
  0.6 3.0 collective-permute-start.1
  4.4 3.2 %slab.1.refs_1_.refs_2_ = bf16[256,640]{1,0:T(8,128)(2,1)} custom-call(s32[4]{0:T(128)} %pad_add_fusion.1.refs_0_.refs_1_, bf16[640,1280]{1,0:T(8,128)(2,1)} %refs_2_.3, bf16[640,1280]{1,0:T(8,128)(2,1)} %refs_2_.3, bf16[640,1280]{1,0:T(8,128)(2,1)} %refs_4_.2, bf16[640,1280]{1,0:T(8,128)(2,1)} %refs_4_.2, bf16[640,1280]{1,0:T(8,128)(2,1)} %refs_6_.1, ...), custom_call_target="tpu_custom_call" | custom-call | flops 3449999872 | bytes 1 | tf_op jit(solution)/shard_map/slab/pallas_call | solution.py:76
  7.7 1.9 collective-permute-start.4
  11.6 1.7 collective-permute-start.3
  13.7 4.8 %collective-permute-done.4.refs_2_.refs_1_ = bf16[256,640]{1,0:T(8,128)(2,1)S(1)} collective-permute-done((bf16[256,640]{1,0:T(8,128)(2,1)}, bf16[256,640]{1,0:T(8,128)(2,1)S(1)}, u32[]{:S(2)}, u32[]{:S(2)}) %collective-permute-start.4) | collective-permute-done | bytes 327712 | tf_op jit(solution)/shard_map/ppermute | solution.py:679
  18.5 5.6 %collective-permute-done.5.refs_5_.refs_0_ = bf16[128,1280]{1,0:T(8,128)(2,1)S(1)} collective-permute-done((bf16[128,1280]{1,0:T(8,128)(2,1)S(1)}, bf16[128,1280]{1,0:T(8,128)(2,1)S(1)}, u32[]{:S(2)}, u32[]{:S(2)}) %collective-permute-start.5) | collective-permute-done | bytes 327712 | tf_op jit(solution)/shard_map/ppermute | solution.py:679
  28.6 1.7 collective-permute-start.11
  30.7 1.6 collective-permute-start.14
  33.1 4.7 %project.2 = (bf16[8,128,1280]{2,1,0:T(8,128)(2,1)}, bf16[5,80,128]{2,1,0:T(8,128)(2,1)}, bf16[5,160,128]{2,1,0:T(8,128)(2,1)}, bf16[5,240,128]{2,1,0:T(8,128)(2,1)}, bf16[5,160,128]{2,1,0:T(8,128)(2,1)}) custom-call(s32[4]{0:T(128)} %pad_add_fusion.1.refs_0_.refs_1_, bf16[128,1280]{1,0:T(8,128)(2,1)} %bitcast.32, bf16[128,1280]{1,0:T(8,128)(2,1)} %copy-done.73, ...), custom_call_target="tpu_custom_call" | custom-call | flops 3449999872 | bytes 1 | tf_op jit(solution)/shard_map/project/pallas_call | solution.py:76
  41.0 1.6 collective-permute-start.13
  43.9 1.6 collective-permute-start.7
  46.4 1.6 collective-permute-done.12.refs_3_
  48.7 4.7 %project.3 = (bf16[8,128,1280]{2,1,0:T(8,128)(2,1)}, bf16[3,80,128]{2,1,0:T(8,128)(2,1)}, bf16[3,160,128]{2,1,0:T(8,128)(2,1)}, bf16[3,240,128]{2,1,0:T(8,128)(2...) custom-call(s32[4]{0:T(128)} %pad_add_fusion.1.refs_0_.refs_1_, ...), custom_call_target="tpu_custom_call", output_to_operand_aliasing={{0}: (11, {})} | custom-call | flops 3449999872 | bytes 1 | tf_op jit(solution)/shard_map/project/pallas_call | solution.py:76
  56.0 3.2 %collective-permute-done.17.refs_15_.refs_4_ = bf16[3,160,128]{2,1,0:T(8,128)(2,1)S(1)} collective-permute-done((bf16[3,160,128]{2,1,0:T(8,128)(2,1)}, bf16[3,160,128]{2,1,0:T(8,128)(2,1)S(1)}, u32[]{:S(2)}, u32[]{:S(2)}) %collective-permute-start.17) | collective-permute-done | bytes 122912 | tf_op jit(solution)/shard_map/ppermute | solution.py:676
  59.3 2.7 collective-permute-done.15.refs_13_.refs_3_
  64.0 2.0 collective-permute-start.21
  66.1 16.6 %attention_forward.1 = (bf16[16,80,128]{2,1,0:T(8,128)(2,1)S(1)}, bf16[4,80,512]{2,1,0:T(8,128)(2,1)S(1)}, bf16[8,80,512]{2,1,0:T(8,128)(2,1)S(1)}, bf16[8,512,8...) custom-call(s32[16,2]{1,0:T(8,128)S(1)} %gather_fusion, ...), custom_call_target="tpu_custom_call" | custom-call | flops 23000000512 | bytes 1 | tf_op jit(solution)/shard_map/attention_forward/pallas_call | solution.py:76
  86.0 15.3 %all_to_all.10 = bf16[16,80,128]{2,1,0:T(8,128)(2,1)S(1)} all-to-all(bf16[16,80,128]{2,1,0:T(8,128)(2,1)S(1)} %get-tuple-element.90.refs_1_), channel_id=1, replica_groups=mesh['ctx'=16,'fsdp'=2] {'ctx'}, dimensions={0} | all-to-all | bytes 655360 | tf_op jit(solution)/shard_map/all_to_all | solution.py:698
  104.2 2.5 collective-permute-done.18.refs_7_
  108.3 10.8 %row_part.1 = (bf16[128,1280]{1,0:T(8,128)(2,1)}, f32[128,1280]{1,0:T(8,128)}, bf16[1280,128]{1,0:T(8,128)(2,1)}, bf16[3776,128]{1,0:T(8,128)(2,1)}, bf16[3776,1...) custom-call(s32[4]{0:T(128)} %pad_add_fusion.1.refs_0_.refs_1_, bf16[1280,128]{1,0:T(8,128)(2,1)} %bitcast.25, ...), custom_call_target="tpu_custom_call" | custom-call | flops 11500000256 | bytes 1 | tf_op jit(solution)/shard_map/row_part/pallas_call | solution.py:76
  120.8 4.2 %all-to-all-start.1 = ((bf16[16,80,128]{2,1,0:T(8,128)(2,1)}), bf16[16,80,128]{2,1,0:T(8,128)(2,1)}, u32[]{:S(2)}, u32[]{:S(2)}) async-start(bf16[16,80,128]{2,1,0:T(8,128)(2,1)} %bitcast.23), calls=%async_computation.1 | async-start | bytes 655360 | tf_op jit(solution)/shard_map/all_to_all | solution.py:698
  126.3 4.2 %collective-permute-done.25.refs_12_ = bf16[1200,128]{1,0:T(8,128)(2,1)} collective-permute-done((bf16[1200,128]{1,0:T(8,128)(2,1)}, bf16[1200,128]{1,0:T(8,128)(2,1)}, u32[]{:S(2)}, u32[]{:S(2)}) %collective-permute-start.25) | collective-permute-done | bytes 307232 | tf_op jit(solution)/shard_map/ppermute | solution.py:670
  130.8 5.4 %all-to-all-done.1.refs_5_ = bf16[16,80,128]{2,1,0:T(8,128)(2,1)} async-done(((bf16[16,80,128]{2,1,0:T(8,128)(2,1)}), bf16[16,80,128]{2,1,0:T(8,128)(2,1)}, u32[]{:S(2)}, u32[]{:S(2)}) %all-to-all-start.1) | async-done | bytes 327712 | tf_op jit(solution)/shard_map/all_to_all | solution.py:698
  136.2 20.0 %attention_backward.2 = (f32[7,160,256]{2,1,0:T(8,128)}, bf16[7,160,256]{2,1,0:T(8,128)(2,1)}, bf16[4,80,512]{2,1,0:T(8,128)(2,1)}, f32[4,1,512]{2,1,0:T(1,128)}, f32[4,80,512]{2,1,0:T(8,128)}) custom-call(s32[16,2]{1,0:T(8,128)} %copy-done.13, s32[8]{0:T(128)} %constant.102.clone.refs_1_, s32[8]{0:T(128)} %constant.103.clone.refs_2_, ...), custom_call_target="tpu_custom_call" | custom-call | flops 23000000512 | bytes 1 | tf_op jit(solution)/shard_map/attention_backward/pallas_call | solution.py:76
  159.7 7.6 %attention_backward.3 = (f32[1,160,256]{2,1,0:T(8,128)}, bf16[1,160,256]{2,1,0:T(8,128)(2,1)}, bf16[16,80,128]{2,1,0:T(8,128)(2,1)}, f32[80,512]{1,0:T(8,128)}) custom-call(s32[16,2]{1,0:T(8,128)} %copy-done.13, s32[8]{0:T(128)} %constant.102.clone.refs_1_, s32[8]{0:T(128)} %constant.103.clone.refs_2_, s32[4,1,512]{2,1,0:T(1,128)} %constant.99.clone.refs_5_.refs_3_, ...), custom_call_target="tpu_custom_call" | custom-call | flops 8049999872 | bytes 1 | tf_op jit(solution)/shard_map/attention_backward/pallas_call | solution.py:76
  167.2 1.8 collective-permute-start.26
  171.2 3.7 %pooled_grads.1.refs_1_ = bf16[5,256,1280]{2,1,0:T(8,128)(2,1)S(1)} custom-call(bf16[3776,128]{1,0:T(8,128)(2,1)S(1)} %copy-done.55, bf16[3776,128]{1,0:T(8,128)(2,1)} %get-tuple-element.118.refs_1_, bf16[3776,128]{1,0:T(8,128)(2,1)} %get-tuple-element.119.refs_2_, bf16[1200,128]{1,0:T(8,128)(2,1)S(1)} %get-tuple-element.120.refs_3_, ...), custom_call_target="tpu_custom_call" | custom-call | flops 3449999872 | bytes 1 | tf_op jit(solution)/shard_map/pooled_grads/pallas_call | solution.py:76
  175.5 1.9 collective-permute-start.36
  177.5 2.3 join.1
  179.9 4.5 %qkv_grads.1 = (f32[256,640]{1,0:T(8,128)S(1)}, bf16[256,640]{1,0:T(8,128)(2,1)S(1)}) custom-call(s32[16]{0:T(128)S(1)} %fusion.1.refs_0_, s32[4]{0:T(128)S(1)} %copy-done.26, bf16[16,240,128]{2,1,0:T(8,128)(2,1)S(1)} %get-tuple-element.122.refs_2_.refs_1_, f32[80,512]{1,0:T(8,128)S(1)} %copy-done.65, bf16[8,128,1280]{2,1,0:T(8,128)(2,1)S(1)} %copy-done, ...), custom_call_target="tpu_custom_call" | custom-call | flops 5405000192 | bytes 1 | tf_op jit(solution)/shard_map/qkv_grads/pallas_call | solution.py:76
  187.1 2.5 products.1.refs_1_
  191.7 3.0 collective-permute-done.39.refs_1_
  194.8 4.9 %collective-permute-done.37.refs_4_.refs_2_ = bf16[256,640]{1,0:T(8,128)(2,1)S(1)} collective-permute-done((bf16[256,640]{1,0:T(8,128)(2,1)S(1)}, bf16[256,640]{1,0:T(8,128)(2,1)S(1)}, u32[]{:S(2)}, u32[]{:S(2)}) %collective-permute-start.37) | collective-permute-done | bytes 327712 | tf_op jit(solution)/shard_map/ppermute | solution.py:667
  204.1 6.9 %collective-permute-done.41.refs_2_ = bf16[256,1280]{1,0:T(8,128)(2,1)S(1)} collective-permute-done((bf16[256,1280]{1,0:T(8,128)(2,1)S(1)}, bf16[256,1280]{1,0:T(8,128)(2,1)S(1)}, u32[]{:S(2)}, u32[]{:S(2)}) %collective-permute-start.41) | collective-permute-done | bytes 655392 | tf_op jit(solution)/shard_map/ppermute | solution.py:667
  216.2 6.2 %collective-permute-done.45.refs_2_ = bf16[256,1280]{1,0:T(8,128)(2,1)S(1)} collective-permute-done((bf16[256,1280]{1,0:T(8,128)(2,1)S(1)}, bf16[256,1280]{1,0:T(8,128)(2,1)S(1)}, u32[]{:S(2)}, u32[]{:S(2)}) %collective-permute-start.45) | collective-permute-done | bytes 655392 | tf_op jit(solution)/shard_map/ppermute | solution.py:667
  222.4 7.0 %collective-permute-done.43.refs_4_.refs_2_ = bf16[512,640]{1,0:T(8,128)(2,1)S(1)} collective-permute-done((bf16[512,640]{1,0:T(8,128)(2,1)S(1)}, bf16[512,640]{1,0:T(8,128)(2,1)S(1)}, u32[]{:S(2)}, u32[]{:S(2)}) %collective-permute-start.43) | collective-permute-done | bytes 655392 | tf_op jit(solution)/shard_map/ppermute | solution.py:667
  230.8 5.6 %collective-permute-done.40.refs_2_ = bf16[256,1280]{1,0:T(8,128)(2,1)S(1)} collective-permute-done((bf16[256,1280]{1,0:T(8,128)(2,1)S(1)}, bf16[256,1280]{1,0:T(8,128)(2,1)S(1)}, u32[]{:S(2)}, u32[]{:S(2)}) %collective-permute-start.40) | collective-permute-done | bytes 655392 | tf_op jit(solution)/shard_map/ppermute | solution.py:667
  240.9 2.5 collective-permute-done.47.refs_4_.refs_3_
  243.4 7.0 %collective-permute-done.44.refs_2_ = bf16[256,1280]{1,0:T(8,128)(2,1)S(1)} collective-permute-done((bf16[256,1280]{1,0:T(8,128)(2,1)S(1)}, bf16[256,1280]{1,0:T(8,128)(2,1)S(1)}, u32[]{:S(2)}, u32[]{:S(2)}) %collective-permute-start.44) | collective-permute-done | bytes 655392 | tf_op jit(solution)/shard_map/ppermute | solution.py:667
  254.9 2.7 collective-permute-done.50.refs_2_
  259.0 5.6 %collective-permute-done.48.refs_2_ = bf16[256,1280]{1,0:T(8,128)(2,1)} collective-permute-done((bf16[256,1280]{1,0:T(8,128)(2,1)}, bf16[256,1280]{1,0:T(8,128)(2,1)}, u32[]{:S(2)}, u32[]{:S(2)}) %collective-permute-start.48) | collective-permute-done | bytes 655392 | tf_op jit(solution)/shard_map/ppermute | solution.py:667
  264.6 6.9 %collective-permute-done.52.refs_8_.refs_4_ = bf16[512,640]{1,0:T(8,128)(2,1)S(1)} collective-permute-done((bf16[512,640]{1,0:T(8,128)(2,1)S(1)}, bf16[512,640]{1,0:T(8,128)(2,1)S(1)}, u32[]{:S(2)}, u32[]{:S(2)}) %collective-permute-start.52) | collective-permute-done | bytes 655392 | tf_op jit(solution)/shard_map/ppermute | solution.py:667
  273.1 5.6 %collective-permute-done.51.refs_7_.refs_3_ = bf16[256,1280]{1,0:T(8,128)(2,1)} collective-permute-done((bf16[256,1280]{1,0:T(8,128)(2,1)}, bf16[256,1280]{1,0:T(8,128)(2,1)}, u32[]{:S(2)}, u32[]{:S(2)}) %collective-permute-start.51) | collective-permute-done | bytes 655392 | tf_op jit(solution)/shard_map/ppermute | solution.py:667
  282.6 1.9 copy-done.53
  285.6 3.0 inputs_grad.1.refs_12_
  292.6 7.2 %qkv_place.1 = (f32[640,1280]{1,0:T(8,128)}, f32[640,1280]{1,0:T(8,128)}, f32[640,1280]{1,0:T(8,128)}, f32[640]{0:T(1024)}, f32[40]{0:T(128)}) custom-call(s32[4]{0:T(128)S(1)} %copy-done.26, bf16[512,640]{1,0:T(8,128)(2,1)S(1)} %copy-done.29, bf16[512,640]{1,0:T(8,128)(2,1)S(1)} %copy-done.33, bf16[512,640]{1,0:T(8,128)(2,1)S(1)} %copy-done.35, ...), custom_call_target="tpu_custom_call" | custom-call | flops 6899999744 | bytes 1 | tf_op jit(solution)/shard_map/qkv_place/pallas_call | solution.py:76
  299.8 1.9 copy-done.1
  303.4 5.7 %rows_place.1 = (f32[640,1280]{1,0:T(8,128)}, f32[640,1280]{1,0:T(8,128)}, f32[640,1280]{1,0:T(8,128)}, f32[640]{0:T(1024)}, f32[2]{0:T(128)}) custom-call(s32[4]{0:T(128)S(1)} %copy-done.26, bf16[256,1280]{1,0:T(8,128)(2,1)S(1)} %copy-done.31, bf16[256,1280]{1,0:T(8,128)(2,1)} %collective-permute-done.50.refs_2_, ...), custom_call_target="tpu_custom_call" | custom-call | flops 5750000128 | bytes 1 | tf_op jit(solution)/shard_map/rows_place/pallas_call | solution.py:76
  (290 shorter events, 75.2 us)
Async XLA Ops:
  0.6 11.0 %collective-permute-start.1 = (bf16[128,1280]{1,0:T(8,128)(2,1)}, bf16[128,1280]{1,0:T(8,128)(2,1)S(1)}, u32[]{:S(2)}, u32[]{:S(2)}) collective-permute-start(bf16[128,1280]{1,0:T(8,128)(2,1)} %bitcast.30), channel_id=1, source_target_pairs={{0,4},{2,6},{8,0},{10,2},{16,8},{18,10},{24,16},{26,18},{28,24},{3... | collective-permute-start | bytes 983048 | tf_op jit(solution)/shard_map/ppermute | solution.py:655
  3.7 9.7 %collective-permute-start = (bf16[128,1280]{1,0:T(8,128)(2,1)}, bf16[128,1280]{1,0:T(8,128)(2,1)S(1)}, u32[]{:S(2)}, u32[]{:S(2)}) collective-permute-start(bf16[128,1280]{1,0:T(8,128)(2,1)} %bitcast.31), channel_id=1, source_target_pairs={{0,8},{2,10},{8,16},{10,18},{16,24},{18,26},{24,28},{26,30},{28,20... | collective-permute-start | bytes 983048 | tf_op jit(solution)/shard_map/ppermute | solution.py:655
  7.7 10.8 %collective-permute-start.4 = (bf16[256,640]{1,0:T(8,128)(2,1)}, bf16[256,640]{1,0:T(8,128)(2,1)S(1)}, u32[]{:S(2)}, u32[]{:S(2)}) collective-permute-start(bf16[256,640]{1,0:T(8,128)(2,1)} %slab.1.refs_1_.refs_2_), channel_id=1, source_target_pairs={{0,1},{1,0},{2,3},{3,2},{4,5},{5,4},{6,7},{7,6},{8,9},{9,8},{10,11... | collective-permute-start | bytes 983048 | tf_op jit(solution)/shard_map/ppermute | solution.py:679
  10.5 13.5 %collective-permute-start.5 = (bf16[128,1280]{1,0:T(8,128)(2,1)S(1)}, bf16[128,1280]{1,0:T(8,128)(2,1)S(1)}, u32[]{:S(2)}, u32[]{:S(2)}) collective-permute-start(bf16[128,1280]{1,0:T(8,128)(2,1)S(1)} %constant_dynamic-slice_fusion.4), channel_id=1, source_target_pairs={{0,1},{1,0},{2,3},{3,2},{4,5},{5,4},{6,7},{7,6},{8,9},{9,8},{10,11... | collective-permute-start | bytes 983048 | tf_op jit(solution)/shard_map/ppermute | solution.py:679
  11.6 12.4 %collective-permute-start.3 = (bf16[128,1280]{1,0:T(8,128)(2,1)S(1)}, bf16[128,1280]{1,0:T(8,128)(2,1)S(1)}, u32[]{:S(2)}, u32[]{:S(2)}) collective-permute-start(bf16[128,1280]{1,0:T(8,128)(2,1)S(1)} %collective-permute-done.1.refs_3_), channel_id=1, source_target_pairs={{0,4},{2,6},{8,0},{10,2},{16,8},{18,10},{24,16},{26,18},{28,24},{3... | collective-permute-start | bytes 983048 | tf_op jit(solution)/shard_map/ppermute | solution.py:655
  13.3 10.8 %collective-permute-start.2 = (bf16[128,1280]{1,0:T(8,128)(2,1)S(1)}, bf16[128,1280]{1,0:T(8,128)(2,1)S(1)}, u32[]{:S(2)}, u32[]{:S(2)}) collective-permute-start(bf16[128,1280]{1,0:T(8,128)(2,1)S(1)} %collective-permute-done.refs_2_), channel_id=1, source_target_pairs={{0,8},{2,10},{8,16},{10,18},{16,24},{18,26},{24,28},{26,30},{28,20... | collective-permute-start | bytes 983048 | tf_op jit(solution)/shard_map/ppermute | solution.py:655
  28.6 9.9 %collective-permute-start.11 = (bf16[128,1280]{1,0:T(8,128)(2,1)S(1)}, bf16[128,1280]{1,0:T(8,128)(2,1)S(1)}, u32[]{:S(2)}, u32[]{:S(2)}) collective-permute-start(bf16[128,1280]{1,0:T(8,128)(2,1)S(1)} %collective-permute-done.3.refs_4_.refs_5_), channel_id=1, source_target_pairs={{0,4},{2,6},{8,0},{10,2},{16,8},{18,10},{24,16},{26,18},{28,24},{3... | collective-permute-start | bytes 983048 | tf_op jit(solution)/shard_map/ppermute | solution.py:655
  30.3 9.8 %collective-permute-start.10 = (bf16[128,1280]{1,0:T(8,128)(2,1)}, bf16[128,1280]{1,0:T(8,128)(2,1)S(1)}, u32[]{:S(2)}, u32[]{:S(2)}) collective-permute-start(bf16[128,1280]{1,0:T(8,128)(2,1)} %copy-done.44), channel_id=1, source_target_pairs={{0,8},{2,10},{8,16},{10,18},{16,24},{18,26},{24,28},{26,30},{28,20... | collective-permute-start | bytes 983048 | tf_op jit(solution)/shard_map/ppermute | solution.py:655
  30.7 14.8 %collective-permute-start.14 = (bf16[192,1280]{1,0:T(8,128)(2,1)S(1)}, bf16[192,1280]{1,0:T(8,128)(2,1)S(1)}, u32[]{:S(2)}, u32[]{:S(2)}) collective-permute-start(bf16[192,1280]{1,0:T(8,128)(2,1)S(1)} %gate.12), channel_id=1, source_target_pairs={{0,1},{1,0},{2,3},{3,2},{4,5},{5,4},{6,7},{7,6},{8,9},{9,8},{10,11... | collective-permute-start | bytes 1474568 | tf_op jit(solution)/shard_map/ppermute | solution.py:679
  43.8 11.2 %collective-permute-start.9 = (bf16[5,160,128]{2,1,0:T(8,128)(2,1)}, bf16[5,160,128]{2,1,0:T(8,128)(2,1)S(1)}, u32[]{:S(2)}, u32[]{:S(2)}) collective-permute-start(bf16[5,160,128]{2,1,0:T(8,128)(2,1)} %get-tuple-element.82), channel_id=1, source_target_pairs={{0,3},{1,2},{2,1},{3,0},{4,7},{5,6},{6,5},{7,4},{8,11},{9,10},{10,... | collective-permute-start | bytes 614408 | tf_op jit(solution)/shard_map/ppermute | solution.py:676
  43.9 12.1 %collective-permute-start.7 = (bf16[5,160,128]{2,1,0:T(8,128)(2,1)}, bf16[5,160,128]{2,1,0:T(8,128)(2,1)S(1)}, u32[]{:S(2)}, u32[]{:S(2)}) collective-permute-start(bf16[5,160,128]{2,1,0:T(8,128)(2,1)} %get-tuple-element.80.refs_7_), channel_id=1, source_target_pairs={{0,1},{1,0},{2,3},{3,2},{4,5},{5,4},{6,7},{7,6},{8,9},{9,8},{10,11... | collective-permute-start | bytes 614408 | tf_op jit(solution)/shard_map/ppermute | solution.py:679
  45.5 20.5 %collective-permute-start.8 = (bf16[5,240,128]{2,1,0:T(8,128)(2,1)}, bf16[5,240,128]{2,1,0:T(8,128)(2,1)S(1)}, u32[]{:S(2)}, u32[]{:S(2)}) collective-permute-start(bf16[5,240,128]{2,1,0:T(8,128)(2,1)} %get-tuple-element.81), channel_id=1, source_target_pairs={{0,2},{2,0},{4,6},{6,4},{8,10},{10,8},{12,14},{14,12},{16,18},{18,... | collective-permute-start | bytes 921608 | tf_op jit(solution)/shard_map/ppermute | solution.py:670
  55.0 11.0 %collective-permute-start.16 = (bf16[3,240,128]{2,1,0:T(8,128)(2,1)}, bf16[3,240,128]{2,1,0:T(8,128)(2,1)S(1)}, u32[]{:S(2)}, u32[]{:S(2)}) collective-permute-start(bf16[3,240,128]{2,1,0:T(8,128)(2,1)} %get-tuple-element.88), channel_id=1, source_target_pairs={{0,2},{2,0},{4,6},{6,4},{8,10},{10,8},{12,14},{14,12},{16,18},{18,... | collective-permute-start | bytes 552968 | tf_op jit(solution)/shard_map/ppermute | solution.py:670
  64.0 37.3 %collective-permute-start.20 = (bf16[320,1280]{1,0:T(8,128)(2,1)}, bf16[320,1280]{1,0:T(8,128)(2,1)S(1)}, u32[]{:S(2)}, u32[]{:S(2)}) collective-permute-start(bf16[320,1280]{1,0:T(8,128)(2,1)} %copy-done.8), channel_id=1, source_target_pairs={{0,1},{1,0},{2,3},{3,2},{4,5},{5,4},{6,7},{7,6},{8,9},{9,8},{10,11... | collective-permute-start | bytes 2457608 | tf_op jit(solution)/shard_map/ppermute | solution.py:679
  64.0 38.0 %collective-permute-start.21 = (bf16[320,1280]{1,0:T(8,128)(2,1)}, bf16[320,1280]{1,0:T(8,128)(2,1)S(1)}, u32[]{:S(2)}, u32[]{:S(2)}) collective-permute-start(bf16[320,1280]{1,0:T(8,128)(2,1)} %gate.16), channel_id=1, source_target_pairs={{0,1},{1,0},{2,3},{3,2},{4,5},{5,4},{6,7},{7,6},{8,9},{9,8},{10,11... | collective-permute-start | bytes 2457608 | tf_op jit(solution)/shard_map/ppermute | solution.py:679
  103.8 15.3 %collective-permute-start.24 = (bf16[128,1280]{1,0:T(8,128)(2,1)S(1)}, bf16[128,1280]{1,0:T(8,128)(2,1)}, u32[]{:S(2)}, u32[]{:S(2)}) collective-permute-start(bf16[128,1280]{1,0:T(8,128)(2,1)S(1)} %gate.18), channel_id=1, source_target_pairs={{0,1},{1,0},{2,3},{3,2},{4,5},{5,4},{6,7},{7,6},{8,9},{9,8},{10,11... | collective-permute-start | bytes 983048 | tf_op jit(solution)/shard_map/ppermute | solution.py:679
  120.8 15.4 %all-to-all-start.1 = ((bf16[16,80,128]{2,1,0:T(8,128)(2,1)}), bf16[16,80,128]{2,1,0:T(8,128)(2,1)}, u32[]{:S(2)}, u32[]{:S(2)}) async-start(bf16[16,80,128]{2,1,0:T(8,128)(2,1)} %bitcast.23), calls=%async_computation.1 | async-start | bytes 655360 | tf_op jit(solution)/shard_map/all_to_all | solution.py:698
  125.0 31.2 %collective-permute-start.32 = (bf16[8,128,1280]{2,1,0:T(8,128)(2,1)S(1)}, bf16[8,128,1280]{2,1,0:T(8,128)(2,1)}, u32[]{:S(2)}, u32[]{:S(2)}) collective-permute-start(bf16[8,128,1280]{2,1,0:T(8,128)(2,1)S(1)} %copy-done), channel_id=1, source_target_pairs={{0,2},{2,0},{4,6},{6,4},{8,10},{10,8},{12,14},{14,12},{16,18},{18,... | collective-permute-start | bytes 7864328 | tf_op jit(solution)/shard_map/ppermute | solution.py:670
  125.6 30.6 %collective-permute-start.31 = (bf16[128,1280]{1,0:T(8,128)(2,1)}, bf16[128,1280]{1,0:T(8,128)(2,1)S(1)}, u32[]{:S(2)}, u32[]{:S(2)}) collective-permute-start(bf16[128,1280]{1,0:T(8,128)(2,1)} %get-tuple-element.117.refs_7_), channel_id=1, source_target_pairs={{0,2},{2,0},{4,6},{6,4},{8,10},{10,8},{12,14},{14,12},{16,18},{18,... | collective-permute-start | bytes 983048 | tf_op jit(solution)/shard_map/ppermute | solution.py:670
  125.9 30.4 %collective-permute-start.28 = (bf16[3776,128]{1,0:T(8,128)(2,1)}, bf16[3776,128]{1,0:T(8,128)(2,1)}, u32[]{:S(2)}, u32[]{:S(2)}) collective-permute-start(bf16[3776,128]{1,0:T(8,128)(2,1)} %get-tuple-element.115), channel_id=1, source_target_pairs={{0,1},{1,0},{2,3},{3,2},{4,5},{5,4},{6,7},{7,6},{8,9},{9,8},{10,11... | collective-permute-start | bytes 2899976 | tf_op jit(solution)/shard_map/ppermute | solution.py:679
  126.3 30.0 %collective-permute-start.29 = (bf16[3776,128]{1,0:T(8,128)(2,1)}, bf16[3776,128]{1,0:T(8,128)(2,1)}, u32[]{:S(2)}, u32[]{:S(2)}) collective-permute-start(bf16[3776,128]{1,0:T(8,128)(2,1)} %get-tuple-element.116), channel_id=1, source_target_pairs={{0,2},{2,0},{4,6},{6,4},{8,10},{10,8},{12,14},{14,12},{16,18},{18,... | collective-permute-start | bytes 2899976 | tf_op jit(solution)/shard_map/ppermute | solution.py:670
  130.5 25.8 %collective-permute-start.30 = (bf16[1200,128]{1,0:T(8,128)(2,1)}, bf16[1200,128]{1,0:T(8,128)(2,1)S(1)}, u32[]{:S(2)}, u32[]{:S(2)}) collective-permute-start(bf16[1200,128]{1,0:T(8,128)(2,1)} %collective-permute-done.25.refs_12_), channel_id=1, source_target_pairs={{0,1},{1,0},{2,3},{3,2},{4,5},{5,4},{6,7},{7,6},{8,9},{9,8},{10,11... | collective-permute-start | bytes 921608 | tf_op jit(solution)/shard_map/ppermute | solution.py:679
  157.6 11.4 %collective-permute-start.33 = (bf16[3776,128]{1,0:T(8,128)(2,1)}, bf16[3776,128]{1,0:T(8,128)(2,1)}, u32[]{:S(2)}, u32[]{:S(2)}) collective-permute-start(bf16[3776,128]{1,0:T(8,128)(2,1)} %get-tuple-element.119.refs_2_), channel_id=1, source_target_pairs={{0,2},{2,0},{4,6},{6,4},{8,10},{10,8},{12,14},{14,12},{16,18},{18,... | collective-permute-start | bytes 2899976 | tf_op jit(solution)/shard_map/ppermute | solution.py:670
  158.5 10.5 %collective-permute-start.34 = (bf16[128,1280]{1,0:T(8,128)(2,1)S(1)}, bf16[128,1280]{1,0:T(8,128)(2,1)}, u32[]{:S(2)}, u32[]{:S(2)}) collective-permute-start(bf16[128,1280]{1,0:T(8,128)(2,1)S(1)} %bitcast.28), channel_id=1, source_target_pairs={{0,2},{2,0},{4,6},{6,4},{8,10},{10,8},{12,14},{14,12},{16,18},{18,... | collective-permute-start | bytes 983048 | tf_op jit(solution)/shard_map/ppermute | solution.py:670
  159.3 18.1 %collective-permute-start.27 = (bf16[7,160,256]{2,1,0:T(8,128)(2,1)}, bf16[7,160,256]{2,1,0:T(8,128)(2,1)}, u32[]{:S(2)}, u32[]{:S(2)}) collective-permute-start(bf16[7,160,256]{2,1,0:T(8,128)(2,1)} %get-tuple-element.113), channel_id=1, source_target_pairs={{0,1},{1,0},{2,3},{3,2},{4,5},{5,4},{6,7},{7,6},{8,9},{9,8},{10,11... | collective-permute-start | bytes 1720328 | tf_op jit(solution)/shard_map/ppermute | solution.py:679
  167.2 10.2 %collective-permute-start.26 = (bf16[1,160,256]{2,1,0:T(8,128)(2,1)}, bf16[1,160,256]{2,1,0:T(8,128)(2,1)S(1)}, u32[]{:S(2)}, u32[]{:S(2)}) collective-permute-start(bf16[1,160,256]{2,1,0:T(8,128)(2,1)} %get-tuple-element.112), channel_id=1, source_target_pairs={{0,1},{1,0},{2,3},{3,2},{4,5},{5,4},{6,7},{7,6},{8,9},{9,8},{10,11... | collective-permute-start | bytes 245768 | tf_op jit(solution)/shard_map/ppermute | solution.py:679
  184.5 10.2 %collective-permute-start.39 = (bf16[256,640]{1,0:T(8,128)(2,1)S(1)}, bf16[256,640]{1,0:T(8,128)(2,1)S(1)}, u32[]{:S(2)}, u32[]{:S(2)}) collective-permute-start(bf16[256,640]{1,0:T(8,128)(2,1)S(1)} %get-tuple-element.127), channel_id=1, source_target_pairs={{0,1},{1,0},{2,3},{3,2},{4,5},{5,4},{6,7},{7,6},{8,9},{9,8},{10,11... | collective-permute-start | bytes 983048 | tf_op jit(solution)/shard_map/ppermute | solution.py:679
  185.5 14.2 %collective-permute-start.38 = (bf16[256,1280]{1,0:T(8,128)(2,1)S(1)}, bf16[256,1280]{1,0:T(8,128)(2,1)S(1)}, u32[]{:S(2)}, u32[]{:S(2)}) collective-permute-start(bf16[256,1280]{1,0:T(8,128)(2,1)S(1)} %reduce_step.9.refs_5_), channel_id=1, source_target_pairs={{0,8},{2,6},{8,16},{10,2},{16,24},{18,10},{24,28},{26,18},{28,20},... | collective-permute-start | bytes 1966088 | tf_op jit(solution)/shard_map/ppermute | solution.py:667
  190.2 9.5 %collective-permute-start.37 = (bf16[256,640]{1,0:T(8,128)(2,1)S(1)}, bf16[256,640]{1,0:T(8,128)(2,1)S(1)}, u32[]{:S(2)}, u32[]{:S(2)}) collective-permute-start(bf16[256,640]{1,0:T(8,128)(2,1)S(1)} %reduce_step.10.refs_3_), channel_id=1, source_target_pairs={{0,8},{2,6},{8,16},{10,2},{16,24},{18,10},{24,28},{26,18},{28,20},... | collective-permute-start | bytes 983048 | tf_op jit(solution)/shard_map/ppermute | solution.py:667
  200.4 10.6 %collective-permute-start.41 = (bf16[256,1280]{1,0:T(8,128)(2,1)S(1)}, bf16[256,1280]{1,0:T(8,128)(2,1)S(1)}, u32[]{:S(2)}, u32[]{:S(2)}) collective-permute-start(bf16[256,1280]{1,0:T(8,128)(2,1)S(1)} %reduce_step.11.refs_3_), channel_id=1, source_target_pairs={{0,8},{2,6},{8,16},{10,2},{16,24},{18,10},{24,28},{26,18},{28,20},... | collective-permute-start | bytes 1966088 | tf_op jit(solution)/shard_map/ppermute | solution.py:667
  211.7 10.6 %collective-permute-start.45 = (bf16[256,1280]{1,0:T(8,128)(2,1)S(1)}, bf16[256,1280]{1,0:T(8,128)(2,1)S(1)}, u32[]{:S(2)}, u32[]{:S(2)}) collective-permute-start(bf16[256,1280]{1,0:T(8,128)(2,1)S(1)} %reduce_step.13.refs_3_), channel_id=1, source_target_pairs={{0,8},{2,6},{8,16},{10,2},{16,24},{18,10},{24,28},{26,18},{28,20},... | collective-permute-start | bytes 1966088 | tf_op jit(solution)/shard_map/ppermute | solution.py:667
  213.2 16.2 %collective-permute-start.43 = (bf16[512,640]{1,0:T(8,128)(2,1)S(1)}, bf16[512,640]{1,0:T(8,128)(2,1)S(1)}, u32[]{:S(2)}, u32[]{:S(2)}) collective-permute-start(bf16[512,640]{1,0:T(8,128)(2,1)S(1)} %chip_pack.1.refs_3_.refs_1_), channel_id=1, source_target_pairs={{0,8},{2,6},{8,16},{10,2},{16,24},{18,10},{24,28},{26,18},{28,20},... | collective-permute-start | bytes 1966088 | tf_op jit(solution)/shard_map/ppermute | solution.py:667
  214.7 21.7 %collective-permute-start.40 = (bf16[256,1280]{1,0:T(8,128)(2,1)S(1)}, bf16[256,1280]{1,0:T(8,128)(2,1)S(1)}, u32[]{:S(2)}, u32[]{:S(2)}) collective-permute-start(bf16[256,1280]{1,0:T(8,128)(2,1)S(1)} %reduce_step.12.refs_3_), channel_id=1, source_target_pairs={{0,8},{2,6},{8,16},{10,2},{16,24},{18,10},{24,28},{26,18},{28,20},... | collective-permute-start | bytes 1966088 | tf_op jit(solution)/shard_map/ppermute | solution.py:667
  222.4 16.2 %collective-permute-start.46 = (bf16[256,1280]{1,0:T(8,128)(2,1)S(1)}, bf16[256,1280]{1,0:T(8,128)(2,1)S(1)}, u32[]{:S(2)}, u32[]{:S(2)}) collective-permute-start(bf16[256,1280]{1,0:T(8,128)(2,1)S(1)} %collective-permute-done.45.refs_2_), channel_id=1, source_target_pairs={{0,2},{2,0},{4,6},{6,4},{8,10},{10,8},{12,14},{14,12},{16,18},{18,... | collective-permute-start | bytes 1966088 | tf_op jit(solution)/shard_map/ppermute | solution.py:670
  229.4 14.0 %collective-permute-start.47 = (bf16[512,640]{1,0:T(8,128)(2,1)S(1)}, bf16[512,640]{1,0:T(8,128)(2,1)S(1)}, u32[]{:S(2)}, u32[]{:S(2)}) collective-permute-start(bf16[512,640]{1,0:T(8,128)(2,1)S(1)} %collective-permute-done.43.refs_4_.refs_2_), channel_id=1, source_target_pairs={{0,8},{2,6},{8,16},{10,2},{16,24},{18,10},{24,28},{26,18},{28,20},... | collective-permute-start | bytes 1966088 | tf_op jit(solution)/shard_map/ppermute | solution.py:667
  237.1 13.3 %collective-permute-start.44 = (bf16[256,1280]{1,0:T(8,128)(2,1)S(1)}, bf16[256,1280]{1,0:T(8,128)(2,1)S(1)}, u32[]{:S(2)}, u32[]{:S(2)}) collective-permute-start(bf16[256,1280]{1,0:T(8,128)(2,1)S(1)} %reduce_step.14.refs_4_), channel_id=1, source_target_pairs={{0,8},{2,6},{8,16},{10,2},{16,24},{18,10},{24,28},{26,18},{28,20},... | collective-permute-start | bytes 1966088 | tf_op jit(solution)/shard_map/ppermute | solution.py:667
  239.4 18.2 %collective-permute-start.50 = (bf16[256,1280]{1,0:T(8,128)(2,1)S(1)}, bf16[256,1280]{1,0:T(8,128)(2,1)}, u32[]{:S(2)}, u32[]{:S(2)}) collective-permute-start(bf16[256,1280]{1,0:T(8,128)(2,1)S(1)} %reduce_end.1.refs_3_.refs_1_), channel_id=1, source_target_pairs={{0,8},{2,6},{8,16},{10,2},{16,24},{18,10},{24,28},{26,18},{28,20},... | collective-permute-start | bytes 1966088 | tf_op jit(solution)/shard_map/ppermute | solution.py:667
  252.0 12.6 %collective-permute-start.48 = (bf16[256,1280]{1,0:T(8,128)(2,1)}, bf16[256,1280]{1,0:T(8,128)(2,1)}, u32[]{:S(2)}, u32[]{:S(2)}) collective-permute-start(bf16[256,1280]{1,0:T(8,128)(2,1)} %reduce_step.15), channel_id=1, source_target_pairs={{0,8},{2,6},{8,16},{10,2},{16,24},{18,10},{24,28},{26,18},{28,20},... | collective-permute-start | bytes 1966088 | tf_op jit(solution)/shard_map/ppermute | solution.py:667
  253.4 18.1 %collective-permute-start.52 = (bf16[512,640]{1,0:T(8,128)(2,1)S(1)}, bf16[512,640]{1,0:T(8,128)(2,1)S(1)}, u32[]{:S(2)}, u32[]{:S(2)}) collective-permute-start(bf16[512,640]{1,0:T(8,128)(2,1)S(1)} %collective-permute-done.47.refs_4_.refs_3_), channel_id=1, source_target_pairs={{0,8},{2,6},{8,16},{10,2},{16,24},{18,10},{24,28},{26,18},{28,20},... | collective-permute-start | bytes 1966088 | tf_op jit(solution)/shard_map/ppermute | solution.py:667
  257.6 21.1 %collective-permute-start.51 = (bf16[256,1280]{1,0:T(8,128)(2,1)}, bf16[256,1280]{1,0:T(8,128)(2,1)}, u32[]{:S(2)}, u32[]{:S(2)}) collective-permute-start(bf16[256,1280]{1,0:T(8,128)(2,1)} %collective-permute-done.50.refs_2_), channel_id=1, source_target_pairs={{0,8},{2,6},{8,16},{10,2},{16,24},{18,10},{24,28},{26,18},{28,20},... | collective-permute-start | bytes 1966088 | tf_op jit(solution)/shard_map/ppermute | solution.py:667
  264.6 17.5 %collective-permute-start.49 = (bf16[256,1280]{1,0:T(8,128)(2,1)}, bf16[256,1280]{1,0:T(8,128)(2,1)}, u32[]{:S(2)}, u32[]{:S(2)}) collective-permute-start(bf16[256,1280]{1,0:T(8,128)(2,1)} %collective-permute-done.48.refs_2_), channel_id=1, source_target_pairs={{0,2},{2,0},{4,6},{6,4},{8,10},{10,8},{12,14},{14,12},{16,18},{18,... | collective-permute-start | bytes 1966088 | tf_op jit(solution)/shard_map/ppermute | solution.py:670
  271.5 10.5 %collective-permute-start.56 = (bf16[256,640]{1,0:T(8,128)(2,1)S(1)}, bf16[256,640]{1,0:T(8,128)(2,1)S(1)}, u32[]{:S(2)}, u32[]{:S(2)}) collective-permute-start(bf16[256,640]{1,0:T(8,128)(2,1)S(1)} %constant_dynamic-slice_fusion.1), channel_id=1, source_target_pairs={{0,8},{2,6},{8,16},{10,2},{16,24},{18,10},{24,28},{26,18},{28,20},... | collective-permute-start | bytes 983048 | tf_op jit(solution)/shard_map/ppermute | solution.py:667
  278.6 10.8 %collective-permute-start.58 = (bf16[256,1280]{1,0:T(8,128)(2,1)}, bf16[256,1280]{1,0:T(8,128)(2,1)S(1)}, u32[]{:S(2)}, u32[]{:S(2)}) collective-permute-start(bf16[256,1280]{1,0:T(8,128)(2,1)} %collective-permute-done.51.refs_7_.refs_3_), channel_id=1, source_target_pairs={{0,8},{2,6},{8,16},{10,2},{16,24},{18,10},{24,28},{26,18},{28,20},... | collective-permute-start | bytes 1966088 | tf_op jit(solution)/shard_map/ppermute | solution.py:667
  280.1 10.0 %collective-permute-start.54 = (bf16[512,640]{1,0:T(8,128)(2,1)S(1)}, bf16[512,640]{1,0:T(8,128)(2,1)}, u32[]{:S(2)}, u32[]{:S(2)}) collective-permute-start(bf16[512,640]{1,0:T(8,128)(2,1)S(1)} %collective-permute-done.47.refs_4_.refs_3_), channel_id=1, source_target_pairs={{0,2},{2,0},{4,6},{6,4},{8,10},{10,8},{12,14},{14,12},{16,18},{18,... | collective-permute-start | bytes 1966088 | tf_op jit(solution)/shard_map/ppermute | solution.py:670
  289.4 12.7 %collective-permute-start.59 = (bf16[256,1280]{1,0:T(8,128)(2,1)}, bf16[256,1280]{1,0:T(8,128)(2,1)S(1)}, u32[]{:S(2)}, u32[]{:S(2)}) collective-permute-start(bf16[256,1280]{1,0:T(8,128)(2,1)} %collective-permute-done.50.refs_2_), channel_id=1, source_target_pairs={{0,2},{2,0},{4,6},{6,4},{8,10},{10,8},{12,14},{14,12},{16,18},{18,... | collective-permute-start | bytes 1966088 | tf_op jit(solution)/shard_map/ppermute | solution.py:670
  289.5 12.7 %collective-permute-start.60 = (bf16[256,1280]{1,0:T(8,128)(2,1)}, bf16[256,1280]{1,0:T(8,128)(2,1)S(1)}, u32[]{:S(2)}, u32[]{:S(2)}) collective-permute-start(bf16[256,1280]{1,0:T(8,128)(2,1)} %collective-permute-done.51.refs_7_.refs_3_), channel_id=1, source_target_pairs={{0,2},{2,0},{4,6},{6,4},{8,10},{10,8},{12,14},{14,12},{16,18},{18,... | collective-permute-start | bytes 1966088 | tf_op jit(solution)/shard_map/ppermute | solution.py:670
  290.1 9.7 %collective-permute-start.62 = (bf16[256,640]{1,0:T(8,128)(2,1)S(1)}, bf16[256,640]{1,0:T(8,128)(2,1)S(1)}, u32[]{:S(2)}, u32[]{:S(2)}) collective-permute-start(bf16[256,640]{1,0:T(8,128)(2,1)S(1)} %constant_dynamic-slice_fusion), channel_id=1, source_target_pairs={{0,8},{2,6},{8,16},{10,2},{16,24},{18,10},{24,28},{26,18},{28,20},... | collective-permute-start | bytes 983048 | tf_op jit(solution)/shard_map/ppermute | solution.py:667
  291.5 10.7 %collective-permute-start.61 = (bf16[256,1280]{1,0:T(8,128)(2,1)S(1)}, bf16[256,1280]{1,0:T(8,128)(2,1)S(1)}, u32[]{:S(2)}, u32[]{:S(2)}) collective-permute-start(bf16[256,1280]{1,0:T(8,128)(2,1)S(1)} %collective-permute-done.58.refs_4_), channel_id=1, source_target_pairs={{0,2},{2,0},{4,6},{6,4},{8,10},{10,8},{12,14},{14,12},{16,18},{18,... | collective-permute-start | bytes 1966088 | tf_op jit(solution)/shard_map/ppermute | solution.py:670
  (94 other events, 759.3 us)

commit v3 on v2

--- a/solution.py
+++ b/solution.py
@@ -236,92 +236,88 @@
     return lax.broadcasted_iota(jnp.int32, (512, width), 0) % 256 // 64
 
 
-def backward_body(first, last, low, slots_out, begin, clear, qblock, scale, *refs):
-    (given, q_t, stat, lse), refs = refs[:4], refs[4:]
-    if not first:
-        dq_in, refs = refs[0], refs[1:]
-    sources, (dkv_own, dkv_other), refs = refs[:3], refs[3:5], refs[5:]
-    (k_t, k_rows, v_rows, sems), refs = refs[-4:], refs[:-4]
-    size = dkv_own.shape[0]
-    copies = start_copies(
-        [(a.at[pl.ds(low, size)], o) for a, o in zip(sources, (k_t, k_rows, v_rows))], sems
-    )
+def backward_body(
+    slots_out,
+    begin,
+    clear,
+    qblock,
+    scale,
+    grads,
+    q_t,
+    att,
+    lse,
+    k_t_in,
+    k_rows_in,
+    v_rows_in,
+    dkv_own,
+    dkv_other,
+    dq_pieces,
+    scale_sum,
+    grad_t,
+    delta,
+    dq,
+    blocks,
+    k_t,
+    k_rows,
+    v_rows,
+    sems,
+):
+    copies = start_copies([(k_t_in, k_t), (k_rows_in, k_rows), (v_rows_in, v_rows)], sems)
     tiles, _, width = q_t.shape
     per = width // 64
-    if first:
-        (grad_t, delta_out, dq), refs = refs[:3], refs[3:]
-        (blocks,) = refs
-        for c in range(GROUP):
-            for half in range(2):
-                blocks[slots_out[c, half]] = given[c, :, half * 64 : half * 64 + 64]
-
-        @pl.loop(0, tiles)
-        def _(i):
-            grad = jnp.concatenate([blocks[per * i + m] for m in range(per)], axis=1)
-            grad_t[i] = grad
-            delta_out[i] = jnp.sum(grad.astype(F32) * stat[i], axis=0, keepdims=True)
-            dq[i] = jnp.zeros((HD, width), F32)
-
-        delta = delta_out
-    else:
-        grad_t, delta = given, stat
-        if last:
-            (dq_pieces, scale_sum, dq, blocks) = refs
-        else:
-            (dq,) = refs
-        dq[...] = dq_in[...]
+    for c in range(GROUP):
+        for half in range(2):
+            blocks[slots_out[c, half]] = grads[c, :, half * 64 : half * 64 + 64]
+
+    @pl.loop(0, tiles)
+    def _(i):
+        grad = jnp.concatenate([blocks[per * i + m] for m in range(per)], axis=1)
+        grad_t[i] = grad
+        delta[i] = jnp.sum(grad.astype(F32) * att[i], axis=0, keepdims=True)
+        dq[i] = jnp.zeros((HD, width), F32)
 
     for copy in copies:
         copy.wait()
 
-    @pl.loop(0, size)
-    def _(at):
-        c = low + at
-
+    @pl.loop(0, k_t.shape[0])
+    def _(c):
         def step(masked, i, carry):
             d_k, d_v = carry
             query, grad = q_t[i], grad_t[i]
-            prob = jnp.exp(dot(k_rows[at], query, NN) - lse[i])
+            prob = jnp.exp(dot(k_rows[c], query, NN) - lse[i])
             if masked:
                 prob = jnp.where(block_of_row(width) + 4 * c <= qblock[i], prob, 0.0)
-            d_score = (prob * (dot(v_rows[at], grad, NN) - delta[i])).astype(BF)
-            dq[i] += dot(k_t[at], d_score, NN)
+            d_score = (prob * (dot(v_rows[c], grad, NN) - delta[i])).astype(BF)
+            dq[i] += dot(k_t[c], d_score, NN)
             return d_k + dot(query, d_score, NT), d_v + dot(grad, prob.astype(BF), NT)
 
         carry = (jnp.zeros((HD, 512), F32), jnp.zeros((HD, 512), F32))
         carry = lax.fori_loop(begin[c], clear[c], functools.partial(step, True), carry)
         d_k, d_v = lax.fori_loop(clear[c], tiles, functools.partial(step, False), carry)
-        dkv_own[at, :HD] = d_k[:, :256]
-        dkv_own[at, HD:] = d_v[:, :256]
-        dkv_other[at, :HD] = d_k[:, 256:].astype(BF)
-        dkv_other[at, HD:] = d_v[:, 256:].astype(BF)
-
-    if last:
-        total = jnp.zeros((HD, width), F32)
-        for i in range(tiles):
-            total = total + dq[i] * q_t[i].astype(F32)
-            rounded = (dq[i] * scale[...]).astype(BF)
-            for m in range(per):
-                blocks[per * i + m] = rounded[:, m * 64 : m * 64 + 64]
-        scale_sum[...] = total
-        for c in range(GROUP):
-            dq_pieces[c] = jnp.concatenate(
-                [blocks[slots_out[c, 0]], blocks[slots_out[c, 1]]], axis=1
-            )
-
-
-def join_body(slots_kv, spot, dq_pieces, *refs):
-    parts, (pieces, other, blocks) = refs[:-3], refs[-3:]
-    low = 0
-    for own, received in zip(parts[: len(parts) // 2], parts[len(parts) // 2 :]):
-
-        @pl.loop(0, own.shape[0])
-        def _(at, low=low, own=own, received=received):
-            tile = (own[at] + received[at].astype(F32)).astype(BF)
-            for m in range(4):
-                blocks[4 * (low + at) + m] = tile[:, m * 64 : m * 64 + 64]
-
-        low += own.shape[0]
+        dkv_own[c, :HD] = d_k[:, :256]
+        dkv_own[c, HD:] = d_v[:, :256]
+        dkv_other[c, :HD] = d_k[:, 256:].astype(BF)
+        dkv_other[c, HD:] = d_v[:, 256:].astype(BF)
+
+    total = jnp.zeros((HD, width), F32)
+    for i in range(tiles):
+        total = total + dq[i] * q_t[i].astype(F32)
+        rounded = (dq[i] * scale[...]).astype(BF)
+        for m in range(per):
+            blocks[per * i + m] = rounded[:, m * 64 : m * 64 + 64]
+    scale_sum[...] = total
+    for c in range(GROUP):
+        dq_pieces[c] = jnp.concatenate(
+            [blocks[slots_out[c, 0]], blocks[slots_out[c, 1]]], axis=1
+        )
+
+
+def join_body(slots_kv, spot, dq_pieces, own, received, pieces, other, blocks):
+    @pl.loop(0, own.shape[0])
+    def _(c):
+        tile = (own[c] + received[c].astype(F32)).astype(BF)
+        for m in range(4):
+            blocks[4 * c + m] = tile[:, m * 64 : m * 64 + 64]
 
     for p in range(CHIPS):
         for core in range(2):
@@ -573,35 +569,54 @@
     out[...] = (block[0].astype(F32) + mine[...].astype(F32) + near[...].astype(F32)).astype(BF)
 
 
-def rows_place_body(elements, spot, *refs):
-    arrays, (w_hidden, gain), refs = refs[:9], refs[9:11], refs[11:]
-    outs, (gain_out, means_out) = refs[:3], refs[3:]
-    chunk = outs[0].shape[0] // CHIPS
+def rows_place_body(first, elements, spot, *refs):
+    use = (0, 1, 2, 4, 5) if first else (3, 6, 7, 8)
+    arrays, refs = refs[: len(use)], refs[len(use) :]
+    if first:
+        w_hidden, *outs, sums_out, tail_out, staged, sems = refs
+    else:
+        (w_hidden, gain, sums_in, tail_in), refs = refs[:4], refs[4:]
+        outs, (gain_out, means_out, staged, sums, sems) = refs[3:6], refs[6:]
+        sums[...] = sums_in[...]
+        sums_out = sums
+    rows = staged.shape[2]
+    half, model = w_hidden.shape
+    if first:
+        sums_out[...] = jnp.zeros_like(sums_out)
     tail = jnp.zeros((8, 128), F32)
     positions = ring_positions(spot)
-    for at in range(9):
-        block = arrays[at][...].astype(F32)
-        rows = pl.ds(pl.multiple_of(positions[min(at, 7)] * chunk, 16), chunk)
+    copies = []
+    for at, ref in zip(use, arrays):
+        block = ref[...].astype(F32)
+        place = pl.ds(pl.multiple_of(positions[min(at, 7)] * rows, 16), rows)
         core = spot[1] if at == 7 else 1 - spot[1]
         width = block.shape[1]
+        lanes = pl.ds(pl.multiple_of(core * width, 128), width) if at >= 7 else pl.ds(0, width)
+        slot = at % 4 if first else min(use.index(at), 2)
+        stage = {0: 0, 1: 1, 2: 2, 4: 3, 5: 4}[at] if first else slot
         for w in range(3):
-            part = block[w * chunk : (w + 1) * chunk]
-            if at < 7:
-                outs[w][rows] = part
-            else:
-                outs[w][rows, pl.ds(pl.multiple_of(core * width, 128), width)] = part
-        if at < 7:
-            tail = tail + block[3 * chunk : 3 * chunk + 8, :128]
-        else:
-            tail = tail + jnp.where(core == 0, block[3 * chunk : 3 * chunk + 8, :128], 0.0)
-    means = jnp.sqrt((tail[0:1, :2] + tail[1:2, :2]) / elements)
-    means_out[...] = means.reshape(2)
-    half, model = w_hidden.shape
-    total = jnp.zeros((half, 128), F32)
-    for at in range(0, model, 128):
-        total = total + outs[1][:, at : at + 128] * w_hidden[:, at : at + 128].astype(F32)
-    line = jnp.sum(total.T, axis=0, keepdims=True) / line_of(gain)
-    gain_out[...] = line.reshape(half)
+            staged[stage, w, :, lanes] = block[w * rows : (w + 1) * rows]
+        total = jnp.zeros((rows, 128), F32)
+        weight = w_hidden[place, lanes].astype(F32)
+        for c in range(0, width, 128):
+            total = total + block[rows : 2 * rows, c : c + 128] * weight[:, c : c + 128]
+        sums_out[place] = sums_out[place] + total
+        extra = block[3 * rows : 3 * rows + 8, :128]
+        tail = tail + (extra if at < 7 else jnp.where(core == 0, extra, 0.0))
+        if at != 7:
+            for w in range(3):
+                copy = pltpu.make_async_copy(staged.at[stage, w], outs[w].at[place], sems.at[stage, w])
+                copy.start()
+                copies.append(copy)
+    if first:
+        tail_out[...] = tail
+    else:
+        tail = tail + tail_in[...]
+        means_out[...] = jnp.sqrt((tail[0:1, :2] + tail[1:2, :2]) / elements).reshape(2)
+        line = jnp.sum(sums[...].T, axis=0, keepdims=True) / line_of(gain)
+        gain_out[...] = line.reshape(half)
+    for copy in copies:
+        copy.wait()
 
 
 def inputs_grad_body(spot, block, mine, near, x_in, dy_in, gains, out):
@@ -925,8 +940,9 @@
         smem=5,
         name="attention_forward",
         us=20,
-        mib=36 if groups == 1 else 60,
-    )
+        mib=60,
+    )
+    (pieces,) = gates([pieces], [parts[2], parts[4]])
     att_t = exchange(pieces).reshape(model, dev_rows)
     hid_x, ret_x = gates([hid_x, ret_x], [att_t])
     for w, first in ((w_hidden, hid_x), (w_return, ret_x)):
@@ -992,64 +1008,53 @@
         )
         return [ring_by_core(outs[0])], outs
 
-    cuts = (chunks, chunks // 8, 0)
-    state = [((tiles, HD, width), BF), ((tiles, 1, width), F32), ((tiles, HD, width), F32)]
-    owns, receiveds = [], []
-    handed = [grads, att]
-    dq, done = [], [forward]
-    for at in range(2):
-        low, size = cuts[at + 1], cuts[at] - cuts[at + 1]
-        given, stat = handed
-        outs = [((size, 2 * HD, 256), F32), ((size, 2 * HD, 256), BF)]
-        outs += [((GROUP, HD, 128), BF), ((HD, width), F32)] if at else state
-        own, other, *more = call(
-            functools.partial(backward_body, at == 0, at == 1, low),
-            outs,
-            [slots_out, begin, clear, qblock, scale_col]
-            + [given, q_t, stat, lse, *dq, k_t, k_rows, v_rows],
-            specs=[vmem_spec] * (6 + len(dq)) + [any_spec] * 3,
-            scratch=[pltpu.VMEM((tiles, HD, width), F32)] * at
-            + [
-                pltpu.VMEM((2 * GROUP, HD, 64), BF),
-                pltpu.VMEM((size, HD, 512), BF),
-                pltpu.VMEM((size, 512, HD), BF),
-                pltpu.VMEM((size, 512, HD), BF),
-                pltpu.SemaphoreType.DMA((3,)),
-            ],
-            smem=3,
-            after=done,
-            name="attention_backward",
-            us=[20, 7][at],
-            mib=60,
-        )
-        owns.insert(0, own)
-        receiveds.insert(0, swap_x(other))
-        if not at:
-            *handed, dq_now = more
-            dq, done = [dq_now], []
-            from_x, from_sib, from_xs, g_xs, norms_sib = gates(
-                [from_x, from_sib, from_xs, g_xs, norms_sib], [own]
-            )
-            back_xs = swap_core(from_x)
-    dq_pieces, scale_sum = more
+    own, other, dq_pieces, scale_sum = call(
+        backward_body,
+        [
+            ((chunks, 2 * HD, 256), F32),
+            ((chunks, 2 * HD, 256), BF),
+            ((GROUP, HD, 128), BF),
+            ((HD, width), F32),
+        ],
+        [slots_out, begin, clear, qblock, scale_col, grads, q_t, att, lse, k_t, k_rows, v_rows],
+        specs=[vmem_spec] * 6 + [any_spec] * 3,
+        scratch=[
+            pltpu.VMEM((tiles, HD, width), BF),
+            pltpu.VMEM((tiles, 1, width), F32),
+            pltpu.VMEM((tiles, HD, width), F32),
+            pltpu.VMEM((2 * GROUP, HD, 64), BF),
+            pltpu.VMEM((chunks, HD, 512), BF),
+            pltpu.VMEM((chunks, 512, HD), BF),
+            pltpu.VMEM((chunks, 512, HD), BF),
+            pltpu.SemaphoreType.DMA((3,)),
+        ],
+        smem=3,
+        after=[forward],
+        name="attention_backward",
+        us=25,
+        mib=60,
+    )
+    other_x = swap_x(other)
+    from_x, from_sib, from_xs, g_xs, norms_sib = gates(
+        [from_x, from_sib, from_xs, g_xs, norms_sib], [own]
+    )
     (partial,) = call(
         pooled_grad_body,
         [((5, 256, model), BF)],
-        [f_own, from_sib, from_x, from_xs, back_xs, g_rows, g_sib, g_x, g_xs],
-        after=[dq_pieces],
+        [f_own, from_sib, from_x, from_xs, swap_core(from_x), g_rows, g_sib, g_x, g_xs],
         name="pooled_grads",
         us=3,
         mib=24,
     )
     received, done = reduce_step(partial, 0, (), ())
     if groups > 1:
-        for at in range(2):
-            owns[at] = sum_groups(owns[at] + receiveds[at].astype(F32), BF)
-            receiveds[at] = jnp.zeros_like(receiveds[at])
+        own = sum_groups(own + other_x.astype(F32), BF)
+        other_x = jnp.zeros_like(other_x)
+    received, done = reduce_step(partial, 1, received, ())
     d_pieces, d_other = call(
         join_body,
         [((GROUP, 3 * HD, 128), BF), ((10, 3 * HD, 128), BF)],
-        [slots_ctx, spot, dq_pieces, *owns, *receiveds],
+        [slots_ctx, spot, dq_pieces, own, other_x],
         scratch=[pltpu.VMEM((blocks, 2 * HD, 64), BF)],
         smem=2,
         after=done,
@@ -1069,7 +1074,7 @@
         mib=24,
     )
     share_x = swap_x(other_share)
-    received, done = reduce_step(partial, 1, received, [own_share])
+    received, done = reduce_step(partial, 2, received, [own_share])
 
     (table,) = call(
         products_body,
@@ -1093,8 +1098,8 @@
     )
     share = sum_groups(share.astype(F32), BF).astype(BF) if groups > 1 else share
     share_near = swap_core(share)
-    received, done = reduce_step(partial, 2, received, [share, *first])
-    first, done = reduce_step(table, 1, first, done)
+    received, done = reduce_step(partial, 3, received, [share])
+    received_near = swap_core(received[0])
     (chip_share,) = call(
         chip_pack_body,
         [((2 * (3 * HD + 16), half), BF)],
@@ -1106,9 +1111,7 @@
         mib=8,
     )
     q_steps = [chip_share, ring_by_core(chip_share)]
-    received, done = reduce_step(partial, 3, received, [chip_share])
-    received_near = swap_core(received[0])
-    first, done = reduce_step(table, 2, first, [*done, q_steps[1]])
+    first, done = reduce_step(table, 1, first, [chip_share])
     (mine,) = chunk_call(
         partial,
         reduce_end_body,
@@ -1116,12 +1119,13 @@
         (*received, received_near),
         [((256, model), BF)],
         "reduce_end",
-        done,
-    )
+        [chip_share],
+    )
+    first, done = reduce_step(table, 2, first, [mine, q_steps[1]])
     mine = sum_groups(mine.astype(F32), BF).astype(BF) if groups > 1 else mine
     m_steps = [mine, ring_by_core(mine)]
     q_steps.append(ring_by_core(q_steps[-1]))
-    first, done = reduce_step(table, 3, first, [mine, q_steps[2]])
+    first, done = reduce_step(table, 3, first, [*done, q_steps[2]])
     m_steps.append(ring_by_core(m_steps[-1]))
     q_steps.append(ring_by_core(q_steps[-1]))
     m_steps.append(ring_by_core(m_steps[-1]))
@@ -1135,34 +1139,60 @@
         "inputs_grad",
         [m_steps[2], q_steps[3]],
     )
+    q_near = [swap_core(a) for a in q_steps[1:3]]
+    m_near = [swap_core(a) for a in m_steps[1:3]]
+    elements = float(ctx_count * 2 * dev_rows * model)
+    chunk = half // CHIPS
+    grads_shape = [((half, model), F32)] * 3
+    *rows_grads, gain_sums, tails = call(
+        functools.partial(rows_place_body, True, elements),
+        [*grads_shape, ((half, 128), F32), ((8, 128), F32)],
+        [spot, *m_steps[:3], *m_near, w_hidden],
+        out_specs=[any_spec] * 3 + [vmem_spec] * 2,
+        scratch=[pltpu.VMEM((5, 3, chunk, model), F32), pltpu.SemaphoreType.DMA((5, 3))],
+        smem=1,
+        after=q_near,
+        name="rows_place",
+        us=4,
+        mib=40,
+    )
 
     def last_step(a, axis):
         size = a.shape[axis] // 2
         return ring_by_core(lax.dynamic_slice_in_dim(a, k * size, size, axis))
 
-    q_last, m_last = last_step(q_steps[-1], 0), last_step(m_steps[-1], 1)
-    q_near = [swap_core(a) for a in q_steps[1:]]
-    m_near = [swap_core(a) for a in m_steps[1:]]
+    q_last = last_step(q_steps[-1], 0)
+    (m_held,) = gates([m_steps[-1]], [d_in, tails])
+    m_last = last_step(m_held, 1)
+    q_near += [swap_core(a) for a in q_steps[3:]]
+    m_near += [swap_core(m_held)]
     grad_query, grad_key, grad_value, gain_one_grad, scale_grad = call(
         qkv_place_body,
         [((half, model), F32)] * 3 + [((half,), F32), ((part,), F32)],
         [spot, *q_steps, *q_near, q_last, swap_core(q_last), gain_attn, scale_row],
         scratch=[pltpu.VMEM((3, model, half), BF)],
         smem=1,
-        after=[d_in],
         name="qkv_place",
         us=6,
         mib=40,
     )
     (m_last,) = gates([m_last], [grad_query])
-    elements = float(ctx_count * 2 * dev_rows * model)
+    ins = [spot, m_held, m_near[2], m_last, swap_core(m_last), w_hidden, gain_mlp, gain_sums, tails]
     grad_output, grad_hidden, grad_return, gain_two_grad, root_means = call(
-        functools.partial(rows_place_body, elements),
-        [((half, model), F32)] * 3 + [((half,), F32), ((2,), F32)],
-        [spot, *m_steps, *m_near, m_last, swap_core(m_last), w_hidden, gain_mlp],
+        functools.partial(rows_place_body, False, elements),
+        [*grads_shape, ((half,), F32), ((2,), F32)],
+        [*ins, *rows_grads],
+        specs=[vmem_spec] * (len(ins) - 1) + [any_spec] * 3,
+        out_specs=[any_spec] * 3 + [vmem_spec] * 2,
+        scratch=[
+            pltpu.VMEM((3, 3, chunk, model), F32),
+            pltpu.VMEM((half, 128), F32),
+            pltpu.SemaphoreType.DMA((3, 3)),
+        ],
         smem=1,
+        aliases={len(ins) + at: at for at in range(3)},
         name="rows_place",
-        us=5,
+        us=3,
         mib=40,
     )
     return (

time: 310 us -> 299 us (0.965)
  blocking collectives: 15.3 us -> 0 us
  waiting for transfers between devices: 103 us -> 113 us
  starting transfers between devices: 54.8 us -> 50.2 us
  local copies, waits for them, and re-layouts: 28.4 us -> 25 us
    all_to_all x1 -> x0, blocking collectives: 15.3 us -> none  [exchange(): return lax.all_to_all(a, 'ctx', 0, 0, axis_index_groups=which, tiled=True)]
    ppermute x13 -> x12, waiting for transfers between devices: 16.7 us -> 28.3 us  [swap_x(): return lax.ppermute(a, 'fsdp', [(0, 1), (1, 0)])]
    ppermute x16, starting transfers between devices: 24.1 us -> 12.9 us  [ring_by_core(): return lax.ppermute(a, 'ctx', pairs)]
    ppermute x25, waiting for transfers between devices: 8.95 us -> 3.19 us  [swap_core(): return lax.ppermute(a, 'ctx', [(c, c ^ 1) for c in range(ctx_count)])]
    ppermute x16, waiting for transfers between devices: 63.2 us -> 67.4 us  [ring_by_core(): return lax.ppermute(a, 'ctx', pairs)]
    all_to_all x1 -> x2, starting transfers between devices: 4.22 us -> 8.34 us  [exchange(): return lax.all_to_all(a, 'ctx', 0, 0, axis_index_groups=which, tiled=True)]
    unnamed x155 -> x119, local copies, waits for them, and re-layouts: 24.7 us -> 20.7 us
    all_to_all x1 -> x2, waiting for transfers between devices: 5.4 us -> 9.41 us  [exchange(): return lax.all_to_all(a, 'ctx', 0, 0, axis_index_groups=which, tiled=True)]
  transfers between devices with their start and end apart: 65 -> 65, of which waited for: 29 -> 30; matrix products, arithmetic and copies ran while one was open for 2% -> 2% of each run, Pallas kernels for 31% -> 34%
where the time goes in v3:
time: 299 us; the launch traced here: 298 us
  waiting for transfers between devices  113 us (38%)
  Pallas kernels  106 us (35%)
  starting transfers between devices  50.2 us (17%)
  local copies, waits for them, and re-layouts  25 us (8%)
    pallas_call x39, Pallas kernels, call(): pl.pallas_call(run, out_shape=[jax.ShapeDtypeStruct(shape, kind) for shap...  106 us
    ppermute x16, waiting for transfers between devices, ring_by_core(): return lax.ppermute(a, 'ctx', pairs)  67.4 us
    ppermute x12, waiting for transfers between devices, swap_x(): return lax.ppermute(a, 'fsdp', [(0, 1), (1, 0)])  28.3 us
    unnamed x119, local copies, waits for them, and re-layouts  20.7 us
    ppermute x12, starting transfers between devices, swap_x(): return lax.ppermute(a, 'fsdp', [(0, 1), (1, 0)])  15.2 us
    ppermute x16, starting transfers between devices, ring_by_core(): return lax.ppermute(a, 'ctx', pairs)  12.9 us
    all_to_all x2, waiting for transfers between devices, exchange(): return lax.all_to_all(a, 'ctx', 0, 0, axis_index_groups=which, tiled=True)  9.41 us
    ppermute x8, starting transfers between devices, ring(): return lax.ppermute(a, 'ctx', pairs)  9.33 us
  transfers between devices with their start and end apart: 65, of which 30 were waited for; matrix products, arithmetic and copies ran while one was open for 2% of the time, Pallas kernels for 34%

profile of v3, /device:TPU:0, one launch (start us, length us, event | category | flops | bytes accessed | tf_op | source)
XLA Modules:
  0.0 297.7 jit_solution(17193424568135430027)
XLA Ops:
  0.6 3.0 %collective-permute-start.1 = (bf16[128,1280]{1,0:T(8,128)(2,1)}, bf16[128,1280]{1,0:T(8,128)(2,1)S(1)}, u32[]{:S(2)}, u32[]{:S(2)}) collective-permute-start(bf16[128,1280]{1,0:T(8,128)(2,1)} %bitcast.31), channel_id=1, source_target_pairs={{0,4},{2,6},{8,0},{10,2},{16,8},{18,10},{24,16},{26,18},{28,24},{3... | collective-permute-start | bytes 983048 | tf_op jit(solution)/shard_map/ppermute | solution.py:670
  4.5 3.2 %slab.1.refs_1_.refs_2_ = bf16[256,640]{1,0:T(8,128)(2,1)} custom-call(s32[4]{0:T(128)} %pad_add_fusion.1.refs_0_.refs_1_, bf16[640,1280]{1,0:T(8,128)(2,1)} %refs_2_.2, bf16[640,1280]{1,0:T(8,128)(2,1)} %refs_2_.2, bf16[640,1280]{1,0:T(8,128)(2,1)} %refs_4_.2, bf16[640,1280]{1,0:T(8,128)(2,1)} %refs_4_.2, bf16[640,1280]{1,0:T(8,128)(2,1)} %refs_6_.3, ...), custom_call_target="tpu_custom_call" | custom-call | flops 3449999872 | bytes 1 | tf_op jit(solution)/shard_map/slab/pallas_call | solution.py:76
  7.7 1.9 collective-permute-start.4
  11.6 1.7 collective-permute-start.3
  13.7 4.9 %collective-permute-done.4.refs_2_.refs_1_ = bf16[256,640]{1,0:T(8,128)(2,1)S(1)} collective-permute-done((bf16[256,640]{1,0:T(8,128)(2,1)}, bf16[256,640]{1,0:T(8,128)(2,1)S(1)}, u32[]{:S(2)}, u32[]{:S(2)}) %collective-permute-start.4) | collective-permute-done | bytes 327712 | tf_op jit(solution)/shard_map/ppermute | solution.py:694
  18.5 5.7 %collective-permute-done.5.refs_5_.refs_0_ = bf16[128,1280]{1,0:T(8,128)(2,1)} collective-permute-done((bf16[128,1280]{1,0:T(8,128)(2,1)S(1)}, bf16[128,1280]{1,0:T(8,128)(2,1)}, u32[]{:S(2)}, u32[]{:S(2)}) %collective-permute-start.5) | collective-permute-done | bytes 327712 | tf_op jit(solution)/shard_map/ppermute | solution.py:694
  28.6 1.7 collective-permute-start.11
  30.7 1.6 collective-permute-start.14
  33.2 4.7 %project.2 = (bf16[8,128,1280]{2,1,0:T(8,128)(2,1)}, bf16[5,80,128]{2,1,0:T(8,128)(2,1)}, bf16[5,160,128]{2,1,0:T(8,128)(2,1)}, bf16[5,240,128]{2,1,0:T(8,128)(2,1)}, bf16[5,160,128]{2,1,0:T(8,128)(2,1)}) custom-call(s32[4]{0:T(128)} %pad_add_fusion.1.refs_0_.refs_1_, bf16[128,1280]{1,0:T(8,128)(2,1)} %bitcast.33, bf16[128,1280]{1,0:T(8,128)(2,1)} %copy-done.56, ...), custom_call_target="tpu_custom_call" | custom-call | flops 3449999872 | bytes 1 | tf_op jit(solution)/shard_map/project/pallas_call | solution.py:76
  40.9 1.6 collective-permute-start.13
  48.5 4.7 %project.3 = (bf16[8,128,1280]{2,1,0:T(8,128)(2,1)}, bf16[3,80,128]{2,1,0:T(8,128)(2,1)}, bf16[3,160,128]{2,1,0:T(8,128)(2,1)}, bf16[3,240,128]{2,1,0:T(8,128)(2...) custom-call(s32[4]{0:T(128)} %pad_add_fusion.1.refs_0_.refs_1_, ...), custom_call_target="tpu_custom_call", output_to_operand_aliasing={{0}: (11, {})} | custom-call | flops 3449999872 | bytes 1 | tf_op jit(solution)/shard_map/project/pallas_call | solution.py:76
  57.1 1.7 copy-done
  58.9 1.7 copy-done.1
  61.2 1.8 collective-permute-done.15.refs_13_.refs_3_
  65.0 19.0 %attention_forward.1 = (bf16[16,80,128]{2,1,0:T(8,128)(2,1)}, bf16[4,80,512]{2,1,0:T(8,128)(2,1)}, bf16[8,80,512]{2,1,0:T(8,128)(2,1)}, bf16[8,512,80]{2,1,0:T(8...) custom-call(s32[16,2]{1,0:T(8,128)} %gather_fusion, s32[16,2]{1,0:T(8,128)} %gather_fusion, ...), custom_call_target="tpu_custom_call" | custom-call | flops 23000000512 | bytes 1 | tf_op jit(solution)/shard_map/attention_forward/pallas_call | solution.py:76
  87.2 4.0 %all-to-all-start = ((bf16[16,80,128]{2,1,0:T(8,128)(2,1)}), bf16[16,80,128]{2,1,0:T(8,128)(2,1)S(1)}, u32[]{:S(2)}, u32[]{:S(2)}) async-start(bf16[16,80,128]{2,1,0:T(8,128)(2,1)} %copy-done.4), calls=%async_computation | async-start | bytes 655360 | tf_op jit(solution)/shard_map/all_to_all | solution.py:713
  91.2 9.2 %collective-permute-done.21.refs_1_ = bf16[320,1280]{1,0:T(8,128)(2,1)} collective-permute-done((bf16[320,1280]{1,0:T(8,128)(2,1)}, bf16[320,1280]{1,0:T(8,128)(2,1)}, u32[]{:S(2)}, u32[]{:S(2)}) %collective-permute-start.21) | collective-permute-done | bytes 819232 | tf_op jit(solution)/shard_map/ppermute | solution.py:694
  100.5 1.8 all-to-all-done
  106.2 10.8 %row_part.1 = (bf16[128,1280]{1,0:T(8,128)(2,1)}, f32[128,1280]{1,0:T(8,128)}, bf16[1280,128]{1,0:T(8,128)(2,1)}, bf16[3776,128]{1,0:T(8,128)(2,1)}, bf16[3776,1...) custom-call(s32[4]{0:T(128)} %pad_add_fusion.1.refs_0_.refs_1_, bf16[1280,128]{1,0:T(8,128)(2,1)} %bitcast.25, ...), custom_call_target="tpu_custom_call" | custom-call | flops 11500000256 | bytes 1 | tf_op jit(solution)/shard_map/row_part/pallas_call | solution.py:76
  118.7 4.4 %all-to-all-start.1 = ((bf16[16,80,128]{2,1,0:T(8,128)(2,1)}), bf16[16,80,128]{2,1,0:T(8,128)(2,1)}, u32[]{:S(2)}, u32[]{:S(2)}) async-start(bf16[16,80,128]{2,1,0:T(8,128)(2,1)} %bitcast.23), calls=%async_computation.1 | async-start | bytes 655360 | tf_op jit(solution)/shard_map/all_to_all | solution.py:713
  126.6 7.6 %all-to-all-done.1.refs_5_ = bf16[16,80,128]{2,1,0:T(8,128)(2,1)} async-done(((bf16[16,80,128]{2,1,0:T(8,128)(2,1)}), bf16[16,80,128]{2,1,0:T(8,128)(2,1)}, u32[]{:S(2)}, u32[]{:S(2)}) %all-to-all-start.1) | async-done | bytes 327712 | tf_op jit(solution)/shard_map/all_to_all | solution.py:713
  134.2 24.4 %attention_backward.1 = (f32[8,160,256]{2,1,0:T(8,128)}, bf16[8,160,256]{2,1,0:T(8,128)(2,1)}, bf16[16,80,128]{2,1,0:T(8,128)(2,1)}, f32[80,512]{1,0:T(8,128)}) custom-call(s32[16,2]{1,0:T(8,128)} %copy-done.16, s32[8]{0:T(128)} %constant.102.clone.refs_1_, s32[8]{0:T(128)} %constant.103.clone.refs_2_, s32[4,1,512]{2,1,0:T(1,128)} %constant.99.clone.refs_5_.refs_3_, ...), custom_call_target="tpu_custom_call" | custom-call | flops 28750000128 | bytes 1 | tf_op jit(solution)/shard_map/attention_backward/pallas_call | solution.py:76
  163.0 3.3 %pooled_grads.1.refs_1_ = bf16[5,256,1280]{2,1,0:T(8,128)(2,1)S(1)} custom-call(bf16[3776,128]{1,0:T(8,128)(2,1)S(1)} %copy-done.47, bf16[3776,128]{1,0:T(8,128)(2,1)} %get-tuple-element.113.refs_1_, bf16[3776,128]{1,0:T(8,128)(2,1)} %get-tuple-element.114.refs_2_, bf16[1200,128]{1,0:T(8,128)(2,1)} %get-tuple-element.115.refs_3_, ...), custom_call_target="tpu_custom_call" | custom-call | flops 3449999872 | bytes 1 | tf_op jit(solution)/shard_map/pooled_grads/pallas_call | solution.py:76
  168.3 5.8 %collective-permute-done.34.refs_2_ = bf16[256,640]{1,0:T(8,128)(2,1)S(1)} collective-permute-done((bf16[256,640]{1,0:T(8,128)(2,1)S(1)}, bf16[256,640]{1,0:T(8,128)(2,1)S(1)}, u32[]{:S(2)}, u32[]{:S(2)}) %collective-permute-start.34) | collective-permute-done | bytes 327712 | tf_op jit(solution)/shard_map/ppermute | solution.py:682
  175.4 2.7 collective-permute-done.26.refs_4_
  178.2 1.9 join.1
  180.1 4.5 %qkv_grads.1 = (f32[256,640]{1,0:T(8,128)S(1)}, bf16[256,640]{1,0:T(8,128)(2,1)S(1)}) custom-call(s32[16]{0:T(128)S(1)} %fusion.1.refs_0_, s32[4]{0:T(128)S(1)} %copy-done.26, bf16[16,240,128]{2,1,0:T(8,128)(2,1)S(1)} %get-tuple-element.117.refs_2_.refs_1_, f32[80,512]{1,0:T(8,128)S(1)} %copy-done.52, bf16[8,128,1280]{2,1,0:T(8,128)(2,1)S(1)} %copy-done.1, ...), custom_call_target="tpu_custom_call" | custom-call | flops 5405000192 | bytes 1 | tf_op jit(solution)/shard_map/qkv_grads/pallas_call | solution.py:76
  184.6 1.6 collective-permute-start.38
  187.7 2.5 products.1.refs_1_
  190.8 4.0 %collective-permute-done.38.refs_1_ = bf16[256,640]{1,0:T(8,128)(2,1)S(1)} collective-permute-done((bf16[256,640]{1,0:T(8,128)(2,1)S(1)}, bf16[256,640]{1,0:T(8,128)(2,1)S(1)}, u32[]{:S(2)}, u32[]{:S(2)}) %collective-permute-start.38) | collective-permute-done | bytes 327712 | tf_op jit(solution)/shard_map/ppermute | solution.py:694
  195.0 2.6 collective-permute-done.40.refs_2_
  202.6 6.4 %collective-permute-done.42.refs_2_ = bf16[256,1280]{1,0:T(8,128)(2,1)S(1)} collective-permute-done((bf16[256,1280]{1,0:T(8,128)(2,1)S(1)}, bf16[256,1280]{1,0:T(8,128)(2,1)S(1)}, u32[]{:S(2)}, u32[]{:S(2)}) %collective-permute-start.42) | collective-permute-done | bytes 655392 | tf_op jit(solution)/shard_map/ppermute | solution.py:682
  208.9 3.5 %collective-permute-done.37.refs_2_ = bf16[256,640]{1,0:T(8,128)(2,1)S(1)} collective-permute-done((bf16[256,640]{1,0:T(8,128)(2,1)S(1)}, bf16[256,640]{1,0:T(8,128)(2,1)S(1)}, u32[]{:S(2)}, u32[]{:S(2)}) %collective-permute-start.37) | collective-permute-done | bytes 327712 | tf_op jit(solution)/shard_map/ppermute | solution.py:682
  213.9 5.6 %collective-permute-done.44.refs_4_.refs_2_ = bf16[512,640]{1,0:T(8,128)(2,1)S(1)} collective-permute-done((bf16[512,640]{1,0:T(8,128)(2,1)S(1)}, bf16[512,640]{1,0:T(8,128)(2,1)S(1)}, u32[]{:S(2)}, u32[]{:S(2)}) %collective-permute-start.44) | collective-permute-done | bytes 655392 | tf_op jit(solution)/shard_map/ppermute | solution.py:682
  222.3 4.2 %collective-permute-done.41.refs_2_ = bf16[256,1280]{1,0:T(8,128)(2,1)S(1)} collective-permute-done((bf16[256,1280]{1,0:T(8,128)(2,1)S(1)}, bf16[256,1280]{1,0:T(8,128)(2,1)S(1)}, u32[]{:S(2)}, u32[]{:S(2)}) %collective-permute-start.41) | collective-permute-done | bytes 655392 | tf_op jit(solution)/shard_map/ppermute | solution.py:682
  227.9 5.7 %collective-permute-done.46.refs_4_.refs_3_ = bf16[512,640]{1,0:T(8,128)(2,1)} collective-permute-done((bf16[512,640]{1,0:T(8,128)(2,1)S(1)}, bf16[512,640]{1,0:T(8,128)(2,1)}, u32[]{:S(2)}, u32[]{:S(2)}) %collective-permute-start.46) | collective-permute-done | bytes 655392 | tf_op jit(solution)/shard_map/ppermute | solution.py:682
  234.3 6.3 %collective-permute-done.49.refs_2_ = bf16[256,1280]{1,0:T(8,128)(2,1)} collective-permute-done((bf16[256,1280]{1,0:T(8,128)(2,1)S(1)}, bf16[256,1280]{1,0:T(8,128)(2,1)}, u32[]{:S(2)}, u32[]{:S(2)}) %collective-permute-start.49) | collective-permute-done | bytes 655392 | tf_op jit(solution)/shard_map/ppermute | solution.py:682
  241.3 6.2 %collective-permute-done.45.refs_2_ = bf16[256,1280]{1,0:T(8,128)(2,1)S(1)} collective-permute-done((bf16[256,1280]{1,0:T(8,128)(2,1)S(1)}, bf16[256,1280]{1,0:T(8,128)(2,1)S(1)}, u32[]{:S(2)}, u32[]{:S(2)}) %collective-permute-start.45) | collective-permute-done | bytes 655392 | tf_op jit(solution)/shard_map/ppermute | solution.py:682
  249.8 4.8 %collective-permute-done.51.refs_8_.refs_4_ = bf16[512,640]{1,0:T(8,128)(2,1)S(1)} collective-permute-done((bf16[512,640]{1,0:T(8,128)(2,1)}, bf16[512,640]{1,0:T(8,128)(2,1)S(1)}, u32[]{:S(2)}, u32[]{:S(2)}) %collective-permute-start.51) | collective-permute-done | bytes 655392 | tf_op jit(solution)/shard_map/ppermute | solution.py:682
  254.6 7.1 %collective-permute-done.50.refs_7_.refs_3_ = bf16[256,1280]{1,0:T(8,128)(2,1)} collective-permute-done((bf16[256,1280]{1,0:T(8,128)(2,1)}, bf16[256,1280]{1,0:T(8,128)(2,1)}, u32[]{:S(2)}, u32[]{:S(2)}) %collective-permute-start.50) | collective-permute-done | bytes 655392 | tf_op jit(solution)/shard_map/ppermute | solution.py:682
  262.5 6.2 %collective-permute-done.47.refs_2_ = bf16[256,1280]{1,0:T(8,128)(2,1)} collective-permute-done((bf16[256,1280]{1,0:T(8,128)(2,1)}, bf16[256,1280]{1,0:T(8,128)(2,1)}, u32[]{:S(2)}, u32[]{:S(2)}) %collective-permute-start.47) | collective-permute-done | bytes 655392 | tf_op jit(solution)/shard_map/ppermute | solution.py:682
  269.4 2.8 collective-permute-done.55.refs_8_
  273.9 4.7 %rows_place.2 = (f32[640,1280]{1,0:T(8,128)}, f32[640,1280]{1,0:T(8,128)}, f32[640,1280]{1,0:T(8,128)}, f32[640,128]{1,0:T(8,128)S(1)}, f32[8,128]{1,0:T(8,128)S(1)}) custom-call(s32[4]{0:T(128)S(1)} %copy-done.26, bf16[256,1280]{1,0:T(8,128)(2,1)S(1)} %copy-done.33, bf16[256,1280]{1,0:T(8,128)(2,1)} %collective-permute-done.49.refs_2_, ...), custom_call_target="tpu_custom_call" | custom-call | flops 4600000000 | bytes 1 | tf_op jit(solution)/shard_map/rows_place/pallas_call | solution.py:76
  278.6 3.0 inputs_grad.1.refs_1_
  283.4 7.1 %qkv_place.1 = (f32[640,1280]{1,0:T(8,128)}, f32[640,1280]{1,0:T(8,128)}, f32[640,1280]{1,0:T(8,128)}, f32[640]{0:T(1024)}, f32[40]{0:T(128)}) custom-call(s32[4]{0:T(128)S(1)} %copy-done.26, bf16[512,640]{1,0:T(8,128)(2,1)S(1)} %copy-done.29, bf16[512,640]{1,0:T(8,128)(2,1)S(1)} %copy-done.31, bf16[512,640]{1,0:T(8,128)(2,1)} %collective-permute-done.46.refs_4_.refs_3_, ...), custom_call_target="tpu_custom_call" | custom-call | flops 6899999744 | bytes 1 | tf_op jit(solution)/shard_map/qkv_place/pallas_call | solution.py:76
  290.6 1.9 copy-done.2
  292.5 1.6 collective-permute-done.62.refs_4_
  294.1 3.4 %rows_place.3 = (f32[640,1280]{1,0:T(8,128)}, f32[640,1280]{1,0:T(8,128)}, f32[640,1280]{1,0:T(8,128)}, f32[640]{0:T(1024)}, f32[2]{0:T(128)}) custom-call(s32[4]{0:T(128)S(1)} %copy-done.26, bf16[256,1280]{1,0:T(8,128)(2,1)S(1)} %gate.24.refs_1_, ...), custom_call_target="tpu_custom_call", output_to_operand_aliasing={{0}: (9, {}), {1}: (10, {}), {2}: (11, {})} | custom-call | flops 3449999872 | bytes 1 | tf_op jit(solution)/shard_map/rows_place/pallas_call | solution.py:76
  (255 shorter events, 65.5 us)
Async XLA Ops:
  0.6 11.0 %collective-permute-start.1 = (bf16[128,1280]{1,0:T(8,128)(2,1)}, bf16[128,1280]{1,0:T(8,128)(2,1)S(1)}, u32[]{:S(2)}, u32[]{:S(2)}) collective-permute-start(bf16[128,1280]{1,0:T(8,128)(2,1)} %bitcast.31), channel_id=1, source_target_pairs={{0,4},{2,6},{8,0},{10,2},{16,8},{18,10},{24,16},{26,18},{28,24},{3... | collective-permute-start | bytes 983048 | tf_op jit(solution)/shard_map/ppermute | solution.py:670
  7.7 10.8 %collective-permute-start.4 = (bf16[256,640]{1,0:T(8,128)(2,1)}, bf16[256,640]{1,0:T(8,128)(2,1)S(1)}, u32[]{:S(2)}, u32[]{:S(2)}) collective-permute-start(bf16[256,640]{1,0:T(8,128)(2,1)} %slab.1.refs_1_.refs_2_), channel_id=1, source_target_pairs={{0,1},{1,0},{2,3},{3,2},{4,5},{5,4},{6,7},{7,6},{8,9},{9,8},{10,11... | collective-permute-start | bytes 983048 | tf_op jit(solution)/shard_map/ppermute | solution.py:694
  10.6 13.6 %collective-permute-start.5 = (bf16[128,1280]{1,0:T(8,128)(2,1)S(1)}, bf16[128,1280]{1,0:T(8,128)(2,1)}, u32[]{:S(2)}, u32[]{:S(2)}) collective-permute-start(bf16[128,1280]{1,0:T(8,128)(2,1)S(1)} %constant_dynamic-slice_fusion.4), channel_id=1, source_target_pairs={{0,1},{1,0},{2,3},{3,2},{4,5},{5,4},{6,7},{7,6},{8,9},{9,8},{10,11... | collective-permute-start | bytes 983048 | tf_op jit(solution)/shard_map/ppermute | solution.py:694
  11.6 12.6 %collective-permute-start.3 = (bf16[128,1280]{1,0:T(8,128)(2,1)S(1)}, bf16[128,1280]{1,0:T(8,128)(2,1)S(1)}, u32[]{:S(2)}, u32[]{:S(2)}) collective-permute-start(bf16[128,1280]{1,0:T(8,128)(2,1)S(1)} %collective-permute-done.1.refs_3_), channel_id=1, source_target_pairs={{0,4},{2,6},{8,0},{10,2},{16,8},{18,10},{24,16},{26,18},{28,24},{3... | collective-permute-start | bytes 983048 | tf_op jit(solution)/shard_map/ppermute | solution.py:670
  13.3 10.9 %collective-permute-start.2 = (bf16[128,1280]{1,0:T(8,128)(2,1)S(1)}, bf16[128,1280]{1,0:T(8,128)(2,1)S(1)}, u32[]{:S(2)}, u32[]{:S(2)}) collective-permute-start(bf16[128,1280]{1,0:T(8,128)(2,1)S(1)} %collective-permute-done.refs_2_), channel_id=1, source_target_pairs={{0,8},{2,10},{8,16},{10,18},{16,24},{18,26},{24,28},{26,30},{28,20... | collective-permute-start | bytes 983048 | tf_op jit(solution)/shard_map/ppermute | solution.py:670
  28.6 9.9 %collective-permute-start.11 = (bf16[128,1280]{1,0:T(8,128)(2,1)S(1)}, bf16[128,1280]{1,0:T(8,128)(2,1)S(1)}, u32[]{:S(2)}, u32[]{:S(2)}) collective-permute-start(bf16[128,1280]{1,0:T(8,128)(2,1)S(1)} %collective-permute-done.3.refs_4_.refs_5_), channel_id=1, source_target_pairs={{0,4},{2,6},{8,0},{10,2},{16,8},{18,10},{24,16},{26,18},{28,24},{3... | collective-permute-start | bytes 983048 | tf_op jit(solution)/shard_map/ppermute | solution.py:670
  30.7 14.6 %collective-permute-start.14 = (bf16[192,1280]{1,0:T(8,128)(2,1)S(1)}, bf16[192,1280]{1,0:T(8,128)(2,1)}, u32[]{:S(2)}, u32[]{:S(2)}) collective-permute-start(bf16[192,1280]{1,0:T(8,128)(2,1)S(1)} %gate.14), channel_id=1, source_target_pairs={{0,1},{1,0},{2,3},{3,2},{4,5},{5,4},{6,7},{7,6},{8,9},{9,8},{10,11... | collective-permute-start | bytes 1474568 | tf_op jit(solution)/shard_map/ppermute | solution.py:694
  43.6 12.4 %collective-permute-start.9 = (bf16[5,160,128]{2,1,0:T(8,128)(2,1)}, bf16[5,160,128]{2,1,0:T(8,128)(2,1)S(1)}, u32[]{:S(2)}, u32[]{:S(2)}) collective-permute-start(bf16[5,160,128]{2,1,0:T(8,128)(2,1)} %get-tuple-element.82), channel_id=1, source_target_pairs={{0,3},{1,2},{2,1},{3,0},{4,7},{5,6},{6,5},{7,4},{8,11},{9,10},{10,... | collective-permute-start | bytes 614408 | tf_op jit(solution)/shard_map/ppermute | solution.py:691
  43.7 16.9 %collective-permute-start.7 = (bf16[5,160,128]{2,1,0:T(8,128)(2,1)}, bf16[5,160,128]{2,1,0:T(8,128)(2,1)S(1)}, u32[]{:S(2)}, u32[]{:S(2)}) collective-permute-start(bf16[5,160,128]{2,1,0:T(8,128)(2,1)} %get-tuple-element.80.refs_7_), channel_id=1, source_target_pairs={{0,1},{1,0},{2,3},{3,2},{4,5},{5,4},{6,7},{7,6},{8,9},{9,8},{10,11... | collective-permute-start | bytes 614408 | tf_op jit(solution)/shard_map/ppermute | solution.py:694
  45.3 19.2 %collective-permute-start.8 = (bf16[5,240,128]{2,1,0:T(8,128)(2,1)}, bf16[5,240,128]{2,1,0:T(8,128)(2,1)}, u32[]{:S(2)}, u32[]{:S(2)}) collective-permute-start(bf16[5,240,128]{2,1,0:T(8,128)(2,1)} %get-tuple-element.81), channel_id=1, source_target_pairs={{0,2},{2,0},{4,6},{6,4},{8,10},{10,8},{12,14},{14,12},{16,18},{18,... | collective-permute-start | bytes 921608 | tf_op jit(solution)/shard_map/ppermute | solution.py:685
  53.2 11.8 %collective-permute-start.16 = (bf16[3,240,128]{2,1,0:T(8,128)(2,1)}, bf16[3,240,128]{2,1,0:T(8,128)(2,1)}, u32[]{:S(2)}, u32[]{:S(2)}) collective-permute-start(bf16[3,240,128]{2,1,0:T(8,128)(2,1)} %get-tuple-element.88), channel_id=1, source_target_pairs={{0,2},{2,0},{4,6},{6,4},{8,10},{10,8},{12,14},{14,12},{16,18},{18,... | collective-permute-start | bytes 552968 | tf_op jit(solution)/shard_map/ppermute | solution.py:685
  60.6 23.4 %collective-permute-start.18 = (bf16[128,1280]{1,0:T(8,128)(2,1)}, bf16[128,1280]{1,0:T(8,128)(2,1)S(1)}, u32[]{:S(2)}, u32[]{:S(2)}) collective-permute-start(bf16[128,1280]{1,0:T(8,128)(2,1)} %gate.15.refs_6_), channel_id=1, source_target_pairs={{0,2},{2,0},{4,6},{6,4},{8,10},{10,8},{12,14},{14,12},{16,18},{18,... | collective-permute-start | bytes 983048 | tf_op jit(solution)/shard_map/ppermute | solution.py:685
  60.7 23.3 %collective-permute-start.19 = (bf16[192,1280]{1,0:T(8,128)(2,1)}, bf16[192,1280]{1,0:T(8,128)(2,1)S(1)}, u32[]{:S(2)}, u32[]{:S(2)}) collective-permute-start(bf16[192,1280]{1,0:T(8,128)(2,1)} %gate.16.refs_8_), channel_id=1, source_target_pairs={{0,2},{2,0},{4,6},{6,4},{8,10},{10,8},{12,14},{14,12},{16,18},{18,... | collective-permute-start | bytes 1474568 | tf_op jit(solution)/shard_map/ppermute | solution.py:685
  63.0 28.3 %collective-permute-start.20 = (bf16[320,1280]{1,0:T(8,128)(2,1)}, bf16[320,1280]{1,0:T(8,128)(2,1)}, u32[]{:S(2)}, u32[]{:S(2)}) collective-permute-start(bf16[320,1280]{1,0:T(8,128)(2,1)} %gate.18), channel_id=1, source_target_pairs={{0,1},{1,0},{2,3},{3,2},{4,5},{5,4},{6,7},{7,6},{8,9},{9,8},{10,11... | collective-permute-start | bytes 2457608 | tf_op jit(solution)/shard_map/ppermute | solution.py:694
  64.5 36.0 %collective-permute-start.21 = (bf16[320,1280]{1,0:T(8,128)(2,1)}, bf16[320,1280]{1,0:T(8,128)(2,1)}, u32[]{:S(2)}, u32[]{:S(2)}) collective-permute-start(bf16[320,1280]{1,0:T(8,128)(2,1)} %gate.19), channel_id=1, source_target_pairs={{0,1},{1,0},{2,3},{3,2},{4,5},{5,4},{6,7},{7,6},{8,9},{9,8},{10,11... | collective-permute-start | bytes 2457608 | tf_op jit(solution)/shard_map/ppermute | solution.py:694
  87.2 15.1 %all-to-all-start = ((bf16[16,80,128]{2,1,0:T(8,128)(2,1)}), bf16[16,80,128]{2,1,0:T(8,128)(2,1)S(1)}, u32[]{:S(2)}, u32[]{:S(2)}) async-start(bf16[16,80,128]{2,1,0:T(8,128)(2,1)} %copy-done.4), calls=%async_computation | async-start | bytes 655360 | tf_op jit(solution)/shard_map/all_to_all | solution.py:713
  103.8 13.2 %collective-permute-start.24 = (bf16[128,1280]{1,0:T(8,128)(2,1)S(1)}, bf16[128,1280]{1,0:T(8,128)(2,1)S(1)}, u32[]{:S(2)}, u32[]{:S(2)}) collective-permute-start(bf16[128,1280]{1,0:T(8,128)(2,1)S(1)} %gate.21), channel_id=1, source_target_pairs={{0,1},{1,0},{2,3},{3,2},{4,5},{5,4},{6,7},{7,6},{8,9},{9,8},{10,11... | collective-permute-start | bytes 983048 | tf_op jit(solution)/shard_map/ppermute | solution.py:694
  118.7 15.5 %all-to-all-start.1 = ((bf16[16,80,128]{2,1,0:T(8,128)(2,1)}), bf16[16,80,128]{2,1,0:T(8,128)(2,1)}, u32[]{:S(2)}, u32[]{:S(2)}) async-start(bf16[16,80,128]{2,1,0:T(8,128)(2,1)} %bitcast.23), calls=%async_computation.1 | async-start | bytes 655360 | tf_op jit(solution)/shard_map/all_to_all | solution.py:713
  123.3 35.3 %collective-permute-start.31 = (bf16[8,128,1280]{2,1,0:T(8,128)(2,1)S(1)}, bf16[8,128,1280]{2,1,0:T(8,128)(2,1)}, u32[]{:S(2)}, u32[]{:S(2)}) collective-permute-start(bf16[8,128,1280]{2,1,0:T(8,128)(2,1)S(1)} %copy-done.1), channel_id=1, source_target_pairs={{0,2},{2,0},{4,6},{6,4},{8,10},{10,8},{12,14},{14,12},{16,18},{18,... | collective-permute-start | bytes 7864328 | tf_op jit(solution)/shard_map/ppermute | solution.py:685
  123.7 35.0 %collective-permute-start.30 = (bf16[128,1280]{1,0:T(8,128)(2,1)S(1)}, bf16[128,1280]{1,0:T(8,128)(2,1)S(1)}, u32[]{:S(2)}, u32[]{:S(2)}) collective-permute-start(bf16[128,1280]{1,0:T(8,128)(2,1)S(1)} %get-tuple-element.112.refs_7_), channel_id=1, source_target_pairs={{0,2},{2,0},{4,6},{6,4},{8,10},{10,8},{12,14},{14,12},{16,18},{18,... | collective-permute-start | bytes 983048 | tf_op jit(solution)/shard_map/ppermute | solution.py:685
  123.9 34.8 %collective-permute-start.27 = (bf16[3776,128]{1,0:T(8,128)(2,1)}, bf16[3776,128]{1,0:T(8,128)(2,1)}, u32[]{:S(2)}, u32[]{:S(2)}) collective-permute-start(bf16[3776,128]{1,0:T(8,128)(2,1)} %get-tuple-element.110), channel_id=1, source_target_pairs={{0,1},{1,0},{2,3},{3,2},{4,5},{5,4},{6,7},{7,6},{8,9},{9,8},{10,11... | collective-permute-start | bytes 2899976 | tf_op jit(solution)/shard_map/ppermute | solution.py:694
  125.4 33.3 %collective-permute-start.28 = (bf16[3776,128]{1,0:T(8,128)(2,1)}, bf16[3776,128]{1,0:T(8,128)(2,1)}, u32[]{:S(2)}, u32[]{:S(2)}) collective-permute-start(bf16[3776,128]{1,0:T(8,128)(2,1)} %get-tuple-element.111), channel_id=1, source_target_pairs={{0,2},{2,0},{4,6},{6,4},{8,10},{10,8},{12,14},{14,12},{16,18},{18,... | collective-permute-start | bytes 2899976 | tf_op jit(solution)/shard_map/ppermute | solution.py:685
  125.4 33.2 %collective-permute-start.29 = (bf16[1200,128]{1,0:T(8,128)(2,1)}, bf16[1200,128]{1,0:T(8,128)(2,1)}, u32[]{:S(2)}, u32[]{:S(2)}) collective-permute-start(bf16[1200,128]{1,0:T(8,128)(2,1)} %collective-permute-done.25.refs_12_), channel_id=1, source_target_pairs={{0,1},{1,0},{2,3},{3,2},{4,5},{5,4},{6,7},{7,6},{8,9},{9,8},{10,11... | collective-permute-start | bytes 921608 | tf_op jit(solution)/shard_map/ppermute | solution.py:694
  161.2 16.9 %collective-permute-start.26 = (bf16[8,160,256]{2,1,0:T(8,128)(2,1)S(1)}, bf16[8,160,256]{2,1,0:T(8,128)(2,1)S(1)}, u32[]{:S(2)}, u32[]{:S(2)}) collective-permute-start(bf16[8,160,256]{2,1,0:T(8,128)(2,1)S(1)} %copy-done.54), channel_id=1, source_target_pairs={{0,1},{1,0},{2,3},{3,2},{4,5},{5,4},{6,7},{7,6},{8,9},{9,8},{10,11... | collective-permute-start | bytes 1966088 | tf_op jit(solution)/shard_map/ppermute | solution.py:694
  174.8 11.5 %collective-permute-start.36 = (bf16[256,1280]{1,0:T(8,128)(2,1)S(1)}, bf16[256,1280]{1,0:T(8,128)(2,1)S(1)}, u32[]{:S(2)}, u32[]{:S(2)}) collective-permute-start(bf16[256,1280]{1,0:T(8,128)(2,1)S(1)} %reduce_step.9.refs_5_), channel_id=1, source_target_pairs={{0,8},{2,6},{8,16},{10,2},{16,24},{18,10},{24,28},{26,18},{28,20},... | collective-permute-start | bytes 1966088 | tf_op jit(solution)/shard_map/ppermute | solution.py:682
  184.6 10.2 %collective-permute-start.38 = (bf16[256,640]{1,0:T(8,128)(2,1)S(1)}, bf16[256,640]{1,0:T(8,128)(2,1)S(1)}, u32[]{:S(2)}, u32[]{:S(2)}) collective-permute-start(bf16[256,640]{1,0:T(8,128)(2,1)S(1)} %get-tuple-element.122), channel_id=1, source_target_pairs={{0,1},{1,0},{2,3},{3,2},{4,5},{5,4},{6,7},{7,6},{8,9},{9,8},{10,11... | collective-permute-start | bytes 983048 | tf_op jit(solution)/shard_map/ppermute | solution.py:694
  187.0 10.6 %collective-permute-start.40 = (bf16[256,1280]{1,0:T(8,128)(2,1)S(1)}, bf16[256,1280]{1,0:T(8,128)(2,1)S(1)}, u32[]{:S(2)}, u32[]{:S(2)}) collective-permute-start(bf16[256,1280]{1,0:T(8,128)(2,1)S(1)} %reduce_step.10.refs_5_), channel_id=1, source_target_pairs={{0,8},{2,6},{8,16},{10,2},{16,24},{18,10},{24,28},{26,18},{28,20},... | collective-permute-start | bytes 1966088 | tf_op jit(solution)/shard_map/ppermute | solution.py:682
  198.3 10.6 %collective-permute-start.42 = (bf16[256,1280]{1,0:T(8,128)(2,1)S(1)}, bf16[256,1280]{1,0:T(8,128)(2,1)S(1)}, u32[]{:S(2)}, u32[]{:S(2)}) collective-permute-start(bf16[256,1280]{1,0:T(8,128)(2,1)S(1)} %reduce_step.12.refs_3_), channel_id=1, source_target_pairs={{0,8},{2,6},{8,16},{10,2},{16,24},{18,10},{24,28},{26,18},{28,20},... | collective-permute-start | bytes 1966088 | tf_op jit(solution)/shard_map/ppermute | solution.py:682
  199.0 13.4 %collective-permute-start.37 = (bf16[256,640]{1,0:T(8,128)(2,1)S(1)}, bf16[256,640]{1,0:T(8,128)(2,1)S(1)}, u32[]{:S(2)}, u32[]{:S(2)}) collective-permute-start(bf16[256,640]{1,0:T(8,128)(2,1)S(1)} %reduce_step.11.refs_3_), channel_id=1, source_target_pairs={{0,8},{2,6},{8,16},{10,2},{16,24},{18,10},{24,28},{26,18},{28,20},... | collective-permute-start | bytes 983048 | tf_op jit(solution)/shard_map/ppermute | solution.py:682
  201.3 18.2 %collective-permute-start.44 = (bf16[512,640]{1,0:T(8,128)(2,1)S(1)}, bf16[512,640]{1,0:T(8,128)(2,1)S(1)}, u32[]{:S(2)}, u32[]{:S(2)}) collective-permute-start(bf16[512,640]{1,0:T(8,128)(2,1)S(1)} %chip_pack.1.refs_3_.refs_4_.refs_1_), channel_id=1, source_target_pairs={{0,8},{2,6},{8,16},{10,2},{16,24},{18,10},{24,28},{26,18},{28,20},... | collective-permute-start | bytes 1966088 | tf_op jit(solution)/shard_map/ppermute | solution.py:682
  208.9 11.2 %collective-permute-start.43 = (bf16[256,1280]{1,0:T(8,128)(2,1)S(1)}, bf16[256,1280]{1,0:T(8,128)(2,1)S(1)}, u32[]{:S(2)}, u32[]{:S(2)}) collective-permute-start(bf16[256,1280]{1,0:T(8,128)(2,1)S(1)} %collective-permute-done.42.refs_2_), channel_id=1, source_target_pairs={{0,2},{2,0},{4,6},{6,4},{8,10},{10,8},{12,14},{14,12},{16,18},{18,... | collective-permute-start | bytes 1966088 | tf_op jit(solution)/shard_map/ppermute | solution.py:685
  213.1 13.4 %collective-permute-start.41 = (bf16[256,1280]{1,0:T(8,128)(2,1)S(1)}, bf16[256,1280]{1,0:T(8,128)(2,1)S(1)}, u32[]{:S(2)}, u32[]{:S(2)}) collective-permute-start(bf16[256,1280]{1,0:T(8,128)(2,1)S(1)} %reduce_step.13), channel_id=1, source_target_pairs={{0,8},{2,6},{8,16},{10,2},{16,24},{18,10},{24,28},{26,18},{28,20},... | collective-permute-start | bytes 1966088 | tf_op jit(solution)/shard_map/ppermute | solution.py:682
  219.5 14.1 %collective-permute-start.46 = (bf16[512,640]{1,0:T(8,128)(2,1)S(1)}, bf16[512,640]{1,0:T(8,128)(2,1)}, u32[]{:S(2)}, u32[]{:S(2)}) collective-permute-start(bf16[512,640]{1,0:T(8,128)(2,1)S(1)} %collective-permute-done.44.refs_4_.refs_2_), channel_id=1, source_target_pairs={{0,8},{2,6},{8,16},{10,2},{16,24},{18,10},{24,28},{26,18},{28,20},... | collective-permute-start | bytes 1966088 | tf_op jit(solution)/shard_map/ppermute | solution.py:682
  221.0 19.7 %collective-permute-start.49 = (bf16[256,1280]{1,0:T(8,128)(2,1)S(1)}, bf16[256,1280]{1,0:T(8,128)(2,1)}, u32[]{:S(2)}, u32[]{:S(2)}) collective-permute-start(bf16[256,1280]{1,0:T(8,128)(2,1)S(1)} %reduce_end.1.refs_3_.refs_1_), channel_id=1, source_target_pairs={{0,8},{2,6},{8,16},{10,2},{16,24},{18,10},{24,28},{26,18},{28,20},... | collective-permute-start | bytes 1966088 | tf_op jit(solution)/shard_map/ppermute | solution.py:682
  227.2 20.3 %collective-permute-start.45 = (bf16[256,1280]{1,0:T(8,128)(2,1)S(1)}, bf16[256,1280]{1,0:T(8,128)(2,1)S(1)}, u32[]{:S(2)}, u32[]{:S(2)}) collective-permute-start(bf16[256,1280]{1,0:T(8,128)(2,1)S(1)} %reduce_step.14.refs_3_), channel_id=1, source_target_pairs={{0,8},{2,6},{8,16},{10,2},{16,24},{18,10},{24,28},{26,18},{28,20},... | collective-permute-start | bytes 1966088 | tf_op jit(solution)/shard_map/ppermute | solution.py:682
  233.6 21.0 %collective-permute-start.51 = (bf16[512,640]{1,0:T(8,128)(2,1)}, bf16[512,640]{1,0:T(8,128)(2,1)S(1)}, u32[]{:S(2)}, u32[]{:S(2)}) collective-permute-start(bf16[512,640]{1,0:T(8,128)(2,1)} %collective-permute-done.46.refs_4_.refs_3_), channel_id=1, source_target_pairs={{0,8},{2,6},{8,16},{10,2},{16,24},{18,10},{24,28},{26,18},{28,20},... | collective-permute-start | bytes 1966088 | tf_op jit(solution)/shard_map/ppermute | solution.py:682
  240.6 21.1 %collective-permute-start.50 = (bf16[256,1280]{1,0:T(8,128)(2,1)}, bf16[256,1280]{1,0:T(8,128)(2,1)}, u32[]{:S(2)}, u32[]{:S(2)}) collective-permute-start(bf16[256,1280]{1,0:T(8,128)(2,1)} %collective-permute-done.49.refs_2_), channel_id=1, source_target_pairs={{0,8},{2,6},{8,16},{10,2},{16,24},{18,10},{24,28},{26,18},{28,20},... | collective-permute-start | bytes 1966088 | tf_op jit(solution)/shard_map/ppermute | solution.py:682
  241.3 20.4 %collective-permute-start.52 = (bf16[512,640]{1,0:T(8,128)(2,1)S(1)}, bf16[512,640]{1,0:T(8,128)(2,1)}, u32[]{:S(2)}, u32[]{:S(2)}) collective-permute-start(bf16[512,640]{1,0:T(8,128)(2,1)S(1)} %collective-permute-done.44.refs_4_.refs_2_), channel_id=1, source_target_pairs={{0,2},{2,0},{4,6},{6,4},{8,10},{10,8},{12,14},{14,12},{16,18},{18,... | collective-permute-start | bytes 1966088 | tf_op jit(solution)/shard_map/ppermute | solution.py:685
  249.1 19.6 %collective-permute-start.47 = (bf16[256,1280]{1,0:T(8,128)(2,1)}, bf16[256,1280]{1,0:T(8,128)(2,1)}, u32[]{:S(2)}, u32[]{:S(2)}) collective-permute-start(bf16[256,1280]{1,0:T(8,128)(2,1)} %reduce_step.15), channel_id=1, source_target_pairs={{0,8},{2,6},{8,16},{10,2},{16,24},{18,10},{24,28},{26,18},{28,20},... | collective-permute-start | bytes 1966088 | tf_op jit(solution)/shard_map/ppermute | solution.py:682
  249.8 19.0 %collective-permute-start.53 = (bf16[512,640]{1,0:T(8,128)(2,1)}, bf16[512,640]{1,0:T(8,128)(2,1)}, u32[]{:S(2)}, u32[]{:S(2)}) collective-permute-start(bf16[512,640]{1,0:T(8,128)(2,1)} %collective-permute-done.46.refs_4_.refs_3_), channel_id=1, source_target_pairs={{0,2},{2,0},{4,6},{6,4},{8,10},{10,8},{12,14},{14,12},{16,18},{18,... | collective-permute-start | bytes 1966088 | tf_op jit(solution)/shard_map/ppermute | solution.py:685
  254.6 17.7 %collective-permute-start.58 = (bf16[256,1280]{1,0:T(8,128)(2,1)}, bf16[256,1280]{1,0:T(8,128)(2,1)}, u32[]{:S(2)}, u32[]{:S(2)}) collective-permute-start(bf16[256,1280]{1,0:T(8,128)(2,1)} %collective-permute-done.49.refs_2_), channel_id=1, source_target_pairs={{0,2},{2,0},{4,6},{6,4},{8,10},{10,8},{12,14},{14,12},{16,18},{18,... | collective-permute-start | bytes 1966088 | tf_op jit(solution)/shard_map/ppermute | solution.py:685
  261.7 11.1 %collective-permute-start.59 = (bf16[256,1280]{1,0:T(8,128)(2,1)}, bf16[256,1280]{1,0:T(8,128)(2,1)}, u32[]{:S(2)}, u32[]{:S(2)}) collective-permute-start(bf16[256,1280]{1,0:T(8,128)(2,1)} %collective-permute-done.50.refs_7_.refs_3_), channel_id=1, source_target_pairs={{0,2},{2,0},{4,6},{6,4},{8,10},{10,8},{12,14},{14,12},{16,18},{18,... | collective-permute-start | bytes 1966088 | tf_op jit(solution)/shard_map/ppermute | solution.py:685
  261.8 10.5 %collective-permute-start.55 = (bf16[256,640]{1,0:T(8,128)(2,1)S(1)}, bf16[256,640]{1,0:T(8,128)(2,1)}, u32[]{:S(2)}, u32[]{:S(2)}) collective-permute-start(bf16[256,640]{1,0:T(8,128)(2,1)S(1)} %constant_dynamic-slice_fusion.1), channel_id=1, source_target_pairs={{0,8},{2,6},{8,16},{10,2},{16,24},{18,10},{24,28},{26,18},{28,20},... | collective-permute-start | bytes 983048 | tf_op jit(solution)/shard_map/ppermute | solution.py:682
  268.7 9.8 %collective-permute-start.48 = (bf16[256,1280]{1,0:T(8,128)(2,1)}, bf16[256,1280]{1,0:T(8,128)(2,1)}, u32[]{:S(2)}, u32[]{:S(2)}) collective-permute-start(bf16[256,1280]{1,0:T(8,128)(2,1)} %collective-permute-done.47.refs_2_), channel_id=1, source_target_pairs={{0,2},{2,0},{4,6},{6,4},{8,10},{10,8},{12,14},{14,12},{16,18},{18,... | collective-permute-start | bytes 1966088 | tf_op jit(solution)/shard_map/ppermute | solution.py:685
  268.7 12.9 %collective-permute-start.57 = (bf16[256,1280]{1,0:T(8,128)(2,1)}, bf16[256,1280]{1,0:T(8,128)(2,1)S(1)}, u32[]{:S(2)}, u32[]{:S(2)}) collective-permute-start(bf16[256,1280]{1,0:T(8,128)(2,1)} %collective-permute-done.50.refs_7_.refs_3_), channel_id=1, source_target_pairs={{0,8},{2,6},{8,16},{10,2},{16,24},{18,10},{24,28},{26,18},{28,20},... | collective-permute-start | bytes 1966088 | tf_op jit(solution)/shard_map/ppermute | solution.py:682
  272.2 11.1 %collective-permute-start.54 = (bf16[512,640]{1,0:T(8,128)(2,1)S(1)}, bf16[512,640]{1,0:T(8,128)(2,1)S(1)}, u32[]{:S(2)}, u32[]{:S(2)}) collective-permute-start(bf16[512,640]{1,0:T(8,128)(2,1)S(1)} %collective-permute-done.51.refs_8_.refs_4_), channel_id=1, source_target_pairs={{0,2},{2,0},{4,6},{6,4},{8,10},{10,8},{12,14},{14,12},{16,18},{18,... | collective-permute-start | bytes 1966088 | tf_op jit(solution)/shard_map/ppermute | solution.py:685
  272.3 11.1 %collective-permute-start.56 = (bf16[256,640]{1,0:T(8,128)(2,1)}, bf16[256,640]{1,0:T(8,128)(2,1)S(1)}, u32[]{:S(2)}, u32[]{:S(2)}) collective-permute-start(bf16[256,640]{1,0:T(8,128)(2,1)} %collective-permute-done.55.refs_8_), channel_id=1, source_target_pairs={{0,2},{2,0},{4,6},{6,4},{8,10},{10,8},{12,14},{14,12},{16,18},{18,... | collective-permute-start | bytes 983048 | tf_op jit(solution)/shard_map/ppermute | solution.py:685
  282.6 11.5 %collective-permute-start.60 = (bf16[256,1280]{1,0:T(8,128)(2,1)S(1)}, bf16[256,1280]{1,0:T(8,128)(2,1)S(1)}, u32[]{:S(2)}, u32[]{:S(2)}) collective-permute-start(bf16[256,1280]{1,0:T(8,128)(2,1)S(1)} %gate.24.refs_1_), channel_id=1, source_target_pairs={{0,2},{2,0},{4,6},{6,4},{8,10},{10,8},{12,14},{14,12},{16,18},{18,... | collective-permute-start | bytes 1966088 | tf_op jit(solution)/shard_map/ppermute | solution.py:685
  (76 other events, 483.5 us)

commit v4 on v3

--- a/solution.py
+++ b/solution.py
@@ -1121,7 +1121,7 @@
         "reduce_end",
         [chip_share],
     )
-    first, done = reduce_step(table, 2, first, [mine, q_steps[1]])
+    first, done = reduce_step(table, 2, first, [mine])
     mine = sum_groups(mine.astype(F32), BF).astype(BF) if groups > 1 else mine
     m_steps = [mine, ring_by_core(mine)]
     q_steps.append(ring_by_core(q_steps[-1]))
@@ -1129,16 +1129,6 @@
     m_steps.append(ring_by_core(m_steps[-1]))
     q_steps.append(ring_by_core(q_steps[-1]))
     m_steps.append(ring_by_core(m_steps[-1]))
-    first_near = swap_core(first[0])
-    (d_in,) = chunk_call(
-        table,
-        inputs_grad_body,
-        0,
-        (*first, first_near, x, dy, gains),
-        [((dev_rows, model), BF)],
-        "inputs_grad",
-        [m_steps[2], q_steps[3]],
-    )
     q_near = [swap_core(a) for a in q_steps[1:3]]
     m_near = [swap_core(a) for a in m_steps[1:3]]
     elements = float(ctx_count * 2 * dev_rows * model)
@@ -1151,18 +1141,28 @@
         out_specs=[any_spec] * 3 + [vmem_spec] * 2,
         scratch=[pltpu.VMEM((5, 3, chunk, model), F32), pltpu.SemaphoreType.DMA((5, 3))],
         smem=1,
-        after=q_near,
         name="rows_place",
         us=4,
         mib=40,
     )
 
+    first_near = swap_core(first[0])
+    (d_in,) = chunk_call(
+        table,
+        inputs_grad_body,
+        0,
+        (*first, first_near, x, dy, gains),
+        [((dev_rows, model), BF)],
+        "inputs_grad",
+        [m_steps[2], tails],
+    )
+
     def last_step(a, axis):
         size = a.shape[axis] // 2
         return ring_by_core(lax.dynamic_slice_in_dim(a, k * size, size, axis))
 
     q_last = last_step(q_steps[-1], 0)
-    (m_held,) = gates([m_steps[-1]], [d_in, tails])
+    m_held = m_steps[-1]
     m_last = last_step(m_held, 1)
     q_near += [swap_core(a) for a in q_steps[3:]]
     m_near += [swap_core(m_held)]
@@ -1176,7 +1176,7 @@
         us=6,
         mib=40,
     )
-    (m_last,) = gates([m_last], [grad_query])
+    (m_last,) = gates([m_last], [grad_query, d_in])
     ins = [spot, m_held, m_near[2], m_last, swap_core(m_last), w_hidden, gain_mlp, gain_sums, tails]
     grad_output, grad_hidden, grad_return, gain_two_grad, root_means = call(
         functools.partial(rows_place_body, False, elements),

time: 299 us -> 295 us (0.987)
  waiting for transfers between devices: 113 us -> 108 us
    ppermute x16, waiting for transfers between devices: 67.4 us -> 62.6 us  [ring_by_core(): return lax.ppermute(a, 'ctx', pairs)]
    pallas_call x39 -> x38, Pallas kernels: 106 us -> 107 us  [call(): pl.pallas_call(run, out_shape=[jax.ShapeDtypeStruct(shape, kind) for shap...]
    unnamed x119 -> x113, local copies, waits for them, and re-layouts: 20.7 us -> 19.5 us
  transfers between devices with their start and end apart: 65 -> 65, of which waited for: 30 -> 28; matrix products, arithmetic and copies ran while one was open for 2% -> 2% of each run, Pallas kernels for 34% -> 35%
where the time goes in v4:
time: 295 us; the launch traced here: 294 us
  waiting for transfers between devices  108 us (37%)
  Pallas kernels  107 us (36%)
  starting transfers between devices  51.5 us (17%)
  local copies, waits for them, and re-layouts  23.8 us (8%)
    pallas_call x38, Pallas kernels, call(): pl.pallas_call(run, out_shape=[jax.ShapeDtypeStruct(shape, kind) for shap...  107 us
    ppermute x16, waiting for transfers between devices, ring_by_core(): return lax.ppermute(a, 'ctx', pairs)  62.6 us
    ppermute x12, waiting for transfers between devices, swap_x(): return lax.ppermute(a, 'fsdp', [(0, 1), (1, 0)])  28.2 us
    unnamed x113, local copies, waits for them, and re-layouts  19.5 us
    ppermute x12, starting transfers between devices, swap_x(): return lax.ppermute(a, 'fsdp', [(0, 1), (1, 0)])  14.9 us
    ppermute x16, starting transfers between devices, ring_by_core(): return lax.ppermute(a, 'ctx', pairs)  12.8 us
    all_to_all x2, waiting for transfers between devices, exchange(): return lax.all_to_all(a, 'ctx', 0, 0, axis_index_groups=which, tiled=True)  9.49 us
    ppermute x8, starting transfers between devices, ring(): return lax.ppermute(a, 'ctx', pairs)  9.33 us
  transfers between devices with their start and end apart: 65, of which 28 were waited for; matrix products, arithmetic and copies ran while one was open for 2% of the time, Pallas kernels for 35%

profile of v4, /device:TPU:0, one launch (start us, length us, event | category | flops | bytes accessed | tf_op | source)
XLA Modules:
  0.0 293.8 jit_solution(3651588594318047134)
XLA Ops:
  0.6 3.0 %collective-permute-start.1 = (bf16[128,1280]{1,0:T(8,128)(2,1)}, bf16[128,1280]{1,0:T(8,128)(2,1)S(1)}, u32[]{:S(2)}, u32[]{:S(2)}) collective-permute-start(bf16[128,1280]{1,0:T(8,128)(2,1)} %bitcast.31), channel_id=1, source_target_pairs={{0,4},{2,6},{8,0},{10,2},{16,8},{18,10},{24,16},{26,18},{28,24},{3... | collective-permute-start | bytes 983048 | tf_op jit(solution)/shard_map/ppermute | solution.py:670
  4.4 3.2 %slab.1.refs_1_.refs_2_ = bf16[256,640]{1,0:T(8,128)(2,1)} custom-call(s32[4]{0:T(128)} %pad_add_fusion.1.refs_0_.refs_1_, bf16[640,1280]{1,0:T(8,128)(2,1)} %refs_2_.2, bf16[640,1280]{1,0:T(8,128)(2,1)} %refs_2_.2, bf16[640,1280]{1,0:T(8,128)(2,1)} %refs_4_.2, bf16[640,1280]{1,0:T(8,128)(2,1)} %refs_4_.2, bf16[640,1280]{1,0:T(8,128)(2,1)} %refs_6_.3, ...), custom_call_target="tpu_custom_call" | custom-call | flops 3449999872 | bytes 1 | tf_op jit(solution)/shard_map/slab/pallas_call | solution.py:76
  7.6 1.9 collective-permute-start.4
  11.6 1.7 collective-permute-start.3
  13.7 4.8 %collective-permute-done.4.refs_2_.refs_1_ = bf16[256,640]{1,0:T(8,128)(2,1)S(1)} collective-permute-done((bf16[256,640]{1,0:T(8,128)(2,1)}, bf16[256,640]{1,0:T(8,128)(2,1)S(1)}, u32[]{:S(2)}, u32[]{:S(2)}) %collective-permute-start.4) | collective-permute-done | bytes 327712 | tf_op jit(solution)/shard_map/ppermute | solution.py:694
  18.5 5.7 %collective-permute-done.5.refs_5_.refs_0_ = bf16[128,1280]{1,0:T(8,128)(2,1)} collective-permute-done((bf16[128,1280]{1,0:T(8,128)(2,1)S(1)}, bf16[128,1280]{1,0:T(8,128)(2,1)}, u32[]{:S(2)}, u32[]{:S(2)}) %collective-permute-start.5) | collective-permute-done | bytes 327712 | tf_op jit(solution)/shard_map/ppermute | solution.py:694
  28.6 1.7 collective-permute-start.11
  30.7 1.6 collective-permute-start.14
  33.1 4.7 %project.2 = (bf16[8,128,1280]{2,1,0:T(8,128)(2,1)}, bf16[5,80,128]{2,1,0:T(8,128)(2,1)}, bf16[5,160,128]{2,1,0:T(8,128)(2,1)}, bf16[5,240,128]{2,1,0:T(8,128)(2,1)}, bf16[5,160,128]{2,1,0:T(8,128)(2,1)}) custom-call(s32[4]{0:T(128)} %pad_add_fusion.1.refs_0_.refs_1_, bf16[128,1280]{1,0:T(8,128)(2,1)} %bitcast.33, bf16[128,1280]{1,0:T(8,128)(2,1)} %copy-done.53, ...), custom_call_target="tpu_custom_call" | custom-call | flops 3449999872 | bytes 1 | tf_op jit(solution)/shard_map/project/pallas_call | solution.py:76
  40.8 1.6 collective-permute-start.13
  43.7 1.6 collective-permute-start.7
  46.2 1.5 collective-permute-done.12.refs_3_
  48.4 4.7 %project.3 = (bf16[8,128,1280]{2,1,0:T(8,128)(2,1)}, bf16[3,80,128]{2,1,0:T(8,128)(2,1)}, bf16[3,160,128]{2,1,0:T(8,128)(2,1)}, bf16[3,240,128]{2,1,0:T(8,128)(2...) custom-call(s32[4]{0:T(128)} %pad_add_fusion.1.refs_0_.refs_1_, ...), custom_call_target="tpu_custom_call", output_to_operand_aliasing={{0}: (11, {})} | custom-call | flops 3449999872 | bytes 1 | tf_op jit(solution)/shard_map/project/pallas_call | solution.py:76
  54.4 1.6 collective-permute-start.17
  57.1 1.7 copy-done
  58.8 1.7 copy-done.1
  61.2 1.8 collective-permute-done.15.refs_13_.refs_3_
  65.0 19.0 %attention_forward.1 = (bf16[16,80,128]{2,1,0:T(8,128)(2,1)}, bf16[4,80,512]{2,1,0:T(8,128)(2,1)}, bf16[8,80,512]{2,1,0:T(8,128)(2,1)}, bf16[8,512,80]{2,1,0:T(8...) custom-call(s32[16,2]{1,0:T(8,128)} %gather_fusion, s32[16,2]{1,0:T(8,128)} %gather_fusion, ...), custom_call_target="tpu_custom_call" | custom-call | flops 23000000512 | bytes 1 | tf_op jit(solution)/shard_map/attention_forward/pallas_call | solution.py:76
  87.2 4.0 %all-to-all-start = ((bf16[16,80,128]{2,1,0:T(8,128)(2,1)}), bf16[16,80,128]{2,1,0:T(8,128)(2,1)S(1)}, u32[]{:S(2)}, u32[]{:S(2)}) async-start(bf16[16,80,128]{2,1,0:T(8,128)(2,1)} %copy-done.4), calls=%async_computation | async-start | bytes 655360 | tf_op jit(solution)/shard_map/all_to_all | solution.py:713
  91.2 9.2 %collective-permute-done.21.refs_1_ = bf16[320,1280]{1,0:T(8,128)(2,1)} collective-permute-done((bf16[320,1280]{1,0:T(8,128)(2,1)}, bf16[320,1280]{1,0:T(8,128)(2,1)}, u32[]{:S(2)}, u32[]{:S(2)}) %collective-permute-start.21) | collective-permute-done | bytes 819232 | tf_op jit(solution)/shard_map/ppermute | solution.py:694
  100.4 1.8 all-to-all-done
  106.1 10.9 %row_part.1 = (bf16[128,1280]{1,0:T(8,128)(2,1)}, f32[128,1280]{1,0:T(8,128)}, bf16[1280,128]{1,0:T(8,128)(2,1)}, bf16[3776,128]{1,0:T(8,128)(2,1)}, bf16[3776,1...) custom-call(s32[4]{0:T(128)} %pad_add_fusion.1.refs_0_.refs_1_, bf16[1280,128]{1,0:T(8,128)(2,1)} %bitcast.25, ...), custom_call_target="tpu_custom_call" | custom-call | flops 11500000256 | bytes 1 | tf_op jit(solution)/shard_map/row_part/pallas_call | solution.py:76
  118.7 4.4 %all-to-all-start.1 = ((bf16[16,80,128]{2,1,0:T(8,128)(2,1)}), bf16[16,80,128]{2,1,0:T(8,128)(2,1)}, u32[]{:S(2)}, u32[]{:S(2)}) async-start(bf16[16,80,128]{2,1,0:T(8,128)(2,1)} %bitcast.23), calls=%async_computation.1 | async-start | bytes 655360 | tf_op jit(solution)/shard_map/all_to_all | solution.py:713
  126.6 7.6 %all-to-all-done.1.refs_5_ = bf16[16,80,128]{2,1,0:T(8,128)(2,1)} async-done(((bf16[16,80,128]{2,1,0:T(8,128)(2,1)}), bf16[16,80,128]{2,1,0:T(8,128)(2,1)}, u32[]{:S(2)}, u32[]{:S(2)}) %all-to-all-start.1) | async-done | bytes 327712 | tf_op jit(solution)/shard_map/all_to_all | solution.py:713
  134.2 24.4 %attention_backward.1 = (f32[8,160,256]{2,1,0:T(8,128)}, bf16[8,160,256]{2,1,0:T(8,128)(2,1)}, bf16[16,80,128]{2,1,0:T(8,128)(2,1)}, f32[80,512]{1,0:T(8,128)}) custom-call(s32[16,2]{1,0:T(8,128)} %copy-done.16, s32[8]{0:T(128)} %constant.102.clone.refs_1_, s32[8]{0:T(128)} %constant.103.clone.refs_2_, s32[4,1,512]{2,1,0:T(1,128)} %constant.99.clone.refs_5_.refs_3_, ...), custom_call_target="tpu_custom_call" | custom-call | flops 28750000128 | bytes 1 | tf_op jit(solution)/shard_map/attention_backward/pallas_call | solution.py:76
  163.0 3.3 %pooled_grads.1.refs_1_ = bf16[5,256,1280]{2,1,0:T(8,128)(2,1)S(1)} custom-call(bf16[3776,128]{1,0:T(8,128)(2,1)S(1)} %copy-done.44, bf16[3776,128]{1,0:T(8,128)(2,1)} %get-tuple-element.113.refs_1_, bf16[3776,128]{1,0:T(8,128)(2,1)} %get-tuple-element.114.refs_2_, bf16[1200,128]{1,0:T(8,128)(2,1)} %get-tuple-element.115.refs_3_, ...), custom_call_target="tpu_custom_call" | custom-call | flops 3449999872 | bytes 1 | tf_op jit(solution)/shard_map/pooled_grads/pallas_call | solution.py:76
  168.3 5.8 %collective-permute-done.34.refs_2_ = bf16[256,640]{1,0:T(8,128)(2,1)S(1)} collective-permute-done((bf16[256,640]{1,0:T(8,128)(2,1)S(1)}, bf16[256,640]{1,0:T(8,128)(2,1)S(1)}, u32[]{:S(2)}, u32[]{:S(2)}) %collective-permute-start.34) | collective-permute-done | bytes 327712 | tf_op jit(solution)/shard_map/ppermute | solution.py:682
  175.4 2.7 collective-permute-done.26.refs_4_
  178.1 1.9 join.1
  180.1 4.5 %qkv_grads.1 = (f32[256,640]{1,0:T(8,128)S(1)}, bf16[256,640]{1,0:T(8,128)(2,1)S(1)}) custom-call(s32[16]{0:T(128)S(1)} %fusion.1.refs_0_, s32[4]{0:T(128)S(1)} %copy-done.26, bf16[16,240,128]{2,1,0:T(8,128)(2,1)S(1)} %get-tuple-element.117.refs_2_.refs_1_, f32[80,512]{1,0:T(8,128)S(1)} %copy-done.49, bf16[8,128,1280]{2,1,0:T(8,128)(2,1)S(1)} %copy-done.1, ...), custom_call_target="tpu_custom_call" | custom-call | flops 5405000192 | bytes 1 | tf_op jit(solution)/shard_map/qkv_grads/pallas_call | solution.py:76
  187.6 2.5 products.1.refs_1_
  190.7 4.1 %collective-permute-done.38.refs_1_ = bf16[256,640]{1,0:T(8,128)(2,1)S(1)} collective-permute-done((bf16[256,640]{1,0:T(8,128)(2,1)S(1)}, bf16[256,640]{1,0:T(8,128)(2,1)S(1)}, u32[]{:S(2)}, u32[]{:S(2)}) %collective-permute-start.38) | collective-permute-done | bytes 327712 | tf_op jit(solution)/shard_map/ppermute | solution.py:694
  195.0 2.5 collective-permute-done.40.refs_2_
  201.3 7.6 %collective-permute-done.42.refs_2_ = bf16[256,1280]{1,0:T(8,128)(2,1)S(1)} collective-permute-done((bf16[256,1280]{1,0:T(8,128)(2,1)S(1)}, bf16[256,1280]{1,0:T(8,128)(2,1)S(1)}, u32[]{:S(2)}, u32[]{:S(2)}) %collective-permute-start.42) | collective-permute-done | bytes 655392 | tf_op jit(solution)/shard_map/ppermute | solution.py:682
  208.9 7.0 %collective-permute-done.45.refs_2_ = bf16[512,640]{1,0:T(8,128)(2,1)S(1)} collective-permute-done((bf16[512,640]{1,0:T(8,128)(2,1)S(1)}, bf16[512,640]{1,0:T(8,128)(2,1)S(1)}, u32[]{:S(2)}, u32[]{:S(2)}) %collective-permute-start.45) | collective-permute-done | bytes 655392 | tf_op jit(solution)/shard_map/ppermute | solution.py:682
  216.6 2.8 collective-permute-done.37.refs_2_
  222.9 3.7 %collective-permute-done.46.refs_4_.refs_3_ = bf16[512,640]{1,0:T(8,128)(2,1)} collective-permute-done((bf16[512,640]{1,0:T(8,128)(2,1)S(1)}, bf16[512,640]{1,0:T(8,128)(2,1)}, u32[]{:S(2)}, u32[]{:S(2)}) %collective-permute-start.46) | collective-permute-done | bytes 655392 | tf_op jit(solution)/shard_map/ppermute | solution.py:682
  227.3 6.2 %collective-permute-done.41.refs_2_ = bf16[256,1280]{1,0:T(8,128)(2,1)S(1)} collective-permute-done((bf16[256,1280]{1,0:T(8,128)(2,1)S(1)}, bf16[256,1280]{1,0:T(8,128)(2,1)S(1)}, u32[]{:S(2)}, u32[]{:S(2)}) %collective-permute-start.41) | collective-permute-done | bytes 655392 | tf_op jit(solution)/shard_map/ppermute | solution.py:682
  236.2 11.3 %collective-permute-done.53.refs_4_ = bf16[512,640]{1,0:T(8,128)(2,1)S(1)} collective-permute-done((bf16[512,640]{1,0:T(8,128)(2,1)}, bf16[512,640]{1,0:T(8,128)(2,1)S(1)}, u32[]{:S(2)}, u32[]{:S(2)}) %collective-permute-start.53) | collective-permute-done | bytes 655392 | tf_op jit(solution)/shard_map/ppermute | solution.py:682
  249.6 5.1 %collective-permute-done.44.refs_2_ = bf16[256,1280]{1,0:T(8,128)(2,1)} collective-permute-done((bf16[256,1280]{1,0:T(8,128)(2,1)}, bf16[256,1280]{1,0:T(8,128)(2,1)}, u32[]{:S(2)}, u32[]{:S(2)}) %collective-permute-start.44) | collective-permute-done | bytes 655392 | tf_op jit(solution)/shard_map/ppermute | solution.py:682
  254.7 1.9 copy-done.41
  256.6 2.6 reduce_step.15
  260.4 4.8 %collective-permute-done.50.refs_3_.refs_7_ = bf16[256,1280]{1,0:T(8,128)(2,1)} collective-permute-done((bf16[256,1280]{1,0:T(8,128)(2,1)S(1)}, bf16[256,1280]{1,0:T(8,128)(2,1)}, u32[]{:S(2)}, u32[]{:S(2)}) %collective-permute-start.50) | collective-permute-done | bytes 655392 | tf_op jit(solution)/shard_map/ppermute | solution.py:682
  266.4 5.8 %collective-permute-done.47.refs_2_ = bf16[256,1280]{1,0:T(8,128)(2,1)} collective-permute-done((bf16[256,1280]{1,0:T(8,128)(2,1)}, bf16[256,1280]{1,0:T(8,128)(2,1)}, u32[]{:S(2)}, u32[]{:S(2)}) %collective-permute-start.47) | collective-permute-done | bytes 655392 | tf_op jit(solution)/shard_map/ppermute | solution.py:682
  272.3 6.8 %qkv_place.1 = (f32[640,1280]{1,0:T(8,128)}, f32[640,1280]{1,0:T(8,128)}, f32[640,1280]{1,0:T(8,128)}, f32[640]{0:T(1024)}, f32[40]{0:T(128)}) custom-call(s32[4]{0:T(128)S(1)} %copy-done.26, bf16[512,640]{1,0:T(8,128)(2,1)S(1)} %chip_pack.1.refs_3_.refs_4_.refs_1_, bf16[512,640]{1,0:T(8,128)(2,1)S(1)} %collective-permute-done.45.refs_2_, ...), custom_call_target="tpu_custom_call" | custom-call | flops 6899999744 | bytes 1 | tf_op jit(solution)/shard_map/qkv_place/pallas_call | solution.py:76
  280.0 4.3 %rows_place.2 = (f32[640,1280]{1,0:T(8,128)}, f32[640,1280]{1,0:T(8,128)}, f32[640,1280]{1,0:T(8,128)}, f32[640,128]{1,0:T(8,128)S(1)}, f32[8,128]{1,0:T(8,128)S(1)}) custom-call(s32[4]{0:T(128)S(1)} %copy-done.26, bf16[256,1280]{1,0:T(8,128)(2,1)S(1)} %reduce_end.1.refs_3_.refs_1_, bf16[256,1280]{1,0:T(8,128)(2,1)S(1)} %copy-done.29, ...), custom_call_target="tpu_custom_call" | custom-call | flops 4600000000 | bytes 1 | tf_op jit(solution)/shard_map/rows_place/pallas_call | solution.py:76
  284.4 3.0 %inputs_grad.1.refs_2_ = bf16[128,1280]{1,0:T(8,128)(2,1)} custom-call(s32[4]{0:T(128)S(1)} %copy-done.26, bf16[5,256,1280]{2,1,0:T(8,128)(2,1)S(1)} %copy-done.42, bf16[256,1280]{1,0:T(8,128)(2,1)} %collective-permute-done.47.refs_2_, bf16[256,1280]{1,0:T(8,128)(2,1)S(1)} %collective-permute-done.48.refs_3_, bf16[128,1280]{1,0:T(8,128)(2,1)S(1)} %bitcast.35, ...), custom_call_target="tpu_custom_call" | custom-call | flops 2300000000 | bytes 1 | tf_op jit(solution)/shard_map/inputs_grad/pallas_call | solution.py:76
  290.2 3.4 %rows_place.3 = (f32[640,1280]{1,0:T(8,128)}, f32[640,1280]{1,0:T(8,128)}, f32[640,1280]{1,0:T(8,128)}, f32[640]{0:T(1024)}, f32[2]{0:T(128)}) custom-call(s32[4]{0:T(128)S(1)} %copy-done.26, bf16[256,1280]{1,0:T(8,128)(2,1)S(1)} %collective-permute-done.59.refs_1_, ...), custom_call_target="tpu_custom_call", output_to_operand_aliasing={{0}: (9, {}), {1}: (10, {}), {2}: (11, {})} | custom-call | flops 3449999872 | bytes 1 | tf_op jit(solution)/shard_map/rows_place/pallas_call | solution.py:76
  (248 shorter events, 62.8 us)
Async XLA Ops:
  0.6 11.0 %collective-permute-start.1 = (bf16[128,1280]{1,0:T(8,128)(2,1)}, bf16[128,1280]{1,0:T(8,128)(2,1)S(1)}, u32[]{:S(2)}, u32[]{:S(2)}) collective-permute-start(bf16[128,1280]{1,0:T(8,128)(2,1)} %bitcast.31), channel_id=1, source_target_pairs={{0,4},{2,6},{8,0},{10,2},{16,8},{18,10},{24,16},{26,18},{28,24},{3... | collective-permute-start | bytes 983048 | tf_op jit(solution)/shard_map/ppermute | solution.py:670
  3.7 9.7 %collective-permute-start = (bf16[128,1280]{1,0:T(8,128)(2,1)}, bf16[128,1280]{1,0:T(8,128)(2,1)S(1)}, u32[]{:S(2)}, u32[]{:S(2)}) collective-permute-start(bf16[128,1280]{1,0:T(8,128)(2,1)} %bitcast.32), channel_id=1, source_target_pairs={{0,8},{2,10},{8,16},{10,18},{16,24},{18,26},{24,28},{26,30},{28,20... | collective-permute-start | bytes 983048 | tf_op jit(solution)/shard_map/ppermute | solution.py:670
  7.6 10.8 %collective-permute-start.4 = (bf16[256,640]{1,0:T(8,128)(2,1)}, bf16[256,640]{1,0:T(8,128)(2,1)S(1)}, u32[]{:S(2)}, u32[]{:S(2)}) collective-permute-start(bf16[256,640]{1,0:T(8,128)(2,1)} %slab.1.refs_1_.refs_2_), channel_id=1, source_target_pairs={{0,1},{1,0},{2,3},{3,2},{4,5},{5,4},{6,7},{7,6},{8,9},{9,8},{10,11... | collective-permute-start | bytes 983048 | tf_op jit(solution)/shard_map/ppermute | solution.py:694
  10.5 13.6 %collective-permute-start.5 = (bf16[128,1280]{1,0:T(8,128)(2,1)S(1)}, bf16[128,1280]{1,0:T(8,128)(2,1)}, u32[]{:S(2)}, u32[]{:S(2)}) collective-permute-start(bf16[128,1280]{1,0:T(8,128)(2,1)S(1)} %constant_dynamic-slice_fusion.4), channel_id=1, source_target_pairs={{0,1},{1,0},{2,3},{3,2},{4,5},{5,4},{6,7},{7,6},{8,9},{9,8},{10,11... | collective-permute-start | bytes 983048 | tf_op jit(solution)/shard_map/ppermute | solution.py:694
  11.6 12.5 %collective-permute-start.3 = (bf16[128,1280]{1,0:T(8,128)(2,1)S(1)}, bf16[128,1280]{1,0:T(8,128)(2,1)S(1)}, u32[]{:S(2)}, u32[]{:S(2)}) collective-permute-start(bf16[128,1280]{1,0:T(8,128)(2,1)S(1)} %collective-permute-done.1.refs_3_), channel_id=1, source_target_pairs={{0,4},{2,6},{8,0},{10,2},{16,8},{18,10},{24,16},{26,18},{28,24},{3... | collective-permute-start | bytes 983048 | tf_op jit(solution)/shard_map/ppermute | solution.py:670
  13.3 10.8 %collective-permute-start.2 = (bf16[128,1280]{1,0:T(8,128)(2,1)S(1)}, bf16[128,1280]{1,0:T(8,128)(2,1)S(1)}, u32[]{:S(2)}, u32[]{:S(2)}) collective-permute-start(bf16[128,1280]{1,0:T(8,128)(2,1)S(1)} %collective-permute-done.refs_2_), channel_id=1, source_target_pairs={{0,8},{2,10},{8,16},{10,18},{16,24},{18,26},{24,28},{26,30},{28,20... | collective-permute-start | bytes 983048 | tf_op jit(solution)/shard_map/ppermute | solution.py:670
  28.6 9.9 %collective-permute-start.11 = (bf16[128,1280]{1,0:T(8,128)(2,1)S(1)}, bf16[128,1280]{1,0:T(8,128)(2,1)S(1)}, u32[]{:S(2)}, u32[]{:S(2)}) collective-permute-start(bf16[128,1280]{1,0:T(8,128)(2,1)S(1)} %collective-permute-done.3.refs_4_.refs_5_), channel_id=1, source_target_pairs={{0,4},{2,6},{8,0},{10,2},{16,8},{18,10},{24,16},{26,18},{28,24},{3... | collective-permute-start | bytes 983048 | tf_op jit(solution)/shard_map/ppermute | solution.py:670
  30.3 9.6 %collective-permute-start.10 = (bf16[128,1280]{1,0:T(8,128)(2,1)S(1)}, bf16[128,1280]{1,0:T(8,128)(2,1)S(1)}, u32[]{:S(2)}, u32[]{:S(2)}) collective-permute-start(bf16[128,1280]{1,0:T(8,128)(2,1)S(1)} %collective-permute-done.2.refs_3_.refs_4_), channel_id=1, source_target_pairs={{0,8},{2,10},{8,16},{10,18},{16,24},{18,26},{24,28},{26,30},{28,20... | collective-permute-start | bytes 983048 | tf_op jit(solution)/shard_map/ppermute | solution.py:670
  30.7 14.6 %collective-permute-start.14 = (bf16[192,1280]{1,0:T(8,128)(2,1)S(1)}, bf16[192,1280]{1,0:T(8,128)(2,1)}, u32[]{:S(2)}, u32[]{:S(2)}) collective-permute-start(bf16[192,1280]{1,0:T(8,128)(2,1)S(1)} %gate.13), channel_id=1, source_target_pairs={{0,1},{1,0},{2,3},{3,2},{4,5},{5,4},{6,7},{7,6},{8,9},{9,8},{10,11... | collective-permute-start | bytes 1474568 | tf_op jit(solution)/shard_map/ppermute | solution.py:694
  43.6 12.4 %collective-permute-start.9 = (bf16[5,160,128]{2,1,0:T(8,128)(2,1)}, bf16[5,160,128]{2,1,0:T(8,128)(2,1)S(1)}, u32[]{:S(2)}, u32[]{:S(2)}) collective-permute-start(bf16[5,160,128]{2,1,0:T(8,128)(2,1)} %get-tuple-element.82), channel_id=1, source_target_pairs={{0,3},{1,2},{2,1},{3,0},{4,7},{5,6},{6,5},{7,4},{8,11},{9,10},{10,... | collective-permute-start | bytes 614408 | tf_op jit(solution)/shard_map/ppermute | solution.py:691
  43.7 16.9 %collective-permute-start.7 = (bf16[5,160,128]{2,1,0:T(8,128)(2,1)}, bf16[5,160,128]{2,1,0:T(8,128)(2,1)S(1)}, u32[]{:S(2)}, u32[]{:S(2)}) collective-permute-start(bf16[5,160,128]{2,1,0:T(8,128)(2,1)} %get-tuple-element.80.refs_7_), channel_id=1, source_target_pairs={{0,1},{1,0},{2,3},{3,2},{4,5},{5,4},{6,7},{7,6},{8,9},{9,8},{10,11... | collective-permute-start | bytes 614408 | tf_op jit(solution)/shard_map/ppermute | solution.py:694
  45.2 19.2 %collective-permute-start.8 = (bf16[5,240,128]{2,1,0:T(8,128)(2,1)}, bf16[5,240,128]{2,1,0:T(8,128)(2,1)}, u32[]{:S(2)}, u32[]{:S(2)}) collective-permute-start(bf16[5,240,128]{2,1,0:T(8,128)(2,1)} %get-tuple-element.81), channel_id=1, source_target_pairs={{0,2},{2,0},{4,6},{6,4},{8,10},{10,8},{12,14},{14,12},{16,18},{18,... | collective-permute-start | bytes 921608 | tf_op jit(solution)/shard_map/ppermute | solution.py:685
  53.1 11.8 %collective-permute-start.16 = (bf16[3,240,128]{2,1,0:T(8,128)(2,1)}, bf16[3,240,128]{2,1,0:T(8,128)(2,1)}, u32[]{:S(2)}, u32[]{:S(2)}) collective-permute-start(bf16[3,240,128]{2,1,0:T(8,128)(2,1)} %get-tuple-element.88), channel_id=1, source_target_pairs={{0,2},{2,0},{4,6},{6,4},{8,10},{10,8},{12,14},{14,12},{16,18},{18,... | collective-permute-start | bytes 552968 | tf_op jit(solution)/shard_map/ppermute | solution.py:685
  60.6 23.4 %collective-permute-start.18 = (bf16[128,1280]{1,0:T(8,128)(2,1)}, bf16[128,1280]{1,0:T(8,128)(2,1)S(1)}, u32[]{:S(2)}, u32[]{:S(2)}) collective-permute-start(bf16[128,1280]{1,0:T(8,128)(2,1)} %gate.14.refs_6_), channel_id=1, source_target_pairs={{0,2},{2,0},{4,6},{6,4},{8,10},{10,8},{12,14},{14,12},{16,18},{18,... | collective-permute-start | bytes 983048 | tf_op jit(solution)/shard_map/ppermute | solution.py:685
  60.7 23.3 %collective-permute-start.19 = (bf16[192,1280]{1,0:T(8,128)(2,1)}, bf16[192,1280]{1,0:T(8,128)(2,1)S(1)}, u32[]{:S(2)}, u32[]{:S(2)}) collective-permute-start(bf16[192,1280]{1,0:T(8,128)(2,1)} %gate.15.refs_8_), channel_id=1, source_target_pairs={{0,2},{2,0},{4,6},{6,4},{8,10},{10,8},{12,14},{14,12},{16,18},{18,... | collective-permute-start | bytes 1474568 | tf_op jit(solution)/shard_map/ppermute | solution.py:685
  62.9 28.3 %collective-permute-start.20 = (bf16[320,1280]{1,0:T(8,128)(2,1)}, bf16[320,1280]{1,0:T(8,128)(2,1)}, u32[]{:S(2)}, u32[]{:S(2)}) collective-permute-start(bf16[320,1280]{1,0:T(8,128)(2,1)} %gate.17), channel_id=1, source_target_pairs={{0,1},{1,0},{2,3},{3,2},{4,5},{5,4},{6,7},{7,6},{8,9},{9,8},{10,11... | collective-permute-start | bytes 2457608 | tf_op jit(solution)/shard_map/ppermute | solution.py:694
  64.4 36.0 %collective-permute-start.21 = (bf16[320,1280]{1,0:T(8,128)(2,1)}, bf16[320,1280]{1,0:T(8,128)(2,1)}, u32[]{:S(2)}, u32[]{:S(2)}) collective-permute-start(bf16[320,1280]{1,0:T(8,128)(2,1)} %gate.18), channel_id=1, source_target_pairs={{0,1},{1,0},{2,3},{3,2},{4,5},{5,4},{6,7},{7,6},{8,9},{9,8},{10,11... | collective-permute-start | bytes 2457608 | tf_op jit(solution)/shard_map/ppermute | solution.py:694
  87.2 15.1 %all-to-all-start = ((bf16[16,80,128]{2,1,0:T(8,128)(2,1)}), bf16[16,80,128]{2,1,0:T(8,128)(2,1)S(1)}, u32[]{:S(2)}, u32[]{:S(2)}) async-start(bf16[16,80,128]{2,1,0:T(8,128)(2,1)} %copy-done.4), calls=%async_computation | async-start | bytes 655360 | tf_op jit(solution)/shard_map/all_to_all | solution.py:713
  103.8 13.2 %collective-permute-start.24 = (bf16[128,1280]{1,0:T(8,128)(2,1)S(1)}, bf16[128,1280]{1,0:T(8,128)(2,1)S(1)}, u32[]{:S(2)}, u32[]{:S(2)}) collective-permute-start(bf16[128,1280]{1,0:T(8,128)(2,1)S(1)} %gate.20), channel_id=1, source_target_pairs={{0,1},{1,0},{2,3},{3,2},{4,5},{5,4},{6,7},{7,6},{8,9},{9,8},{10,11... | collective-permute-start | bytes 983048 | tf_op jit(solution)/shard_map/ppermute | solution.py:694
  118.7 15.5 %all-to-all-start.1 = ((bf16[16,80,128]{2,1,0:T(8,128)(2,1)}), bf16[16,80,128]{2,1,0:T(8,128)(2,1)}, u32[]{:S(2)}, u32[]{:S(2)}) async-start(bf16[16,80,128]{2,1,0:T(8,128)(2,1)} %bitcast.23), calls=%async_computation.1 | async-start | bytes 655360 | tf_op jit(solution)/shard_map/all_to_all | solution.py:713
  123.3 35.3 %collective-permute-start.31 = (bf16[8,128,1280]{2,1,0:T(8,128)(2,1)S(1)}, bf16[8,128,1280]{2,1,0:T(8,128)(2,1)}, u32[]{:S(2)}, u32[]{:S(2)}) collective-permute-start(bf16[8,128,1280]{2,1,0:T(8,128)(2,1)S(1)} %copy-done.1), channel_id=1, source_target_pairs={{0,2},{2,0},{4,6},{6,4},{8,10},{10,8},{12,14},{14,12},{16,18},{18,... | collective-permute-start | bytes 7864328 | tf_op jit(solution)/shard_map/ppermute | solution.py:685
  123.7 34.9 %collective-permute-start.30 = (bf16[128,1280]{1,0:T(8,128)(2,1)S(1)}, bf16[128,1280]{1,0:T(8,128)(2,1)S(1)}, u32[]{:S(2)}, u32[]{:S(2)}) collective-permute-start(bf16[128,1280]{1,0:T(8,128)(2,1)S(1)} %get-tuple-element.112.refs_7_), channel_id=1, source_target_pairs={{0,2},{2,0},{4,6},{6,4},{8,10},{10,8},{12,14},{14,12},{16,18},{18,... | collective-permute-start | bytes 983048 | tf_op jit(solution)/shard_map/ppermute | solution.py:685
  123.9 34.8 %collective-permute-start.27 = (bf16[3776,128]{1,0:T(8,128)(2,1)}, bf16[3776,128]{1,0:T(8,128)(2,1)}, u32[]{:S(2)}, u32[]{:S(2)}) collective-permute-start(bf16[3776,128]{1,0:T(8,128)(2,1)} %get-tuple-element.110), channel_id=1, source_target_pairs={{0,1},{1,0},{2,3},{3,2},{4,5},{5,4},{6,7},{7,6},{8,9},{9,8},{10,11... | collective-permute-start | bytes 2899976 | tf_op jit(solution)/shard_map/ppermute | solution.py:694
  125.3 33.3 %collective-permute-start.28 = (bf16[3776,128]{1,0:T(8,128)(2,1)}, bf16[3776,128]{1,0:T(8,128)(2,1)}, u32[]{:S(2)}, u32[]{:S(2)}) collective-permute-start(bf16[3776,128]{1,0:T(8,128)(2,1)} %get-tuple-element.111), channel_id=1, source_target_pairs={{0,2},{2,0},{4,6},{6,4},{8,10},{10,8},{12,14},{14,12},{16,18},{18,... | collective-permute-start | bytes 2899976 | tf_op jit(solution)/shard_map/ppermute | solution.py:685
  125.4 33.3 %collective-permute-start.29 = (bf16[1200,128]{1,0:T(8,128)(2,1)}, bf16[1200,128]{1,0:T(8,128)(2,1)}, u32[]{:S(2)}, u32[]{:S(2)}) collective-permute-start(bf16[1200,128]{1,0:T(8,128)(2,1)} %collective-permute-done.25.refs_12_), channel_id=1, source_target_pairs={{0,1},{1,0},{2,3},{3,2},{4,5},{5,4},{6,7},{7,6},{8,9},{9,8},{10,11... | collective-permute-start | bytes 921608 | tf_op jit(solution)/shard_map/ppermute | solution.py:694
  161.2 16.9 %collective-permute-start.26 = (bf16[8,160,256]{2,1,0:T(8,128)(2,1)S(1)}, bf16[8,160,256]{2,1,0:T(8,128)(2,1)S(1)}, u32[]{:S(2)}, u32[]{:S(2)}) collective-permute-start(bf16[8,160,256]{2,1,0:T(8,128)(2,1)S(1)} %copy-done.51), channel_id=1, source_target_pairs={{0,1},{1,0},{2,3},{3,2},{4,5},{5,4},{6,7},{7,6},{8,9},{9,8},{10,11... | collective-permute-start | bytes 1966088 | tf_op jit(solution)/shard_map/ppermute | solution.py:694
  174.7 11.4 %collective-permute-start.36 = (bf16[256,1280]{1,0:T(8,128)(2,1)S(1)}, bf16[256,1280]{1,0:T(8,128)(2,1)S(1)}, u32[]{:S(2)}, u32[]{:S(2)}) collective-permute-start(bf16[256,1280]{1,0:T(8,128)(2,1)S(1)} %reduce_step.9.refs_5_), channel_id=1, source_target_pairs={{0,8},{2,6},{8,16},{10,2},{16,24},{18,10},{24,28},{26,18},{28,20},... | collective-permute-start | bytes 1966088 | tf_op jit(solution)/shard_map/ppermute | solution.py:682
  184.6 10.2 %collective-permute-start.38 = (bf16[256,640]{1,0:T(8,128)(2,1)S(1)}, bf16[256,640]{1,0:T(8,128)(2,1)S(1)}, u32[]{:S(2)}, u32[]{:S(2)}) collective-permute-start(bf16[256,640]{1,0:T(8,128)(2,1)S(1)} %get-tuple-element.122), channel_id=1, source_target_pairs={{0,1},{1,0},{2,3},{3,2},{4,5},{5,4},{6,7},{7,6},{8,9},{9,8},{10,11... | collective-permute-start | bytes 983048 | tf_op jit(solution)/shard_map/ppermute | solution.py:694
  186.9 10.6 %collective-permute-start.40 = (bf16[256,1280]{1,0:T(8,128)(2,1)S(1)}, bf16[256,1280]{1,0:T(8,128)(2,1)S(1)}, u32[]{:S(2)}, u32[]{:S(2)}) collective-permute-start(bf16[256,1280]{1,0:T(8,128)(2,1)S(1)} %reduce_step.10.refs_5_), channel_id=1, source_target_pairs={{0,8},{2,6},{8,16},{10,2},{16,24},{18,10},{24,28},{26,18},{28,20},... | collective-permute-start | bytes 1966088 | tf_op jit(solution)/shard_map/ppermute | solution.py:682
  198.2 10.6 %collective-permute-start.42 = (bf16[256,1280]{1,0:T(8,128)(2,1)S(1)}, bf16[256,1280]{1,0:T(8,128)(2,1)S(1)}, u32[]{:S(2)}, u32[]{:S(2)}) collective-permute-start(bf16[256,1280]{1,0:T(8,128)(2,1)S(1)} %reduce_step.12.refs_3_), channel_id=1, source_target_pairs={{0,8},{2,6},{8,16},{10,2},{16,24},{18,10},{24,28},{26,18},{28,20},... | collective-permute-start | bytes 1966088 | tf_op jit(solution)/shard_map/ppermute | solution.py:682
  199.6 16.3 %collective-permute-start.45 = (bf16[512,640]{1,0:T(8,128)(2,1)S(1)}, bf16[512,640]{1,0:T(8,128)(2,1)S(1)}, u32[]{:S(2)}, u32[]{:S(2)}) collective-permute-start(bf16[512,640]{1,0:T(8,128)(2,1)S(1)} %chip_pack.1.refs_3_.refs_4_.refs_1_), channel_id=1, source_target_pairs={{0,8},{2,6},{8,16},{10,2},{16,24},{18,10},{24,28},{26,18},{28,20},... | collective-permute-start | bytes 1966088 | tf_op jit(solution)/shard_map/ppermute | solution.py:682
  200.9 18.5 %collective-permute-start.37 = (bf16[256,640]{1,0:T(8,128)(2,1)S(1)}, bf16[256,640]{1,0:T(8,128)(2,1)S(1)}, u32[]{:S(2)}, u32[]{:S(2)}) collective-permute-start(bf16[256,640]{1,0:T(8,128)(2,1)S(1)} %reduce_step.11.refs_3_), channel_id=1, source_target_pairs={{0,8},{2,6},{8,16},{10,2},{16,24},{18,10},{24,28},{26,18},{28,20},... | collective-permute-start | bytes 983048 | tf_op jit(solution)/shard_map/ppermute | solution.py:682
  208.9 11.9 %collective-permute-start.43 = (bf16[256,1280]{1,0:T(8,128)(2,1)S(1)}, bf16[256,1280]{1,0:T(8,128)(2,1)S(1)}, u32[]{:S(2)}, u32[]{:S(2)}) collective-permute-start(bf16[256,1280]{1,0:T(8,128)(2,1)S(1)} %collective-permute-done.42.refs_2_), channel_id=1, source_target_pairs={{0,2},{2,0},{4,6},{6,4},{8,10},{10,8},{12,14},{14,12},{16,18},{18,... | collective-permute-start | bytes 1966088 | tf_op jit(solution)/shard_map/ppermute | solution.py:685
  215.9 10.7 %collective-permute-start.46 = (bf16[512,640]{1,0:T(8,128)(2,1)S(1)}, bf16[512,640]{1,0:T(8,128)(2,1)}, u32[]{:S(2)}, u32[]{:S(2)}) collective-permute-start(bf16[512,640]{1,0:T(8,128)(2,1)S(1)} %collective-permute-done.45.refs_2_), channel_id=1, source_target_pairs={{0,8},{2,6},{8,16},{10,2},{16,24},{18,10},{24,28},{26,18},{28,20},... | collective-permute-start | bytes 1966088 | tf_op jit(solution)/shard_map/ppermute | solution.py:682
  220.1 13.4 %collective-permute-start.41 = (bf16[256,1280]{1,0:T(8,128)(2,1)S(1)}, bf16[256,1280]{1,0:T(8,128)(2,1)S(1)}, u32[]{:S(2)}, u32[]{:S(2)}) collective-permute-start(bf16[256,1280]{1,0:T(8,128)(2,1)S(1)} %reduce_step.13), channel_id=1, source_target_pairs={{0,8},{2,6},{8,16},{10,2},{16,24},{18,10},{24,28},{26,18},{28,20},... | collective-permute-start | bytes 1966088 | tf_op jit(solution)/shard_map/ppermute | solution.py:682
  221.6 26.7 %collective-permute-start.49 = (bf16[256,1280]{1,0:T(8,128)(2,1)S(1)}, bf16[256,1280]{1,0:T(8,128)(2,1)S(1)}, u32[]{:S(2)}, u32[]{:S(2)}) collective-permute-start(bf16[256,1280]{1,0:T(8,128)(2,1)S(1)} %reduce_end.1.refs_3_.refs_1_), channel_id=1, source_target_pairs={{0,8},{2,6},{8,16},{10,2},{16,24},{18,10},{24,28},{26,18},{28,20},... | collective-permute-start | bytes 1966088 | tf_op jit(solution)/shard_map/ppermute | solution.py:682
  226.6 21.0 %collective-permute-start.53 = (bf16[512,640]{1,0:T(8,128)(2,1)}, bf16[512,640]{1,0:T(8,128)(2,1)S(1)}, u32[]{:S(2)}, u32[]{:S(2)}) collective-permute-start(bf16[512,640]{1,0:T(8,128)(2,1)} %collective-permute-done.46.refs_4_.refs_3_), channel_id=1, source_target_pairs={{0,8},{2,6},{8,16},{10,2},{16,24},{18,10},{24,28},{26,18},{28,20},... | collective-permute-start | bytes 1966088 | tf_op jit(solution)/shard_map/ppermute | solution.py:682
  235.0 19.6 %collective-permute-start.44 = (bf16[256,1280]{1,0:T(8,128)(2,1)}, bf16[256,1280]{1,0:T(8,128)(2,1)}, u32[]{:S(2)}, u32[]{:S(2)}) collective-permute-start(bf16[256,1280]{1,0:T(8,128)(2,1)} %reduce_step.14.refs_3_), channel_id=1, source_target_pairs={{0,8},{2,6},{8,16},{10,2},{16,24},{18,10},{24,28},{26,18},{28,20},... | collective-permute-start | bytes 1966088 | tf_op jit(solution)/shard_map/ppermute | solution.py:682
  235.7 24.2 %collective-permute-start.54 = (bf16[512,640]{1,0:T(8,128)(2,1)S(1)}, bf16[512,640]{1,0:T(8,128)(2,1)}, u32[]{:S(2)}, u32[]{:S(2)}) collective-permute-start(bf16[512,640]{1,0:T(8,128)(2,1)S(1)} %collective-permute-done.45.refs_2_), channel_id=1, source_target_pairs={{0,2},{2,0},{4,6},{6,4},{8,10},{10,8},{12,14},{14,12},{16,18},{18,... | collective-permute-start | bytes 1966088 | tf_op jit(solution)/shard_map/ppermute | solution.py:685
  235.7 30.2 %collective-permute-start.55 = (bf16[512,640]{1,0:T(8,128)(2,1)}, bf16[512,640]{1,0:T(8,128)(2,1)}, u32[]{:S(2)}, u32[]{:S(2)}) collective-permute-start(bf16[512,640]{1,0:T(8,128)(2,1)} %collective-permute-done.46.refs_4_.refs_3_), channel_id=1, source_target_pairs={{0,2},{2,0},{4,6},{6,4},{8,10},{10,8},{12,14},{14,12},{16,18},{18,... | collective-permute-start | bytes 1966088 | tf_op jit(solution)/shard_map/ppermute | solution.py:685
  247.6 12.3 %collective-permute-start.57 = (bf16[256,640]{1,0:T(8,128)(2,1)S(1)}, bf16[256,640]{1,0:T(8,128)(2,1)}, u32[]{:S(2)}, u32[]{:S(2)}) collective-permute-start(bf16[256,640]{1,0:T(8,128)(2,1)S(1)} %constant_dynamic-slice_fusion.1), channel_id=1, source_target_pairs={{0,8},{2,6},{8,16},{10,2},{16,24},{18,10},{24,28},{26,18},{28,20},... | collective-permute-start | bytes 983048 | tf_op jit(solution)/shard_map/ppermute | solution.py:682
  248.3 16.9 %collective-permute-start.50 = (bf16[256,1280]{1,0:T(8,128)(2,1)S(1)}, bf16[256,1280]{1,0:T(8,128)(2,1)}, u32[]{:S(2)}, u32[]{:S(2)}) collective-permute-start(bf16[256,1280]{1,0:T(8,128)(2,1)S(1)} %collective-permute-done.49.refs_2_), channel_id=1, source_target_pairs={{0,8},{2,6},{8,16},{10,2},{16,24},{18,10},{24,28},{26,18},{28,20},... | collective-permute-start | bytes 1966088 | tf_op jit(solution)/shard_map/ppermute | solution.py:682
  259.2 13.0 %collective-permute-start.47 = (bf16[256,1280]{1,0:T(8,128)(2,1)}, bf16[256,1280]{1,0:T(8,128)(2,1)}, u32[]{:S(2)}, u32[]{:S(2)}) collective-permute-start(bf16[256,1280]{1,0:T(8,128)(2,1)} %reduce_step.15), channel_id=1, source_target_pairs={{0,8},{2,6},{8,16},{10,2},{16,24},{18,10},{24,28},{26,18},{28,20},... | collective-permute-start | bytes 1966088 | tf_op jit(solution)/shard_map/ppermute | solution.py:682
  259.9 12.3 %collective-permute-start.56 = (bf16[512,640]{1,0:T(8,128)(2,1)S(1)}, bf16[512,640]{1,0:T(8,128)(2,1)}, u32[]{:S(2)}, u32[]{:S(2)}) collective-permute-start(bf16[512,640]{1,0:T(8,128)(2,1)S(1)} %collective-permute-done.53.refs_4_), channel_id=1, source_target_pairs={{0,2},{2,0},{4,6},{6,4},{8,10},{10,8},{12,14},{14,12},{16,18},{18,... | collective-permute-start | bytes 1966088 | tf_op jit(solution)/shard_map/ppermute | solution.py:685
  265.2 13.9 %collective-permute-start.59 = (bf16[256,1280]{1,0:T(8,128)(2,1)}, bf16[256,1280]{1,0:T(8,128)(2,1)S(1)}, u32[]{:S(2)}, u32[]{:S(2)}) collective-permute-start(bf16[256,1280]{1,0:T(8,128)(2,1)} %collective-permute-done.50.refs_3_.refs_7_), channel_id=1, source_target_pairs={{0,8},{2,6},{8,16},{10,2},{16,24},{18,10},{24,28},{26,18},{28,20},... | collective-permute-start | bytes 1966088 | tf_op jit(solution)/shard_map/ppermute | solution.py:682
  265.9 14.1 %collective-permute-start.51 = (bf16[256,1280]{1,0:T(8,128)(2,1)}, bf16[256,1280]{1,0:T(8,128)(2,1)S(1)}, u32[]{:S(2)}, u32[]{:S(2)}) collective-permute-start(bf16[256,1280]{1,0:T(8,128)(2,1)} %copy-done.28), channel_id=1, source_target_pairs={{0,2},{2,0},{4,6},{6,4},{8,10},{10,8},{12,14},{14,12},{16,18},{18,... | collective-permute-start | bytes 1966088 | tf_op jit(solution)/shard_map/ppermute | solution.py:685
  265.9 14.1 %collective-permute-start.52 = (bf16[256,1280]{1,0:T(8,128)(2,1)}, bf16[256,1280]{1,0:T(8,128)(2,1)S(1)}, u32[]{:S(2)}, u32[]{:S(2)}) collective-permute-start(bf16[256,1280]{1,0:T(8,128)(2,1)} %collective-permute-done.50.refs_3_.refs_7_), channel_id=1, source_target_pairs={{0,2},{2,0},{4,6},{6,4},{8,10},{10,8},{12,14},{14,12},{16,18},{18,... | collective-permute-start | bytes 1966088 | tf_op jit(solution)/shard_map/ppermute | solution.py:685
  272.2 12.1 %collective-permute-start.48 = (bf16[256,1280]{1,0:T(8,128)(2,1)}, bf16[256,1280]{1,0:T(8,128)(2,1)S(1)}, u32[]{:S(2)}, u32[]{:S(2)}) collective-permute-start(bf16[256,1280]{1,0:T(8,128)(2,1)} %collective-permute-done.47.refs_2_), channel_id=1, source_target_pairs={{0,2},{2,0},{4,6},{6,4},{8,10},{10,8},{12,14},{14,12},{16,18},{18,... | collective-permute-start | bytes 1966088 | tf_op jit(solution)/shard_map/ppermute | solution.py:685
  (73 other events, 410.8 us)

commit v5 on v4

--- a/solution.py
+++ b/solution.py
@@ -831,7 +831,8 @@
     )
     slab_x = swap_x(slab)
     late = lax.dynamic_slice_in_dim(w_output, k * quarter + early, quarter - early, 0)
-    out_xs.append(swap_x(gate(late, [slab_x])))
+    late, slab_x = gates([late, slab_x], out_xs)
+    out_xs.append(swap_x(late))
     weight_t, gains, scale_col, scale_row = call(
         setup_body,
         [((3 * HD, model), BF), ((8, model), F32), ((HD, 1), F32), ((8, 128), F32)],
@@ -839,7 +840,7 @@
         smem=1,
         after=[*steps[2], *out_xs[:1]],
         name="setup",
-        mib=6,
+        mib=60,
         us=2,
     )
     weight_sib = swap_core(weight_t)

time: 295 us -> 294 us (level)
  local copies, waits for them, and re-layouts: 23.8 us -> 19.4 us
    unnamed x113 -> x111, local copies, waits for them, and re-layouts: 19.5 us -> 17.3 us
  transfers between devices with their start and end apart: 65 -> 65, of which waited for: 28 -> 27; matrix products, arithmetic and copies ran while one was open for 2% -> 2% of each run, Pallas kernels for 35% -> 35%
where the time goes in v5:
time: 294 us; the launch traced here: 293 us
  Pallas kernels  109 us (37%)
  waiting for transfers between devices  109 us (37%)
  starting transfers between devices  51.6 us (18%)
  local copies, waits for them, and re-layouts  19.4 us (7%)
    pallas_call x38, Pallas kernels, call(): pl.pallas_call(run, out_shape=[jax.ShapeDtypeStruct(shape, kind) for shap...  109 us
    ppermute x16, waiting for transfers between devices, ring_by_core(): return lax.ppermute(a, 'ctx', pairs)  62.5 us
    ppermute x12, waiting for transfers between devices, swap_x(): return lax.ppermute(a, 'fsdp', [(0, 1), (1, 0)])  28.8 us
    unnamed x111, local copies, waits for them, and re-layouts  17.3 us
    ppermute x12, starting transfers between devices, swap_x(): return lax.ppermute(a, 'fsdp', [(0, 1), (1, 0)])  15 us
    ppermute x16, starting transfers between devices, ring_by_core(): return lax.ppermute(a, 'ctx', pairs)  12.8 us
    ppermute x8, starting transfers between devices, ring(): return lax.ppermute(a, 'ctx', pairs)  9.33 us
    all_to_all x2, waiting for transfers between devices, exchange(): return lax.all_to_all(a, 'ctx', 0, 0, axis_index_groups=which, tiled=True)  8.87 us
  transfers between devices with their start and end apart: 65, of which 27 were waited for; matrix products, arithmetic and copies ran while one was open for 2% of the time, Pallas kernels for 35%

profile of v5, /device:TPU:0, one launch (start us, length us, event | category | flops | bytes accessed | tf_op | source)
XLA Modules:
  0.0 292.6 jit_solution(10074912414559940448)
XLA Ops:
  0.6 3.0 %collective-permute-start.1 = (bf16[128,1280]{1,0:T(8,128)(2,1)}, bf16[128,1280]{1,0:T(8,128)(2,1)S(1)}, u32[]{:S(2)}, u32[]{:S(2)}) collective-permute-start(bf16[128,1280]{1,0:T(8,128)(2,1)} %bitcast.31), channel_id=1, source_target_pairs={{0,4},{2,6},{8,0},{10,2},{16,8},{18,10},{24,16},{26,18},{28,24},{3... | collective-permute-start | bytes 983048 | tf_op jit(solution)/shard_map/ppermute | solution.py:670
  4.4 3.2 %slab.1.refs_1_.refs_2_ = bf16[256,640]{1,0:T(8,128)(2,1)} custom-call(s32[4]{0:T(128)} %pad_add_fusion.1.refs_0_.refs_1_, bf16[640,1280]{1,0:T(8,128)(2,1)} %refs_2_.2, bf16[640,1280]{1,0:T(8,128)(2,1)} %refs_2_.2, bf16[640,1280]{1,0:T(8,128)(2,1)} %refs_4_.2, bf16[640,1280]{1,0:T(8,128)(2,1)} %refs_4_.2, bf16[640,1280]{1,0:T(8,128)(2,1)} %refs_6_.3, ...), custom_call_target="tpu_custom_call" | custom-call | flops 3449999872 | bytes 1 | tf_op jit(solution)/shard_map/slab/pallas_call | solution.py:76
  7.7 1.9 collective-permute-start.4
  9.8 1.8 collective-permute-done.1.refs_3_
  11.6 1.7 collective-permute-start.3
  13.7 4.8 %collective-permute-done.4.refs_1_ = bf16[256,640]{1,0:T(8,128)(2,1)S(1)} collective-permute-done((bf16[256,640]{1,0:T(8,128)(2,1)}, bf16[256,640]{1,0:T(8,128)(2,1)S(1)}, u32[]{:S(2)}, u32[]{:S(2)}) %collective-permute-start.4) | collective-permute-done | bytes 327712 | tf_op jit(solution)/shard_map/ppermute | solution.py:694
  18.5 5.6 %collective-permute-done.5.refs_2_.refs_5_.refs_0_ = bf16[128,1280]{1,0:T(8,128)(2,1)S(1)} collective-permute-done((bf16[128,1280]{1,0:T(8,128)(2,1)S(1)}, bf16[128,1280]{1,0:T(8,128)(2,1)S(1)}, u32[]{:S(2)}, u32[]{:S(2)}) %collective-permute-start.5) | collective-permute-done | bytes 327712 | tf_op jit(solution)/shard_map/ppermute | solution.py:694
  24.9 2.1 setup.1
  27.0 1.7 collective-permute-start.11
  29.1 1.6 collective-permute-start.14
  31.5 4.7 %project.2 = (bf16[8,128,1280]{2,1,0:T(8,128)(2,1)}, bf16[5,80,128]{2,1,0:T(8,128)(2,1)}, bf16[5,160,128]{2,1,0:T(8,128)(2,1)}, bf16[5,240,128]{2,1,0:T(8,128)(2,1)}, bf16[5,160,128]{2,1,0:T(8,128)(2,1)}) custom-call(s32[4]{0:T(128)} %pad_add_fusion.1.refs_0_.refs_1_, bf16[128,1280]{1,0:T(8,128)(2,1)} %bitcast.33, ...), custom_call_target="tpu_custom_call" | custom-call | flops 3449999872 | bytes 1 | tf_op jit(solution)/shard_map/project/pallas_call | solution.py:76
  39.6 1.6 collective-permute-start.13
  42.5 1.6 collective-permute-start.7
  47.2 4.7 %project.3 = (bf16[8,128,1280]{2,1,0:T(8,128)(2,1)}, bf16[3,80,128]{2,1,0:T(8,128)(2,1)}, bf16[3,160,128]{2,1,0:T(8,128)(2,1)}, bf16[3,240,128]{2,1,0:T(8,128)(2...) custom-call(s32[4]{0:T(128)} %pad_add_fusion.1.refs_0_.refs_1_, ...), custom_call_target="tpu_custom_call", output_to_operand_aliasing={{0}: (11, {})} | custom-call | flops 3449999872 | bytes 1 | tf_op jit(solution)/shard_map/project/pallas_call | solution.py:76
  53.3 1.6 collective-permute-start.17
  55.9 1.7 copy-done
  57.7 1.7 copy-done.1
  60.0 1.7 collective-permute-done.15.refs_13_.refs_3_
  63.9 19.0 %attention_forward.1 = (bf16[16,80,128]{2,1,0:T(8,128)(2,1)}, bf16[4,80,512]{2,1,0:T(8,128)(2,1)}, bf16[8,80,512]{2,1,0:T(8,128)(2,1)}, bf16[8,512,80]{2,1,0:T(8...) custom-call(s32[16,2]{1,0:T(8,128)} %gather_fusion, s32[16,2]{1,0:T(8,128)} %gather_fusion, ...), custom_call_target="tpu_custom_call" | custom-call | flops 23000000512 | bytes 1 | tf_op jit(solution)/shard_map/attention_forward/pallas_call | solution.py:76
  85.4 4.0 %all-to-all-start = ((bf16[16,80,128]{2,1,0:T(8,128)(2,1)}), bf16[16,80,128]{2,1,0:T(8,128)(2,1)S(1)}, u32[]{:S(2)}, u32[]{:S(2)}) async-start(bf16[16,80,128]{2,1,0:T(8,128)(2,1)} %copy-done.4), calls=%async_computation | async-start | bytes 655360 | tf_op jit(solution)/shard_map/all_to_all | solution.py:713
  89.4 9.9 %collective-permute-done.21.refs_1_ = bf16[320,1280]{1,0:T(8,128)(2,1)} collective-permute-done((bf16[320,1280]{1,0:T(8,128)(2,1)}, bf16[320,1280]{1,0:T(8,128)(2,1)}, u32[]{:S(2)}, u32[]{:S(2)}) %collective-permute-start.21) | collective-permute-done | bytes 819232 | tf_op jit(solution)/shard_map/ppermute | solution.py:694
  104.3 10.8 %row_part.1 = (bf16[128,1280]{1,0:T(8,128)(2,1)}, f32[128,1280]{1,0:T(8,128)}, bf16[1280,128]{1,0:T(8,128)(2,1)}, bf16[3776,128]{1,0:T(8,128)(2,1)}, bf16[3776,1...) custom-call(s32[4]{0:T(128)} %pad_add_fusion.1.refs_0_.refs_1_, bf16[1280,128]{1,0:T(8,128)(2,1)} %bitcast.25, ...), custom_call_target="tpu_custom_call" | custom-call | flops 11500000256 | bytes 1 | tf_op jit(solution)/shard_map/row_part/pallas_call | solution.py:76
  116.8 4.4 %all-to-all-start.1 = ((bf16[16,80,128]{2,1,0:T(8,128)(2,1)}), bf16[16,80,128]{2,1,0:T(8,128)(2,1)}, u32[]{:S(2)}, u32[]{:S(2)}) async-start(bf16[16,80,128]{2,1,0:T(8,128)(2,1)} %bitcast.23), calls=%async_computation.1 | async-start | bytes 655360 | tf_op jit(solution)/shard_map/all_to_all | solution.py:713
  124.7 7.7 %all-to-all-done.1.refs_5_ = bf16[16,80,128]{2,1,0:T(8,128)(2,1)} async-done(((bf16[16,80,128]{2,1,0:T(8,128)(2,1)}), bf16[16,80,128]{2,1,0:T(8,128)(2,1)}, u32[]{:S(2)}, u32[]{:S(2)}) %all-to-all-start.1) | async-done | bytes 327712 | tf_op jit(solution)/shard_map/all_to_all | solution.py:713
  132.3 24.4 %attention_backward.1 = (f32[8,160,256]{2,1,0:T(8,128)}, bf16[8,160,256]{2,1,0:T(8,128)(2,1)}, bf16[16,80,128]{2,1,0:T(8,128)(2,1)}, f32[80,512]{1,0:T(8,128)}) custom-call(s32[16,2]{1,0:T(8,128)} %copy-done.19, s32[8]{0:T(128)} %constant.102.clone.refs_1_, s32[8]{0:T(128)} %constant.103.clone.refs_2_, s32[4,1,512]{2,1,0:T(1,128)} %constant.99.clone.refs_5_.refs_3_, ...), custom_call_target="tpu_custom_call" | custom-call | flops 28750000128 | bytes 1 | tf_op jit(solution)/shard_map/attention_backward/pallas_call | solution.py:76
  161.2 3.2 %pooled_grads.1.refs_1_ = bf16[5,256,1280]{2,1,0:T(8,128)(2,1)S(1)} custom-call(bf16[3776,128]{1,0:T(8,128)(2,1)S(1)} %copy-done.44, bf16[3776,128]{1,0:T(8,128)(2,1)} %get-tuple-element.117.refs_1_, bf16[3776,128]{1,0:T(8,128)(2,1)} %get-tuple-element.118.refs_2_, bf16[1200,128]{1,0:T(8,128)(2,1)S(1)} %get-tuple-element.119.refs_3_, ...), custom_call_target="tpu_custom_call" | custom-call | flops 3449999872 | bytes 1 | tf_op jit(solution)/shard_map/pooled_grads/pallas_call | solution.py:76
  166.4 5.8 %collective-permute-done.34.refs_2_ = bf16[256,640]{1,0:T(8,128)(2,1)S(1)} collective-permute-done((bf16[256,640]{1,0:T(8,128)(2,1)S(1)}, bf16[256,640]{1,0:T(8,128)(2,1)S(1)}, u32[]{:S(2)}, u32[]{:S(2)}) %collective-permute-start.34) | collective-permute-done | bytes 327712 | tf_op jit(solution)/shard_map/ppermute | solution.py:682
  173.5 2.7 collective-permute-done.26.refs_4_
  176.2 1.9 join.1
  178.2 4.5 %qkv_grads.1 = (f32[256,640]{1,0:T(8,128)S(1)}, bf16[256,640]{1,0:T(8,128)(2,1)S(1)}) custom-call(s32[16]{0:T(128)S(1)} %fusion.1.refs_0_, s32[4]{0:T(128)S(1)} %copy-done.30, bf16[16,240,128]{2,1,0:T(8,128)(2,1)S(1)} %get-tuple-element.121.refs_2_.refs_1_, f32[80,512]{1,0:T(8,128)S(1)} %copy-done.47, bf16[8,128,1280]{2,1,0:T(8,128)(2,1)S(1)} %copy-done.1, ...), custom_call_target="tpu_custom_call" | custom-call | flops 5405000192 | bytes 1 | tf_op jit(solution)/shard_map/qkv_grads/pallas_call | solution.py:76
  185.7 2.5 products.1.refs_1_
  188.8 4.1 %collective-permute-done.38.refs_1_ = bf16[256,640]{1,0:T(8,128)(2,1)S(1)} collective-permute-done((bf16[256,640]{1,0:T(8,128)(2,1)S(1)}, bf16[256,640]{1,0:T(8,128)(2,1)S(1)}, u32[]{:S(2)}, u32[]{:S(2)}) %collective-permute-start.38) | collective-permute-done | bytes 327712 | tf_op jit(solution)/shard_map/ppermute | solution.py:694
  193.1 2.5 collective-permute-done.40.refs_2_
  199.3 7.6 %collective-permute-done.42.refs_2_ = bf16[256,1280]{1,0:T(8,128)(2,1)S(1)} collective-permute-done((bf16[256,1280]{1,0:T(8,128)(2,1)S(1)}, bf16[256,1280]{1,0:T(8,128)(2,1)S(1)}, u32[]{:S(2)}, u32[]{:S(2)}) %collective-permute-start.42) | collective-permute-done | bytes 655392 | tf_op jit(solution)/shard_map/ppermute | solution.py:682
  206.9 7.0 %collective-permute-done.45.refs_2_ = bf16[512,640]{1,0:T(8,128)(2,1)S(1)} collective-permute-done((bf16[512,640]{1,0:T(8,128)(2,1)S(1)}, bf16[512,640]{1,0:T(8,128)(2,1)S(1)}, u32[]{:S(2)}, u32[]{:S(2)}) %collective-permute-start.45) | collective-permute-done | bytes 655392 | tf_op jit(solution)/shard_map/ppermute | solution.py:682
  214.6 2.8 collective-permute-done.37.refs_2_
  220.9 3.7 %collective-permute-done.46.refs_4_.refs_3_ = bf16[512,640]{1,0:T(8,128)(2,1)} collective-permute-done((bf16[512,640]{1,0:T(8,128)(2,1)S(1)}, bf16[512,640]{1,0:T(8,128)(2,1)}, u32[]{:S(2)}, u32[]{:S(2)}) %collective-permute-start.46) | collective-permute-done | bytes 655392 | tf_op jit(solution)/shard_map/ppermute | solution.py:682
  225.3 6.2 %collective-permute-done.41.refs_2_ = bf16[256,1280]{1,0:T(8,128)(2,1)S(1)} collective-permute-done((bf16[256,1280]{1,0:T(8,128)(2,1)S(1)}, bf16[256,1280]{1,0:T(8,128)(2,1)S(1)}, u32[]{:S(2)}, u32[]{:S(2)}) %collective-permute-start.41) | collective-permute-done | bytes 655392 | tf_op jit(solution)/shard_map/ppermute | solution.py:682
  234.3 11.3 %collective-permute-done.53.refs_4_ = bf16[512,640]{1,0:T(8,128)(2,1)S(1)} collective-permute-done((bf16[512,640]{1,0:T(8,128)(2,1)}, bf16[512,640]{1,0:T(8,128)(2,1)S(1)}, u32[]{:S(2)}, u32[]{:S(2)}) %collective-permute-start.53) | collective-permute-done | bytes 655392 | tf_op jit(solution)/shard_map/ppermute | solution.py:682
  247.6 5.1 %collective-permute-done.44.refs_2_ = bf16[256,1280]{1,0:T(8,128)(2,1)} collective-permute-done((bf16[256,1280]{1,0:T(8,128)(2,1)}, bf16[256,1280]{1,0:T(8,128)(2,1)}, u32[]{:S(2)}, u32[]{:S(2)}) %collective-permute-start.44) | collective-permute-done | bytes 655392 | tf_op jit(solution)/shard_map/ppermute | solution.py:682
  252.7 1.9 copy-done.41
  254.6 2.6 reduce_step.15
  258.5 4.8 %collective-permute-done.50.refs_3_.refs_7_ = bf16[256,1280]{1,0:T(8,128)(2,1)} collective-permute-done((bf16[256,1280]{1,0:T(8,128)(2,1)}, bf16[256,1280]{1,0:T(8,128)(2,1)}, u32[]{:S(2)}, u32[]{:S(2)}) %collective-permute-start.50) | collective-permute-done | bytes 655392 | tf_op jit(solution)/shard_map/ppermute | solution.py:682
  264.5 5.8 %collective-permute-done.47.refs_2_ = bf16[256,1280]{1,0:T(8,128)(2,1)} collective-permute-done((bf16[256,1280]{1,0:T(8,128)(2,1)}, bf16[256,1280]{1,0:T(8,128)(2,1)}, u32[]{:S(2)}, u32[]{:S(2)}) %collective-permute-start.47) | collective-permute-done | bytes 655392 | tf_op jit(solution)/shard_map/ppermute | solution.py:682
  270.3 7.5 %qkv_place.1 = (f32[640,1280]{1,0:T(8,128)}, f32[640,1280]{1,0:T(8,128)}, f32[640,1280]{1,0:T(8,128)}, f32[640]{0:T(1024)}, f32[40]{0:T(128)}) custom-call(s32[4]{0:T(128)S(1)} %copy-done.30, bf16[512,640]{1,0:T(8,128)(2,1)S(1)} %chip_pack.1.refs_3_.refs_4_.refs_1_, bf16[512,640]{1,0:T(8,128)(2,1)S(1)} %collective-permute-done.45.refs_2_, ...), custom_call_target="tpu_custom_call" | custom-call | flops 6899999744 | bytes 1 | tf_op jit(solution)/shard_map/qkv_place/pallas_call | solution.py:76
  278.7 4.5 %rows_place.2 = (f32[640,1280]{1,0:T(8,128)}, f32[640,1280]{1,0:T(8,128)}, f32[640,1280]{1,0:T(8,128)}, f32[640,128]{1,0:T(8,128)S(1)}, f32[8,128]{1,0:T(8,128)S(1)}) custom-call(s32[4]{0:T(128)S(1)} %copy-done.30, bf16[256,1280]{1,0:T(8,128)(2,1)S(1)} %copy-done.33, bf16[256,1280]{1,0:T(8,128)(2,1)} %collective-permute-done.49.refs_2_, ...), custom_call_target="tpu_custom_call" | custom-call | flops 4600000000 | bytes 1 | tf_op jit(solution)/shard_map/rows_place/pallas_call | solution.py:76
  283.3 3.0 %inputs_grad.1.refs_2_ = bf16[128,1280]{1,0:T(8,128)(2,1)} custom-call(s32[4]{0:T(128)S(1)} %copy-done.30, bf16[5,256,1280]{2,1,0:T(8,128)(2,1)S(1)} %copy-done.42, bf16[256,1280]{1,0:T(8,128)(2,1)} %collective-permute-done.47.refs_2_, bf16[256,1280]{1,0:T(8,128)(2,1)S(1)} %collective-permute-done.48.refs_3_, bf16[128,1280]{1,0:T(8,128)(2,1)S(1)} %bitcast.35, ...), custom_call_target="tpu_custom_call" | custom-call | flops 2300000000 | bytes 1 | tf_op jit(solution)/shard_map/inputs_grad/pallas_call | solution.py:76
  289.0 3.4 %rows_place.3 = (f32[640,1280]{1,0:T(8,128)}, f32[640,1280]{1,0:T(8,128)}, f32[640,1280]{1,0:T(8,128)}, f32[640]{0:T(1024)}, f32[2]{0:T(128)}) custom-call(s32[4]{0:T(128)S(1)} %copy-done.30, bf16[256,1280]{1,0:T(8,128)(2,1)S(1)} %collective-permute-done.59.refs_1_, ...), custom_call_target="tpu_custom_call", output_to_operand_aliasing={{0}: (9, {}), {1}: (10, {}), {2}: (11, {})} | custom-call | flops 3449999872 | bytes 1 | tf_op jit(solution)/shard_map/rows_place/pallas_call | solution.py:76
  (246 shorter events, 60.0 us)
Async XLA Ops:
  0.6 11.0 %collective-permute-start.1 = (bf16[128,1280]{1,0:T(8,128)(2,1)}, bf16[128,1280]{1,0:T(8,128)(2,1)S(1)}, u32[]{:S(2)}, u32[]{:S(2)}) collective-permute-start(bf16[128,1280]{1,0:T(8,128)(2,1)} %bitcast.31), channel_id=1, source_target_pairs={{0,4},{2,6},{8,0},{10,2},{16,8},{18,10},{24,16},{26,18},{28,24},{3... | collective-permute-start | bytes 983048 | tf_op jit(solution)/shard_map/ppermute | solution.py:670
  3.7 9.7 %collective-permute-start = (bf16[128,1280]{1,0:T(8,128)(2,1)}, bf16[128,1280]{1,0:T(8,128)(2,1)}, u32[]{:S(2)}, u32[]{:S(2)}) collective-permute-start(bf16[128,1280]{1,0:T(8,128)(2,1)} %bitcast.32), channel_id=1, source_target_pairs={{0,8},{2,10},{8,16},{10,18},{16,24},{18,26},{24,28},{26,30},{28,20... | collective-permute-start | bytes 983048 | tf_op jit(solution)/shard_map/ppermute | solution.py:670
  7.7 10.8 %collective-permute-start.4 = (bf16[256,640]{1,0:T(8,128)(2,1)}, bf16[256,640]{1,0:T(8,128)(2,1)S(1)}, u32[]{:S(2)}, u32[]{:S(2)}) collective-permute-start(bf16[256,640]{1,0:T(8,128)(2,1)} %slab.1.refs_1_.refs_2_), channel_id=1, source_target_pairs={{0,1},{1,0},{2,3},{3,2},{4,5},{5,4},{6,7},{7,6},{8,9},{9,8},{10,11... | collective-permute-start | bytes 983048 | tf_op jit(solution)/shard_map/ppermute | solution.py:694
  9.6 14.5 %collective-permute-start.5 = (bf16[128,1280]{1,0:T(8,128)(2,1)S(1)}, bf16[128,1280]{1,0:T(8,128)(2,1)S(1)}, u32[]{:S(2)}, u32[]{:S(2)}) collective-permute-start(bf16[128,1280]{1,0:T(8,128)(2,1)S(1)} %constant_dynamic-slice_fusion.3), channel_id=1, source_target_pairs={{0,1},{1,0},{2,3},{3,2},{4,5},{5,4},{6,7},{7,6},{8,9},{9,8},{10,11... | collective-permute-start | bytes 983048 | tf_op jit(solution)/shard_map/ppermute | solution.py:694
  11.6 13.2 %collective-permute-start.3 = (bf16[128,1280]{1,0:T(8,128)(2,1)S(1)}, bf16[128,1280]{1,0:T(8,128)(2,1)}, u32[]{:S(2)}, u32[]{:S(2)}) collective-permute-start(bf16[128,1280]{1,0:T(8,128)(2,1)S(1)} %collective-permute-done.1.refs_3_), channel_id=1, source_target_pairs={{0,4},{2,6},{8,0},{10,2},{16,8},{18,10},{24,16},{26,18},{28,24},{3... | collective-permute-start | bytes 983048 | tf_op jit(solution)/shard_map/ppermute | solution.py:670
  13.3 11.5 %collective-permute-start.2 = (bf16[128,1280]{1,0:T(8,128)(2,1)}, bf16[128,1280]{1,0:T(8,128)(2,1)}, u32[]{:S(2)}, u32[]{:S(2)}) collective-permute-start(bf16[128,1280]{1,0:T(8,128)(2,1)} %collective-permute-done.refs_2_), channel_id=1, source_target_pairs={{0,8},{2,10},{8,16},{10,18},{16,24},{18,26},{24,28},{26,30},{28,20... | collective-permute-start | bytes 983048 | tf_op jit(solution)/shard_map/ppermute | solution.py:670
  27.0 10.3 %collective-permute-start.11 = (bf16[128,1280]{1,0:T(8,128)(2,1)}, bf16[128,1280]{1,0:T(8,128)(2,1)S(1)}, u32[]{:S(2)}, u32[]{:S(2)}) collective-permute-start(bf16[128,1280]{1,0:T(8,128)(2,1)} %collective-permute-done.3.refs_4_.refs_5_), channel_id=1, source_target_pairs={{0,4},{2,6},{8,0},{10,2},{16,8},{18,10},{24,16},{26,18},{28,24},{3... | collective-permute-start | bytes 983048 | tf_op jit(solution)/shard_map/ppermute | solution.py:670
  28.7 10.0 %collective-permute-start.10 = (bf16[128,1280]{1,0:T(8,128)(2,1)}, bf16[128,1280]{1,0:T(8,128)(2,1)S(1)}, u32[]{:S(2)}, u32[]{:S(2)}) collective-permute-start(bf16[128,1280]{1,0:T(8,128)(2,1)} %collective-permute-done.2.refs_3_.refs_4_), channel_id=1, source_target_pairs={{0,8},{2,10},{8,16},{10,18},{16,24},{18,26},{24,28},{26,30},{28,20... | collective-permute-start | bytes 983048 | tf_op jit(solution)/shard_map/ppermute | solution.py:670
  29.1 14.9 %collective-permute-start.14 = (bf16[192,1280]{1,0:T(8,128)(2,1)S(1)}, bf16[192,1280]{1,0:T(8,128)(2,1)}, u32[]{:S(2)}, u32[]{:S(2)}) collective-permute-start(bf16[192,1280]{1,0:T(8,128)(2,1)S(1)} %get-tuple-element.89), channel_id=1, source_target_pairs={{0,1},{1,0},{2,3},{3,2},{4,5},{5,4},{6,7},{7,6},{8,9},{9,8},{10,11... | collective-permute-start | bytes 1474568 | tf_op jit(solution)/shard_map/ppermute | solution.py:694
  42.4 12.5 %collective-permute-start.9 = (bf16[5,160,128]{2,1,0:T(8,128)(2,1)}, bf16[5,160,128]{2,1,0:T(8,128)(2,1)S(1)}, u32[]{:S(2)}, u32[]{:S(2)}) collective-permute-start(bf16[5,160,128]{2,1,0:T(8,128)(2,1)} %get-tuple-element.85), channel_id=1, source_target_pairs={{0,3},{1,2},{2,1},{3,0},{4,7},{5,6},{6,5},{7,4},{8,11},{9,10},{10,... | collective-permute-start | bytes 614408 | tf_op jit(solution)/shard_map/ppermute | solution.py:691
  42.5 16.9 %collective-permute-start.7 = (bf16[5,160,128]{2,1,0:T(8,128)(2,1)}, bf16[5,160,128]{2,1,0:T(8,128)(2,1)S(1)}, u32[]{:S(2)}, u32[]{:S(2)}) collective-permute-start(bf16[5,160,128]{2,1,0:T(8,128)(2,1)} %get-tuple-element.83.refs_7_), channel_id=1, source_target_pairs={{0,1},{1,0},{2,3},{3,2},{4,5},{5,4},{6,7},{7,6},{8,9},{9,8},{10,11... | collective-permute-start | bytes 614408 | tf_op jit(solution)/shard_map/ppermute | solution.py:694
  44.0 19.2 %collective-permute-start.8 = (bf16[5,240,128]{2,1,0:T(8,128)(2,1)}, bf16[5,240,128]{2,1,0:T(8,128)(2,1)}, u32[]{:S(2)}, u32[]{:S(2)}) collective-permute-start(bf16[5,240,128]{2,1,0:T(8,128)(2,1)} %get-tuple-element.84), channel_id=1, source_target_pairs={{0,2},{2,0},{4,6},{6,4},{8,10},{10,8},{12,14},{14,12},{16,18},{18,... | collective-permute-start | bytes 921608 | tf_op jit(solution)/shard_map/ppermute | solution.py:685
  51.9 11.9 %collective-permute-start.16 = (bf16[3,240,128]{2,1,0:T(8,128)(2,1)}, bf16[3,240,128]{2,1,0:T(8,128)(2,1)}, u32[]{:S(2)}, u32[]{:S(2)}) collective-permute-start(bf16[3,240,128]{2,1,0:T(8,128)(2,1)} %get-tuple-element.92), channel_id=1, source_target_pairs={{0,2},{2,0},{4,6},{6,4},{8,10},{10,8},{12,14},{14,12},{16,18},{18,... | collective-permute-start | bytes 552968 | tf_op jit(solution)/shard_map/ppermute | solution.py:685
  59.4 23.5 %collective-permute-start.18 = (bf16[128,1280]{1,0:T(8,128)(2,1)S(1)}, bf16[128,1280]{1,0:T(8,128)(2,1)}, u32[]{:S(2)}, u32[]{:S(2)}) collective-permute-start(bf16[128,1280]{1,0:T(8,128)(2,1)S(1)} %gate.14.refs_6_), channel_id=1, source_target_pairs={{0,2},{2,0},{4,6},{6,4},{8,10},{10,8},{12,14},{14,12},{16,18},{18,... | collective-permute-start | bytes 983048 | tf_op jit(solution)/shard_map/ppermute | solution.py:685
  59.5 23.4 %collective-permute-start.19 = (bf16[192,1280]{1,0:T(8,128)(2,1)}, bf16[192,1280]{1,0:T(8,128)(2,1)S(1)}, u32[]{:S(2)}, u32[]{:S(2)}) collective-permute-start(bf16[192,1280]{1,0:T(8,128)(2,1)} %gate.15.refs_8_), channel_id=1, source_target_pairs={{0,2},{2,0},{4,6},{6,4},{8,10},{10,8},{12,14},{14,12},{16,18},{18,... | collective-permute-start | bytes 1474568 | tf_op jit(solution)/shard_map/ppermute | solution.py:685
  61.7 27.6 %collective-permute-start.20 = (bf16[320,1280]{1,0:T(8,128)(2,1)}, bf16[320,1280]{1,0:T(8,128)(2,1)}, u32[]{:S(2)}, u32[]{:S(2)}) collective-permute-start(bf16[320,1280]{1,0:T(8,128)(2,1)} %gate.17), channel_id=1, source_target_pairs={{0,1},{1,0},{2,3},{3,2},{4,5},{5,4},{6,7},{7,6},{8,9},{9,8},{10,11... | collective-permute-start | bytes 2457608 | tf_op jit(solution)/shard_map/ppermute | solution.py:694
  63.2 36.0 %collective-permute-start.21 = (bf16[320,1280]{1,0:T(8,128)(2,1)}, bf16[320,1280]{1,0:T(8,128)(2,1)}, u32[]{:S(2)}, u32[]{:S(2)}) collective-permute-start(bf16[320,1280]{1,0:T(8,128)(2,1)} %gate.18), channel_id=1, source_target_pairs={{0,1},{1,0},{2,3},{3,2},{4,5},{5,4},{6,7},{7,6},{8,9},{9,8},{10,11... | collective-permute-start | bytes 2457608 | tf_op jit(solution)/shard_map/ppermute | solution.py:694
  85.4 15.1 %all-to-all-start = ((bf16[16,80,128]{2,1,0:T(8,128)(2,1)}), bf16[16,80,128]{2,1,0:T(8,128)(2,1)S(1)}, u32[]{:S(2)}, u32[]{:S(2)}) async-start(bf16[16,80,128]{2,1,0:T(8,128)(2,1)} %copy-done.4), calls=%async_computation | async-start | bytes 655360 | tf_op jit(solution)/shard_map/all_to_all | solution.py:713
  102.0 13.1 %collective-permute-start.24 = (bf16[128,1280]{1,0:T(8,128)(2,1)S(1)}, bf16[128,1280]{1,0:T(8,128)(2,1)S(1)}, u32[]{:S(2)}, u32[]{:S(2)}) collective-permute-start(bf16[128,1280]{1,0:T(8,128)(2,1)S(1)} %gate.20), channel_id=1, source_target_pairs={{0,1},{1,0},{2,3},{3,2},{4,5},{5,4},{6,7},{7,6},{8,9},{9,8},{10,11... | collective-permute-start | bytes 983048 | tf_op jit(solution)/shard_map/ppermute | solution.py:694
  116.8 15.5 %all-to-all-start.1 = ((bf16[16,80,128]{2,1,0:T(8,128)(2,1)}), bf16[16,80,128]{2,1,0:T(8,128)(2,1)}, u32[]{:S(2)}, u32[]{:S(2)}) async-start(bf16[16,80,128]{2,1,0:T(8,128)(2,1)} %bitcast.23), calls=%async_computation.1 | async-start | bytes 655360 | tf_op jit(solution)/shard_map/all_to_all | solution.py:713
  121.4 35.3 %collective-permute-start.31 = (bf16[8,128,1280]{2,1,0:T(8,128)(2,1)S(1)}, bf16[8,128,1280]{2,1,0:T(8,128)(2,1)}, u32[]{:S(2)}, u32[]{:S(2)}) collective-permute-start(bf16[8,128,1280]{2,1,0:T(8,128)(2,1)S(1)} %copy-done.1), channel_id=1, source_target_pairs={{0,2},{2,0},{4,6},{6,4},{8,10},{10,8},{12,14},{14,12},{16,18},{18,... | collective-permute-start | bytes 7864328 | tf_op jit(solution)/shard_map/ppermute | solution.py:685
  121.8 34.9 %collective-permute-start.30 = (bf16[128,1280]{1,0:T(8,128)(2,1)}, bf16[128,1280]{1,0:T(8,128)(2,1)S(1)}, u32[]{:S(2)}, u32[]{:S(2)}) collective-permute-start(bf16[128,1280]{1,0:T(8,128)(2,1)} %copy-done.26), channel_id=1, source_target_pairs={{0,2},{2,0},{4,6},{6,4},{8,10},{10,8},{12,14},{14,12},{16,18},{18,... | collective-permute-start | bytes 983048 | tf_op jit(solution)/shard_map/ppermute | solution.py:685
  122.0 34.8 %collective-permute-start.27 = (bf16[3776,128]{1,0:T(8,128)(2,1)}, bf16[3776,128]{1,0:T(8,128)(2,1)}, u32[]{:S(2)}, u32[]{:S(2)}) collective-permute-start(bf16[3776,128]{1,0:T(8,128)(2,1)} %get-tuple-element.114), channel_id=1, source_target_pairs={{0,1},{1,0},{2,3},{3,2},{4,5},{5,4},{6,7},{7,6},{8,9},{9,8},{10,11... | collective-permute-start | bytes 2899976 | tf_op jit(solution)/shard_map/ppermute | solution.py:694
  123.4 33.4 %collective-permute-start.28 = (bf16[3776,128]{1,0:T(8,128)(2,1)}, bf16[3776,128]{1,0:T(8,128)(2,1)}, u32[]{:S(2)}, u32[]{:S(2)}) collective-permute-start(bf16[3776,128]{1,0:T(8,128)(2,1)} %get-tuple-element.115), channel_id=1, source_target_pairs={{0,2},{2,0},{4,6},{6,4},{8,10},{10,8},{12,14},{14,12},{16,18},{18,... | collective-permute-start | bytes 2899976 | tf_op jit(solution)/shard_map/ppermute | solution.py:685
  123.5 33.3 %collective-permute-start.29 = (bf16[1200,128]{1,0:T(8,128)(2,1)}, bf16[1200,128]{1,0:T(8,128)(2,1)S(1)}, u32[]{:S(2)}, u32[]{:S(2)}) collective-permute-start(bf16[1200,128]{1,0:T(8,128)(2,1)} %collective-permute-done.25.refs_12_), channel_id=1, source_target_pairs={{0,1},{1,0},{2,3},{3,2},{4,5},{5,4},{6,7},{7,6},{8,9},{9,8},{10,11... | collective-permute-start | bytes 921608 | tf_op jit(solution)/shard_map/ppermute | solution.py:694
  159.3 16.9 %collective-permute-start.26 = (bf16[8,160,256]{2,1,0:T(8,128)(2,1)S(1)}, bf16[8,160,256]{2,1,0:T(8,128)(2,1)S(1)}, u32[]{:S(2)}, u32[]{:S(2)}) collective-permute-start(bf16[8,160,256]{2,1,0:T(8,128)(2,1)S(1)} %copy-done.51), channel_id=1, source_target_pairs={{0,1},{1,0},{2,3},{3,2},{4,5},{5,4},{6,7},{7,6},{8,9},{9,8},{10,11... | collective-permute-start | bytes 1966088 | tf_op jit(solution)/shard_map/ppermute | solution.py:694
  172.9 11.4 %collective-permute-start.36 = (bf16[256,1280]{1,0:T(8,128)(2,1)S(1)}, bf16[256,1280]{1,0:T(8,128)(2,1)S(1)}, u32[]{:S(2)}, u32[]{:S(2)}) collective-permute-start(bf16[256,1280]{1,0:T(8,128)(2,1)S(1)} %reduce_step.9.refs_5_), channel_id=1, source_target_pairs={{0,8},{2,6},{8,16},{10,2},{16,24},{18,10},{24,28},{26,18},{28,20},... | collective-permute-start | bytes 1966088 | tf_op jit(solution)/shard_map/ppermute | solution.py:682
  182.7 10.2 %collective-permute-start.38 = (bf16[256,640]{1,0:T(8,128)(2,1)S(1)}, bf16[256,640]{1,0:T(8,128)(2,1)S(1)}, u32[]{:S(2)}, u32[]{:S(2)}) collective-permute-start(bf16[256,640]{1,0:T(8,128)(2,1)S(1)} %get-tuple-element.126), channel_id=1, source_target_pairs={{0,1},{1,0},{2,3},{3,2},{4,5},{5,4},{6,7},{7,6},{8,9},{9,8},{10,11... | collective-permute-start | bytes 983048 | tf_op jit(solution)/shard_map/ppermute | solution.py:694
  184.9 10.6 %collective-permute-start.40 = (bf16[256,1280]{1,0:T(8,128)(2,1)S(1)}, bf16[256,1280]{1,0:T(8,128)(2,1)S(1)}, u32[]{:S(2)}, u32[]{:S(2)}) collective-permute-start(bf16[256,1280]{1,0:T(8,128)(2,1)S(1)} %reduce_step.10.refs_5_), channel_id=1, source_target_pairs={{0,8},{2,6},{8,16},{10,2},{16,24},{18,10},{24,28},{26,18},{28,20},... | collective-permute-start | bytes 1966088 | tf_op jit(solution)/shard_map/ppermute | solution.py:682
  196.3 10.6 %collective-permute-start.42 = (bf16[256,1280]{1,0:T(8,128)(2,1)S(1)}, bf16[256,1280]{1,0:T(8,128)(2,1)S(1)}, u32[]{:S(2)}, u32[]{:S(2)}) collective-permute-start(bf16[256,1280]{1,0:T(8,128)(2,1)S(1)} %reduce_step.12.refs_3_), channel_id=1, source_target_pairs={{0,8},{2,6},{8,16},{10,2},{16,24},{18,10},{24,28},{26,18},{28,20},... | collective-permute-start | bytes 1966088 | tf_op jit(solution)/shard_map/ppermute | solution.py:682
  197.6 16.3 %collective-permute-start.45 = (bf16[512,640]{1,0:T(8,128)(2,1)S(1)}, bf16[512,640]{1,0:T(8,128)(2,1)S(1)}, u32[]{:S(2)}, u32[]{:S(2)}) collective-permute-start(bf16[512,640]{1,0:T(8,128)(2,1)S(1)} %chip_pack.1.refs_3_.refs_4_.refs_1_), channel_id=1, source_target_pairs={{0,8},{2,6},{8,16},{10,2},{16,24},{18,10},{24,28},{26,18},{28,20},... | collective-permute-start | bytes 1966088 | tf_op jit(solution)/shard_map/ppermute | solution.py:682
  198.9 18.5 %collective-permute-start.37 = (bf16[256,640]{1,0:T(8,128)(2,1)S(1)}, bf16[256,640]{1,0:T(8,128)(2,1)S(1)}, u32[]{:S(2)}, u32[]{:S(2)}) collective-permute-start(bf16[256,640]{1,0:T(8,128)(2,1)S(1)} %reduce_step.11.refs_3_), channel_id=1, source_target_pairs={{0,8},{2,6},{8,16},{10,2},{16,24},{18,10},{24,28},{26,18},{28,20},... | collective-permute-start | bytes 983048 | tf_op jit(solution)/shard_map/ppermute | solution.py:682
  206.9 12.0 %collective-permute-start.43 = (bf16[256,1280]{1,0:T(8,128)(2,1)S(1)}, bf16[256,1280]{1,0:T(8,128)(2,1)S(1)}, u32[]{:S(2)}, u32[]{:S(2)}) collective-permute-start(bf16[256,1280]{1,0:T(8,128)(2,1)S(1)} %collective-permute-done.42.refs_2_), channel_id=1, source_target_pairs={{0,2},{2,0},{4,6},{6,4},{8,10},{10,8},{12,14},{14,12},{16,18},{18,... | collective-permute-start | bytes 1966088 | tf_op jit(solution)/shard_map/ppermute | solution.py:685
  213.9 10.7 %collective-permute-start.46 = (bf16[512,640]{1,0:T(8,128)(2,1)S(1)}, bf16[512,640]{1,0:T(8,128)(2,1)}, u32[]{:S(2)}, u32[]{:S(2)}) collective-permute-start(bf16[512,640]{1,0:T(8,128)(2,1)S(1)} %collective-permute-done.45.refs_2_), channel_id=1, source_target_pairs={{0,8},{2,6},{8,16},{10,2},{16,24},{18,10},{24,28},{26,18},{28,20},... | collective-permute-start | bytes 1966088 | tf_op jit(solution)/shard_map/ppermute | solution.py:682
  218.1 13.4 %collective-permute-start.41 = (bf16[256,1280]{1,0:T(8,128)(2,1)S(1)}, bf16[256,1280]{1,0:T(8,128)(2,1)S(1)}, u32[]{:S(2)}, u32[]{:S(2)}) collective-permute-start(bf16[256,1280]{1,0:T(8,128)(2,1)S(1)} %reduce_step.13), channel_id=1, source_target_pairs={{0,8},{2,6},{8,16},{10,2},{16,24},{18,10},{24,28},{26,18},{28,20},... | collective-permute-start | bytes 1966088 | tf_op jit(solution)/shard_map/ppermute | solution.py:682
  219.7 26.7 %collective-permute-start.49 = (bf16[256,1280]{1,0:T(8,128)(2,1)S(1)}, bf16[256,1280]{1,0:T(8,128)(2,1)}, u32[]{:S(2)}, u32[]{:S(2)}) collective-permute-start(bf16[256,1280]{1,0:T(8,128)(2,1)S(1)} %reduce_end.1.refs_3_.refs_1_), channel_id=1, source_target_pairs={{0,8},{2,6},{8,16},{10,2},{16,24},{18,10},{24,28},{26,18},{28,20},... | collective-permute-start | bytes 1966088 | tf_op jit(solution)/shard_map/ppermute | solution.py:682
  224.6 21.0 %collective-permute-start.53 = (bf16[512,640]{1,0:T(8,128)(2,1)}, bf16[512,640]{1,0:T(8,128)(2,1)S(1)}, u32[]{:S(2)}, u32[]{:S(2)}) collective-permute-start(bf16[512,640]{1,0:T(8,128)(2,1)} %collective-permute-done.46.refs_4_.refs_3_), channel_id=1, source_target_pairs={{0,8},{2,6},{8,16},{10,2},{16,24},{18,10},{24,28},{26,18},{28,20},... | collective-permute-start | bytes 1966088 | tf_op jit(solution)/shard_map/ppermute | solution.py:682
  233.1 19.6 %collective-permute-start.44 = (bf16[256,1280]{1,0:T(8,128)(2,1)}, bf16[256,1280]{1,0:T(8,128)(2,1)}, u32[]{:S(2)}, u32[]{:S(2)}) collective-permute-start(bf16[256,1280]{1,0:T(8,128)(2,1)} %reduce_step.14.refs_3_), channel_id=1, source_target_pairs={{0,8},{2,6},{8,16},{10,2},{16,24},{18,10},{24,28},{26,18},{28,20},... | collective-permute-start | bytes 1966088 | tf_op jit(solution)/shard_map/ppermute | solution.py:682
  233.8 24.2 %collective-permute-start.54 = (bf16[512,640]{1,0:T(8,128)(2,1)S(1)}, bf16[512,640]{1,0:T(8,128)(2,1)}, u32[]{:S(2)}, u32[]{:S(2)}) collective-permute-start(bf16[512,640]{1,0:T(8,128)(2,1)S(1)} %collective-permute-done.45.refs_2_), channel_id=1, source_target_pairs={{0,2},{2,0},{4,6},{6,4},{8,10},{10,8},{12,14},{14,12},{16,18},{18,... | collective-permute-start | bytes 1966088 | tf_op jit(solution)/shard_map/ppermute | solution.py:685
  233.8 30.2 %collective-permute-start.55 = (bf16[512,640]{1,0:T(8,128)(2,1)}, bf16[512,640]{1,0:T(8,128)(2,1)}, u32[]{:S(2)}, u32[]{:S(2)}) collective-permute-start(bf16[512,640]{1,0:T(8,128)(2,1)} %collective-permute-done.46.refs_4_.refs_3_), channel_id=1, source_target_pairs={{0,2},{2,0},{4,6},{6,4},{8,10},{10,8},{12,14},{14,12},{16,18},{18,... | collective-permute-start | bytes 1966088 | tf_op jit(solution)/shard_map/ppermute | solution.py:685
  245.6 12.3 %collective-permute-start.57 = (bf16[256,640]{1,0:T(8,128)(2,1)S(1)}, bf16[256,640]{1,0:T(8,128)(2,1)S(1)}, u32[]{:S(2)}, u32[]{:S(2)}) collective-permute-start(bf16[256,640]{1,0:T(8,128)(2,1)S(1)} %constant_dynamic-slice_fusion.1), channel_id=1, source_target_pairs={{0,8},{2,6},{8,16},{10,2},{16,24},{18,10},{24,28},{26,18},{28,20},... | collective-permute-start | bytes 983048 | tf_op jit(solution)/shard_map/ppermute | solution.py:682
  246.4 16.9 %collective-permute-start.50 = (bf16[256,1280]{1,0:T(8,128)(2,1)}, bf16[256,1280]{1,0:T(8,128)(2,1)}, u32[]{:S(2)}, u32[]{:S(2)}) collective-permute-start(bf16[256,1280]{1,0:T(8,128)(2,1)} %collective-permute-done.49.refs_2_), channel_id=1, source_target_pairs={{0,8},{2,6},{8,16},{10,2},{16,24},{18,10},{24,28},{26,18},{28,20},... | collective-permute-start | bytes 1966088 | tf_op jit(solution)/shard_map/ppermute | solution.py:682
  257.2 13.0 %collective-permute-start.47 = (bf16[256,1280]{1,0:T(8,128)(2,1)}, bf16[256,1280]{1,0:T(8,128)(2,1)}, u32[]{:S(2)}, u32[]{:S(2)}) collective-permute-start(bf16[256,1280]{1,0:T(8,128)(2,1)} %reduce_step.15), channel_id=1, source_target_pairs={{0,8},{2,6},{8,16},{10,2},{16,24},{18,10},{24,28},{26,18},{28,20},... | collective-permute-start | bytes 1966088 | tf_op jit(solution)/shard_map/ppermute | solution.py:682
  258.0 12.3 %collective-permute-start.56 = (bf16[512,640]{1,0:T(8,128)(2,1)S(1)}, bf16[512,640]{1,0:T(8,128)(2,1)}, u32[]{:S(2)}, u32[]{:S(2)}) collective-permute-start(bf16[512,640]{1,0:T(8,128)(2,1)S(1)} %collective-permute-done.53.refs_4_), channel_id=1, source_target_pairs={{0,2},{2,0},{4,6},{6,4},{8,10},{10,8},{12,14},{14,12},{16,18},{18,... | collective-permute-start | bytes 1966088 | tf_op jit(solution)/shard_map/ppermute | solution.py:685
  263.2 14.6 %collective-permute-start.59 = (bf16[256,1280]{1,0:T(8,128)(2,1)}, bf16[256,1280]{1,0:T(8,128)(2,1)S(1)}, u32[]{:S(2)}, u32[]{:S(2)}) collective-permute-start(bf16[256,1280]{1,0:T(8,128)(2,1)} %collective-permute-done.50.refs_3_.refs_7_), channel_id=1, source_target_pairs={{0,8},{2,6},{8,16},{10,2},{16,24},{18,10},{24,28},{26,18},{28,20},... | collective-permute-start | bytes 1966088 | tf_op jit(solution)/shard_map/ppermute | solution.py:682
  263.9 14.7 %collective-permute-start.51 = (bf16[256,1280]{1,0:T(8,128)(2,1)}, bf16[256,1280]{1,0:T(8,128)(2,1)S(1)}, u32[]{:S(2)}, u32[]{:S(2)}) collective-permute-start(bf16[256,1280]{1,0:T(8,128)(2,1)} %collective-permute-done.49.refs_2_), channel_id=1, source_target_pairs={{0,2},{2,0},{4,6},{6,4},{8,10},{10,8},{12,14},{14,12},{16,18},{18,... | collective-permute-start | bytes 1966088 | tf_op jit(solution)/shard_map/ppermute | solution.py:685
  264.0 14.7 %collective-permute-start.52 = (bf16[256,1280]{1,0:T(8,128)(2,1)}, bf16[256,1280]{1,0:T(8,128)(2,1)S(1)}, u32[]{:S(2)}, u32[]{:S(2)}) collective-permute-start(bf16[256,1280]{1,0:T(8,128)(2,1)} %collective-permute-done.50.refs_3_.refs_7_), channel_id=1, source_target_pairs={{0,2},{2,0},{4,6},{6,4},{8,10},{10,8},{12,14},{14,12},{16,18},{18,... | collective-permute-start | bytes 1966088 | tf_op jit(solution)/shard_map/ppermute | solution.py:685
  270.3 13.0 %collective-permute-start.48 = (bf16[256,1280]{1,0:T(8,128)(2,1)}, bf16[256,1280]{1,0:T(8,128)(2,1)S(1)}, u32[]{:S(2)}, u32[]{:S(2)}) collective-permute-start(bf16[256,1280]{1,0:T(8,128)(2,1)} %collective-permute-done.47.refs_2_), channel_id=1, source_target_pairs={{0,2},{2,0},{4,6},{6,4},{8,10},{10,8},{12,14},{14,12},{16,18},{18,... | collective-permute-start | bytes 1966088 | tf_op jit(solution)/shard_map/ppermute | solution.py:685
  (72 other events, 426.8 us)

commit v6 on v5

--- a/solution.py
+++ b/solution.py
@@ -1045,7 +1045,7 @@
         [f_own, from_sib, from_x, from_xs, swap_core(from_x), g_rows, g_sib, g_x, g_xs],
         name="pooled_grads",
         us=3,
-        mib=24,
+        mib=40,
     )
     received, done = reduce_step(partial, 0, (), ())
     if groups > 1:

time: 294 us -> 294 us (level)
  no operation moved by 1% of the time
where the time goes in v6:
time: 294 us; the launch traced here: 293 us
  Pallas kernels  109 us (37%)
  waiting for transfers between devices  109 us (37%)
  starting transfers between devices  51.5 us (18%)
  local copies, waits for them, and re-layouts  19.4 us (7%)
    pallas_call x38, Pallas kernels, call(): pl.pallas_call(run, out_shape=[jax.ShapeDtypeStruct(shape, kind) for shap...  109 us
    ppermute x16, waiting for transfers between devices, ring_by_core(): return lax.ppermute(a, 'ctx', pairs)  62.6 us
    ppermute x12, waiting for transfers between devices, swap_x(): return lax.ppermute(a, 'fsdp', [(0, 1), (1, 0)])  28.8 us
    unnamed x111, local copies, waits for them, and re-layouts  17.3 us
    ppermute x12, starting transfers between devices, swap_x(): return lax.ppermute(a, 'fsdp', [(0, 1), (1, 0)])  15 us
    ppermute x16, starting transfers between devices, ring_by_core(): return lax.ppermute(a, 'ctx', pairs)  12.7 us
    ppermute x8, starting transfers between devices, ring(): return lax.ppermute(a, 'ctx', pairs)  9.33 us
    all_to_all x2, waiting for transfers between devices, exchange(): return lax.all_to_all(a, 'ctx', 0, 0, axis_index_groups=which, tiled=True)  8.87 us
  transfers between devices with their start and end apart: 65, of which 27 were waited for; matrix products, arithmetic and copies ran while one was open for 2% of the time, Pallas kernels for 35%

profile of v6, /device:TPU:0, one launch (start us, length us, event | category | flops | bytes accessed | tf_op | source)
XLA Modules:
  0.0 292.6 jit_solution(7825393677151647778)
XLA Ops:
  0.6 3.0 %collective-permute-start.1 = (bf16[128,1280]{1,0:T(8,128)(2,1)}, bf16[128,1280]{1,0:T(8,128)(2,1)S(1)}, u32[]{:S(2)}, u32[]{:S(2)}) collective-permute-start(bf16[128,1280]{1,0:T(8,128)(2,1)} %bitcast.31), channel_id=1, source_target_pairs={{0,4},{2,6},{8,0},{10,2},{16,8},{18,10},{24,16},{26,18},{28,24},{3... | collective-permute-start | bytes 983048 | tf_op jit(solution)/shard_map/ppermute | solution.py:670
  4.4 3.2 %slab.1.refs_1_.refs_2_ = bf16[256,640]{1,0:T(8,128)(2,1)} custom-call(s32[4]{0:T(128)} %pad_add_fusion.1.refs_0_.refs_1_, bf16[640,1280]{1,0:T(8,128)(2,1)} %refs_2_.2, bf16[640,1280]{1,0:T(8,128)(2,1)} %refs_2_.2, bf16[640,1280]{1,0:T(8,128)(2,1)} %refs_4_.2, bf16[640,1280]{1,0:T(8,128)(2,1)} %refs_4_.2, bf16[640,1280]{1,0:T(8,128)(2,1)} %refs_6_.3, ...), custom_call_target="tpu_custom_call" | custom-call | flops 3449999872 | bytes 1 | tf_op jit(solution)/shard_map/slab/pallas_call | solution.py:76
  7.7 1.9 collective-permute-start.4
  9.8 1.8 collective-permute-done.1.refs_3_
  11.6 1.7 collective-permute-start.3
  13.7 4.8 %collective-permute-done.4.refs_1_ = bf16[256,640]{1,0:T(8,128)(2,1)S(1)} collective-permute-done((bf16[256,640]{1,0:T(8,128)(2,1)}, bf16[256,640]{1,0:T(8,128)(2,1)S(1)}, u32[]{:S(2)}, u32[]{:S(2)}) %collective-permute-start.4) | collective-permute-done | bytes 327712 | tf_op jit(solution)/shard_map/ppermute | solution.py:694
  18.5 5.6 %collective-permute-done.5.refs_2_.refs_5_.refs_0_ = bf16[128,1280]{1,0:T(8,128)(2,1)S(1)} collective-permute-done((bf16[128,1280]{1,0:T(8,128)(2,1)S(1)}, bf16[128,1280]{1,0:T(8,128)(2,1)S(1)}, u32[]{:S(2)}, u32[]{:S(2)}) %collective-permute-start.5) | collective-permute-done | bytes 327712 | tf_op jit(solution)/shard_map/ppermute | solution.py:694
  24.9 2.1 setup.1
  27.0 1.7 collective-permute-start.11
  29.1 1.6 collective-permute-start.14
  31.5 4.7 %project.2 = (bf16[8,128,1280]{2,1,0:T(8,128)(2,1)}, bf16[5,80,128]{2,1,0:T(8,128)(2,1)}, bf16[5,160,128]{2,1,0:T(8,128)(2,1)}, bf16[5,240,128]{2,1,0:T(8,128)(2,1)}, bf16[5,160,128]{2,1,0:T(8,128)(2,1)}) custom-call(s32[4]{0:T(128)} %pad_add_fusion.1.refs_0_.refs_1_, bf16[128,1280]{1,0:T(8,128)(2,1)} %bitcast.33, ...), custom_call_target="tpu_custom_call" | custom-call | flops 3449999872 | bytes 1 | tf_op jit(solution)/shard_map/project/pallas_call | solution.py:76
  39.6 1.6 collective-permute-start.13
  42.5 1.6 collective-permute-start.7
  47.2 4.7 %project.3 = (bf16[8,128,1280]{2,1,0:T(8,128)(2,1)}, bf16[3,80,128]{2,1,0:T(8,128)(2,1)}, bf16[3,160,128]{2,1,0:T(8,128)(2,1)}, bf16[3,240,128]{2,1,0:T(8,128)(2...) custom-call(s32[4]{0:T(128)} %pad_add_fusion.1.refs_0_.refs_1_, ...), custom_call_target="tpu_custom_call", output_to_operand_aliasing={{0}: (11, {})} | custom-call | flops 3449999872 | bytes 1 | tf_op jit(solution)/shard_map/project/pallas_call | solution.py:76
  53.3 1.6 collective-permute-start.17
  55.9 1.7 copy-done
  57.7 1.7 copy-done.1
  60.0 1.7 collective-permute-done.15.refs_13_.refs_3_
  63.9 19.0 %attention_forward.1 = (bf16[16,80,128]{2,1,0:T(8,128)(2,1)}, bf16[4,80,512]{2,1,0:T(8,128)(2,1)}, bf16[8,80,512]{2,1,0:T(8,128)(2,1)}, bf16[8,512,80]{2,1,0:T(8...) custom-call(s32[16,2]{1,0:T(8,128)} %gather_fusion, s32[16,2]{1,0:T(8,128)} %gather_fusion, ...), custom_call_target="tpu_custom_call" | custom-call | flops 23000000512 | bytes 1 | tf_op jit(solution)/shard_map/attention_forward/pallas_call | solution.py:76
  85.4 4.0 %all-to-all-start = ((bf16[16,80,128]{2,1,0:T(8,128)(2,1)}), bf16[16,80,128]{2,1,0:T(8,128)(2,1)S(1)}, u32[]{:S(2)}, u32[]{:S(2)}) async-start(bf16[16,80,128]{2,1,0:T(8,128)(2,1)} %copy-done.4), calls=%async_computation | async-start | bytes 655360 | tf_op jit(solution)/shard_map/all_to_all | solution.py:713
  89.4 9.9 %collective-permute-done.21.refs_1_ = bf16[320,1280]{1,0:T(8,128)(2,1)} collective-permute-done((bf16[320,1280]{1,0:T(8,128)(2,1)}, bf16[320,1280]{1,0:T(8,128)(2,1)}, u32[]{:S(2)}, u32[]{:S(2)}) %collective-permute-start.21) | collective-permute-done | bytes 819232 | tf_op jit(solution)/shard_map/ppermute | solution.py:694
  104.3 10.8 %row_part.1 = (bf16[128,1280]{1,0:T(8,128)(2,1)}, f32[128,1280]{1,0:T(8,128)}, bf16[1280,128]{1,0:T(8,128)(2,1)}, bf16[3776,128]{1,0:T(8,128)(2,1)}, bf16[3776,1...) custom-call(s32[4]{0:T(128)} %pad_add_fusion.1.refs_0_.refs_1_, bf16[1280,128]{1,0:T(8,128)(2,1)} %bitcast.25, ...), custom_call_target="tpu_custom_call" | custom-call | flops 11500000256 | bytes 1 | tf_op jit(solution)/shard_map/row_part/pallas_call | solution.py:76
  116.8 4.4 %all-to-all-start.1 = ((bf16[16,80,128]{2,1,0:T(8,128)(2,1)}), bf16[16,80,128]{2,1,0:T(8,128)(2,1)}, u32[]{:S(2)}, u32[]{:S(2)}) async-start(bf16[16,80,128]{2,1,0:T(8,128)(2,1)} %bitcast.23), calls=%async_computation.1 | async-start | bytes 655360 | tf_op jit(solution)/shard_map/all_to_all | solution.py:713
  124.7 7.7 %all-to-all-done.1.refs_5_ = bf16[16,80,128]{2,1,0:T(8,128)(2,1)} async-done(((bf16[16,80,128]{2,1,0:T(8,128)(2,1)}), bf16[16,80,128]{2,1,0:T(8,128)(2,1)}, u32[]{:S(2)}, u32[]{:S(2)}) %all-to-all-start.1) | async-done | bytes 327712 | tf_op jit(solution)/shard_map/all_to_all | solution.py:713
  132.3 24.4 %attention_backward.1 = (f32[8,160,256]{2,1,0:T(8,128)}, bf16[8,160,256]{2,1,0:T(8,128)(2,1)}, bf16[16,80,128]{2,1,0:T(8,128)(2,1)}, f32[80,512]{1,0:T(8,128)}) custom-call(s32[16,2]{1,0:T(8,128)} %copy-done.19, s32[8]{0:T(128)} %constant.102.clone.refs_1_, s32[8]{0:T(128)} %constant.103.clone.refs_2_, s32[4,1,512]{2,1,0:T(1,128)} %constant.99.clone.refs_5_.refs_3_, ...), custom_call_target="tpu_custom_call" | custom-call | flops 28750000128 | bytes 1 | tf_op jit(solution)/shard_map/attention_backward/pallas_call | solution.py:76
  161.2 3.2 %pooled_grads.1.refs_1_ = bf16[5,256,1280]{2,1,0:T(8,128)(2,1)S(1)} custom-call(bf16[3776,128]{1,0:T(8,128)(2,1)S(1)} %copy-done.44, bf16[3776,128]{1,0:T(8,128)(2,1)} %get-tuple-element.117.refs_1_, bf16[3776,128]{1,0:T(8,128)(2,1)} %get-tuple-element.118.refs_2_, bf16[1200,128]{1,0:T(8,128)(2,1)S(1)} %get-tuple-element.119.refs_3_, ...), custom_call_target="tpu_custom_call" | custom-call | flops 3449999872 | bytes 1 | tf_op jit(solution)/shard_map/pooled_grads/pallas_call | solution.py:76
  166.4 5.8 %collective-permute-done.34.refs_2_ = bf16[256,640]{1,0:T(8,128)(2,1)S(1)} collective-permute-done((bf16[256,640]{1,0:T(8,128)(2,1)S(1)}, bf16[256,640]{1,0:T(8,128)(2,1)S(1)}, u32[]{:S(2)}, u32[]{:S(2)}) %collective-permute-start.34) | collective-permute-done | bytes 327712 | tf_op jit(solution)/shard_map/ppermute | solution.py:682
  173.5 2.7 collective-permute-done.26.refs_4_
  176.2 1.9 join.1
  178.2 4.5 %qkv_grads.1 = (f32[256,640]{1,0:T(8,128)S(1)}, bf16[256,640]{1,0:T(8,128)(2,1)S(1)}) custom-call(s32[16]{0:T(128)S(1)} %fusion.1.refs_0_, s32[4]{0:T(128)S(1)} %copy-done.30, bf16[16,240,128]{2,1,0:T(8,128)(2,1)S(1)} %get-tuple-element.121.refs_2_.refs_1_, f32[80,512]{1,0:T(8,128)S(1)} %copy-done.47, bf16[8,128,1280]{2,1,0:T(8,128)(2,1)S(1)} %copy-done.1, ...), custom_call_target="tpu_custom_call" | custom-call | flops 5405000192 | bytes 1 | tf_op jit(solution)/shard_map/qkv_grads/pallas_call | solution.py:76
  185.7 2.5 products.1.refs_1_
  188.8 4.1 %collective-permute-done.38.refs_1_ = bf16[256,640]{1,0:T(8,128)(2,1)S(1)} collective-permute-done((bf16[256,640]{1,0:T(8,128)(2,1)S(1)}, bf16[256,640]{1,0:T(8,128)(2,1)S(1)}, u32[]{:S(2)}, u32[]{:S(2)}) %collective-permute-start.38) | collective-permute-done | bytes 327712 | tf_op jit(solution)/shard_map/ppermute | solution.py:694
  193.1 2.5 collective-permute-done.40.refs_2_
  199.3 7.6 %collective-permute-done.42.refs_2_ = bf16[256,1280]{1,0:T(8,128)(2,1)S(1)} collective-permute-done((bf16[256,1280]{1,0:T(8,128)(2,1)S(1)}, bf16[256,1280]{1,0:T(8,128)(2,1)S(1)}, u32[]{:S(2)}, u32[]{:S(2)}) %collective-permute-start.42) | collective-permute-done | bytes 655392 | tf_op jit(solution)/shard_map/ppermute | solution.py:682
  206.9 7.0 %collective-permute-done.45.refs_2_ = bf16[512,640]{1,0:T(8,128)(2,1)S(1)} collective-permute-done((bf16[512,640]{1,0:T(8,128)(2,1)S(1)}, bf16[512,640]{1,0:T(8,128)(2,1)S(1)}, u32[]{:S(2)}, u32[]{:S(2)}) %collective-permute-start.45) | collective-permute-done | bytes 655392 | tf_op jit(solution)/shard_map/ppermute | solution.py:682
  214.6 2.8 collective-permute-done.37.refs_2_
  220.9 3.7 %collective-permute-done.46.refs_4_.refs_3_ = bf16[512,640]{1,0:T(8,128)(2,1)} collective-permute-done((bf16[512,640]{1,0:T(8,128)(2,1)S(1)}, bf16[512,640]{1,0:T(8,128)(2,1)}, u32[]{:S(2)}, u32[]{:S(2)}) %collective-permute-start.46) | collective-permute-done | bytes 655392 | tf_op jit(solution)/shard_map/ppermute | solution.py:682
  225.3 6.2 %collective-permute-done.41.refs_2_ = bf16[256,1280]{1,0:T(8,128)(2,1)S(1)} collective-permute-done((bf16[256,1280]{1,0:T(8,128)(2,1)S(1)}, bf16[256,1280]{1,0:T(8,128)(2,1)S(1)}, u32[]{:S(2)}, u32[]{:S(2)}) %collective-permute-start.41) | collective-permute-done | bytes 655392 | tf_op jit(solution)/shard_map/ppermute | solution.py:682
  234.3 11.3 %collective-permute-done.53.refs_4_ = bf16[512,640]{1,0:T(8,128)(2,1)S(1)} collective-permute-done((bf16[512,640]{1,0:T(8,128)(2,1)}, bf16[512,640]{1,0:T(8,128)(2,1)S(1)}, u32[]{:S(2)}, u32[]{:S(2)}) %collective-permute-start.53) | collective-permute-done | bytes 655392 | tf_op jit(solution)/shard_map/ppermute | solution.py:682
  247.6 5.1 %collective-permute-done.44.refs_2_ = bf16[256,1280]{1,0:T(8,128)(2,1)} collective-permute-done((bf16[256,1280]{1,0:T(8,128)(2,1)}, bf16[256,1280]{1,0:T(8,128)(2,1)}, u32[]{:S(2)}, u32[]{:S(2)}) %collective-permute-start.44) | collective-permute-done | bytes 655392 | tf_op jit(solution)/shard_map/ppermute | solution.py:682
  252.7 1.9 copy-done.41
  254.6 2.6 reduce_step.15
  258.5 4.8 %collective-permute-done.50.refs_3_.refs_7_ = bf16[256,1280]{1,0:T(8,128)(2,1)} collective-permute-done((bf16[256,1280]{1,0:T(8,128)(2,1)}, bf16[256,1280]{1,0:T(8,128)(2,1)}, u32[]{:S(2)}, u32[]{:S(2)}) %collective-permute-start.50) | collective-permute-done | bytes 655392 | tf_op jit(solution)/shard_map/ppermute | solution.py:682
  264.5 5.8 %collective-permute-done.47.refs_2_ = bf16[256,1280]{1,0:T(8,128)(2,1)} collective-permute-done((bf16[256,1280]{1,0:T(8,128)(2,1)}, bf16[256,1280]{1,0:T(8,128)(2,1)}, u32[]{:S(2)}, u32[]{:S(2)}) %collective-permute-start.47) | collective-permute-done | bytes 655392 | tf_op jit(solution)/shard_map/ppermute | solution.py:682
  270.3 7.5 %qkv_place.1 = (f32[640,1280]{1,0:T(8,128)}, f32[640,1280]{1,0:T(8,128)}, f32[640,1280]{1,0:T(8,128)}, f32[640]{0:T(1024)}, f32[40]{0:T(128)}) custom-call(s32[4]{0:T(128)S(1)} %copy-done.30, bf16[512,640]{1,0:T(8,128)(2,1)S(1)} %chip_pack.1.refs_3_.refs_4_.refs_1_, bf16[512,640]{1,0:T(8,128)(2,1)S(1)} %collective-permute-done.45.refs_2_, ...), custom_call_target="tpu_custom_call" | custom-call | flops 6899999744 | bytes 1 | tf_op jit(solution)/shard_map/qkv_place/pallas_call | solution.py:76
  278.7 4.5 %rows_place.2 = (f32[640,1280]{1,0:T(8,128)}, f32[640,1280]{1,0:T(8,128)}, f32[640,1280]{1,0:T(8,128)}, f32[640,128]{1,0:T(8,128)S(1)}, f32[8,128]{1,0:T(8,128)S(1)}) custom-call(s32[4]{0:T(128)S(1)} %copy-done.30, bf16[256,1280]{1,0:T(8,128)(2,1)S(1)} %copy-done.33, bf16[256,1280]{1,0:T(8,128)(2,1)} %collective-permute-done.49.refs_2_, ...), custom_call_target="tpu_custom_call" | custom-call | flops 4600000000 | bytes 1 | tf_op jit(solution)/shard_map/rows_place/pallas_call | solution.py:76
  283.3 3.0 %inputs_grad.1.refs_2_ = bf16[128,1280]{1,0:T(8,128)(2,1)} custom-call(s32[4]{0:T(128)S(1)} %copy-done.30, bf16[5,256,1280]{2,1,0:T(8,128)(2,1)S(1)} %copy-done.42, bf16[256,1280]{1,0:T(8,128)(2,1)} %collective-permute-done.47.refs_2_, bf16[256,1280]{1,0:T(8,128)(2,1)S(1)} %collective-permute-done.48.refs_3_, bf16[128,1280]{1,0:T(8,128)(2,1)S(1)} %bitcast.35, ...), custom_call_target="tpu_custom_call" | custom-call | flops 2300000000 | bytes 1 | tf_op jit(solution)/shard_map/inputs_grad/pallas_call | solution.py:76
  289.0 3.4 %rows_place.3 = (f32[640,1280]{1,0:T(8,128)}, f32[640,1280]{1,0:T(8,128)}, f32[640,1280]{1,0:T(8,128)}, f32[640]{0:T(1024)}, f32[2]{0:T(128)}) custom-call(s32[4]{0:T(128)S(1)} %copy-done.30, bf16[256,1280]{1,0:T(8,128)(2,1)S(1)} %collective-permute-done.59.refs_1_, ...), custom_call_target="tpu_custom_call", output_to_operand_aliasing={{0}: (9, {}), {1}: (10, {}), {2}: (11, {})} | custom-call | flops 3449999872 | bytes 1 | tf_op jit(solution)/shard_map/rows_place/pallas_call | solution.py:76
  (246 shorter events, 59.9 us)
Async XLA Ops:
  0.6 11.0 %collective-permute-start.1 = (bf16[128,1280]{1,0:T(8,128)(2,1)}, bf16[128,1280]{1,0:T(8,128)(2,1)S(1)}, u32[]{:S(2)}, u32[]{:S(2)}) collective-permute-start(bf16[128,1280]{1,0:T(8,128)(2,1)} %bitcast.31), channel_id=1, source_target_pairs={{0,4},{2,6},{8,0},{10,2},{16,8},{18,10},{24,16},{26,18},{28,24},{3... | collective-permute-start | bytes 983048 | tf_op jit(solution)/shard_map/ppermute | solution.py:670
  3.7 9.7 %collective-permute-start = (bf16[128,1280]{1,0:T(8,128)(2,1)}, bf16[128,1280]{1,0:T(8,128)(2,1)}, u32[]{:S(2)}, u32[]{:S(2)}) collective-permute-start(bf16[128,1280]{1,0:T(8,128)(2,1)} %bitcast.32), channel_id=1, source_target_pairs={{0,8},{2,10},{8,16},{10,18},{16,24},{18,26},{24,28},{26,30},{28,20... | collective-permute-start | bytes 983048 | tf_op jit(solution)/shard_map/ppermute | solution.py:670
  7.7 10.8 %collective-permute-start.4 = (bf16[256,640]{1,0:T(8,128)(2,1)}, bf16[256,640]{1,0:T(8,128)(2,1)S(1)}, u32[]{:S(2)}, u32[]{:S(2)}) collective-permute-start(bf16[256,640]{1,0:T(8,128)(2,1)} %slab.1.refs_1_.refs_2_), channel_id=1, source_target_pairs={{0,1},{1,0},{2,3},{3,2},{4,5},{5,4},{6,7},{7,6},{8,9},{9,8},{10,11... | collective-permute-start | bytes 983048 | tf_op jit(solution)/shard_map/ppermute | solution.py:694
  9.6 14.5 %collective-permute-start.5 = (bf16[128,1280]{1,0:T(8,128)(2,1)S(1)}, bf16[128,1280]{1,0:T(8,128)(2,1)S(1)}, u32[]{:S(2)}, u32[]{:S(2)}) collective-permute-start(bf16[128,1280]{1,0:T(8,128)(2,1)S(1)} %constant_dynamic-slice_fusion.3), channel_id=1, source_target_pairs={{0,1},{1,0},{2,3},{3,2},{4,5},{5,4},{6,7},{7,6},{8,9},{9,8},{10,11... | collective-permute-start | bytes 983048 | tf_op jit(solution)/shard_map/ppermute | solution.py:694
  11.6 13.2 %collective-permute-start.3 = (bf16[128,1280]{1,0:T(8,128)(2,1)S(1)}, bf16[128,1280]{1,0:T(8,128)(2,1)}, u32[]{:S(2)}, u32[]{:S(2)}) collective-permute-start(bf16[128,1280]{1,0:T(8,128)(2,1)S(1)} %collective-permute-done.1.refs_3_), channel_id=1, source_target_pairs={{0,4},{2,6},{8,0},{10,2},{16,8},{18,10},{24,16},{26,18},{28,24},{3... | collective-permute-start | bytes 983048 | tf_op jit(solution)/shard_map/ppermute | solution.py:670
  13.3 11.5 %collective-permute-start.2 = (bf16[128,1280]{1,0:T(8,128)(2,1)}, bf16[128,1280]{1,0:T(8,128)(2,1)}, u32[]{:S(2)}, u32[]{:S(2)}) collective-permute-start(bf16[128,1280]{1,0:T(8,128)(2,1)} %collective-permute-done.refs_2_), channel_id=1, source_target_pairs={{0,8},{2,10},{8,16},{10,18},{16,24},{18,26},{24,28},{26,30},{28,20... | collective-permute-start | bytes 983048 | tf_op jit(solution)/shard_map/ppermute | solution.py:670
  27.0 10.3 %collective-permute-start.11 = (bf16[128,1280]{1,0:T(8,128)(2,1)}, bf16[128,1280]{1,0:T(8,128)(2,1)S(1)}, u32[]{:S(2)}, u32[]{:S(2)}) collective-permute-start(bf16[128,1280]{1,0:T(8,128)(2,1)} %collective-permute-done.3.refs_4_.refs_5_), channel_id=1, source_target_pairs={{0,4},{2,6},{8,0},{10,2},{16,8},{18,10},{24,16},{26,18},{28,24},{3... | collective-permute-start | bytes 983048 | tf_op jit(solution)/shard_map/ppermute | solution.py:670
  28.7 10.0 %collective-permute-start.10 = (bf16[128,1280]{1,0:T(8,128)(2,1)}, bf16[128,1280]{1,0:T(8,128)(2,1)S(1)}, u32[]{:S(2)}, u32[]{:S(2)}) collective-permute-start(bf16[128,1280]{1,0:T(8,128)(2,1)} %collective-permute-done.2.refs_3_.refs_4_), channel_id=1, source_target_pairs={{0,8},{2,10},{8,16},{10,18},{16,24},{18,26},{24,28},{26,30},{28,20... | collective-permute-start | bytes 983048 | tf_op jit(solution)/shard_map/ppermute | solution.py:670
  29.1 14.9 %collective-permute-start.14 = (bf16[192,1280]{1,0:T(8,128)(2,1)S(1)}, bf16[192,1280]{1,0:T(8,128)(2,1)}, u32[]{:S(2)}, u32[]{:S(2)}) collective-permute-start(bf16[192,1280]{1,0:T(8,128)(2,1)S(1)} %get-tuple-element.89), channel_id=1, source_target_pairs={{0,1},{1,0},{2,3},{3,2},{4,5},{5,4},{6,7},{7,6},{8,9},{9,8},{10,11... | collective-permute-start | bytes 1474568 | tf_op jit(solution)/shard_map/ppermute | solution.py:694
  42.4 12.5 %collective-permute-start.9 = (bf16[5,160,128]{2,1,0:T(8,128)(2,1)}, bf16[5,160,128]{2,1,0:T(8,128)(2,1)S(1)}, u32[]{:S(2)}, u32[]{:S(2)}) collective-permute-start(bf16[5,160,128]{2,1,0:T(8,128)(2,1)} %get-tuple-element.85), channel_id=1, source_target_pairs={{0,3},{1,2},{2,1},{3,0},{4,7},{5,6},{6,5},{7,4},{8,11},{9,10},{10,... | collective-permute-start | bytes 614408 | tf_op jit(solution)/shard_map/ppermute | solution.py:691
  42.5 16.9 %collective-permute-start.7 = (bf16[5,160,128]{2,1,0:T(8,128)(2,1)}, bf16[5,160,128]{2,1,0:T(8,128)(2,1)S(1)}, u32[]{:S(2)}, u32[]{:S(2)}) collective-permute-start(bf16[5,160,128]{2,1,0:T(8,128)(2,1)} %get-tuple-element.83.refs_7_), channel_id=1, source_target_pairs={{0,1},{1,0},{2,3},{3,2},{4,5},{5,4},{6,7},{7,6},{8,9},{9,8},{10,11... | collective-permute-start | bytes 614408 | tf_op jit(solution)/shard_map/ppermute | solution.py:694
  44.0 19.2 %collective-permute-start.8 = (bf16[5,240,128]{2,1,0:T(8,128)(2,1)}, bf16[5,240,128]{2,1,0:T(8,128)(2,1)}, u32[]{:S(2)}, u32[]{:S(2)}) collective-permute-start(bf16[5,240,128]{2,1,0:T(8,128)(2,1)} %get-tuple-element.84), channel_id=1, source_target_pairs={{0,2},{2,0},{4,6},{6,4},{8,10},{10,8},{12,14},{14,12},{16,18},{18,... | collective-permute-start | bytes 921608 | tf_op jit(solution)/shard_map/ppermute | solution.py:685
  51.9 11.9 %collective-permute-start.16 = (bf16[3,240,128]{2,1,0:T(8,128)(2,1)}, bf16[3,240,128]{2,1,0:T(8,128)(2,1)}, u32[]{:S(2)}, u32[]{:S(2)}) collective-permute-start(bf16[3,240,128]{2,1,0:T(8,128)(2,1)} %get-tuple-element.92), channel_id=1, source_target_pairs={{0,2},{2,0},{4,6},{6,4},{8,10},{10,8},{12,14},{14,12},{16,18},{18,... | collective-permute-start | bytes 552968 | tf_op jit(solution)/shard_map/ppermute | solution.py:685
  59.4 23.5 %collective-permute-start.18 = (bf16[128,1280]{1,0:T(8,128)(2,1)S(1)}, bf16[128,1280]{1,0:T(8,128)(2,1)}, u32[]{:S(2)}, u32[]{:S(2)}) collective-permute-start(bf16[128,1280]{1,0:T(8,128)(2,1)S(1)} %gate.14.refs_6_), channel_id=1, source_target_pairs={{0,2},{2,0},{4,6},{6,4},{8,10},{10,8},{12,14},{14,12},{16,18},{18,... | collective-permute-start | bytes 983048 | tf_op jit(solution)/shard_map/ppermute | solution.py:685
  59.5 23.4 %collective-permute-start.19 = (bf16[192,1280]{1,0:T(8,128)(2,1)}, bf16[192,1280]{1,0:T(8,128)(2,1)S(1)}, u32[]{:S(2)}, u32[]{:S(2)}) collective-permute-start(bf16[192,1280]{1,0:T(8,128)(2,1)} %gate.15.refs_8_), channel_id=1, source_target_pairs={{0,2},{2,0},{4,6},{6,4},{8,10},{10,8},{12,14},{14,12},{16,18},{18,... | collective-permute-start | bytes 1474568 | tf_op jit(solution)/shard_map/ppermute | solution.py:685
  61.7 27.6 %collective-permute-start.20 = (bf16[320,1280]{1,0:T(8,128)(2,1)}, bf16[320,1280]{1,0:T(8,128)(2,1)}, u32[]{:S(2)}, u32[]{:S(2)}) collective-permute-start(bf16[320,1280]{1,0:T(8,128)(2,1)} %gate.17), channel_id=1, source_target_pairs={{0,1},{1,0},{2,3},{3,2},{4,5},{5,4},{6,7},{7,6},{8,9},{9,8},{10,11... | collective-permute-start | bytes 2457608 | tf_op jit(solution)/shard_map/ppermute | solution.py:694
  63.2 36.0 %collective-permute-start.21 = (bf16[320,1280]{1,0:T(8,128)(2,1)}, bf16[320,1280]{1,0:T(8,128)(2,1)}, u32[]{:S(2)}, u32[]{:S(2)}) collective-permute-start(bf16[320,1280]{1,0:T(8,128)(2,1)} %gate.18), channel_id=1, source_target_pairs={{0,1},{1,0},{2,3},{3,2},{4,5},{5,4},{6,7},{7,6},{8,9},{9,8},{10,11... | collective-permute-start | bytes 2457608 | tf_op jit(solution)/shard_map/ppermute | solution.py:694
  85.4 15.1 %all-to-all-start = ((bf16[16,80,128]{2,1,0:T(8,128)(2,1)}), bf16[16,80,128]{2,1,0:T(8,128)(2,1)S(1)}, u32[]{:S(2)}, u32[]{:S(2)}) async-start(bf16[16,80,128]{2,1,0:T(8,128)(2,1)} %copy-done.4), calls=%async_computation | async-start | bytes 655360 | tf_op jit(solution)/shard_map/all_to_all | solution.py:713
  102.0 13.1 %collective-permute-start.24 = (bf16[128,1280]{1,0:T(8,128)(2,1)S(1)}, bf16[128,1280]{1,0:T(8,128)(2,1)S(1)}, u32[]{:S(2)}, u32[]{:S(2)}) collective-permute-start(bf16[128,1280]{1,0:T(8,128)(2,1)S(1)} %gate.20), channel_id=1, source_target_pairs={{0,1},{1,0},{2,3},{3,2},{4,5},{5,4},{6,7},{7,6},{8,9},{9,8},{10,11... | collective-permute-start | bytes 983048 | tf_op jit(solution)/shard_map/ppermute | solution.py:694
  116.8 15.5 %all-to-all-start.1 = ((bf16[16,80,128]{2,1,0:T(8,128)(2,1)}), bf16[16,80,128]{2,1,0:T(8,128)(2,1)}, u32[]{:S(2)}, u32[]{:S(2)}) async-start(bf16[16,80,128]{2,1,0:T(8,128)(2,1)} %bitcast.23), calls=%async_computation.1 | async-start | bytes 655360 | tf_op jit(solution)/shard_map/all_to_all | solution.py:713
  121.4 35.3 %collective-permute-start.31 = (bf16[8,128,1280]{2,1,0:T(8,128)(2,1)S(1)}, bf16[8,128,1280]{2,1,0:T(8,128)(2,1)}, u32[]{:S(2)}, u32[]{:S(2)}) collective-permute-start(bf16[8,128,1280]{2,1,0:T(8,128)(2,1)S(1)} %copy-done.1), channel_id=1, source_target_pairs={{0,2},{2,0},{4,6},{6,4},{8,10},{10,8},{12,14},{14,12},{16,18},{18,... | collective-permute-start | bytes 7864328 | tf_op jit(solution)/shard_map/ppermute | solution.py:685
  121.8 35.0 %collective-permute-start.30 = (bf16[128,1280]{1,0:T(8,128)(2,1)}, bf16[128,1280]{1,0:T(8,128)(2,1)S(1)}, u32[]{:S(2)}, u32[]{:S(2)}) collective-permute-start(bf16[128,1280]{1,0:T(8,128)(2,1)} %copy-done.26), channel_id=1, source_target_pairs={{0,2},{2,0},{4,6},{6,4},{8,10},{10,8},{12,14},{14,12},{16,18},{18,... | collective-permute-start | bytes 983048 | tf_op jit(solution)/shard_map/ppermute | solution.py:685
  122.0 34.8 %collective-permute-start.27 = (bf16[3776,128]{1,0:T(8,128)(2,1)}, bf16[3776,128]{1,0:T(8,128)(2,1)}, u32[]{:S(2)}, u32[]{:S(2)}) collective-permute-start(bf16[3776,128]{1,0:T(8,128)(2,1)} %get-tuple-element.114), channel_id=1, source_target_pairs={{0,1},{1,0},{2,3},{3,2},{4,5},{5,4},{6,7},{7,6},{8,9},{9,8},{10,11... | collective-permute-start | bytes 2899976 | tf_op jit(solution)/shard_map/ppermute | solution.py:694
  123.4 33.4 %collective-permute-start.28 = (bf16[3776,128]{1,0:T(8,128)(2,1)}, bf16[3776,128]{1,0:T(8,128)(2,1)}, u32[]{:S(2)}, u32[]{:S(2)}) collective-permute-start(bf16[3776,128]{1,0:T(8,128)(2,1)} %get-tuple-element.115), channel_id=1, source_target_pairs={{0,2},{2,0},{4,6},{6,4},{8,10},{10,8},{12,14},{14,12},{16,18},{18,... | collective-permute-start | bytes 2899976 | tf_op jit(solution)/shard_map/ppermute | solution.py:685
  123.5 33.3 %collective-permute-start.29 = (bf16[1200,128]{1,0:T(8,128)(2,1)}, bf16[1200,128]{1,0:T(8,128)(2,1)S(1)}, u32[]{:S(2)}, u32[]{:S(2)}) collective-permute-start(bf16[1200,128]{1,0:T(8,128)(2,1)} %collective-permute-done.25.refs_12_), channel_id=1, source_target_pairs={{0,1},{1,0},{2,3},{3,2},{4,5},{5,4},{6,7},{7,6},{8,9},{9,8},{10,11... | collective-permute-start | bytes 921608 | tf_op jit(solution)/shard_map/ppermute | solution.py:694
  159.3 16.9 %collective-permute-start.26 = (bf16[8,160,256]{2,1,0:T(8,128)(2,1)S(1)}, bf16[8,160,256]{2,1,0:T(8,128)(2,1)S(1)}, u32[]{:S(2)}, u32[]{:S(2)}) collective-permute-start(bf16[8,160,256]{2,1,0:T(8,128)(2,1)S(1)} %copy-done.51), channel_id=1, source_target_pairs={{0,1},{1,0},{2,3},{3,2},{4,5},{5,4},{6,7},{7,6},{8,9},{9,8},{10,11... | collective-permute-start | bytes 1966088 | tf_op jit(solution)/shard_map/ppermute | solution.py:694
  172.9 11.4 %collective-permute-start.36 = (bf16[256,1280]{1,0:T(8,128)(2,1)S(1)}, bf16[256,1280]{1,0:T(8,128)(2,1)S(1)}, u32[]{:S(2)}, u32[]{:S(2)}) collective-permute-start(bf16[256,1280]{1,0:T(8,128)(2,1)S(1)} %reduce_step.9.refs_5_), channel_id=1, source_target_pairs={{0,8},{2,6},{8,16},{10,2},{16,24},{18,10},{24,28},{26,18},{28,20},... | collective-permute-start | bytes 1966088 | tf_op jit(solution)/shard_map/ppermute | solution.py:682
  182.7 10.2 %collective-permute-start.38 = (bf16[256,640]{1,0:T(8,128)(2,1)S(1)}, bf16[256,640]{1,0:T(8,128)(2,1)S(1)}, u32[]{:S(2)}, u32[]{:S(2)}) collective-permute-start(bf16[256,640]{1,0:T(8,128)(2,1)S(1)} %get-tuple-element.126), channel_id=1, source_target_pairs={{0,1},{1,0},{2,3},{3,2},{4,5},{5,4},{6,7},{7,6},{8,9},{9,8},{10,11... | collective-permute-start | bytes 983048 | tf_op jit(solution)/shard_map/ppermute | solution.py:694
  184.9 10.6 %collective-permute-start.40 = (bf16[256,1280]{1,0:T(8,128)(2,1)S(1)}, bf16[256,1280]{1,0:T(8,128)(2,1)S(1)}, u32[]{:S(2)}, u32[]{:S(2)}) collective-permute-start(bf16[256,1280]{1,0:T(8,128)(2,1)S(1)} %reduce_step.10.refs_5_), channel_id=1, source_target_pairs={{0,8},{2,6},{8,16},{10,2},{16,24},{18,10},{24,28},{26,18},{28,20},... | collective-permute-start | bytes 1966088 | tf_op jit(solution)/shard_map/ppermute | solution.py:682
  196.3 10.6 %collective-permute-start.42 = (bf16[256,1280]{1,0:T(8,128)(2,1)S(1)}, bf16[256,1280]{1,0:T(8,128)(2,1)S(1)}, u32[]{:S(2)}, u32[]{:S(2)}) collective-permute-start(bf16[256,1280]{1,0:T(8,128)(2,1)S(1)} %reduce_step.12.refs_3_), channel_id=1, source_target_pairs={{0,8},{2,6},{8,16},{10,2},{16,24},{18,10},{24,28},{26,18},{28,20},... | collective-permute-start | bytes 1966088 | tf_op jit(solution)/shard_map/ppermute | solution.py:682
  197.6 16.3 %collective-permute-start.45 = (bf16[512,640]{1,0:T(8,128)(2,1)S(1)}, bf16[512,640]{1,0:T(8,128)(2,1)S(1)}, u32[]{:S(2)}, u32[]{:S(2)}) collective-permute-start(bf16[512,640]{1,0:T(8,128)(2,1)S(1)} %chip_pack.1.refs_3_.refs_4_.refs_1_), channel_id=1, source_target_pairs={{0,8},{2,6},{8,16},{10,2},{16,24},{18,10},{24,28},{26,18},{28,20},... | collective-permute-start | bytes 1966088 | tf_op jit(solution)/shard_map/ppermute | solution.py:682
  198.9 18.5 %collective-permute-start.37 = (bf16[256,640]{1,0:T(8,128)(2,1)S(1)}, bf16[256,640]{1,0:T(8,128)(2,1)S(1)}, u32[]{:S(2)}, u32[]{:S(2)}) collective-permute-start(bf16[256,640]{1,0:T(8,128)(2,1)S(1)} %reduce_step.11.refs_3_), channel_id=1, source_target_pairs={{0,8},{2,6},{8,16},{10,2},{16,24},{18,10},{24,28},{26,18},{28,20},... | collective-permute-start | bytes 983048 | tf_op jit(solution)/shard_map/ppermute | solution.py:682
  206.9 12.0 %collective-permute-start.43 = (bf16[256,1280]{1,0:T(8,128)(2,1)S(1)}, bf16[256,1280]{1,0:T(8,128)(2,1)S(1)}, u32[]{:S(2)}, u32[]{:S(2)}) collective-permute-start(bf16[256,1280]{1,0:T(8,128)(2,1)S(1)} %collective-permute-done.42.refs_2_), channel_id=1, source_target_pairs={{0,2},{2,0},{4,6},{6,4},{8,10},{10,8},{12,14},{14,12},{16,18},{18,... | collective-permute-start | bytes 1966088 | tf_op jit(solution)/shard_map/ppermute | solution.py:685
  213.9 10.7 %collective-permute-start.46 = (bf16[512,640]{1,0:T(8,128)(2,1)S(1)}, bf16[512,640]{1,0:T(8,128)(2,1)}, u32[]{:S(2)}, u32[]{:S(2)}) collective-permute-start(bf16[512,640]{1,0:T(8,128)(2,1)S(1)} %collective-permute-done.45.refs_2_), channel_id=1, source_target_pairs={{0,8},{2,6},{8,16},{10,2},{16,24},{18,10},{24,28},{26,18},{28,20},... | collective-permute-start | bytes 1966088 | tf_op jit(solution)/shard_map/ppermute | solution.py:682
  218.1 13.4 %collective-permute-start.41 = (bf16[256,1280]{1,0:T(8,128)(2,1)S(1)}, bf16[256,1280]{1,0:T(8,128)(2,1)S(1)}, u32[]{:S(2)}, u32[]{:S(2)}) collective-permute-start(bf16[256,1280]{1,0:T(8,128)(2,1)S(1)} %reduce_step.13), channel_id=1, source_target_pairs={{0,8},{2,6},{8,16},{10,2},{16,24},{18,10},{24,28},{26,18},{28,20},... | collective-permute-start | bytes 1966088 | tf_op jit(solution)/shard_map/ppermute | solution.py:682
  219.7 26.7 %collective-permute-start.49 = (bf16[256,1280]{1,0:T(8,128)(2,1)S(1)}, bf16[256,1280]{1,0:T(8,128)(2,1)}, u32[]{:S(2)}, u32[]{:S(2)}) collective-permute-start(bf16[256,1280]{1,0:T(8,128)(2,1)S(1)} %reduce_end.1.refs_3_.refs_1_), channel_id=1, source_target_pairs={{0,8},{2,6},{8,16},{10,2},{16,24},{18,10},{24,28},{26,18},{28,20},... | collective-permute-start | bytes 1966088 | tf_op jit(solution)/shard_map/ppermute | solution.py:682
  224.6 21.0 %collective-permute-start.53 = (bf16[512,640]{1,0:T(8,128)(2,1)}, bf16[512,640]{1,0:T(8,128)(2,1)S(1)}, u32[]{:S(2)}, u32[]{:S(2)}) collective-permute-start(bf16[512,640]{1,0:T(8,128)(2,1)} %collective-permute-done.46.refs_4_.refs_3_), channel_id=1, source_target_pairs={{0,8},{2,6},{8,16},{10,2},{16,24},{18,10},{24,28},{26,18},{28,20},... | collective-permute-start | bytes 1966088 | tf_op jit(solution)/shard_map/ppermute | solution.py:682
  233.1 19.6 %collective-permute-start.44 = (bf16[256,1280]{1,0:T(8,128)(2,1)}, bf16[256,1280]{1,0:T(8,128)(2,1)}, u32[]{:S(2)}, u32[]{:S(2)}) collective-permute-start(bf16[256,1280]{1,0:T(8,128)(2,1)} %reduce_step.14.refs_3_), channel_id=1, source_target_pairs={{0,8},{2,6},{8,16},{10,2},{16,24},{18,10},{24,28},{26,18},{28,20},... | collective-permute-start | bytes 1966088 | tf_op jit(solution)/shard_map/ppermute | solution.py:682
  233.8 24.2 %collective-permute-start.54 = (bf16[512,640]{1,0:T(8,128)(2,1)S(1)}, bf16[512,640]{1,0:T(8,128)(2,1)}, u32[]{:S(2)}, u32[]{:S(2)}) collective-permute-start(bf16[512,640]{1,0:T(8,128)(2,1)S(1)} %collective-permute-done.45.refs_2_), channel_id=1, source_target_pairs={{0,2},{2,0},{4,6},{6,4},{8,10},{10,8},{12,14},{14,12},{16,18},{18,... | collective-permute-start | bytes 1966088 | tf_op jit(solution)/shard_map/ppermute | solution.py:685
  233.8 30.2 %collective-permute-start.55 = (bf16[512,640]{1,0:T(8,128)(2,1)}, bf16[512,640]{1,0:T(8,128)(2,1)}, u32[]{:S(2)}, u32[]{:S(2)}) collective-permute-start(bf16[512,640]{1,0:T(8,128)(2,1)} %collective-permute-done.46.refs_4_.refs_3_), channel_id=1, source_target_pairs={{0,2},{2,0},{4,6},{6,4},{8,10},{10,8},{12,14},{14,12},{16,18},{18,... | collective-permute-start | bytes 1966088 | tf_op jit(solution)/shard_map/ppermute | solution.py:685
  245.6 12.3 %collective-permute-start.57 = (bf16[256,640]{1,0:T(8,128)(2,1)S(1)}, bf16[256,640]{1,0:T(8,128)(2,1)S(1)}, u32[]{:S(2)}, u32[]{:S(2)}) collective-permute-start(bf16[256,640]{1,0:T(8,128)(2,1)S(1)} %constant_dynamic-slice_fusion.1), channel_id=1, source_target_pairs={{0,8},{2,6},{8,16},{10,2},{16,24},{18,10},{24,28},{26,18},{28,20},... | collective-permute-start | bytes 983048 | tf_op jit(solution)/shard_map/ppermute | solution.py:682
  246.4 16.9 %collective-permute-start.50 = (bf16[256,1280]{1,0:T(8,128)(2,1)}, bf16[256,1280]{1,0:T(8,128)(2,1)}, u32[]{:S(2)}, u32[]{:S(2)}) collective-permute-start(bf16[256,1280]{1,0:T(8,128)(2,1)} %collective-permute-done.49.refs_2_), channel_id=1, source_target_pairs={{0,8},{2,6},{8,16},{10,2},{16,24},{18,10},{24,28},{26,18},{28,20},... | collective-permute-start | bytes 1966088 | tf_op jit(solution)/shard_map/ppermute | solution.py:682
  257.3 13.0 %collective-permute-start.47 = (bf16[256,1280]{1,0:T(8,128)(2,1)}, bf16[256,1280]{1,0:T(8,128)(2,1)}, u32[]{:S(2)}, u32[]{:S(2)}) collective-permute-start(bf16[256,1280]{1,0:T(8,128)(2,1)} %reduce_step.15), channel_id=1, source_target_pairs={{0,8},{2,6},{8,16},{10,2},{16,24},{18,10},{24,28},{26,18},{28,20},... | collective-permute-start | bytes 1966088 | tf_op jit(solution)/shard_map/ppermute | solution.py:682
  258.0 12.3 %collective-permute-start.56 = (bf16[512,640]{1,0:T(8,128)(2,1)S(1)}, bf16[512,640]{1,0:T(8,128)(2,1)}, u32[]{:S(2)}, u32[]{:S(2)}) collective-permute-start(bf16[512,640]{1,0:T(8,128)(2,1)S(1)} %collective-permute-done.53.refs_4_), channel_id=1, source_target_pairs={{0,2},{2,0},{4,6},{6,4},{8,10},{10,8},{12,14},{14,12},{16,18},{18,... | collective-permute-start | bytes 1966088 | tf_op jit(solution)/shard_map/ppermute | solution.py:685
  263.3 14.6 %collective-permute-start.59 = (bf16[256,1280]{1,0:T(8,128)(2,1)}, bf16[256,1280]{1,0:T(8,128)(2,1)S(1)}, u32[]{:S(2)}, u32[]{:S(2)}) collective-permute-start(bf16[256,1280]{1,0:T(8,128)(2,1)} %collective-permute-done.50.refs_3_.refs_7_), channel_id=1, source_target_pairs={{0,8},{2,6},{8,16},{10,2},{16,24},{18,10},{24,28},{26,18},{28,20},... | collective-permute-start | bytes 1966088 | tf_op jit(solution)/shard_map/ppermute | solution.py:682
  264.0 14.7 %collective-permute-start.51 = (bf16[256,1280]{1,0:T(8,128)(2,1)}, bf16[256,1280]{1,0:T(8,128)(2,1)S(1)}, u32[]{:S(2)}, u32[]{:S(2)}) collective-permute-start(bf16[256,1280]{1,0:T(8,128)(2,1)} %collective-permute-done.49.refs_2_), channel_id=1, source_target_pairs={{0,2},{2,0},{4,6},{6,4},{8,10},{10,8},{12,14},{14,12},{16,18},{18,... | collective-permute-start | bytes 1966088 | tf_op jit(solution)/shard_map/ppermute | solution.py:685
  264.0 14.7 %collective-permute-start.52 = (bf16[256,1280]{1,0:T(8,128)(2,1)}, bf16[256,1280]{1,0:T(8,128)(2,1)S(1)}, u32[]{:S(2)}, u32[]{:S(2)}) collective-permute-start(bf16[256,1280]{1,0:T(8,128)(2,1)} %collective-permute-done.50.refs_3_.refs_7_), channel_id=1, source_target_pairs={{0,2},{2,0},{4,6},{6,4},{8,10},{10,8},{12,14},{14,12},{16,18},{18,... | collective-permute-start | bytes 1966088 | tf_op jit(solution)/shard_map/ppermute | solution.py:685
  270.3 12.9 %collective-permute-start.48 = (bf16[256,1280]{1,0:T(8,128)(2,1)}, bf16[256,1280]{1,0:T(8,128)(2,1)S(1)}, u32[]{:S(2)}, u32[]{:S(2)}) collective-permute-start(bf16[256,1280]{1,0:T(8,128)(2,1)} %collective-permute-done.47.refs_2_), channel_id=1, source_target_pairs={{0,2},{2,0},{4,6},{6,4},{8,10},{10,8},{12,14},{14,12},{16,18},{18,... | collective-permute-start | bytes 1966088 | tf_op jit(solution)/shard_map/ppermute | solution.py:685
  (72 other events, 426.7 us)
